TPU v7x, 32 devices: a whole 2x2x4 slice. The times are simulated.
32 devices in a mesh: dp: 8 (over z, y), mp: 4 (over x, core).
Axes of the slice: x: 2, y: 2, z: 4, core: 2. Of those that a mesh axis runs over, the one named last changes fastest.
Arguments:
- tokens: bfloat16 [16384, 1152], P('dp'), may hold values from -6 to 6
- seg_ids: int32 [16384], P('dp'), may hold values from 0 to 15, as said below
- time_steps: int32 [16, 16], P('dp'), may hold values from 0 to 999
- cotangent: bfloat16 [16384, 1152], P('dp'), may hold values from -6 to 6
- weight_cols: float32 [15, 1152, 1152], P(None, 'dp', 'mp')
- weight_rows: float32 [5, 1152, 1152], P(None, 'mp', 'dp')
- bias_cols: float32 [12, 1152], P(None, 'mp'), may hold values from -3 to 3
- bias_rows: float32 [2, 1152], replicated, may hold values from -3 to 3
- first_cols: float32 [15, 1152, 1152], P(None, 'dp', 'mp'), may hold values from -80 to 80
- first_rows: float32 [5, 1152, 1152], P(None, 'mp', 'dp'), may hold values from -80 to 80
- first_bias_cols: float32 [12, 1152], P(None, 'mp'), may hold values from -80 to 80
- first_bias_rows: float32 [2, 1152], replicated, may hold values from -80 to 80
- second_cols: float32 [15, 1152, 1152], P(None, 'dp', 'mp'), may hold values from 16.384 to 65.536
- second_rows: float32 [5, 1152, 1152], P(None, 'mp', 'dp'), may hold values from 16.384 to 65.536
- second_bias_cols: float32 [12, 1152], P(None, 'mp'), may hold values from 16.384 to 65.536
- second_bias_rows: float32 [2, 1152], replicated, may hold values from 16.384 to 65.536
- ema_cols: float32 [15, 1152, 1152], P(None, 'dp', 'mp'), may hold values from -0.1875 to 0.1875
- ema_rows: float32 [5, 1152, 1152], P(None, 'mp', 'dp'), may hold values from -0.1875 to 0.1875
- ema_bias_cols: float32 [12, 1152], P(None, 'mp'), may hold values from -3 to 3
- ema_bias_rows: float32 [2, 1152], replicated, may hold values from -3 to 3
Outputs:
- out_tokens: bfloat16 [16384, 1152], P('dp')
- input_grad: float32 [16384, 1152], P('dp')
- first_cols_new: float32 [15, 1152, 1152], P(None, 'dp', 'mp')
- second_cols_new: float32 [15, 1152, 1152], P(None, 'dp', 'mp')
- weight_cols_new: float32 [15, 1152, 1152], P(None, 'dp', 'mp')
- ema_cols_new: float32 [15, 1152, 1152], P(None, 'dp', 'mp')
- first_rows_new: float32 [5, 1152, 1152], P(None, 'mp', 'dp')
- second_rows_new: float32 [5, 1152, 1152], P(None, 'mp', 'dp')
- weight_rows_new: float32 [5, 1152, 1152], P(None, 'mp', 'dp')
- ema_rows_new: float32 [5, 1152, 1152], P(None, 'mp', 'dp')
- first_bias_cols_new: float32 [12, 1152], P(None, 'mp')
- second_bias_cols_new: float32 [12, 1152], P(None, 'mp')
- bias_cols_new: float32 [12, 1152], P(None, 'mp')
- ema_bias_cols_new: float32 [12, 1152], P(None, 'mp')
- first_bias_rows_new: float32 [2, 1152], replicated
- second_bias_rows_new: float32 [2, 1152], replicated
- bias_rows_new: float32 [2, 1152], replicated
- ema_bias_rows_new: float32 [2, 1152], replicated
Inputs may be any that keep to these rules, and one draw needn't show every extreme that they name: `seg_ids`: within each packed row of 1024 tokens the image number starts at 0 and rises by one from image to image; an image holds a multiple of 64 tokens, 64 to 256; in every draw one row holds 16 images of 64 tokens and every other row an image of 256 tokens. `time_steps`: entry j of a row is the timestep of that row's image j; entries past the row's last image are not read.
All inputs are finite; a program needn't handle non-finite values.
Results may differ from a plain program's by a relative error of at most 0.039.
Values may be sent and summed in bfloat16 or wider, within the bound.
No kernel may reach another device: no remote copies, remote signals or barrier semaphores. Data moves between devices by JAX's collectives and lax.ppermute only.
A program may use at most 320 MiB of HBM per device.

v0:
```python
import math

import jax
import jax.numpy as jnp
from jax import lax
from jax.sharding import PartitionSpec as P

HEAD_DIM = 72
STEP = 10


highest = lax.Precision.HIGHEST
beta_one = 0.9
beta_two = 0.999
adam_eps = 1e-08
decay_rate = 0.1
rate_matrix = 0.05
rate_vector = 0.5
ema_keep = 0.7
norm_eps = 1e-06
neg_large = -1e30


def embedding_table(step_values, width_all):
    half_width = width_all // 2
    frequency = jnp.exp(-math.log(10000.0) * jnp.arange(half_width, dtype=jnp.float32) / half_width)
    angles = step_values.astype(jnp.float32)[..., None] * frequency
    return jnp.concatenate([jnp.cos(angles), jnp.sin(angles)], axis=-1)


def layer_norm(values):
    centre = values - jnp.mean(values, axis=-1, keepdims=True)
    return centre * lax.rsqrt(jnp.mean(centre * centre, axis=-1, keepdims=True) + norm_eps)


def modulate(values, shift_rows, scale_rows):
    return layer_norm(values) * (1.0 + scale_rows) + shift_rows


def gelu_tanh(values):
    return jax.nn.gelu(values, approximate=True)


def masked_scores(query_block, seg_block, keys_row, seg_row):
    scores = jnp.einsum(
        "qhd,khd->hqk", query_block, keys_row, preferred_element_type=jnp.float32
    ) * HEAD_DIM ** (-0.5)
    return jnp.where((seg_block[:, None] == seg_row[None, :])[None], scores, neg_large)


def attend_forward(query_block, seg_block, keys_row, values_row, seg_row):
    scores = masked_scores(query_block, seg_block, keys_row, seg_row)
    row_max = jnp.max(scores, axis=-1, keepdims=True)
    weights = jnp.exp(scores - row_max)
    row_total = jnp.sum(weights, axis=-1, keepdims=True)
    prob_low = (weights / row_total).astype(jnp.bfloat16)
    mixed_out = jnp.einsum("hqk,khd->qhd", prob_low, values_row, preferred_element_type=jnp.float32)
    return (mixed_out.astype(jnp.bfloat16), row_max + jnp.log(row_total))


def attend_backward(query_block, seg_block, grad_block, log_total, keys_row, values_row, seg_row):
    scale_factor = HEAD_DIM ** (-0.5)
    scores = masked_scores(query_block, seg_block, keys_row, seg_row)
    prob_rows = jnp.exp(scores - log_total)
    grad_prob = jnp.einsum(
        "qhd,khd->hqk", grad_block, values_row, preferred_element_type=jnp.float32
    )
    grad_values = jnp.einsum(
        "hqk,qhd->khd",
        prob_rows.astype(jnp.bfloat16),
        grad_block,
        preferred_element_type=jnp.float32,
    )
    row_inner = jnp.sum(grad_prob * prob_rows, axis=-1, keepdims=True)
    grad_scores = (prob_rows * (grad_prob - row_inner)).astype(jnp.bfloat16)
    grad_queries = (
        jnp.einsum("hqk,khd->qhd", grad_scores, keys_row, preferred_element_type=jnp.float32)
        * scale_factor
    )
    grad_keys = (
        jnp.einsum("hqk,qhd->khd", grad_scores, query_block, preferred_element_type=jnp.float32)
        * scale_factor
    )
    return (grad_queries, grad_keys, grad_values)


def adam_step(weight, gradient, first_old, second_old, ema_old, step_rate):
    first_new = beta_one * first_old + (1.0 - beta_one) * gradient
    second_new = beta_two * second_old + (1.0 - beta_two) * gradient * gradient
    first_hat = first_new / (1.0 - beta_one**STEP)
    second_hat = second_new / (1.0 - beta_two**STEP)
    weight_new = weight - step_rate * (
        first_hat / (jnp.sqrt(second_hat) + adam_eps) + decay_rate * weight
    )
    ema_new = ema_keep * ema_old + (1.0 - ema_keep) * weight_new
    return (first_new, second_new, weight_new, ema_new)


def per_device(
    tokens,
    seg_ids,
    time_steps,
    cotangent,
    weight_cols,
    weight_rows,
    bias_cols,
    bias_rows,
    first_cols,
    first_rows,
    first_bias_cols,
    first_bias_rows,
    second_cols,
    second_rows,
    second_bias_cols,
    second_bias_rows,
    ema_cols,
    ema_rows,
    ema_bias_cols,
    ema_bias_rows,
):
    own_width = weight_cols.shape[2]
    model_width = tokens.shape[1]
    rows_here = time_steps.shape[0]
    unit_slots = time_steps.shape[1]
    token_count = tokens.shape[0]
    row_len = token_count // rows_here
    head_count = own_width // HEAD_DIM
    block_len = min(512, row_len)
    block_count = row_len // block_len
    cols_low, rows_low = (
        lax.all_gather(weight_cols.astype(jnp.bfloat16), "dp", axis=1, tiled=True),
        lax.all_gather(weight_rows.astype(jnp.bfloat16), "dp", axis=2, tiled=True),
    )
    time_rows = embedding_table(time_steps, model_width)
    time_low = time_rows.astype(jnp.bfloat16)
    ada_input = jax.nn.silu(time_rows).astype(jnp.bfloat16)
    own_mod = (
        jnp.einsum("rud,jde->ruje", ada_input, cols_low[9:15], preferred_element_type=jnp.float32)
        + bias_cols[6:12][None, None]
    )
    modulation = lax.all_gather(own_mod.astype(jnp.bfloat16), "mp", axis=3, tiled=True).astype(
        own_mod.dtype
    )
    seg_grid = seg_ids.reshape(rows_here, row_len)
    onehot = (seg_grid[:, :, None] == jnp.arange(unit_slots, dtype=jnp.int32)).astype(jnp.float32)

    def spread(lookup):
        return jnp.einsum("rlu,rux->rlx", onehot, lookup, precision=highest).reshape(
            token_count, lookup.shape[-1]
        )

    def per_image(values):
        return jnp.einsum(
            "rlu,rlx->rux",
            onehot,
            values.reshape(rows_here, row_len, values.shape[-1]),
            precision=highest,
        )

    shift_one, scale_one, gate_one, shift_two, scale_two, gate_two = [
        spread(modulation[:, :, column]) for column in range(6)
    ]
    source = tokens.astype(jnp.float32)
    input_one = modulate(source, shift_one, scale_one).astype(jnp.bfloat16)
    time_query = spread(
        jnp.einsum("rud,de->rue", time_low, cols_low[3], preferred_element_type=jnp.float32)
    )
    time_value = spread(
        jnp.einsum("rud,de->rue", time_low, cols_low[4], preferred_element_type=jnp.float32)
    )
    queries = (
        jnp.dot(input_one, cols_low[0], preferred_element_type=jnp.float32)
        + time_query
        + bias_cols[0]
    ).astype(jnp.bfloat16)
    keys_low = jnp.dot(input_one, cols_low[1], preferred_element_type=jnp.float32).astype(
        jnp.bfloat16
    )
    values_low = (
        jnp.dot(input_one, cols_low[2], preferred_element_type=jnp.float32)
        + time_value
        + bias_cols[1]
    ).astype(jnp.bfloat16)
    query_grid = queries.reshape(rows_here, block_count, block_len, head_count, HEAD_DIM)
    key_grid = keys_low.reshape(rows_here, row_len, head_count, HEAD_DIM)
    value_grid = values_low.reshape(rows_here, row_len, head_count, HEAD_DIM)
    mixed_rows = []
    lse_rows = []
    for row_number in range(rows_here):

        def forward_block(blocked, row_number=row_number):
            return attend_forward(
                blocked[0],
                blocked[1],
                key_grid[row_number],
                value_grid[row_number],
                seg_grid[row_number],
            )

        mixed_row, lse_row = lax.map(
            forward_block,
            (query_grid[row_number], seg_grid[row_number].reshape(block_count, block_len)),
        )
        mixed_rows.append(mixed_row.reshape(row_len, own_width))
        lse_rows.append(lse_row)
    mixed_all = jnp.concatenate(mixed_rows, 0)
    attn_part = jnp.dot(mixed_all, rows_low[0], preferred_element_type=jnp.float32)
    attended = lax.psum(attn_part.astype(jnp.bfloat16), "mp").astype(jnp.float32) + bias_rows[0]
    hidden_one = source + gate_one * attended
    input_two = modulate(hidden_one, shift_two, scale_two).astype(jnp.bfloat16)
    inner_act = (
        jnp.einsum("td,rde->tre", input_two, cols_low[5:9], preferred_element_type=jnp.float32)
        + bias_cols[2:6][None]
    )
    active = gelu_tanh(inner_act).astype(jnp.bfloat16)
    mlp_part = jnp.einsum("tre,red->td", active, rows_low[1:5], preferred_element_type=jnp.float32)
    mlp_out = lax.psum(mlp_part.astype(jnp.bfloat16), "mp").astype(jnp.float32) + bias_rows[1]
    out_tokens = (hidden_one + gate_two * mlp_out).astype(jnp.bfloat16)
    grad_out = cotangent.astype(jnp.float32)
    grad_gate_two = grad_out * mlp_out
    grad_mlp = grad_out * gate_two
    bias_row_two = jnp.sum(grad_mlp, axis=0)
    grad_mlp_low = grad_mlp.astype(jnp.bfloat16)
    grad_fc_two = jnp.einsum(
        "tre,td->red", active, grad_mlp_low, preferred_element_type=jnp.float32
    )
    grad_active = jnp.einsum(
        "td,red->tre", grad_mlp_low, rows_low[1:5], preferred_element_type=jnp.float32
    )
    gelu_value, gelu_back = jax.vjp(gelu_tanh, inner_act)
    grad_inner = gelu_back(grad_active)[0].astype(jnp.bfloat16)
    bias_fc_one = jnp.sum(grad_inner.astype(jnp.float32), axis=0)
    grad_fc_one = jnp.einsum(
        "td,tre->rde", input_two, grad_inner, preferred_element_type=jnp.float32
    )
    grad_input_two = jnp.einsum(
        "tre,rde->td", grad_inner, cols_low[5:9], preferred_element_type=jnp.float32
    )
    grad_hidden_two = lax.psum(grad_input_two.astype(jnp.bfloat16), "mp").astype(jnp.float32)
    norm_two_value, norm_two_back = jax.vjp(modulate, hidden_one, shift_two, scale_two)
    grad_hidden_norm, grad_shift_two, grad_scale_two = norm_two_back(grad_hidden_two)
    grad_hidden_one = grad_out + grad_hidden_norm
    grad_gate_one = grad_hidden_one * attended
    grad_attended = grad_hidden_one * gate_one
    bias_row_one = jnp.sum(grad_attended, axis=0)
    grad_attended_low = grad_attended.astype(jnp.bfloat16)
    grad_out_proj = jnp.einsum(
        "te,td->ed", mixed_all, grad_attended_low, preferred_element_type=jnp.float32
    )
    grad_mixed = jnp.einsum(
        "td,ed->te", grad_attended_low, rows_low[0], preferred_element_type=jnp.float32
    ).astype(jnp.bfloat16)
    grad_mixed_grid = grad_mixed.reshape(rows_here, block_count, block_len, head_count, HEAD_DIM)
    query_grads = []
    key_grads = []
    value_grads = []
    for row_number in range(rows_here):

        def backward_block(running, blocked, row_number=row_number):
            grad_queries, grad_keys, grad_values = attend_backward(
                blocked[0],
                blocked[1],
                blocked[2],
                blocked[3],
                key_grid[row_number],
                value_grid[row_number],
                seg_grid[row_number],
            )
            return ((running[0] + grad_keys, running[1] + grad_values), grad_queries)

        zero_rows = jnp.zeros((row_len, head_count, HEAD_DIM), jnp.float32)
        (key_row_grad, value_row_grad), query_row_grad = lax.scan(
            backward_block,
            (zero_rows, zero_rows),
            (
                query_grid[row_number],
                seg_grid[row_number].reshape(block_count, block_len),
                grad_mixed_grid[row_number],
                lse_rows[row_number],
            ),
        )
        query_grads.append(query_row_grad.reshape(row_len, own_width))
        key_grads.append(key_row_grad.reshape(row_len, own_width))
        value_grads.append(value_row_grad.reshape(row_len, own_width))
    grad_query_low = jnp.concatenate(query_grads, 0).astype(jnp.bfloat16)
    grad_key_low = jnp.concatenate(key_grads, 0).astype(jnp.bfloat16)
    grad_value_low = jnp.concatenate(value_grads, 0).astype(jnp.bfloat16)
    grad_query_wide = grad_query_low.astype(jnp.float32)
    grad_value_wide = grad_value_low.astype(jnp.float32)
    bias_query = jnp.sum(grad_query_wide, axis=0)
    bias_value = jnp.sum(grad_value_wide, axis=0)
    grad_qkv_stack = jnp.stack([grad_query_low, grad_key_low, grad_value_low], 1)
    grad_qkv_weights = jnp.einsum(
        "td,tje->jde", input_one, grad_qkv_stack, preferred_element_type=jnp.float32
    )
    time_float = time_low.astype(jnp.float32)
    grad_time_query = jnp.einsum(
        "rud,rue->de", time_float, per_image(grad_query_wide), precision=highest
    )
    grad_time_value = jnp.einsum(
        "rud,rue->de", time_float, per_image(grad_value_wide), precision=highest
    )
    grad_input_one = jnp.einsum(
        "tje,jde->td", grad_qkv_stack, cols_low[0:3], preferred_element_type=jnp.float32
    )
    grad_hidden_in = lax.psum(grad_input_one.astype(jnp.bfloat16), "mp").astype(jnp.float32)
    norm_one_value, norm_one_back = jax.vjp(modulate, source, shift_one, scale_one)
    grad_source_norm, grad_shift_one, grad_scale_one = norm_one_back(grad_hidden_in)
    input_grad = grad_hidden_one + grad_source_norm
    mp_start = lax.axis_index("mp") * own_width
    grad_fields = jnp.stack(
        [
            lax.dynamic_slice_in_dim(grad_field, mp_start, own_width, 1)
            for grad_field in (
                grad_shift_one,
                grad_scale_one,
                grad_gate_one,
                grad_shift_two,
                grad_scale_two,
                grad_gate_two,
            )
        ],
        1,
    )
    grad_mod = per_image(grad_fields.reshape(token_count, 6 * own_width)).reshape(
        rows_here, unit_slots, 6, own_width
    )
    grad_ada = jnp.einsum(
        "rud,rujx->jdx", ada_input.astype(jnp.float32), grad_mod, precision=highest
    )
    bias_ada = jnp.sum(grad_mod, axis=(0, 1))
    attn_stack = jnp.concatenate(
        [grad_qkv_weights, grad_time_query[None], grad_time_value[None], grad_ada], 0
    )
    grad_cols_all = jnp.concatenate([attn_stack[0:5], grad_fc_one, attn_stack[5:11]], 0)
    grad_rows_all = jnp.concatenate([grad_out_proj[None], grad_fc_two], 0)
    grad_cols_sum, grad_rows_sum = (
        lax.psum_scatter(grad_cols_all, "dp", scatter_dimension=1, tiled=True),
        lax.psum_scatter(grad_rows_all, "dp", scatter_dimension=2, tiled=True),
    )
    bias_cols_grad = jnp.concatenate([bias_query[None], bias_value[None], bias_fc_one, bias_ada], 0)
    bias_rows_grad = jnp.stack([bias_row_one, bias_row_two], 0)
    bias_cols_sum, bias_rows_sum = lax.psum((bias_cols_grad, bias_rows_grad), "dp")
    cols_state = adam_step(
        weight_cols, grad_cols_sum, first_cols, second_cols, ema_cols, rate_matrix
    )
    rows_state = adam_step(
        weight_rows, grad_rows_sum, first_rows, second_rows, ema_rows, rate_matrix
    )
    bias_cols_state = adam_step(
        bias_cols, bias_cols_sum, first_bias_cols, second_bias_cols, ema_bias_cols, rate_vector
    )
    bias_rows_state = adam_step(
        bias_rows, bias_rows_sum, first_bias_rows, second_bias_rows, ema_bias_rows, rate_vector
    )
    return (
        out_tokens,
        input_grad,
        cols_state[0],
        cols_state[1],
        cols_state[2],
        cols_state[3],
        rows_state[0],
        rows_state[1],
        rows_state[2],
        rows_state[3],
        bias_cols_state[0],
        bias_cols_state[1],
        bias_cols_state[2],
        bias_cols_state[3],
        bias_rows_state[0],
        bias_rows_state[1],
        bias_rows_state[2],
        bias_rows_state[3],
    )


def solution(mesh):
    placed = (
        P("dp", None),
        P("dp"),
        P("dp", None),
        P("dp", None),
        P(None, "dp", "mp"),
        P(None, "mp", "dp"),
        P(None, "mp"),
        P(),
        P(None, "dp", "mp"),
        P(None, "mp", "dp"),
        P(None, "mp"),
        P(),
        P(None, "dp", "mp"),
        P(None, "mp", "dp"),
        P(None, "mp"),
        P(),
        P(None, "dp", "mp"),
        P(None, "mp", "dp"),
        P(None, "mp"),
        P(),
    )
    return jax.shard_map(
        per_device,
        mesh=mesh,
        in_specs=placed,
        out_specs=(
            P("dp", None),
            P("dp", None),
            P(None, "dp", "mp"),
            P(None, "dp", "mp"),
            P(None, "dp", "mp"),
            P(None, "dp", "mp"),
            P(None, "mp", "dp"),
            P(None, "mp", "dp"),
            P(None, "mp", "dp"),
            P(None, "mp", "dp"),
            P(None, "mp"),
            P(None, "mp"),
            P(None, "mp"),
            P(None, "mp"),
            P(),
            P(),
            P(),
            P(),
        ),
        check_vma=False,
    )
```

profile of v0, /device:TPU:0, one launch (start us, length us, event | category | flops | bytes accessed | tf_op | source)
XLA Modules:
  0.0 1494.5 jit_solution(14794557482732813369)
XLA Ops:
  21.7 176.8 %all-gather.3.cloned.1.call-done = bf16[15,1152,288]{2,1,0:T(8,128)(2,1)} async-done(((bf16[15,144,288]{2,1,0:T(8,128)(2,1)}), bf16[15,1152,288]{2,1,0:T(8,128)(2,1)}) %all-gather.3.cloned.1.call-update) | async-done | bytes 9953296 | tf_op jit(solution)/shard_map/all_gather | solution.py:131
  211.0 23.7 %all_gather.10 = bf16[2,16,6,1152]{1,0,2,3:T(2,128)(2,1)S(1)} all-gather(bf16[2,16,6,288]{1,0,2,3:T(2,128)(2,1)S(1)} %copy.288), channel_id=1, replica_groups=mesh['dp'=8,'mp'=4] {'mp'}, dimensions={3}, use_global_device_ids=true | all-gather | bytes 552960 | tf_op jit(solution)/shard_map/all_gather | solution.py:141
  275.7 17.4 %while.54 = (s32[]{:T(128)}, bf16[2,512,4,72]{1,3,2,0:T(8,128)(2,1)}, f32[2,4,512,1]{2,1,3,0:T(4,128)}, s32[2,512]{1,0:T(2,128)S(1)}, s32[2,1024]{1,0:T(2,128)S(...) while((s32[]{:T(128)}, ...), condition=%wide.region_5.6_spmd, body=%wide.region_2.5_spmd.sunk | while | flops 629815296 | bytes 33966308 | solution.py:200
  297.3 17.8 %while.55 = (s32[]{:T(128)}, bf16[2,512,4,72]{1,3,2,0:T(8,128)(2,1)}, f32[2,4,512,1]{2,1,3,0:T(4,128)}, s32[2,512]{1,0:T(2,128)S(1)}, s32[2,1024]{1,0:T(2,128)S(...) while((s32[]{:T(128)}, ...), condition=%wide.region_9.10_spmd, body=%wide.region_6.9_spmd.sunk | while | flops 629815296 | bytes 33966308 | solution.py:200
  356.2 62.5 %all-reduce.6.cloned.1.call-done = bf16[2048,1152]{1,0:T(8,128)(2,1)} async-done(((bf16[2048,1152]{1,0:T(8,128)(2,1)}), bf16[2048,1152]{1,0:T(8,128)(2,1)}) %all-reduce.6.cloned.1.call-update) | async-done | bytes 4718608 | tf_op jit(solution)/shard_map/psum | solution.py:208
  418.7 12.1 fusion.205
  434.4 9.6 fusion.119
  444.0 9.5 fusion.134
  453.6 21.4 %convert_reduce_fusion.1 = (f32[4,288]{1,0:T(4,128)}, bf16[2048,4,288]{0,2,1:T(8,128)(2,1)}) fusion(f32[2048,4,288]{0,2,1:T(8,128)S(1)} %fusion.134, f32[4,288]{1,0:T(4,128)S(1)} %copy-done.85, bf16[5,288,1152]{1,2,0:T(8,128)(2,1)} %all-gather.5.cloned.1.call-done, bf16[2048,1152]{1,0:T(8,128)(2,1)} %get-tuple-element.763), kind=kOutput, calls=%fused_computation.161 | convolution fusion | flops 5490080768 | bytes 22422528 | tf_op jit(solution)/shard_map/td,red->tre/dot_general | solution.py:227
  475.0 12.8 bitcast_convert_fusion.1
  487.8 16.2 %bitcast_convert_fusion.2 = bf16[2048,1152]{1,0:T(8,128)(2,1)} fusion(bf16[5,288,1152]{1,2,0:T(8,128)(2,1)} %all-gather.5.cloned.1.call-done, f32[2048,4,288]{0,2,1:T(8,128)} %copy-done.91, f32[4,288]{1,0:T(4,128)S(1)} %copy-done.85), kind=kOutput, calls=%fused_computation.146 | convolution fusion | flops 5461770240 | bytes 17699328 | tf_op jit(solution)/shard_map/tre,red->td/dot_general | solution.py:216
  504.1 78.0 %all-reduce.8.cloned.1.call-done = bf16[2048,1152]{1,0:T(8,128)(2,1)} async-done(((bf16[2048,1152]{1,0:T(8,128)(2,1)}), bf16[2048,1152]{1,0:T(8,128)(2,1)}) %all-reduce.8.cloned.1.call-update) | async-done | bytes 4718608 | tf_op jit(solution)/shard_map/psum | solution.py:239
  582.1 9.4 multiply_reduce_fusion.2
  591.6 10.0 fusion.204
  608.8 9.4 fusion.141
  626.7 26.7 %while.56 = (s32[]{:T(128)}, f32[1024,4,72]{0,2,1:T(8,128)S(1)}, f32[1024,4,72]{0,2,1:T(8,128)}, bf16[2,512,4,72]{1,3,2,0:T(8,128)(2,1)}, bf16[2,512,4,72]{1,3,2...) while((s32[]{:T(128)}, f32[1024,4,72]{0,2,1:T(8,128)S(1)}, ...), condition=%wide.region_19.20_spmd.clone, body=%wide.region_17.19_spmd.clone.sunk | while | flops 1543550976 | bytes 92219704 | solution.py:272
  667.2 26.7 %while.57 = (s32[]{:T(128)}, f32[1024,4,72]{0,2,1:T(8,128)S(1)}, f32[1024,4,72]{0,2,1:T(8,128)}, bf16[2,512,4,72]{1,3,2,0:T(8,128)(2,1)}, bf16[2,512,4,72]{1,3,2...) while((s32[]{:T(128)}, f32[1024,4,72]{0,2,1:T(8,128)S(1)}, ...), condition=%wide.region_22.23_spmd.clone, body=%wide.region_20.22_spmd.clone.sunk | while | flops 1543550976 | bytes 92219704 | solution.py:272
  697.9 11.8 bitcast_convert_fusion
  710.4 12.3 fusion.126
  730.3 11.6 copy.347
  742.0 11.8 reshape.483
  802.2 78.1 %all-reduce.10.cloned.1.call-done = (bf16[2048,1152]{1,0:T(8,128)(2,1)}, bf16[2048,1152]{1,0:T(8,128)(2,1)}) async-done(((bf16[2048,1152]{1,0:T(8,128)(2,1)}, bf16[2048,1152]{1,0:T(8,128)(2,1)}), (bf16[2048,1152]{1,0:T(8,128)(2,1)}, bf16[2048,1152]{1,0:T(8,128)(2,1)})) %all-reduce.10.cloned.1.call-update) | async-done | bytes 9437200 | tf_op jit(solution)/shard_map/psum | solution.py:217
  880.3 10.9 convert_add_fusion.1
  891.2 10.9 dynamic-slice_multiply_fusion
  933.5 19.0 %reshape_reshape.3 = f32[2,1024,1728]{1,0,2:T(2,128)} reshape(f32[2048,6,288]{0,2,1:T(8,128)} %bitcast_dynamic-update-slice_fusion.5) | data formatting | bytes 28311552 | tf_op jit(solution)/shard_map/reshape;reshape | solution.py:156
  952.6 12.5 fusion.212
  971.0 25.5 %copy.333 = f32[15,1152,288]{2,0,1:T(8,128)} copy(f32[15,1152,288]{1,2,0:T(8,128)} %bitcast_dynamic-update-slice_fusion.2) | data formatting | bytes 39813120 | tf_op jit(solution)/shard_map/concatenate | solution.py:335
  997.3 38.9 %all-reduce = (f32[12,288]{1,0:T(8,128)S(1)}, f32[2,1152]{1,0:T(2,128)S(1)}) all-reduce(f32[12,288]{1,0:T(8,128)S(1)} %pad_maximum_fusion.2, f32[2,1152]{1,0:T(2,128)S(1)} %pad_maximum_fusion.3), channel_id=1, replica_groups=mesh['dp'=8,'mp'=4] {'dp'}, use_global_device_ids=true, to_apply=%region_32.33 | all-reduce | flops 5760 | bytes 46080 | tf_op jit(solution)/shard_map/psum | solution.py:343
  1045.0 11.0 fusion.203
  1057.3 11.3 add_add_fusion.2
  1077.5 387.9 %reduce-scatter.5.cloned.1.call-done = f32[15,144,288]{2,0,1:T(8,128)} async-done(((f32[15,1152,288]{2,0,1:T(8,128)}), f32[15,144,288]{2,0,1:T(8,128)}) %reduce-scatter.5.cloned.1.call-update) | async-done | bytes 2488336 | tf_op jit(solution)/shard_map/reduce_scatter | solution.py:338
  1465.4 11.0 fusion.145
  (482 shorter events, 361.2 us)
Async XLA Ops:
  7.2 191.2 %all-gather.3.cloned.1.call-start = ((), (), s32[]{:S(2)}) async-start(), calls=%async_computation.2 | async-start | bytes 14929920 | tf_op jit(solution)/shard_map/all_gather | solution.py:131
  10.7 309.3 %all-gather.5.cloned.1.call-start = ((), (), s32[]{:S(2)}) async-start(), calls=%async_computation.3 | async-start | bytes 4976640 | tf_op jit(solution)/shard_map/all_gather | solution.py:132
  11.7 407.1 %all-reduce.6.cloned.1.call-start = ((), (), s32[]{:S(2)}) async-start(), calls=%async_computation.4 | async-start | bytes 9437184 | tf_op jit(solution)/shard_map/psum | solution.py:208
  16.8 229.0 %copy-start.56 = (f32[2048]{0:T(1024)}, f32[2048]{0:T(1024)S(1)}, u32[]{:S(2)}) copy-start(f32[2048]{0:T(1024)S(1)} %broadcast_multiply_fusion.1) | copy-start | bytes 24580
  21.6 176.9 %copy-start.39 = (f32[2,16,576]{2,1,0:T(8,128)}, f32[2,16,576]{2,1,0:T(8,128)S(1)}, u32[]{:S(2)}) copy-start(f32[2,16,576]{2,1,0:T(8,128)S(1)} %get-tuple-element.789) | copy-start | bytes 221188
  21.6 176.9 %copy-start.41 = (f32[2,16,576]{2,1,0:T(8,128)}, f32[2,16,576]{2,1,0:T(8,128)S(1)}, u32[]{:S(2)}) copy-start(f32[2,16,576]{2,1,0:T(8,128)S(1)} %get-tuple-element.790) | copy-start | bytes 221188
  21.7 185.2 %copy-start.37 = (bf16[2,16,1152]{2,1,0:T(8,128)(2,1)}, bf16[2,16,1152]{2,1,0:T(8,128)(2,1)S(1)}, u32[]{:S(2)}) copy-start(bf16[2,16,1152]{2,1,0:T(8,128)(2,1)S(1)} %fusion.174) | copy-start | bytes 221188
  275.7 21.6 %copy-start.62 = (s32[2,512]{1,0:T(2,128)S(1)}, s32[2,512]{1,0:T(2,128)}, u32[]{:S(2)}) copy-start(s32[2,512]{1,0:T(2,128)} %slice.177) | copy-start | bytes 12292
  326.6 255.5 %all-reduce.8.cloned.1.call-start = ((), (), s32[]{:S(2)}) async-start(), calls=%async_computation.5 | async-start | bytes 9437184 | tf_op jit(solution)/shard_map/psum | solution.py:239
  348.0 70.7 %copy-start.78 = (f32[1152]{0:T(1024)S(1)}, f32[1152]{0:T(1024)}, u32[]{:S(2)}) copy-start(f32[1152]{0:T(1024)} %get-tuple-element.643) | copy-start | bytes 13828
  348.0 86.4 %slice-start.5 = ((s8[9437184]{0:T(1024)(128)(4,1)}), s8[1048576]{0:T(1024)(128)(4,1)S(1)}, s32[]{:S(2)}) async-start(s8[9437184]{0:T(1024)(128)(4,1)} %bitcast.464), calls=%async_computation.14 | async-start | bytes 2097152
  418.7 15.7 %slice-start.6 = ((s8[9437184]{0:T(1024)(128)(4,1)}), s8[4194304]{0:T(1024)(128)(4,1)S(1)}, s32[]{:S(2)}) async-start(s8[9437184]{0:T(1024)(128)(4,1)} %bitcast.464), calls=%async_computation.15 | async-start | bytes 8388608
  418.7 15.7 %slice-start.7 = ((s8[9437184]{0:T(1024)(128)(4,1)}), s8[4194304]{0:T(1024)(128)(4,1)S(1)}, s32[]{:S(2)}) async-start(s8[9437184]{0:T(1024)(128)(4,1)} %bitcast.464), calls=%async_computation.16 | async-start | bytes 8388608
  453.6 21.4 %copy-start.91 = (f32[2048,4,288]{0,2,1:T(8,128)}, f32[2048,4,288]{0,2,1:T(8,128)S(1)}, u32[]{:S(2)}) copy-start(f32[2048,4,288]{0,2,1:T(8,128)S(1)} %fusion.134) | copy-start | bytes 28311556
  487.8 392.5 %all-reduce.10.cloned.1.call-start = ((), (), s32[]{:S(2)}) async-start(), calls=%async_computation.8 | async-start | bytes 18874368 | tf_op jit(solution)/shard_map/psum | solution.py:217
  582.1 19.5 %slice-start.10 = ((s8[4718592]{0:T(1024)(128)(4,1)}), s8[524288]{0:T(1024)(128)(4,1)S(1)}, s32[]{:S(2)}) async-start(s8[4718592]{0:T(1024)(128)(4,1)} %bitcast.469), calls=%async_computation.19 | async-start | bytes 1048576
  591.6 11.7 slice-start.11
  653.4 13.8 copy-start.5
  653.4 13.8 copy-start.63
  697.2 12.5 copy-start.48
  709.8 358.8 %reduce-scatter.7.cloned.1.call-start = ((), (), s32[]{:S(2)}) async-start(), calls=%async_computation.7 | async-start | bytes 7962624
  753.8 711.6 %reduce-scatter.5.cloned.1.call-start = ((), (), s32[]{:S(2)}) async-start(), calls=%async_computation.6 | async-start | bytes 31850496 | tf_op jit(solution)/shard_map/reduce_scatter | solution.py:338
  779.0 15.1 %slice-start.12 = ((s8[4718592]{0:T(1024)(128)(4,1)}), s8[4194304]{0:T(1024)(128)(4,1)S(1)}, s32[]{:S(2)}) async-start(s8[4718592]{0:T(1024)(128)(4,1)} %bitcast.474), calls=%async_computation.21 | async-start | bytes 8388608
  779.0 15.1 %slice-start.14 = ((s8[4718592]{0:T(1024)(128)(4,1)}), s8[4194304]{0:T(1024)(128)(4,1)S(1)}, s32[]{:S(2)}) async-start(s8[4718592]{0:T(1024)(128)(4,1)} %bitcast.504), calls=%async_computation.23 | async-start | bytes 8388608
  781.6 12.5 slice-start.13
  781.7 12.5 slice-start.15
  794.2 86.1 %copy-start.74 = (f32[1152]{0:T(1024)S(1)}, f32[1152]{0:T(1024)}, u32[]{:S(2)}) copy-start(f32[1152]{0:T(1024)} %get-tuple-element.642) | copy-start | bytes 13828
  952.5 12.7 copy-start.40
  952.5 12.7 copy-start.42
  996.5 39.7 %copy-start.57 = (f32[2048]{0:T(1024)S(1)}, f32[2048]{0:T(1024)}, u32[]{:S(2)}) copy-start(f32[2048]{0:T(1024)} %copy-done.56) | copy-start | bytes 24580
  1044.9 11.7 copy-start.73
  1071.3 394.1 %copy-start.14 = (f32[15,144,288]{2,1,0:T(8,128)S(1)}, f32[15,144,288]{2,1,0:T(8,128)}, u32[]{:S(2)}) copy-start(f32[15,144,288]{2,1,0:T(8,128)} %param.32) | copy-start | bytes 7464964
  (101 other events, 443.3 us)
Sparse Core Ops, SparseCore 0:
  10.9 187.5 all-gather.2
  200.7 74.4 all-gather.4
  326.7 91.9 all-reduce.5
  487.9 94.1 all-reduce.7
  709.9 170.3 all-reduce.9
  883.8 129.6 reduce-scatter.6
  1017.9 447.3 reduce-scatter.4
where the time goes:
time: 1500 us; the launch traced here: 1490 us
  waiting for transfers between devices  783 us (52%)
  matrix products  240 us (16%)
  other arithmetic  208 us (14%)
  local copies, waits for them, and re-layouts  183 us (12%)
  blocking collectives  62.6 us (4%)
  between operations  15.6 us (1%)
    reduce_scatter x1, waiting for transfers between devices, per_device(): lax.psum_scatter(grad_cols_all, 'dp', scatter_dimension=1, tiled=True)  388 us
    all_gather x1, waiting for transfers between devices, per_device(): lax.all_gather(weight_cols.astype(jnp.bfloat16), 'dp', axis=1, tiled=True)  177 us
    psum x1, waiting for transfers between devices, per_device(): lax.psum(mlp_part.astype(jnp.bfloat16), 'mp').astype(jnp.float32)  78.1 us
    psum x1, waiting for transfers between devices, per_device(): lax.psum(grad_input_two.astype(jnp.bfloat16), 'mp').astype(jnp.float32)  78 us
    unnamed x205, local copies, waits for them, and re-layouts  72.1 us
    psum x1, waiting for transfers between devices, per_device(): lax.psum(attn_part.astype(jnp.bfloat16), 'mp').astype(jnp.float32)  62.5 us
    psum x1, blocking collectives, per_device(): lax.psum((bias_cols_grad, bias_rows_grad), 'dp')  38.9 us
    reduce_sum x4, other arithmetic, layer_norm(): centre = values - jnp.mean(values, axis=-1, keepdims=True)  36.3 us
  transfers between devices with their start and end apart: 7, of which 5 were waited for; matrix products, arithmetic and copies ran while one was open for 26% of the time, Pallas kernels for 0%

commit v1 on v0

v1 whole, which is shorter than its diff:
```python
import math

import jax
import jax.numpy as jnp
from jax import lax
from jax.experimental import pallas as pl
from jax.experimental.pallas import tpu as pltpu
from jax.sharding import PartitionSpec as P

HEAD_DIM = 72
STEP = 10
UNIT = 64
REACH = 192


highest = lax.Precision.HIGHEST
beta_one = 0.9
beta_two = 0.999
adam_eps = 1e-08
decay_rate = 0.1
rate_matrix = 0.05
rate_vector = 0.5
ema_keep = 0.7
norm_eps = 1e-06
neg_large = -1e30
score_scale = HEAD_DIM**-0.5
low = jnp.bfloat16
wide = jnp.float32

DOT_NN = (((1,), (0,)), ((), ()))
DOT_NT = (((1,), (1,)), ((), ()))
DOT_TN = (((0,), (0,)), ((), ()))

CORE_SWAP = [(i, i ^ 1) for i in range(4)]
CHIP_SWAP = [(i, i ^ 2) for i in range(4)]


def dot_as(left, right, dims):
    return lax.dot_general(left, right, dims, preferred_element_type=wide)


def ring_order(count):
    return list(range(0, count, 2)) + list(range(count - 1, 0, -2))


def ring_perms(count):
    order = ring_order(count)
    onward = [(order[i], order[(i + 1) % count]) for i in range(count)]
    return onward, [(b, a) for a, b in onward]


def ring_place(count):
    order = ring_order(count)
    spots = [order.index(i) for i in range(count)]
    return jnp.array(order), jnp.array(spots)[lax.axis_index("dp")]


def ring_gather(shard, count):
    if count not in (4, 8):
        return lax.all_gather(shard, "dp", axis=0, tiled=True)
    rows = shard.shape[0]
    half = rows // 2
    onward, backward = ring_perms(count)
    order, spot = ring_place(count)

    def put(whole, piece, back, offset=0):
        at = order[(spot + back) % count] * rows + offset
        return lax.dynamic_update_slice_in_dim(whole, piece, at, 0)

    whole = jnp.zeros((count * rows,) + shard.shape[1:], shard.dtype)
    whole = put(whole, shard, 0)
    ahead = behind = shard
    for hop in range(1, count // 2):
        ahead = lax.ppermute(ahead, "dp", onward)
        behind = lax.ppermute(behind, "dp", backward)
        whole = put(whole, ahead, -hop)
        whole = put(whole, behind, hop)
    ahead = lax.ppermute(ahead[:half], "dp", onward)
    behind = lax.ppermute(behind[half:], "dp", backward)
    whole = put(whole, ahead, count // 2)
    return put(whole, behind, count // 2, half)


def ring_scatter(parts, count):
    if count not in (4, 8):
        return lax.psum_scatter(parts.astype(low), "dp", scatter_dimension=0, tiled=True).astype(
            wide
        )
    rows = parts.shape[0] // count
    half = rows // 2
    onward, backward = ring_perms(count)
    order, spot = ring_place(count)

    def chunk(ahead, start, stop):
        at = order[(spot + ahead) % count] * rows + start
        return lax.dynamic_slice_in_dim(parts, at, stop - start, 0).astype(wide)

    def travel(perm, sign, hops, start, stop):
        running = chunk(sign * hops, start, stop).astype(low)
        for hop in range(hops - 1, 0, -1):
            running = lax.ppermute(running, "dp", perm).astype(wide)
            running = (running + chunk(sign * hop, start, stop)).astype(low)
        return lax.ppermute(running, "dp", perm).astype(wide)

    long, short = count // 2, count // 2 - 1
    first = travel(onward, 1, long, 0, half) + travel(backward, -1, short, 0, half)
    second = travel(onward, 1, short, half, rows) + travel(backward, -1, long, half, rows)
    return jnp.concatenate([first, second], 0) + chunk(0, 0, rows)


def share_steps(steps, count):
    if count not in (4, 8):
        return lax.all_gather(steps, "dp", axis=0, tiled=True)
    blank = jnp.zeros((count,) + steps.shape, steps.dtype)
    known = lax.dynamic_update_slice_in_dim(blank, steps[None], lax.axis_index("dp"), 0)
    reach = 1
    while reach < count:
        known = known + lax.ppermute(known, "dp", [(i, i ^ reach) for i in range(count)])
        reach *= 2
    return known.reshape((count * steps.shape[0],) + steps.shape[1:])


def group_scatter(kept, sent):
    half = kept + lax.ppermute(sent.astype(low), "mp", CORE_SWAP).astype(wide)
    quarter = half.shape[0] // 2
    got = lax.ppermute(half[quarter:].astype(low), "mp", CHIP_SWAP)
    return half[:quarter] + got.astype(wide)


def group_gather(own):
    chip = lax.ppermute(own, "mp", CHIP_SWAP)
    core = lax.ppermute(own, "mp", CORE_SWAP)
    both = lax.ppermute(chip, "mp", CORE_SWAP)
    return [own, chip, core, both]


def in_group_order(pieces, place):
    stacked = jnp.stack(pieces, 0)
    return [
        lax.dynamic_index_in_dim(stacked, jnp.bitwise_xor(place, j), 0, keepdims=False)
        for j in range(4)
    ]


def key_windows(row_len, block):
    return [
        (at, max(0, at - REACH), min(row_len, at + block + REACH))
        for at in range(0, row_len, block)
    ]


def attend_forward_kernel(place_ref, qkv_ref, seg_col_ref, seg_row_ref, out_ref, q_s, k_s, v_s, *, heads):
    row_len = qkv_ref.shape[0]
    width = heads * HEAD_DIM
    block = row_len // 4
    place = place_ref[0]
    for j in range(4):
        at = pl.multiple_of(jnp.bitwise_xor(place, j) * block, block)
        to = slice(j * block, (j + 1) * block)
        for h in range(heads):
            c = h * HEAD_DIM
            q_s[h, to, :] = qkv_ref[pl.ds(at, block), c : c + HEAD_DIM]
            k_s[h, to, :] = qkv_ref[pl.ds(at, block), width + c : width + c + HEAD_DIM]
            v_s[h, to, :] = qkv_ref[pl.ds(at, block), 2 * width + c : 2 * width + c + HEAD_DIM]
    for j, (at, start, stop) in enumerate(key_windows(row_len, block)):
        same = seg_col_ref[start:stop, :] == seg_row_ref[:, at : at + block]
        mixed = []
        for h in range(heads):
            scores = dot_as(k_s[h, start:stop, :], q_s[h, at : at + block, :], DOT_NT)
            scores = jnp.where(same, scores, neg_large)
            top = jnp.max(scores, axis=0, keepdims=True)
            weights = jnp.exp((scores - top) * score_scale)
            total = jnp.sum(weights, axis=0, keepdims=True)
            gathered = dot_as(v_s[h, start:stop, :], weights.astype(low), DOT_TN)
            mixed.append(gathered * (1.0 / total))
        to = pl.multiple_of(jnp.bitwise_xor(place, j) * block, block)
        out_ref[pl.ds(to, block), :] = jnp.concatenate(mixed, axis=0).T.astype(low)


def attend_backward_kernel(
    place_ref, qkv_ref, grad_ref, seg_col_ref, seg_row_ref, out_ref, q_s, k_s, v_s, g_s, dk_s, dv_s, *, heads
):
    row_len = qkv_ref.shape[0]
    width = heads * HEAD_DIM
    block = row_len // 4
    place = place_ref[0]
    dk_s[...] = jnp.zeros_like(dk_s)
    dv_s[...] = jnp.zeros_like(dv_s)
    for j in range(4):
        at = pl.multiple_of(jnp.bitwise_xor(place, j) * block, block)
        to = slice(j * block, (j + 1) * block)
        for h in range(heads):
            c = h * HEAD_DIM
            q_s[h, to, :] = qkv_ref[pl.ds(at, block), c : c + HEAD_DIM]
            k_s[h, to, :] = qkv_ref[pl.ds(at, block), width + c : width + c + HEAD_DIM]
            v_s[h, to, :] = qkv_ref[pl.ds(at, block), 2 * width + c : 2 * width + c + HEAD_DIM]
            g_s[h, to, :] = grad_ref[pl.ds(at, block), c : c + HEAD_DIM]
    for j, (at, start, stop) in enumerate(key_windows(row_len, block)):
        same = seg_col_ref[start:stop, :] == seg_row_ref[:, at : at + block]
        grads = []
        for h in range(heads):
            query = q_s[h, at : at + block, :]
            grad = g_s[h, at : at + block, :]
            keys = k_s[h, start:stop, :]
            scores = jnp.where(same, dot_as(keys, query, DOT_NT), neg_large)
            top = jnp.max(scores, axis=0, keepdims=True)
            weights = jnp.exp((scores - top) * score_scale)
            probs = weights * (1.0 / jnp.sum(weights, axis=0, keepdims=True))
            grad_probs = dot_as(v_s[h, start:stop, :], grad, DOT_NT)
            inner = jnp.sum(grad_probs * probs, axis=0, keepdims=True)
            grad_scores = (probs * (grad_probs - inner)).astype(low)
            dv_s[h, start:stop, :] += dot_as(probs.astype(low), grad, DOT_NN)
            dk_s[h, start:stop, :] += dot_as(grad_scores, query, DOT_NN)
            grads.append(dot_as(keys, grad_scores, DOT_TN) * score_scale)
        to = pl.multiple_of(jnp.bitwise_xor(place, j) * block, block)
        out_ref[pl.ds(to, block), 0:width] = jnp.concatenate(grads, axis=0).T.astype(low)
    for j in range(4):
        at = slice(j * block, (j + 1) * block)
        to = pl.multiple_of(jnp.bitwise_xor(place, j) * block, block)
        out_ref[pl.ds(to, block), width : 2 * width] = jnp.concatenate(
            [(dk_s[h, at, :] * score_scale).astype(low) for h in range(heads)], axis=1
        )
        out_ref[pl.ds(to, block), 2 * width : 3 * width] = jnp.concatenate(
            [dv_s[h, at, :].astype(low) for h in range(heads)], axis=1
        )


def in_vmem(count):
    return [pl.BlockSpec(memory_space=pltpu.SMEM)] + [pl.BlockSpec(memory_space=pltpu.VMEM)] * count


def attend_forward(place, qkv, seg_row):
    row_len, width = qkv.shape[0], qkv.shape[1] // 3
    heads = width // HEAD_DIM

    def body(*refs):
        attend_forward_kernel(*refs, heads=heads)

    return pl.pallas_call(
        body,
        out_shape=jax.ShapeDtypeStruct((row_len, width), low),
        in_specs=in_vmem(3),
        out_specs=pl.BlockSpec(memory_space=pltpu.VMEM),
        scratch_shapes=[pltpu.VMEM((heads, row_len, HEAD_DIM), low)] * 3,
        compiler_params=pltpu.CompilerParams(vmem_limit_bytes=32 * 2**20),
        cost_estimate=pl.CostEstimate(
            flops=4 * row_len * 640 * width, bytes_accessed=8 * row_len * width, transcendentals=heads * row_len * 640
        ),
        name="attend_forward",
    )(place, qkv, seg_row.reshape(row_len, 1), seg_row.reshape(1, row_len))


def attend_backward(place, qkv, grad, seg_row):
    row_len, width = qkv.shape[0], qkv.shape[1] // 3
    heads = width // HEAD_DIM

    def body(*refs):
        attend_backward_kernel(*refs, heads=heads)

    return pl.pallas_call(
        body,
        out_shape=jax.ShapeDtypeStruct((row_len, 3 * width), low),
        in_specs=in_vmem(4),
        out_specs=pl.BlockSpec(memory_space=pltpu.VMEM),
        scratch_shapes=[pltpu.VMEM((heads, row_len, HEAD_DIM), low)] * 4
        + [pltpu.VMEM((heads, row_len, HEAD_DIM), wide)] * 2,
        compiler_params=pltpu.CompilerParams(vmem_limit_bytes=40 * 2**20),
        cost_estimate=pl.CostEstimate(
            flops=10 * row_len * 640 * width, bytes_accessed=14 * row_len * width, transcendentals=heads * row_len * 640
        ),
        name="attend_backward",
    )(place, qkv, grad, seg_row.reshape(row_len, 1), seg_row.reshape(1, row_len))


def norm_parts(values):
    centre = values - jnp.mean(values, axis=-1, keepdims=True)
    inverse = lax.rsqrt(jnp.mean(centre * centre, axis=-1, keepdims=True) + norm_eps)
    return centre * inverse, inverse


def norm_back(normed, inverse, grad):
    return inverse * (
        grad
        - jnp.mean(grad, axis=-1, keepdims=True)
        - normed * jnp.mean(grad * normed, axis=-1, keepdims=True)
    )


def gelu_tanh(values):
    return jax.nn.gelu(values, approximate=True)


def adam_step(weight, gradient, first_old, second_old, ema_old, step_rate):
    first_new = beta_one * first_old + (1.0 - beta_one) * gradient
    second_new = beta_two * second_old + (1.0 - beta_two) * gradient * gradient
    first_hat = first_new / (1.0 - beta_one**STEP)
    second_hat = second_new / (1.0 - beta_two**STEP)
    weight_new = weight - step_rate * (
        first_hat / (jnp.sqrt(second_hat) + adam_eps) + decay_rate * weight
    )
    ema_new = ema_keep * ema_old + (1.0 - ema_keep) * weight_new
    return (first_new, second_new, weight_new, ema_new)


def per_device(
    tokens,
    seg_ids,
    time_steps,
    cotangent,
    weight_cols,
    weight_rows,
    bias_cols,
    bias_rows,
    first_cols,
    first_rows,
    first_bias_cols,
    first_bias_rows,
    second_cols,
    second_rows,
    second_bias_cols,
    second_bias_rows,
    ema_cols,
    ema_rows,
    ema_bias_cols,
    ema_bias_rows,
):
    own_width = weight_cols.shape[2]
    own_depth = weight_cols.shape[1]
    width = tokens.shape[1]
    rows = time_steps.shape[0]
    slots = time_steps.shape[1]
    row_len = tokens.shape[0] // rows
    units = row_len // UNIT
    quarter = row_len // 4
    quarter_units = units // 4
    dp_count = width // own_depth
    dp_place = lax.axis_index("dp")
    mp_place = lax.axis_index("mp")
    core, chip = mp_place % 2, mp_place // 2
    place = 2 * core + chip
    place_arg = place.reshape(1).astype(jnp.int32)

    cols_low = weight_cols.astype(low)
    rows_low = weight_rows.astype(low)
    own_qkv = jnp.concatenate([cols_low[0], cols_low[1], cols_low[2]], 1)
    own_rows = rows_low.transpose(2, 0, 1).reshape(own_depth, 5 * own_width)
    own_rest = jnp.concatenate([own_rows[:, :own_width]] + [cols_low[5 + i] for i in range(4)] + [own_rows[:, own_width:]], 1)
    w_qkv = ring_gather(own_qkv, dp_count)
    w_rest = lax.all_gather(own_rest, "dp", axis=0, tiled=True)
    w_out = w_rest[:, :own_width]
    w_up = w_rest[:, own_width : 5 * own_width]
    w_down = w_rest[:, 5 * own_width :]

    steps_all = share_steps(time_steps, dp_count).reshape(-1)
    half_width = width // 2
    feature = dp_place * own_depth + jnp.arange(own_depth)
    is_cos = feature < half_width
    index = jnp.where(is_cos, feature, feature - half_width).astype(wide)
    frequency = jnp.exp(-math.log(10000.0) * index / half_width)
    angles = steps_all.astype(wide)[:, None] * frequency[None, :]
    time_rows = jnp.where(is_cos[None, :], jnp.cos(angles), jnp.sin(angles))
    time_low = time_rows.astype(low)
    ada_low = jax.nn.silu(time_rows).astype(low)
    part_ada = jnp.einsum("sd,jde->sje", ada_low, cols_low[9:15], preferred_element_type=wide)
    part_time = jnp.einsum("sd,jde->sje", time_low, cols_low[3:5], preferred_element_type=wide)
    part_slots = jnp.concatenate([part_ada, part_time], 1).astype(low).reshape(-1, 8 * own_width)
    own_slots = ring_scatter(part_slots, dp_count).reshape(rows * slots, 8, own_width)
    own_mod = (own_slots[:, :6] + bias_cols[6:12][None]).astype(low)
    pieces = group_gather(own_mod)
    pieces = [pieces[0], pieces[2], pieces[1], pieces[3]]
    modulation = jnp.concatenate(in_group_order(pieces, mp_place), 2).astype(wide)
    modulation = modulation.reshape(rows, slots, 6 * width)
    zero_cols = jnp.zeros((rows * slots, own_width), wide)
    time_add = jnp.concatenate(
        [own_slots[:, 6] + bias_cols[0], zero_cols, own_slots[:, 7] + bias_cols[1]], 1
    ).reshape(rows, slots, 3 * own_width)

    def relative(values):
        return jnp.concatenate(
            [
                lax.dynamic_slice_in_dim(values, jnp.bitwise_xor(place, j) * (values.shape[0] // 4), values.shape[0] // 4, 0)
                for j in range(4)
            ],
            0,
        )

    seg_grid = seg_ids.reshape(rows, row_len)
    token_grid = tokens.reshape(rows, row_len, width)
    cot_grid = cotangent.reshape(rows, row_len, width)
    onehots, unit_mods, own_mods, tokens_rel, cots_rel = [], [], [], [], []
    inputs_one, qkvs, mixed = [], [], []
    for r in range(rows):
        unit_seg = relative(seg_grid[r].reshape(units, UNIT)[:, 0])
        onehot = (unit_seg[:, None] == jnp.arange(slots, dtype=jnp.int32)).astype(wide)
        unit_mod = jnp.dot(onehot, modulation[r], precision=highest).reshape(units, 6, 1, width)
        unit_add = jnp.dot(onehot, time_add[r], precision=highest)
        onehots.append(onehot)
        unit_mods.append(unit_mod)
        source = relative(token_grid[r])
        tokens_rel.append(source)
        cots_rel.append(relative(cot_grid[r]))
        normed, _ = norm_parts(source.astype(wide).reshape(units, UNIT, width))
        input_one = (normed * (1.0 + unit_mod[:, 1]) + unit_mod[:, 0]).astype(low)
        input_one = input_one.reshape(row_len, width)
        qkv = dot_as(input_one, w_qkv, DOT_NN).reshape(units, UNIT, 3 * own_width)
        qkv = (qkv + unit_add[:, None, :]).astype(low).reshape(row_len, 3 * own_width)
        inputs_one.append(input_one)
        qkvs.append(qkv)
        mixed.append(attend_forward(place_arg, qkv, seg_grid[r]))

    half = row_len // 2
    hidden_ones, attendeds, inputs_two = [], [], []
    for r in range(rows):
        sent = dot_as(mixed[r][half:], w_out, DOT_NT).astype(low)
        kept = dot_as(mixed[r][:half], w_out, DOT_NT)
        attended = group_scatter(kept, sent) + bias_rows[0]
        attended = attended.reshape(quarter_units, UNIT, width)
        own = unit_mods[r][:quarter_units]
        source = tokens_rel[r][:quarter].astype(wide).reshape(quarter_units, UNIT, width)
        hidden_one = source + own[:, 2] * attended
        normed, _ = norm_parts(hidden_one)
        input_two = (normed * (1.0 + own[:, 4]) + own[:, 3]).astype(low).reshape(quarter, width)
        hidden_ones.append(hidden_one)
        attendeds.append(attended)
        inputs_two.append(jnp.concatenate(group_gather(input_two), 0))

    bias_up = bias_cols[2:6].reshape(-1)
    out_rows, mlp_kept, grad_rows_low = [], [], []
    fields = [[] for _ in range(rows)]
    grad_w_up = grad_w_down = grad_w_out = grad_w_qkv = 0.0
    bias_up_grad = 0.0
    bias_row_two = bias_row_one = 0.0
    grad_hiddens, grad_attendeds = [], []
    for r in range(rows):
        own = unit_mods[r][:quarter_units]
        inner = dot_as(inputs_two[r], w_up, DOT_NN) + bias_up
        active = gelu_tanh(inner).astype(low)
        grad_mlp = (
            cots_rel[r].astype(wide).reshape(units, UNIT, width) * unit_mods[r][:, 5]
        ).reshape(row_len, width)
        grad_mlp_low = grad_mlp.astype(low)
        grad_active = dot_as(grad_mlp_low, w_down, DOT_NN)
        grad_inner = jax.vjp(gelu_tanh, inner)[1](grad_active)[0].astype(low)
        bias_up_grad = bias_up_grad + jnp.sum(grad_inner.astype(wide), axis=0)
        sent = dot_as(grad_inner[half:], w_up, DOT_NT).astype(low)
        kept = dot_as(grad_inner[:half], w_up, DOT_NT)
        grad_two = group_scatter(kept, sent).reshape(quarter_units, UNIT, width)
        grad_out = cots_rel[r][:quarter].astype(wide).reshape(quarter_units, UNIT, width)
        normed, inverse = norm_parts(hidden_ones[r])
        grad_hidden = grad_out + norm_back(normed, inverse, grad_two * (1.0 + own[:, 4]))
        grad_attended = grad_hidden * own[:, 2]
        grad_attendeds.append(
            jnp.concatenate(group_gather(grad_attended.astype(low).reshape(quarter, width)), 0)
        )
        bias_row_one = bias_row_one + jnp.sum(grad_attended, axis=(0, 1))
        grad_hiddens.append(grad_hidden)
        sent = dot_as(active[half:], w_down, DOT_NT).astype(low)
        kept = dot_as(active[:half], w_down, DOT_NT)
        mlp_out = (group_scatter(kept, sent) + bias_rows[1]).reshape(quarter_units, UNIT, width)
        out_own = (hidden_ones[r] + own[:, 5] * mlp_out).astype(low).reshape(quarter, width)
        out_rows.extend(in_group_order(group_gather(out_own), place))
        bias_row_two = bias_row_two + jnp.sum(grad_mlp[:quarter], axis=0)
        fields[r] = {
            2: jnp.sum(grad_hidden * attendeds[r], axis=1),
            3: jnp.sum(grad_two, axis=1),
            4: jnp.sum(grad_two * normed, axis=1),
            5: jnp.sum(grad_out * mlp_out, axis=1),
        }
        grad_w_up = grad_w_up + dot_as(inputs_two[r], grad_inner, DOT_TN)
        grad_w_down = grad_w_down + dot_as(grad_mlp_low, active, DOT_TN)

    time_sums = []
    input_rows = []
    for r in range(rows):
        grad_mixed = dot_as(grad_attendeds[r], w_out, DOT_NN).astype(low)
        grad_w_out = grad_w_out + dot_as(grad_attendeds[r], mixed[r], DOT_TN)
        grad_qkv = attend_backward(place_arg, qkvs[r], grad_mixed, seg_grid[r])
        sent = dot_as(grad_qkv[half:], w_qkv, DOT_NT).astype(low)
        kept = dot_as(grad_qkv[:half], w_qkv, DOT_NT)
        grad_one = group_scatter(kept, sent).reshape(quarter_units, UNIT, width)
        grad_w_qkv = grad_w_qkv + dot_as(inputs_one[r], grad_qkv, DOT_TN)
        own = unit_mods[r][:quarter_units]
        source = tokens_rel[r][:quarter].astype(wide).reshape(quarter_units, UNIT, width)
        normed, inverse = norm_parts(source)
        input_grad = grad_hiddens[r] + norm_back(normed, inverse, grad_one * (1.0 + own[:, 1]))
        input_rows.extend(
            in_group_order(group_gather(input_grad.astype(low).reshape(quarter, width)), place)
        )
        fields[r][0] = jnp.sum(grad_one, axis=1)
        fields[r][1] = jnp.sum(grad_one * normed, axis=1)
        unit_sums = jnp.sum(grad_qkv.astype(wide).reshape(units, UNIT, 3 * own_width), axis=1)
        slot_sums = jnp.dot(onehots[r].T, unit_sums, precision=highest)
        time_sums.append(
            jnp.stack([slot_sums[:, :own_width], slot_sums[:, 2 * own_width :]], 1)
        )
    out_tokens = jnp.concatenate(out_rows, 0)
    input_grads = jnp.concatenate(input_rows, 0).astype(wide)

    field_grid = jnp.stack(
        [jnp.stack([fields[r][f] for f in range(6)], 1) for r in range(rows)], 0
    ).astype(low)
    field_grid = field_grid.reshape(rows, quarter_units, 6, 2, 2, own_width)

    def side(values, which, axis):
        return lax.dynamic_index_in_dim(values, which, axis, keepdims=False)

    other = lax.ppermute(side(field_grid, 1 - chip, 3), "mp", CHIP_SWAP)
    field_grid = jnp.concatenate([side(field_grid, chip, 3), other], 1)
    other = lax.ppermute(side(field_grid, 1 - core, 3), "mp", CORE_SWAP)
    field_grid = jnp.concatenate([side(field_grid, core, 3), other], 1)
    slot_grads = [
        jnp.dot(onehots[r].T, field_grid[r].reshape(units, 6 * own_width).astype(wide), precision=highest)
        for r in range(rows)
    ]
    slot_grads = jnp.concatenate(
        [jnp.concatenate(slot_grads, 0), jnp.concatenate(time_sums, 0).reshape(rows * slots, 2 * own_width)], 1
    ).astype(low)
    bias_up_rows = jnp.zeros((8, 8 * own_width), low)
    bias_up_rows = bias_up_rows.at[0, : 4 * own_width].set(bias_up_grad.astype(low))
    slot_grads = ring_gather(jnp.concatenate([slot_grads, bias_up_rows], 0), dp_count)
    slot_grads = slot_grads.reshape(dp_count, rows * slots + 8, 8, own_width)
    bias_up_sum = jnp.sum(slot_grads[:, rows * slots, :4].astype(wide), axis=0)
    slot_grads = slot_grads[:, : rows * slots].reshape(dp_count * rows * slots, 8, own_width)
    ada_grad = jnp.einsum("sd,sje->jde", ada_low, slot_grads[:, :6], preferred_element_type=wide)
    time_grad = jnp.einsum("sd,sje->jde", time_low, slot_grads[:, 6:], preferred_element_type=wide)
    slot_sum = jnp.sum(slot_grads.astype(wide), axis=0)

    rest_parts = jnp.concatenate([grad_w_out, grad_w_up, grad_w_down], 1).astype(low)
    rest_sum = lax.psum_scatter(rest_parts, "dp", scatter_dimension=0, tiled=True).astype(wide)
    qkv_sum = ring_scatter(grad_w_qkv.astype(low), dp_count)

    def slabs(values):
        return [values[:, i * own_width : (i + 1) * own_width] for i in range(values.shape[1] // own_width)]

    grad_cols = jnp.concatenate(
        [
            jnp.stack(slabs(qkv_sum), 0),
            time_grad,
            jnp.stack(slabs(rest_sum[:, own_width : 5 * own_width]), 0),
            ada_grad,
        ],
        0,
    )
    rows_sum = jnp.concatenate([rest_sum[:, :own_width], rest_sum[:, 5 * own_width :]], 1)
    grad_rows = rows_sum.reshape(own_depth, 5, own_width).transpose(1, 2, 0)
    bias_cols_sum = jnp.concatenate([slot_sum[6:8], bias_up_sum, slot_sum[:6]], 0)
    bias_rows_sum = lax.psum(jnp.stack([bias_row_one, bias_row_two], 0), ("dp", "mp"))

    cols_state = adam_step(weight_cols, grad_cols, first_cols, second_cols, ema_cols, rate_matrix)
    rows_state = adam_step(weight_rows, grad_rows, first_rows, second_rows, ema_rows, rate_matrix)
    bias_cols_state = adam_step(
        bias_cols, bias_cols_sum, first_bias_cols, second_bias_cols, ema_bias_cols, rate_vector
    )
    bias_rows_state = adam_step(
        bias_rows, bias_rows_sum, first_bias_rows, second_bias_rows, ema_bias_rows, rate_vector
    )
    return (out_tokens, input_grads) + cols_state + rows_state + bias_cols_state + bias_rows_state


def solution(mesh):
    cols, rows, bias = P(None, "dp", "mp"), P(None, "mp", "dp"), P(None, "mp")
    state = (cols, rows, bias, P())
    placed = (P("dp", None), P("dp"), P("dp", None), P("dp", None)) + state * 4
    given = (P("dp", None), P("dp", None)) + (cols,) * 4 + (rows,) * 4 + (bias,) * 4 + (P(),) * 4
    return jax.shard_map(
        per_device, mesh=mesh, in_specs=placed, out_specs=given, check_vma=False
    )
```

time: 1500 us -> 839 us (0.56)
  waiting for transfers between devices: 783 us -> 156 us
  matrix products: 240 us -> 133 us
  starting transfers between devices: 0.46 us -> 86.8 us
  other arithmetic: 208 us -> 126 us
  Pallas kernels: 0 us -> 41.2 us
  between operations: 15.6 us -> 41.9 us
  blocking collectives: 62.6 us -> 44.8 us
  local copies, waits for them, and re-layouts: 183 us -> 199 us
    reduce_scatter x1, waiting for transfers between devices: 388 us -> 0.01 us  [per_device(): lax.psum_scatter(rest_parts, 'dp', scatter_dimension=0, tiled=True)]
    psum x3 -> x0, waiting for transfers between devices: 219 us -> none  [the longest x1 78.1 us: per_device(): lax.psum(mlp_part.astype(jnp.bfloat16), 'mp').astype(jnp.float32)]
    all_gather x2 -> x1, waiting for transfers between devices: 177 us -> 0.01 us  [per_device(): w_rest = lax.all_gather(own_rest, 'dp', axis=0, tiled=True)]
    ppermute x0 -> x92, waiting for transfers between devices: none -> 156 us  [the longest x8 54.1 us: group_scatter(): got = lax.ppermute(half[quarter:].astype(low), 'mp', CHIP_SWAP)]
    dot_general x59 -> x44, matrix products: 240 us -> 133 us  [the longest x32 125 us: dot_as(): return lax.dot_general(left, right, dims, preferred_element_type=wide)]
    ppermute x0 -> x92, starting transfers between devices: none -> 86.7 us  [the longest x20 21.4 us: travel(): running = lax.ppermute(running, 'dp', perm).astype(wide)]
    dynamic_update_slice x0 -> x18, local copies, waits for them, and re-layouts: none -> 51.8 us  [the longest x17 51.2 us: put(): return lax.dynamic_update_slice_in_dim(whole, piece, at, 0)]
    reduce_sum x16 -> x23, other arithmetic: 83.8 us -> 35.3 us  [the longest x2 11.1 us: per_device(): jnp.sum(grad_two * normed, axis=1)]
  transfers between devices with their start and end apart: 7 -> 94, of which waited for: 5 -> 32; matrix products, arithmetic and copies ran while one was open for 26% -> 50% of each run, Pallas kernels for 0% -> 5%
where the time goes in v1:
time: 839 us; the launch traced here: 830 us
  local copies, waits for them, and re-layouts  199 us (24%)
  waiting for transfers between devices  156 us (19%)
  matrix products  133 us (16%)
  other arithmetic  126 us (15%)
  starting transfers between devices  86.8 us (10%)
  blocking collectives  44.8 us (5%)
  between operations  41.9 us (5%)
  Pallas kernels  41.2 us (5%)
    dot_general x32, matrix products, dot_as(): return lax.dot_general(left, right, dims, preferred_element_type=wide)  125 us
    unnamed x442, local copies, waits for them, and re-layouts  64.9 us
    ppermute x8, waiting for transfers between devices, group_scatter(): got = lax.ppermute(half[quarter:].astype(low), 'mp', CHIP_SWAP)  54.1 us
    dynamic_update_slice x17, local copies, waits for them, and re-layouts, put(): return lax.dynamic_update_slice_in_dim(whole, piece, at, 0)  51.2 us
    ppermute x9, waiting for transfers between devices, group_gather(): chip = lax.ppermute(own, 'mp', CHIP_SWAP)  45.6 us
    psum x1, blocking collectives, per_device(): lax.psum(jnp.stack([bias_row_one, bias_row_two], 0), ('dp', 'mp'))  44.8 us
    pallas_call x2, Pallas kernels, attend_backward(): pl.pallas_call(body, out_shape=jax.ShapeDtypeStruct((row_len, 3 * width),...  25.4 us
    ppermute x20, starting transfers between devices, travel(): running = lax.ppermute(running, 'dp', perm).astype(wide)  21.4 us
  transfers between devices with their start and end apart: 94, of which 32 were waited for; matrix products, arithmetic and copies ran while one was open for 50% of the time, Pallas kernels for 5%

profile of v1, /device:TPU:0, one launch (start us, length us, event | category | flops | bytes accessed | tf_op | source)
XLA Modules:
  0.0 829.6 jit_solution(1528728354539477792)
XLA Ops:
  99.6 5.7 dynamic_update_slice.61
  163.9 6.1 dynamic_update_slice.62
  171.2 6.1 dynamic_update_slice.63
  188.2 6.2 dynamic_update_slice.64
  195.5 6.2 dynamic_update_slice.65
  216.3 6.1 dynamic_update_slice.66
  222.7 6.0 dynamic_update_slice.67
  238.1 5.9 add_convert_fusion.3
  244.1 7.7 attend_forward.2
  257.4 8.1 attend_forward.3
  306.9 8.6 %collective-permute-done.29 = bf16[256,1152]{1,0:T(8,128)(2,1)S(1)} collective-permute-done((bf16[256,1152]{1,0:T(8,128)(2,1)S(1)}, bf16[256,1152]{1,0:T(8,128)(2,1)S(1)}, u32[]{:S(2)}, u32[]{:S(2)}) %collective-permute-start.29) | collective-permute-done | bytes 589856 | tf_op jit(solution)/shard_map/ppermute | solution.py:126
  315.5 11.7 %collective-permute-done.39 = bf16[256,1152]{1,0:T(8,128)(2,1)S(1)} collective-permute-done((bf16[256,1152]{1,0:T(8,128)(2,1)S(1)}, bf16[256,1152]{1,0:T(8,128)(2,1)S(1)}, u32[]{:S(2)}, u32[]{:S(2)}) %collective-permute-start.39) | collective-permute-done | bytes 589856 | tf_op jit(solution)/shard_map/ppermute | solution.py:126
  333.0 12.8 %collective-permute-done.30 = bf16[256,1152]{1,0:T(8,128)(2,1)} collective-permute-done((bf16[256,1152]{1,0:T(8,128)(2,1)S(1)}, bf16[256,1152]{1,0:T(8,128)(2,1)}, u32[]{:S(2)}, u32[]{:S(2)}) %collective-permute-start.30) | collective-permute-done | bytes 589856 | tf_op jit(solution)/shard_map/ppermute | solution.py:131
  358.1 6.2 multiply_convert_fusion.1
  368.8 8.3 %convert_reduce_fusion.1 = (f32[1152]{0:T(1024)S(1)}, bf16[1024,1152]{1,0:T(8,128)(2,1)S(1)}) fusion(f32[1024,1152]{1,0:T(8,128)S(1)} %get-tuple-element.227, bf16[1024,1152]{1,0:T(8,128)(2,1)S(1)} %copy-done.90, bf16[1152,2592]{1,0:T(8,128)(2,1)} %all-gather.2.cloned.1.call-done), kind=kOutput, calls=%fused_computation.35 | convolution fusion | flops 2743860224 | bytes 12096000 | tf_op jit(solution)/shard_map/dot_general | solution.py:39
  382.6 7.6 multiply_convert_fusion
  390.2 8.7 %convert_reduce_fusion = (f32[1152]{0:T(1024)S(1)}, bf16[1024,1152]{1,0:T(8,128)(2,1)S(1)}) fusion(f32[1024,1152]{1,0:T(8,128)} %get-tuple-element.229, bf16[1024,1152]{1,0:T(8,128)(2,1)S(1)} %copy-done.89, bf16[1152,2592]{1,0:T(8,128)(2,1)S(1)} %bitcast.474), kind=kOutput, calls=%fused_computation.34 | convolution fusion | flops 2743860224 | bytes 12096000 | tf_op jit(solution)/shard_map/dot_general | solution.py:39
  409.1 7.3 fusion.115
  416.3 8.3 fusion
  436.5 6.4 collective-permute-done.49
  452.9 15.3 %collective-permute-done.59 = bf16[256,1152]{1,0:T(8,128)(2,1)} collective-permute-done((bf16[256,1152]{1,0:T(8,128)(2,1)}, bf16[256,1152]{1,0:T(8,128)(2,1)}, u32[]{:S(2)}, u32[]{:S(2)}) %collective-permute-start.59) | collective-permute-done | bytes 589856 | tf_op jit(solution)/shard_map/ppermute | solution.py:126
  480.9 44.8 %psum.7 = f32[2,1152]{1,0:T(2,128)S(1)} all-reduce(f32[2,1152]{1,0:T(2,128)S(1)} %pad_maximum_fusion.28), channel_id=1, replica_groups=mesh['dp'=8,'mp'=4] {'dp','mp'}, use_global_device_ids=true, to_apply=%region_43.44 | all-reduce | flops 2304 | bytes 18432 | tf_op jit(solution)/shard_map/psum | solution.py:547
  533.0 12.8 %attend_backward.2 = bf16[1024,864]{1,0:T(8,128)(2,1)S(1)} custom-call(s32[1]{0:T(128)} %bitcast.24.refs_0_, bf16[1024,864]{1,0:T(8,128)(2,1)S(1)} %bitcast.453, bf16[1024,288]{1,0:T(8,128)(2,1)S(1)} %copy.295.refs_2_, s32[1024,1]{1,0:T(8,128)S(1)} %copy-done.3, s32[1,1024]{1,0:T(1,128)S(1)} %bitcast.449), custom_call_target="tpu_custom_call" | custom-call | flops 1887436800 | bytes 4128768 | tf_op jit(solution)/shard_map/attend_backward/pallas_call | solution.py:260
  560.2 12.6 %attend_backward.3 = bf16[1024,864]{1,0:T(8,128)(2,1)S(1)} custom-call(s32[1]{0:T(128)} %bitcast.24.refs_0_, bf16[1024,864]{1,0:T(8,128)(2,1)S(1)} %bitcast.451, bf16[1024,288]{1,0:T(8,128)(2,1)S(1)} %copy.297.refs_2_, s32[1024,1]{1,0:T(8,128)S(1)} %copy.294.refs_2_.refs_3_, s32[1,1024]{1,0:T(1,128)S(1)} %bitcast.446), custom_call_target="tpu_custom_call" | custom-call | flops 1887436800 | bytes 4128768 | tf_op jit(solution)/shard_map/attend_backward/pallas_call | solution.py:260
  616.1 9.1 %copy.313 = bf16[1152,2592]{1,0:T(8,128)(2,1)} copy(bf16[1152,2592]{0,1:T(8,128)(2,1)} %pad_maximum_fusion) | data formatting | bytes 11943936
  648.3 12.1 %collective-permute-done.54 = bf16[256,1152]{1,0:T(8,128)(2,1)S(1)} collective-permute-done((bf16[256,1152]{1,0:T(8,128)(2,1)S(1)}, bf16[256,1152]{1,0:T(8,128)(2,1)S(1)}, u32[]{:S(2)}, u32[]{:S(2)}) %collective-permute-start.54) | collective-permute-done | bytes 589856 | tf_op jit(solution)/shard_map/ppermute | solution.py:126
  661.2 5.8 fusion.77
  713.8 8.0 collective-permute-done.86
  731.9 7.9 collective-permute-start.90
  762.1 11.0 %collective-permute-done.65 = bf16[256,1152]{1,0:T(8,128)(2,1)S(1)} collective-permute-done((bf16[256,1152]{1,0:T(8,128)(2,1)}, bf16[256,1152]{1,0:T(8,128)(2,1)S(1)}, u32[]{:S(2)}, u32[]{:S(2)}) %collective-permute-start.65) | collective-permute-done | bytes 589856 | tf_op jit(solution)/shard_map/ppermute | solution.py:131
  773.1 12.2 %collective-permute-done.45 = bf16[256,1152]{1,0:T(8,128)(2,1)S(1)} collective-permute-done((bf16[256,1152]{1,0:T(8,128)(2,1)S(1)}, bf16[256,1152]{1,0:T(8,128)(2,1)S(1)}, u32[]{:S(2)}, u32[]{:S(2)}) %collective-permute-start.45) | collective-permute-done | bytes 589856 | tf_op jit(solution)/shard_map/ppermute | solution.py:131
  814.8 7.8 multiply_add_fusion
  (916 shorter events, 478.2 us)
Async XLA Ops:
  7.2 259.6 %all-gather.2.cloned.1.call-start = ((), (), s32[]{:S(2)}) async-start(), calls=%async_computation.1 | async-start | bytes 6967296 | tf_op jit(solution)/shard_map/all_gather | solution.py:349
  11.6 158.5 %collective-permute-start.21 = (bf16[144,864]{1,0:T(8,128)(2,1)}, bf16[144,864]{1,0:T(8,128)(2,1)}, u32[]{:S(2)}, u32[]{:S(2)}) collective-permute-start(bf16[144,864]{1,0:T(8,128)(2,1)} %pad_maximum_fusion.22), channel_id=1, source_target_pairs={{8,0},{16,8},{24,16},{28,24},{20,28},{12,20},{4,12},{0,4},{9,1},{1... | collective-permute-start | bytes 746504 | tf_op jit(solution)/shard_map/ppermute | solution.py:75
  14.5 147.1 %collective-permute-start.20 = (bf16[144,864]{1,0:T(8,128)(2,1)}, bf16[144,864]{1,0:T(8,128)(2,1)}, u32[]{:S(2)}, u32[]{:S(2)}) collective-permute-start(bf16[144,864]{1,0:T(8,128)(2,1)} %pad_maximum_fusion.22), channel_id=1, source_target_pairs={{0,8},{8,16},{16,24},{24,28},{28,20},{20,12},{12,4},{4,0},{1,9},{9... | collective-permute-start | bytes 746504 | tf_op jit(solution)/shard_map/ppermute | solution.py:74
  15.8 73.7 %collective-permute-start = (s32[8,2,16]{2,1,0:T(2,128)}, s32[8,2,16]{2,1,0:T(2,128)}, u32[]{:S(2)}, u32[]{:S(2)}) collective-permute-start(s32[8,2,16]{2,1,0:T(2,128)} %constant_dynamic-update-slice_fusion.23), channel_id=1, source_target_pairs={{0,4},{4,0},{8,12},{12,8},{16,20},{20,16},{24,28},{28,24},{1,5},{5... | collective-permute-start | bytes 3080 | tf_op jit(solution)/shard_map/ppermute | solution.py:118
  20.2 780.0 %reduce-scatter.4.cloned.1.call-start = ((), (), s32[]{:S(2)}) async-start(), calls=%async_computation.2 | async-start | bytes 6967296 | tf_op jit(solution)/shard_map/reduce_scatter | solution.py:529
  148.7 30.7 %collective-permute-start.9 = (bf16[16,2304]{1,0:T(8,128)(2,1)S(1)}, bf16[16,2304]{1,0:T(8,128)(2,1)S(1)}, u32[]{:S(2)}, u32[]{:S(2)}) collective-permute-start(bf16[16,2304]{1,0:T(8,128)(2,1)S(1)} %add_convert_fusion.27), channel_id=1, source_target_pairs={{8,0},{16,8},{24,16},{28,24},{20,28},{12,20},{4,12},{0,4},{9,1},{1... | collective-permute-start | bytes 221192 | tf_op jit(solution)/shard_map/ppermute | solution.py:103
  150.5 27.2 %collective-permute-start.12 = (bf16[16,2304]{1,0:T(8,128)(2,1)S(1)}, bf16[16,2304]{1,0:T(8,128)(2,1)S(1)}, u32[]{:S(2)}, u32[]{:S(2)}) collective-permute-start(bf16[16,2304]{1,0:T(8,128)(2,1)S(1)} %add_convert_fusion.25), channel_id=1, source_target_pairs={{0,8},{8,16},{16,24},{24,28},{28,20},{20,12},{12,4},{4,0},{1,9},{9... | collective-permute-start | bytes 221192 | tf_op jit(solution)/shard_map/ppermute | solution.py:103
  270.1 26.6 %collective-permute-start.28 = (bf16[512,1152]{1,0:T(8,128)(2,1)}, bf16[512,1152]{1,0:T(8,128)(2,1)}, u32[]{:S(2)}, u32[]{:S(2)}) collective-permute-start(bf16[512,1152]{1,0:T(8,128)(2,1)} %convolution_convert_fusion.7), channel_id=1, source_target_pairs={{0,1},{1,0},{2,3},{3,2},{4,5},{5,4},{6,7},{7,6},{8,9},{9,8},{10,11... | collective-permute-start | bytes 3538952 | tf_op jit(solution)/shard_map/ppermute | solution.py:124
  273.1 27.8 %collective-permute-start.38 = (bf16[512,1152]{1,0:T(8,128)(2,1)}, bf16[512,1152]{1,0:T(8,128)(2,1)}, u32[]{:S(2)}, u32[]{:S(2)}) collective-permute-start(bf16[512,1152]{1,0:T(8,128)(2,1)} %convolution_convert_fusion.5), channel_id=1, source_target_pairs={{0,1},{1,0},{2,3},{3,2},{4,5},{5,4},{6,7},{7,6},{8,9},{9,8},{10,11... | collective-permute-start | bytes 3538952 | tf_op jit(solution)/shard_map/ppermute | solution.py:124
  329.5 28.6 %collective-permute-start.31 = (bf16[256,1152]{1,0:T(8,128)(2,1)S(1)}, bf16[256,1152]{1,0:T(8,128)(2,1)}, u32[]{:S(2)}, u32[]{:S(2)}) collective-permute-start(bf16[256,1152]{1,0:T(8,128)(2,1)S(1)} %fusion.43), channel_id=1, source_target_pairs={{0,1},{1,0},{2,3},{3,2},{4,5},{5,4},{6,7},{7,6},{8,9},{9,8},{10,11... | collective-permute-start | bytes 1769480 | tf_op jit(solution)/shard_map/ppermute | solution.py:132
  351.2 31.4 %collective-permute-start.41 = (bf16[256,1152]{1,0:T(8,128)(2,1)}, bf16[256,1152]{1,0:T(8,128)(2,1)}, u32[]{:S(2)}, u32[]{:S(2)}) collective-permute-start(bf16[256,1152]{1,0:T(8,128)(2,1)} %fusion.46), channel_id=1, source_target_pairs={{0,1},{1,0},{2,3},{3,2},{4,5},{5,4},{6,7},{7,6},{8,9},{9,8},{10,11... | collective-permute-start | bytes 1769480 | tf_op jit(solution)/shard_map/ppermute | solution.py:132
  368.2 60.2 %collective-permute-start.33 = (bf16[512,1152]{1,0:T(8,128)(2,1)S(1)}, bf16[512,1152]{1,0:T(8,128)(2,1)S(1)}, u32[]{:S(2)}, u32[]{:S(2)}) collective-permute-start(bf16[512,1152]{1,0:T(8,128)(2,1)S(1)} %convolution_convert_fusion.6), channel_id=1, source_target_pairs={{0,1},{1,0},{2,3},{3,2},{4,5},{5,4},{6,7},{7,6},{8,9},{9,8},{10,11... | collective-permute-start | bytes 3538952 | tf_op jit(solution)/shard_map/ppermute | solution.py:124
  379.2 45.5 %collective-permute-start.48 = (bf16[512,1152]{1,0:T(8,128)(2,1)S(1)}, bf16[512,1152]{1,0:T(8,128)(2,1)S(1)}, u32[]{:S(2)}, u32[]{:S(2)}) collective-permute-start(bf16[512,1152]{1,0:T(8,128)(2,1)S(1)} %convolution_convert_fusion.3), channel_id=1, source_target_pairs={{0,1},{1,0},{2,3},{3,2},{4,5},{5,4},{6,7},{7,6},{8,9},{9,8},{10,11... | collective-permute-start | bytes 3538952 | tf_op jit(solution)/shard_map/ppermute | solution.py:124
  406.4 41.0 %collective-permute-start.43 = (bf16[512,1152]{1,0:T(8,128)(2,1)S(1)}, bf16[512,1152]{1,0:T(8,128)(2,1)S(1)}, u32[]{:S(2)}, u32[]{:S(2)}) collective-permute-start(bf16[512,1152]{1,0:T(8,128)(2,1)S(1)} %convolution_convert_fusion.4), channel_id=1, source_target_pairs={{0,1},{1,0},{2,3},{3,2},{4,5},{5,4},{6,7},{7,6},{8,9},{9,8},{10,11... | collective-permute-start | bytes 3538952 | tf_op jit(solution)/shard_map/ppermute | solution.py:124
  431.5 216.8 %collective-permute-start.34 = (bf16[256,1152]{1,0:T(8,128)(2,1)}, bf16[256,1152]{1,0:T(8,128)(2,1)}, u32[]{:S(2)}, u32[]{:S(2)}) collective-permute-start(bf16[256,1152]{1,0:T(8,128)(2,1)} %slice.845), channel_id=1, source_target_pairs={{0,2},{1,3},{2,0},{3,1},{4,6},{5,7},{6,4},{7,5},{8,10},{9,11},{10,... | collective-permute-start | bytes 1769480 | tf_op jit(solution)/shard_map/ppermute | solution.py:126
  434.8 33.5 %collective-permute-start.59 = (bf16[256,1152]{1,0:T(8,128)(2,1)}, bf16[256,1152]{1,0:T(8,128)(2,1)}, u32[]{:S(2)}, u32[]{:S(2)}) collective-permute-start(bf16[256,1152]{1,0:T(8,128)(2,1)} %slice.840), channel_id=1, source_target_pairs={{0,2},{1,3},{2,0},{3,1},{4,6},{5,7},{6,4},{7,5},{8,10},{9,11},{10,... | collective-permute-start | bytes 1769480 | tf_op jit(solution)/shard_map/ppermute | solution.py:126
  445.6 35.3 %collective-permute-start.50 = (bf16[256,1152]{1,0:T(8,128)(2,1)}, bf16[256,1152]{1,0:T(8,128)(2,1)}, u32[]{:S(2)}, u32[]{:S(2)}) collective-permute-start(bf16[256,1152]{1,0:T(8,128)(2,1)} %fusion.83), channel_id=1, source_target_pairs={{0,2},{1,3},{2,0},{3,1},{4,6},{5,7},{6,4},{7,5},{8,10},{9,11},{10,... | collective-permute-start | bytes 1769480 | tf_op jit(solution)/shard_map/ppermute | solution.py:131
  452.9 74.2 %collective-permute-start.51 = (bf16[256,1152]{1,0:T(8,128)(2,1)}, bf16[256,1152]{1,0:T(8,128)(2,1)}, u32[]{:S(2)}, u32[]{:S(2)}) collective-permute-start(bf16[256,1152]{1,0:T(8,128)(2,1)} %fusion.83), channel_id=1, source_target_pairs={{0,1},{1,0},{2,3},{3,2},{4,5},{5,4},{6,7},{7,6},{8,9},{9,8},{10,11... | collective-permute-start | bytes 1769480 | tf_op jit(solution)/shard_map/ppermute | solution.py:132
  474.1 79.5 %collective-permute-start.61 = (bf16[256,1152]{1,0:T(8,128)(2,1)}, bf16[256,1152]{1,0:T(8,128)(2,1)}, u32[]{:S(2)}, u32[]{:S(2)}) collective-permute-start(bf16[256,1152]{1,0:T(8,128)(2,1)} %fusion.85), channel_id=1, source_target_pairs={{0,1},{1,0},{2,3},{3,2},{4,5},{5,4},{6,7},{7,6},{8,9},{9,8},{10,11... | collective-permute-start | bytes 1769480 | tf_op jit(solution)/shard_map/ppermute | solution.py:132
  474.3 52.9 %collective-permute-start.60 = (bf16[256,1152]{1,0:T(8,128)(2,1)}, bf16[256,1152]{1,0:T(8,128)(2,1)}, u32[]{:S(2)}, u32[]{:S(2)}) collective-permute-start(bf16[256,1152]{1,0:T(8,128)(2,1)} %fusion.85), channel_id=1, source_target_pairs={{0,2},{1,3},{2,0},{3,1},{4,6},{5,7},{6,4},{7,5},{8,10},{9,11},{10,... | collective-permute-start | bytes 1769480 | tf_op jit(solution)/shard_map/ppermute | solution.py:131
  480.9 46.2 %collective-permute-start.52 = (bf16[256,1152]{1,0:T(8,128)(2,1)}, bf16[256,1152]{1,0:T(8,128)(2,1)S(1)}, u32[]{:S(2)}, u32[]{:S(2)}) collective-permute-start(bf16[256,1152]{1,0:T(8,128)(2,1)} %collective-permute-done.50), channel_id=1, source_target_pairs={{0,1},{1,0},{2,3},{3,2},{4,5},{5,4},{6,7},{7,6},{8,9},{9,8},{10,11... | collective-permute-start | bytes 1769480 | tf_op jit(solution)/shard_map/ppermute | solution.py:133
  527.1 26.4 %collective-permute-start.62 = (bf16[256,1152]{1,0:T(8,128)(2,1)}, bf16[256,1152]{1,0:T(8,128)(2,1)}, u32[]{:S(2)}, u32[]{:S(2)}) collective-permute-start(bf16[256,1152]{1,0:T(8,128)(2,1)} %collective-permute-done.60), channel_id=1, source_target_pairs={{0,1},{1,0},{2,3},{3,2},{4,5},{5,4},{6,7},{7,6},{8,9},{9,8},{10,11... | collective-permute-start | bytes 1769480 | tf_op jit(solution)/shard_map/ppermute | solution.py:133
  610.4 29.0 %collective-permute-start.63 = (bf16[512,1152]{1,0:T(8,128)(2,1)}, bf16[512,1152]{1,0:T(8,128)(2,1)}, u32[]{:S(2)}, u32[]{:S(2)}) collective-permute-start(bf16[512,1152]{1,0:T(8,128)(2,1)} %convolution_convert_fusion), channel_id=1, source_target_pairs={{0,1},{1,0},{2,3},{3,2},{4,5},{5,4},{6,7},{7,6},{8,9},{9,8},{10,11... | collective-permute-start | bytes 3538952 | tf_op jit(solution)/shard_map/ppermute | solution.py:124
  631.2 44.1 %collective-permute-start.44 = (bf16[256,1152]{1,0:T(8,128)(2,1)}, bf16[256,1152]{1,0:T(8,128)(2,1)}, u32[]{:S(2)}, u32[]{:S(2)}) collective-permute-start(bf16[256,1152]{1,0:T(8,128)(2,1)} %slice.843), channel_id=1, source_target_pairs={{0,2},{1,3},{2,0},{3,1},{4,6},{5,7},{6,4},{7,5},{8,10},{9,11},{10,... | collective-permute-start | bytes 1769480 | tf_op jit(solution)/shard_map/ppermute | solution.py:126
  644.5 30.9 %collective-permute-start.64 = (bf16[256,1152]{1,0:T(8,128)(2,1)}, bf16[256,1152]{1,0:T(8,128)(2,1)}, u32[]{:S(2)}, u32[]{:S(2)}) collective-permute-start(bf16[256,1152]{1,0:T(8,128)(2,1)} %slice.839), channel_id=1, source_target_pairs={{0,2},{1,3},{2,0},{3,1},{4,6},{5,7},{6,4},{7,5},{8,10},{9,11},{10,... | collective-permute-start | bytes 1769480 | tf_op jit(solution)/shard_map/ppermute | solution.py:126
  697.1 64.5 %collective-permute-start.56 = (bf16[256,1152]{1,0:T(8,128)(2,1)}, bf16[256,1152]{1,0:T(8,128)(2,1)}, u32[]{:S(2)}, u32[]{:S(2)}) collective-permute-start(bf16[256,1152]{1,0:T(8,128)(2,1)} %add_convert_fusion.11), channel_id=1, source_target_pairs={{0,1},{1,0},{2,3},{3,2},{4,5},{5,4},{6,7},{7,6},{8,9},{9,8},{10,11... | collective-permute-start | bytes 1769480 | tf_op jit(solution)/shard_map/ppermute | solution.py:132
  697.2 59.5 %collective-permute-start.55 = (bf16[256,1152]{1,0:T(8,128)(2,1)}, bf16[256,1152]{1,0:T(8,128)(2,1)}, u32[]{:S(2)}, u32[]{:S(2)}) collective-permute-start(bf16[256,1152]{1,0:T(8,128)(2,1)} %add_convert_fusion.11), channel_id=1, source_target_pairs={{0,2},{1,3},{2,0},{3,1},{4,6},{5,7},{6,4},{7,5},{8,10},{9,11},{10,... | collective-permute-start | bytes 1769480 | tf_op jit(solution)/shard_map/ppermute | solution.py:131
  698.5 47.0 %collective-permute-start.35 = (bf16[256,1152]{1,0:T(8,128)(2,1)}, bf16[256,1152]{1,0:T(8,128)(2,1)}, u32[]{:S(2)}, u32[]{:S(2)}) collective-permute-start(bf16[256,1152]{1,0:T(8,128)(2,1)} %fusion.81), channel_id=1, source_target_pairs={{0,2},{1,3},{2,0},{3,1},{4,6},{5,7},{6,4},{7,5},{8,10},{9,11},{10,... | collective-permute-start | bytes 1769480 | tf_op jit(solution)/shard_map/ppermute | solution.py:131
  745.5 42.8 %collective-permute-start.66 = (bf16[256,1152]{1,0:T(8,128)(2,1)}, bf16[256,1152]{1,0:T(8,128)(2,1)}, u32[]{:S(2)}, u32[]{:S(2)}) collective-permute-start(bf16[256,1152]{1,0:T(8,128)(2,1)} %add_convert_fusion.10), channel_id=1, source_target_pairs={{0,1},{1,0},{2,3},{3,2},{4,5},{5,4},{6,7},{7,6},{8,9},{9,8},{10,11... | collective-permute-start | bytes 1769480 | tf_op jit(solution)/shard_map/ppermute | solution.py:132
  757.3 28.0 %collective-permute-start.45 = (bf16[256,1152]{1,0:T(8,128)(2,1)S(1)}, bf16[256,1152]{1,0:T(8,128)(2,1)S(1)}, u32[]{:S(2)}, u32[]{:S(2)}) collective-permute-start(bf16[256,1152]{1,0:T(8,128)(2,1)S(1)} %copy-done.80), channel_id=1, source_target_pairs={{0,2},{1,3},{2,0},{3,1},{4,6},{5,7},{6,4},{7,5},{8,10},{9,11},{10,... | collective-permute-start | bytes 1769480 | tf_op jit(solution)/shard_map/ppermute | solution.py:131
  758.8 26.5 %collective-permute-start.57 = (bf16[256,1152]{1,0:T(8,128)(2,1)}, bf16[256,1152]{1,0:T(8,128)(2,1)S(1)}, u32[]{:S(2)}, u32[]{:S(2)}) collective-permute-start(bf16[256,1152]{1,0:T(8,128)(2,1)} %collective-permute-done.55), channel_id=1, source_target_pairs={{0,1},{1,0},{2,3},{3,2},{4,5},{5,4},{6,7},{7,6},{8,9},{9,8},{10,11... | collective-permute-start | bytes 1769480 | tf_op jit(solution)/shard_map/ppermute | solution.py:133
  761.6 34.7 %collective-permute-start.46 = (bf16[256,1152]{1,0:T(8,128)(2,1)S(1)}, bf16[256,1152]{1,0:T(8,128)(2,1)S(1)}, u32[]{:S(2)}, u32[]{:S(2)}) collective-permute-start(bf16[256,1152]{1,0:T(8,128)(2,1)S(1)} %copy-done.80), channel_id=1, source_target_pairs={{0,1},{1,0},{2,3},{3,2},{4,5},{5,4},{6,7},{7,6},{8,9},{9,8},{10,11... | collective-permute-start | bytes 1769480 | tf_op jit(solution)/shard_map/ppermute | solution.py:132
  (253 other events, 3871.5 us)
Sparse Core Ops, SparseCore 0:
  20.3 98.4 all-gather.1
  625.4 125.1 reduce-scatter.3

commit v2 on v1

v2 whole, which is shorter than its diff:
```python
import math

import jax
import jax.numpy as jnp
from jax import lax
from jax.experimental import pallas as pl
from jax.experimental.pallas import tpu as pltpu
from jax.sharding import PartitionSpec as P

HEAD_DIM = 72
STEP = 10
UNIT = 64
REACH = 192


highest = lax.Precision.HIGHEST
beta_one = 0.9
beta_two = 0.999
adam_eps = 1e-08
decay_rate = 0.1
rate_matrix = 0.05
rate_vector = 0.5
ema_keep = 0.7
norm_eps = 1e-06
neg_large = -1e30
score_scale = HEAD_DIM**-0.5
low = jnp.bfloat16
wide = jnp.float32

DOT_NN = (((1,), (0,)), ((), ()))
DOT_NT = (((1,), (1,)), ((), ()))
DOT_TN = (((0,), (0,)), ((), ()))

CORE_SWAP = [(i, i ^ 1) for i in range(4)]
CHIP_SWAP = [(i, i ^ 2) for i in range(4)]


def dot_as(left, right, dims):
    return lax.dot_general(left, right, dims, preferred_element_type=wide)


def ring_order(count):
    return list(range(0, count, 2)) + list(range(count - 1, 0, -2))


def ring_perms(count):
    order = ring_order(count)
    onward = [(order[i], order[(i + 1) % count]) for i in range(count)]
    return onward, [(b, a) for a, b in onward]


def ring_place(count):
    order = ring_order(count)
    spots = [order.index(i) for i in range(count)]
    return jnp.array(order), jnp.array(spots)[lax.axis_index("dp")]


def ring_pieces(shard, count):
    rows = shard.shape[0]
    cut = rows // 32 * 16
    onward, backward = ring_perms(count)
    order, spot = ring_place(count)
    pieces, rows_at = [shard], [order[spot] * rows]
    ahead = behind = shard
    for hop in range(1, count // 2):
        ahead = lax.ppermute(ahead, "dp", onward)
        behind = lax.ppermute(behind, "dp", backward)
        pieces += [ahead, behind]
        rows_at += [order[(spot - hop) % count] * rows, order[(spot + hop) % count] * rows]
    far = order[(spot + count // 2) % count] * rows
    pieces += [
        lax.ppermute(ahead[:cut], "dp", onward),
        lax.ppermute(behind[cut:], "dp", backward),
    ]
    return pieces, jnp.stack(rows_at + [far, far + cut]).astype(jnp.int32)


def place_kernel(at_ref, *refs):
    count = len(refs) // 2 - 1
    pieces, out_ref, sems = refs[:-2], refs[-2], refs[-1]
    copies = [
        pltpu.make_async_copy(
            piece, out_ref.at[pl.ds(pl.multiple_of(at_ref[i], 16), piece.shape[0])], sems.at[i]
        )
        for i, piece in enumerate(pieces)
    ]
    for copy in copies:
        copy.start()
    for copy in copies:
        copy.wait()


def ring_gather(shard, count):
    if count not in (4, 8):
        return lax.all_gather(shard, "dp", axis=0, tiled=True)
    pieces, at = ring_pieces(shard, count)
    return place_pieces(at, pieces)


def ring_scatter(parts, count, split=True):
    if count not in (4, 8):
        return lax.psum_scatter(parts.astype(low), "dp", scatter_dimension=0, tiled=True).astype(
            wide
        )
    rows = parts.shape[0] // count
    half = rows // 2
    onward, backward = ring_perms(count)
    order, spot = ring_place(count)

    def chunk(ahead, start, stop):
        at = order[(spot + ahead) % count] * rows + start
        return lax.dynamic_slice_in_dim(parts, at, stop - start, 0).astype(wide)

    def travel(perm, sign, hops, start, stop):
        running = chunk(sign * hops, start, stop).astype(low)
        for hop in range(hops - 1, 0, -1):
            running = lax.ppermute(running, "dp", perm).astype(wide)
            running = (running + chunk(sign * hop, start, stop)).astype(low)
        return lax.ppermute(running, "dp", perm).astype(wide)

    long, short = count // 2, count // 2 - 1
    if not split:
        both = travel(onward, 1, long, 0, rows) + travel(backward, -1, short, 0, rows)
        return both + chunk(0, 0, rows)
    first = travel(onward, 1, long, 0, half) + travel(backward, -1, short, 0, half)
    second = travel(onward, 1, short, half, rows) + travel(backward, -1, long, half, rows)
    return jnp.concatenate([first, second], 0) + chunk(0, 0, rows)


def share_steps(steps, count):
    if count not in (4, 8):
        return lax.all_gather(steps, "dp", axis=0, tiled=True)
    blank = jnp.zeros((count,) + steps.shape, steps.dtype)
    known = lax.dynamic_update_slice_in_dim(blank, steps[None], lax.axis_index("dp"), 0)
    reach = 1
    while reach < count:
        known = known + lax.ppermute(known, "dp", [(i, i ^ reach) for i in range(count)])
        reach *= 2
    return known.reshape((count * steps.shape[0],) + steps.shape[1:])


def group_scatter(kept, sent):
    quarter = kept.shape[0] // 2
    got = lax.ppermute(sent, "mp", CORE_SWAP)
    passed = (kept[quarter:] + got[quarter:].astype(wide)).astype(low)
    return kept, got, lax.ppermute(passed, "mp", CHIP_SWAP)


def group_gather(own):
    chip = lax.ppermute(own, "mp", CHIP_SWAP)
    core = lax.ppermute(own, "mp", CORE_SWAP)
    both = lax.ppermute(chip, "mp", CORE_SWAP)
    return [own, chip, core, both]


def in_group_order(pieces, place):
    stacked = jnp.stack(pieces, 0)
    return [
        lax.dynamic_index_in_dim(stacked, jnp.bitwise_xor(place, j), 0, keepdims=False)
        for j in range(4)
    ]


def key_windows(row_len, block):
    return [
        (at, max(0, at - REACH), min(row_len, at + block + REACH))
        for at in range(0, row_len, block)
    ]


def relative_at(place, j, block):
    return pl.multiple_of(jnp.bitwise_xor(place, j) * block, block)


def attend_forward_kernel(
    place_ref, qkv_ref, seg_col_ref, seg_row_ref, w_ref, out_ref, kept_ref, sent_ref, q_s, k_s, v_s, *, heads
):
    row_len = qkv_ref.shape[0]
    width = heads * HEAD_DIM
    block = row_len // 4
    place = place_ref[0]
    for j in range(4):
        at = relative_at(place, j, block)
        to = slice(j * block, (j + 1) * block)
        for h in range(heads):
            c = h * HEAD_DIM
            q_s[h, to, :] = qkv_ref[pl.ds(at, block), c : c + HEAD_DIM]
            k_s[h, to, :] = qkv_ref[pl.ds(at, block), width + c : width + c + HEAD_DIM]
            v_s[h, to, :] = qkv_ref[pl.ds(at, block), 2 * width + c : 2 * width + c + HEAD_DIM]
    for j, (at, start, stop) in enumerate(key_windows(row_len, block)):
        same = seg_col_ref[start:stop, :] == seg_row_ref[:, at : at + block]
        mixed = []
        for h in range(heads):
            scores = dot_as(k_s[h, start:stop, :], q_s[h, at : at + block, :], DOT_NT)
            scores = jnp.where(same, scores, neg_large)
            top = jnp.max(scores, axis=0, keepdims=True)
            weights = jnp.exp((scores - top) * score_scale)
            total = jnp.sum(weights, axis=0, keepdims=True)
            gathered = dot_as(v_s[h, start:stop, :], weights.astype(low), DOT_TN)
            mixed.append(gathered * (1.0 / total))
        out_ref[pl.ds(relative_at(place, j, block), block), :] = (
            jnp.concatenate(mixed, axis=0).T.astype(low)
        )
    w_out = w_ref[:, 3 * width :]
    half = row_len // 2
    kept_ref[...] = dot_as(out_ref[:half, :], w_out, DOT_NT)
    sent_ref[...] = dot_as(out_ref[half:, :], w_out, DOT_NT).astype(low)


def attend_backward_kernel(
    place_ref, qkv_ref, g0_ref, g1_ref, g2_ref, g3_ref, seg_col_ref, seg_row_ref, w_ref,
    out_ref, kept_ref, sent_ref, sums_ref, q_s, k_s, v_s, g_s, dk_s, dv_s, *, heads
):
    row_len = qkv_ref.shape[0]
    width = heads * HEAD_DIM
    block = row_len // 4
    place = place_ref[0]
    dk_s[...] = jnp.zeros_like(dk_s)
    dv_s[...] = jnp.zeros_like(dv_s)
    w_out = w_ref[:, 3 * width :]
    for j, g_ref in enumerate((g0_ref, g1_ref, g2_ref, g3_ref)):
        grad = dot_as(g_ref[...], w_out, DOT_NN).astype(low)
        at = relative_at(place, j, block)
        for h in range(heads):
            g_s[h, pl.ds(at, block), :] = grad[:, h * HEAD_DIM : (h + 1) * HEAD_DIM]
    for j in range(4):
        at = relative_at(place, j, block)
        to = slice(j * block, (j + 1) * block)
        for h in range(heads):
            c = h * HEAD_DIM
            q_s[h, to, :] = qkv_ref[pl.ds(at, block), c : c + HEAD_DIM]
            k_s[h, to, :] = qkv_ref[pl.ds(at, block), width + c : width + c + HEAD_DIM]
            v_s[h, to, :] = qkv_ref[pl.ds(at, block), 2 * width + c : 2 * width + c + HEAD_DIM]
    for j, (at, start, stop) in enumerate(key_windows(row_len, block)):
        same = seg_col_ref[start:stop, :] == seg_row_ref[:, at : at + block]
        grads = []
        for h in range(heads):
            query = q_s[h, at : at + block, :]
            grad = g_s[h, at : at + block, :]
            keys = k_s[h, start:stop, :]
            scores = jnp.where(same, dot_as(keys, query, DOT_NT), neg_large)
            top = jnp.max(scores, axis=0, keepdims=True)
            weights = jnp.exp((scores - top) * score_scale)
            probs = weights * (1.0 / jnp.sum(weights, axis=0, keepdims=True))
            grad_probs = dot_as(v_s[h, start:stop, :], grad, DOT_NT)
            inner = jnp.sum(grad_probs * probs, axis=0, keepdims=True)
            grad_scores = (probs * (grad_probs - inner)).astype(low)
            dv_s[h, start:stop, :] += dot_as(probs.astype(low), grad, DOT_NN)
            dk_s[h, start:stop, :] += dot_as(grad_scores, query, DOT_NN)
            grads.append(dot_as(keys, grad_scores, DOT_TN) * score_scale)
        out_ref[pl.ds(relative_at(place, j, block), block), 0:width] = (
            jnp.concatenate(grads, axis=0).T.astype(low)
        )
    for j in range(4):
        at = slice(j * block, (j + 1) * block)
        to = relative_at(place, j, block)
        out_ref[pl.ds(to, block), width : 2 * width] = jnp.concatenate(
            [(dk_s[h, at, :] * score_scale).astype(low) for h in range(heads)], axis=1
        )
        out_ref[pl.ds(to, block), 2 * width : 3 * width] = jnp.concatenate(
            [dv_s[h, at, :].astype(low) for h in range(heads)], axis=1
        )
    half = row_len // 2
    w_qkv = w_ref[:, : 3 * width]
    kept_ref[...] = dot_as(out_ref[:half, :], w_qkv, DOT_NT)
    sent_ref[...] = dot_as(out_ref[half:, :], w_qkv, DOT_NT).astype(low)
    for u in range(row_len // UNIT):
        sums_ref[u : u + 1, :] = jnp.sum(
            out_ref[u * UNIT : (u + 1) * UNIT, :].astype(wide), axis=0, keepdims=True
        )


SMEM_SPEC = pl.BlockSpec(memory_space=pltpu.SMEM)
VMEM_SPEC = pl.BlockSpec(memory_space=pltpu.VMEM)


def shape_of(shape, kind):
    return jax.ShapeDtypeStruct(shape, kind)


def attend_forward(place, qkv, seg_row, weights):
    row_len, width = qkv.shape[0], qkv.shape[1] // 3
    heads = width // HEAD_DIM
    full = weights.shape[0]

    def body(*refs):
        attend_forward_kernel(*refs, heads=heads)

    return pl.pallas_call(
        body,
        out_shape=(
            shape_of((row_len, width), low),
            shape_of((row_len // 2, full), wide),
            shape_of((row_len // 2, full), low),
        ),
        in_specs=[SMEM_SPEC] + [VMEM_SPEC] * 4,
        out_specs=(VMEM_SPEC,) * 3,
        scratch_shapes=[pltpu.VMEM((heads, row_len, HEAD_DIM), low)] * 3,
        compiler_params=pltpu.CompilerParams(vmem_limit_bytes=40 * 2**20),
        cost_estimate=pl.CostEstimate(
            flops=4 * row_len * 640 * width + 2 * row_len * width * full,
            bytes_accessed=8 * row_len * width + 5 * row_len * full,
            transcendentals=heads * row_len * 640,
        ),
        name="attend_forward",
    )(place, qkv, seg_row.reshape(row_len, 1), seg_row.reshape(1, row_len), weights)


def attend_backward(place, qkv, grads, seg_row, weights):
    row_len, width = qkv.shape[0], qkv.shape[1] // 3
    heads = width // HEAD_DIM
    full = weights.shape[0]

    def body(*refs):
        attend_backward_kernel(*refs, heads=heads)

    return pl.pallas_call(
        body,
        out_shape=(
            shape_of((row_len, 3 * width), low),
            shape_of((row_len // 2, full), wide),
            shape_of((row_len // 2, full), low),
            shape_of((row_len // UNIT, 3 * width), wide),
        ),
        in_specs=[SMEM_SPEC] + [VMEM_SPEC] * 8,
        out_specs=(VMEM_SPEC,) * 4,
        scratch_shapes=[pltpu.VMEM((heads, row_len, HEAD_DIM), low)] * 4
        + [pltpu.VMEM((heads, row_len, HEAD_DIM), wide)] * 2,
        compiler_params=pltpu.CompilerParams(vmem_limit_bytes=48 * 2**20),
        cost_estimate=pl.CostEstimate(
            flops=10 * row_len * 640 * width + 8 * row_len * width * full,
            bytes_accessed=14 * row_len * width + 8 * row_len * full,
            transcendentals=heads * row_len * 640,
        ),
        name="attend_backward",
    )(place, qkv, *grads, seg_row.reshape(row_len, 1), seg_row.reshape(1, row_len), weights)


def norm_parts(values):
    centre = values - jnp.mean(values, axis=-1, keepdims=True)
    inverse = lax.rsqrt(jnp.mean(centre * centre, axis=-1, keepdims=True) + norm_eps)
    return centre * inverse, inverse


def norm_back(normed, inverse, grad):
    return inverse * (
        grad
        - jnp.mean(grad, axis=-1, keepdims=True)
        - normed * jnp.mean(grad * normed, axis=-1, keepdims=True)
    )


def unit_rows(ref):
    return [(u, slice(u * UNIT, (u + 1) * UNIT)) for u in range(ref.shape[0] // UNIT)]


def column(values, index, width):
    return values[:, index * width : (index + 1) * width]


def open_kernel(place_ref, x_ref, tab_ref, add_ref, w_ref, a_ref, qkv_ref):
    width = x_ref.shape[1]
    for u, at in unit_rows(x_ref):
        normed, _ = norm_parts(x_ref[at, :].astype(wide))
        table = tab_ref[0, u : u + 1, :]
        a_ref[at, :] = (normed * (1.0 + column(table, 1, width)) + column(table, 0, width)).astype(low)
    qkv = dot_as(a_ref[...], w_ref[:, : qkv_ref.shape[1]], DOT_NN)
    for u, at in unit_rows(x_ref):
        qkv_ref[at, :] = (qkv[at, :] + add_ref[0, u : u + 1, :]).astype(low)


def first_kernel(place_ref, x_ref, kept_ref, got_ref, passed_ref, bias_ref, tab_ref, att_ref, hid_ref, a_ref):
    width = x_ref.shape[1]
    for u, at in unit_rows(x_ref):
        table = tab_ref[0, u : u + 1, :]
        attended = kept_ref[at, :] + got_ref[at, :].astype(wide) + passed_ref[at, :].astype(wide)
        attended = attended + bias_ref[0:1, :]
        hidden = x_ref[at, :].astype(wide) + column(table, 0, width) * attended
        normed, _ = norm_parts(hidden)
        att_ref[at, :] = attended
        hid_ref[at, :] = hidden
        a_ref[at, :] = (normed * (1.0 + column(table, 2, width)) + column(table, 1, width)).astype(low)


def down_back_kernel(place_ref, cot_ref, tab_ref, w_ref, grad_ref, dm_ref):
    width = cot_ref.shape[1]
    for u, at in unit_rows(cot_ref):
        table = tab_ref[0, u : u + 1, :]
        grad_ref[at, :] = (cot_ref[at, :].astype(wide) * column(table, 3, width)).astype(low)
    dm_ref[...] = dot_as(grad_ref[...], w_ref[:, w_ref.shape[1] // 2 :], DOT_NN).astype(low)


def gelu_both(values):
    scale = math.sqrt(2.0 / math.pi)
    square = values * values
    turned = jnp.tanh(scale * values * (1.0 + 0.044715 * square))
    upper = 0.5 * (1.0 + turned)
    slope = upper + 0.5 * values * (1.0 - turned * turned) * scale * (1.0 + 3 * 0.044715 * square)
    return values * upper, slope


def up_kernel(
    a0_ref, a1_ref, a2_ref, a3_ref, dm_ref, bias_ref, w_ref, m_ref, dz_ref, kept_ref, sent_ref, sums_ref, a_s
):
    step = pl.program_id(0)
    for j, piece in enumerate((a0_ref, a1_ref, a2_ref, a3_ref)):

        @pl.when(step == j)
        def _(piece=piece):
            a_s[...] = piece[...]

    w_up = w_ref[:, : w_ref.shape[1] // 2]
    inner = dot_as(a_s[...], w_up, DOT_NN) + bias_ref[...]
    active, slope = gelu_both(inner)
    m_ref[...] = active.astype(low)
    grad = (dm_ref[...].astype(wide) * slope).astype(low)
    dz_ref[...] = grad
    sums_ref[0] = jnp.sum(grad.astype(wide).reshape(-1, 8, grad.shape[1]), axis=0)
    back = dot_as(grad, w_up, DOT_NT)

    @pl.when(step < 2)
    def _():
        kept_ref[...] = back

    @pl.when(step >= 2)
    def _():
        sent_ref[...] = back.astype(low)


def down_kernel(m_ref, w_ref, kept_ref, sent_ref):
    step = pl.program_id(0)
    out = dot_as(m_ref[...], w_ref[:, w_ref.shape[1] // 2 :], DOT_NT)

    @pl.when(step < 2)
    def _():
        kept_ref[...] = out

    @pl.when(step >= 2)
    def _():
        sent_ref[...] = out.astype(low)


def second_kernel(
    place_ref, cot_ref, kept_ref, got_ref, passed_ref, hid_ref, att_ref, tab_ref, gh_ref, ga_ref, sums_ref
):
    width = cot_ref.shape[1]
    bias = jnp.zeros((1, width), wide)
    sums_ref[...] = jnp.zeros_like(sums_ref)
    for u, at in unit_rows(cot_ref):
        table = tab_ref[0, u : u + 1, :]
        grad_two = kept_ref[at, :] + got_ref[at, :].astype(wide) + passed_ref[at, :].astype(wide)
        normed, inverse = norm_parts(hid_ref[at, :])
        grad = cot_ref[at, :].astype(wide) + norm_back(
            normed, inverse, grad_two * (1.0 + column(table, 2, width))
        )
        grad_att = grad * column(table, 0, width)
        gh_ref[at, :] = grad
        ga_ref[at, :] = grad_att.astype(low)
        bias = bias + jnp.sum(grad_att, axis=0, keepdims=True)
        sums_ref[u : u + 1, :] = jnp.sum(grad * att_ref[at, :], axis=0, keepdims=True)
        sums_ref[4 + u : 5 + u, :] = jnp.sum(grad_two, axis=0, keepdims=True)
        sums_ref[8 + u : 9 + u, :] = jnp.sum(grad_two * normed, axis=0, keepdims=True)
    sums_ref[12:13, :] = bias


def out_kernel(
    place_ref, cot_ref, kept_ref, got_ref, passed_ref, hid_ref, bias_ref, tab_ref, out_ref, sums_ref
):
    width = cot_ref.shape[1]
    bias = jnp.zeros((1, width), wide)
    sums_ref[...] = jnp.zeros_like(sums_ref)
    for u, at in unit_rows(cot_ref):
        gate = column(tab_ref[0, u : u + 1, :], 3, width)
        mlp = kept_ref[at, :] + got_ref[at, :].astype(wide) + passed_ref[at, :].astype(wide)
        mlp = mlp + bias_ref[1:2, :]
        out_ref[at, :] = (hid_ref[at, :] + gate * mlp).astype(low)
        cot = cot_ref[at, :].astype(wide)
        sums_ref[u : u + 1, :] = jnp.sum(cot * mlp, axis=0, keepdims=True)
        bias = bias + jnp.sum(cot, axis=0, keepdims=True) * gate
    sums_ref[4:5, :] = bias


def third_kernel(place_ref, x_ref, kept_ref, got_ref, passed_ref, gh_ref, tab_ref, out_ref, sums_ref):
    width = x_ref.shape[1]
    for u, at in unit_rows(x_ref):
        grad_one = kept_ref[at, :] + got_ref[at, :].astype(wide) + passed_ref[at, :].astype(wide)
        normed, inverse = norm_parts(x_ref[at, :].astype(wide))
        table = tab_ref[0, u : u + 1, :]
        back = norm_back(normed, inverse, grad_one * (1.0 + column(table, 1, width)))
        out_ref[at, :] = (gh_ref[at, :] + back).astype(low)
        sums_ref[u : u + 1, :] = jnp.sum(grad_one, axis=0, keepdims=True)
        sums_ref[4 + u : 5 + u, :] = jnp.sum(grad_one * normed, axis=0, keepdims=True)


def row_call(body, name, place, args, in_specs, out_specs, out_shape, grid=1, scratch=(), flops=0):
    moved = sum(math.prod(a.shape) * a.dtype.itemsize for a in args)
    moved += sum(math.prod(o.shape) * o.dtype.itemsize for o in out_shape)
    prefetch = () if place is None else (place,)
    return pl.pallas_call(
        body,
        grid_spec=pltpu.PrefetchScalarGridSpec(
            num_scalar_prefetch=len(prefetch),
            grid=(grid,),
            in_specs=in_specs,
            out_specs=out_specs,
            scratch_shapes=scratch,
        ),
        out_shape=out_shape,
        compiler_params=pltpu.CompilerParams(vmem_limit_bytes=44 * 2**20),
        cost_estimate=pl.CostEstimate(flops=flops, bytes_accessed=moved, transcendentals=0),
        name=name,
    )(*prefetch, *args)


def block_spec(shape, index):
    return pl.BlockSpec(shape, index)


def fixed_spec(shape):
    return pl.BlockSpec(shape, lambda *_: (0,) * len(shape))


def weight_grad(pairs, name):
    depth = pairs[0][0][0][0].shape[1]
    tile = depth // 3
    widths = [pair[0][1].shape[1] for pair in pairs]
    args, specs, plan = [], [], []
    flops = 0
    for pair in pairs:
        rows = []
        for left, right in pair:
            rows.append((len(args), len(left)))
            args += list(left) + [right]
            specs += [pl.BlockSpec((piece.shape[0], tile), lambda i: (0, i)) for piece in left]
            specs.append(fixed_spec(right.shape))
            flops += 2 * depth * math.prod(right.shape)
        plan.append(rows)

    def body(*refs):
        out_ref = refs[-1]
        at = 0
        for rows, cols in zip(plan, widths):
            total = None
            for first, count in rows:
                left = [ref[...] for ref in refs[first : first + count]]
                left = left[0] if count == 1 else jnp.concatenate(left, axis=0)
                part = dot_as(left, refs[first + count][...], DOT_TN)
                total = part if total is None else total + part
            out_ref[:, at : at + cols] = total.astype(low)
            at += cols

    return pl.pallas_call(
        body,
        grid=(3,),
        in_specs=specs,
        out_specs=pl.BlockSpec((tile, sum(widths)), lambda i: (i, 0)),
        out_shape=shape_of((depth, sum(widths)), low),
        compiler_params=pltpu.CompilerParams(vmem_limit_bytes=52 * 2**20),
        cost_estimate=pl.CostEstimate(
            flops=flops,
            bytes_accessed=sum(2 * math.prod(a.shape) for a in args) + 2 * depth * sum(widths),
            transcendentals=0,
        ),
        name=name,
    )(*args)


def widen_pieces(place, pieces, rows):
    quarter, width = pieces[0].shape

    def body(place_ref, *refs):
        step = pl.program_id(0)
        for i, piece in enumerate(refs[:-1]):

            @pl.when(step == i)
            def _(piece=piece):
                refs[-1][...] = piece[...].astype(wide)

    return row_call(
        body,
        "widen_pieces",
        place,
        pieces,
        [fixed_spec((quarter, width))] * len(pieces),
        (
            pl.BlockSpec(
                (quarter, width), lambda i, p: (i // 4 * 4 + jnp.bitwise_xor(p[0], i % 4), 0)
            ),
        ),
        (shape_of((len(pieces) * quarter, width), wide),),
        grid=len(pieces),
    )[0]


def place_pieces(at, pieces):
    rows = sum(piece.shape[0] for piece in pieces)
    whole = (rows,) + pieces[0].shape[1:]
    return pl.pallas_call(
        place_kernel,
        out_shape=jax.ShapeDtypeStruct(whole, pieces[0].dtype),
        in_specs=[SMEM_SPEC] + [VMEM_SPEC] * len(pieces),
        out_specs=pl.BlockSpec(memory_space=pl.ANY),
        scratch_shapes=[pltpu.SemaphoreType.DMA((len(pieces),))],
        compiler_params=pltpu.CompilerParams(vmem_limit_bytes=24 * 2**20),
        cost_estimate=pl.CostEstimate(
            flops=0, bytes_accessed=4 * math.prod(whole), transcendentals=0
        ),
        name="place_pieces",
    )(at, *pieces)


def adam_step(weight, gradient, first_old, second_old, ema_old, step_rate):
    first_new = beta_one * first_old + (1.0 - beta_one) * gradient
    second_new = beta_two * second_old + (1.0 - beta_two) * gradient * gradient
    first_hat = first_new / (1.0 - beta_one**STEP)
    second_hat = second_new / (1.0 - beta_two**STEP)
    weight_new = weight - step_rate * (
        first_hat / (jnp.sqrt(second_hat) + adam_eps) + decay_rate * weight
    )
    ema_new = ema_keep * ema_old + (1.0 - ema_keep) * weight_new
    return (first_new, second_new, weight_new, ema_new)


def after(value, *others):
    return lax.optimization_barrier((value,) + others)[0]


def per_device(
    tokens,
    seg_ids,
    time_steps,
    cotangent,
    weight_cols,
    weight_rows,
    bias_cols,
    bias_rows,
    first_cols,
    first_rows,
    first_bias_cols,
    first_bias_rows,
    second_cols,
    second_rows,
    second_bias_cols,
    second_bias_rows,
    ema_cols,
    ema_rows,
    ema_bias_cols,
    ema_bias_rows,
):
    own_width = weight_cols.shape[2]
    own_depth = weight_cols.shape[1]
    width = tokens.shape[1]
    rows = time_steps.shape[0]
    slots = time_steps.shape[1]
    token_count = tokens.shape[0]
    row_len = token_count // rows
    units = row_len // UNIT
    quarter = row_len // 4
    own_units = units // 4
    dp_count = width // own_depth
    dp_place = lax.axis_index("dp")
    mp_place = lax.axis_index("mp")
    core, chip = mp_place % 2, mp_place // 2
    place = (2 * core + chip).astype(jnp.int32)
    place_arg = place.reshape(1)

    steps_all = share_steps(time_steps, dp_count).reshape(-1)
    cols_low = weight_cols.astype(low)
    own_rows = weight_rows.astype(low).transpose(2, 0, 1).reshape(own_depth, 5 * own_width)
    own_first = jnp.concatenate([cols_low[0], cols_low[1], cols_low[2], own_rows[:, :own_width]], 1)
    own_rest = jnp.concatenate([cols_low[5 + i] for i in range(4)] + [own_rows[:, own_width:]], 1)
    w_first = ring_gather(own_first, dp_count)
    w_rest = ring_gather(after(own_rest, w_first), dp_count)

    half_width = width // 2
    feature = dp_place * own_depth + jnp.arange(own_depth)
    is_cos = feature < half_width
    index = jnp.where(is_cos, feature, feature - half_width).astype(wide)
    frequency = jnp.exp(-math.log(10000.0) * index / half_width)
    angles = steps_all.astype(wide)[:, None] * frequency[None, :]
    time_rows = jnp.where(is_cos[None, :], jnp.cos(angles), jnp.sin(angles))
    time_low = time_rows.astype(low)
    ada_low = jax.nn.silu(time_rows).astype(low)

    def slot_products(left, maps):
        flat = jnp.concatenate([maps[j] for j in range(maps.shape[0])], 1)
        return dot_as(left, flat, DOT_NN).astype(low)

    def spread_columns(own, biases):
        count = biases.shape[0]
        own = (own.reshape(-1, count, own_width) + biases[None]).astype(low)
        pieces = group_gather(own)
        pieces = [pieces[0], pieces[2], pieces[1], pieces[3]]
        return jnp.concatenate(in_group_order(pieces, mp_place), 2).astype(wide)

    near = jnp.concatenate(
        [slot_products(ada_low, cols_low[9:11]), slot_products(time_low, cols_low[3:5])], 1
    )
    near = ring_scatter(near, dp_count, split=False)
    far = slot_products(after(ada_low, near), cols_low[11:15])
    far = ring_scatter(far, dp_count, split=False)
    near_mod = spread_columns(near[:, : 2 * own_width], bias_cols[6:8])
    far_mod = spread_columns(far, bias_cols[8:12])
    time_add = jnp.concatenate(
        [
            near[:, 2 * own_width : 3 * own_width] + bias_cols[0],
            jnp.zeros((rows * slots, own_width), wide),
            near[:, 3 * own_width :] + bias_cols[1],
        ],
        1,
    )

    seg_grid = seg_ids.reshape(rows, row_len)
    unit_seg = seg_grid.reshape(rows, 4, own_units, UNIT)[:, :, :, 0]
    unit_seg = jnp.stack(
        [lax.dynamic_index_in_dim(unit_seg, jnp.bitwise_xor(place, j), 1, keepdims=False) for j in range(4)],
        1,
    ).reshape(rows, units)
    onehot = (unit_seg[:, :, None] == jnp.arange(slots, dtype=jnp.int32)).astype(wide)

    def by_unit(table):
        out = jnp.einsum("rus,rsx->rux", onehot, table.reshape(rows, slots, -1), precision=highest)
        return out.reshape(rows, 4, own_units, out.shape[-1])

    near_tab, far_tab, add_tab = by_unit(near_mod), by_unit(far_mod), by_unit(time_add)

    block = (quarter, width)
    tab_block = lambda tab, j: pl.BlockSpec((1,) + tab.shape[2:], j)
    qkv_width = 3 * own_width
    half = row_len // 2
    lows = lambda *shape: shape_of(shape, low)
    wides = lambda *shape: shape_of(shape, wide)

    def own_block(r):
        return pl.BlockSpec(block, lambda i, p: (r * 4 + p[0], 0))

    def moved_block(r):
        return pl.BlockSpec(block, lambda i, p: (r * 4 + jnp.bitwise_xor(p[0], i), 0))

    here = pl.BlockSpec(block, lambda i, p: (0, 0))
    step_block = pl.BlockSpec(block, lambda i, p: (i, 0))

    inputs_one, qkvs, mixed, parts = [], [], [], []
    for r in range(rows):
        a_one, qkv = row_call(
            open_kernel,
            "open_row",
            place_arg,
            (tokens, near_tab[r], add_tab[r], w_first),
            [
                moved_block(r),
                tab_block(near_tab, lambda i, p: (i, 0, 0)),
                tab_block(add_tab, lambda i, p: (i, 0, 0)),
                fixed_spec(w_first.shape),
            ],
            (step_block, pl.BlockSpec((quarter, qkv_width), lambda i, p: (i, 0))),
            (lows(row_len, width), lows(row_len, qkv_width)),
            grid=4,
            flops=2 * row_len * width * qkv_width,
        )
        inputs_one.append(a_one)
        qkvs.append(qkv)
        out, kept, sent = attend_forward(place_arg, qkv, seg_grid[r], w_first)
        mixed.append(out)
        parts.append(group_scatter(kept, sent))

    down_grads = []
    for r in range(rows):
        down_grads.append(
            row_call(
                down_back_kernel,
                "down_back",
                place_arg,
                (cotangent, far_tab[r], w_rest),
                [moved_block(r), tab_block(far_tab, lambda i, p: (i, 0, 0)), fixed_spec(w_rest.shape)],
                (step_block, step_block),
                (lows(row_len, width), lows(row_len, width)),
                grid=4,
                flops=2 * row_len * width * width,
            )
        )

    attendeds, hiddens, inputs_two = [], [], []
    for r in range(rows):
        attended, hidden, a_two = row_call(
            first_kernel,
            "first_norm",
            place_arg,
            (tokens, *parts[r], bias_rows, far_tab[r]),
            [own_block(r), here, here, here, fixed_spec(bias_rows.shape), tab_block(far_tab, lambda i, p: (0, 0, 0))],
            (here, here, here),
            (wides(*block), wides(*block), lows(*block)),
        )
        attendeds.append(attended)
        hiddens.append(hidden)
        inputs_two.append(group_gather(a_two))

    bias_up = bias_cols[2:6].reshape(1, -1)
    hidden_width = bias_up.shape[1]
    actives, inner_grads, up_parts, up_sums = [], [], [], 0.0
    for r in range(rows):
        active, inner_grad, kept, sent, sums = row_call(
            up_kernel,
            "up_and_back",
            None,
            (*inputs_two[r], down_grads[r][1], bias_up, w_rest),
            [fixed_spec(block)] * 4
            + [pl.BlockSpec(block, lambda i: (i, 0)), fixed_spec(bias_up.shape), fixed_spec(w_rest.shape)],
            (
                pl.BlockSpec((quarter, hidden_width), lambda i: (i, 0)),
                pl.BlockSpec((quarter, hidden_width), lambda i: (i, 0)),
                pl.BlockSpec(block, lambda i: (jnp.minimum(i, 1), 0)),
                pl.BlockSpec(block, lambda i: (jnp.maximum(i - 2, 0), 0)),
                pl.BlockSpec((1, 8, hidden_width), lambda i: (i, 0, 0)),
            ),
            (
                lows(row_len, hidden_width),
                lows(row_len, hidden_width),
                wides(half, width),
                lows(half, width),
                wides(4, 8, hidden_width),
            ),
            grid=4,
            scratch=[pltpu.VMEM(block, low)],
            flops=4 * row_len * width * hidden_width,
        )
        actives.append(active)
        inner_grads.append(inner_grad)
        up_parts.append(group_scatter(kept, sent))
        up_sums = up_sums + jnp.sum(sums, axis=(0, 1))

    grad_hiddens, grad_attendeds, second_sums = [], [], []
    for r in range(rows):
        grad_hidden, grad_attended, sums = row_call(
            second_kernel,
            "second_norm",
            place_arg,
            (cotangent, *up_parts[r], hiddens[r], attendeds[r], far_tab[r]),
            [own_block(r)] + [here] * 5 + [tab_block(far_tab, lambda i, p: (0, 0, 0))],
            (here, here, fixed_spec((16, width))),
            (wides(*block), lows(*block), wides(16, width)),
        )
        grad_hiddens.append(grad_hidden)
        grad_attendeds.append(group_gather(grad_attended))
        second_sums.append(sums)

    out_pieces, out_sums = [], []
    for r in range(rows):
        kept, sent = row_call(
            down_kernel,
            "down",
            None,
            (actives[r], w_rest),
            [pl.BlockSpec((quarter, hidden_width), lambda i: (i, 0)), fixed_spec(w_rest.shape)],
            (
                pl.BlockSpec(block, lambda i: (jnp.minimum(i, 1), 0)),
                pl.BlockSpec(block, lambda i: (jnp.maximum(i - 2, 0), 0)),
            ),
            (wides(half, width), lows(half, width)),
            grid=4,
            flops=2 * row_len * width * hidden_width,
        )
        out_own, sums = row_call(
            out_kernel,
            "out_tokens",
            place_arg,
            (cotangent, *group_scatter(kept, sent), hiddens[r], bias_rows, far_tab[r]),
            [own_block(r)] + [here] * 4 + [fixed_spec(bias_rows.shape), tab_block(far_tab, lambda i, p: (0, 0, 0))],
            (here, fixed_spec((8, width))),
            (lows(*block), wides(8, width)),
        )
        out_pieces.extend(group_gather(out_own))
        out_sums.append(sums)

    rest_grad = weight_grad(
        [
            [(inputs_two[r], inner_grads[r]) for r in range(rows)],
            [([down_grads[r][0]], actives[r]) for r in range(rows)],
        ],
        "grad_rest",
    )
    rest_sum = lax.psum_scatter(rest_grad, "dp", scatter_dimension=0, tiled=True).astype(wide)

    qkv_grads, one_parts, time_sums = [], [], []
    for r in range(rows):
        qkv_grad, kept, sent, sums = attend_backward(
            place_arg, qkvs[r], grad_attendeds[r], seg_grid[r], w_first
        )
        qkv_grads.append(qkv_grad)
        one_parts.append(group_scatter(kept, sent))
        time_sums.append(sums)
    first_grad = weight_grad(
        [
            [([inputs_one[r]], qkv_grads[r]) for r in range(rows)],
            [(grad_attendeds[r], mixed[r]) for r in range(rows)],
        ],
        "grad_first",
    )
    first_sum = ring_scatter(first_grad, dp_count)

    input_pieces, third_sums = [], []
    for r in range(rows):
        input_own, sums = row_call(
            third_kernel,
            "third_norm",
            place_arg,
            (tokens, *one_parts[r], grad_hiddens[r], near_tab[r]),
            [own_block(r)] + [here] * 4 + [tab_block(near_tab, lambda i, p: (0, 0, 0))],
            (here, fixed_spec((8, width))),
            (lows(*block), wides(8, width)),
        )
        input_pieces.extend(group_gather(input_own))
        third_sums.append(sums)

    at = jnp.stack(
        [(r * 4 + jnp.bitwise_xor(place, j)) * quarter for r in range(rows) for j in range(4)]
    ).astype(jnp.int32)
    out_tokens = place_pieces(at, out_pieces)
    input_grads = widen_pieces(place_arg, input_pieces, rows)

    def side(values, which, axis):
        return lax.dynamic_index_in_dim(values, which, axis, keepdims=False)

    def exchange(values):
        values = values.astype(low).reshape(-1, 2, 2, own_width)
        other = lax.ppermute(side(values, 1 - chip, 1), "mp", CHIP_SWAP)
        values = jnp.stack([side(values, chip, 1), other], 0)
        other = lax.ppermute(side(values, 1 - core, 2), "mp", CORE_SWAP)
        values = jnp.stack([side(values, core, 2), other], 0)
        return values.reshape(4, -1, own_width).astype(wide)

    def to_slots(fields):
        fields = fields.reshape(rows, units, -1)
        return jnp.einsum("rus,rux->rsx", onehot, fields, precision=highest).reshape(rows * slots, -1)

    count = 4 * own_units
    far_rows = jnp.stack(
        [jnp.concatenate([second_sums[r][:12], out_sums[r][:4]], 0) for r in range(rows)], 0
    )
    bias_part = jnp.stack(
        [sum(second_sums[r][12] for r in range(rows)), sum(out_sums[r][4] for r in range(rows))], 0
    )
    swapped = exchange(jnp.concatenate([far_rows.reshape(rows * count, width), bias_part], 0))
    far_fields = swapped[:, : rows * count].reshape(4, rows, 4, own_units, own_width)
    far_fields = far_fields.transpose(1, 0, 3, 2, 4)
    bias_part = jnp.sum(swapped[:, rows * count :], axis=0)
    extra = jnp.zeros((16, 4 * own_width), wide).at[0].set(up_sums)
    extra = extra.at[1, : 2 * own_width].set(bias_part.reshape(-1))
    far_all = ring_gather(jnp.concatenate([to_slots(far_fields), extra], 0).astype(low), dp_count)
    far_all = far_all.reshape(dp_count, rows * slots + 16, 4 * own_width)
    extra = jnp.sum(far_all[:, rows * slots :].astype(wide), axis=0)
    far_all = far_all[:, : rows * slots].reshape(-1, 4 * own_width)
    bias_up_sum = extra[0].reshape(4, own_width)
    bias_rows_own = group_gather(extra[1, : 2 * own_width].reshape(2, own_width).astype(low))
    bias_rows_own = [bias_rows_own[0], bias_rows_own[2], bias_rows_own[1], bias_rows_own[3]]
    bias_rows_sum = jnp.concatenate(in_group_order(bias_rows_own, mp_place), 1).astype(wide)

    near_rows = jnp.stack(third_sums, 0)
    near_fields = exchange(near_rows.reshape(rows * 2 * own_units, width))
    near_fields = near_fields.reshape(4, rows, 2, own_units, own_width).transpose(1, 0, 3, 2, 4)
    time_fields = jnp.stack(time_sums, 0).reshape(rows, units, 3, own_width)[:, :, 0::2]
    near_slots = jnp.concatenate([to_slots(near_fields), to_slots(time_fields)], 1).astype(low)
    near_all = ring_gather(near_slots, dp_count)

    def map_grads(left, right):
        out = dot_as(left, right, DOT_TN).reshape(own_depth, -1, own_width)
        return out.transpose(1, 0, 2)

    far_sum = jnp.sum(far_all.astype(wide), axis=0).reshape(4, own_width)
    near_sum = jnp.sum(near_all.astype(wide), axis=0).reshape(4, own_width)

    def slabs(values):
        return values.reshape(own_depth, -1, own_width).transpose(1, 0, 2)

    grad_cols = jnp.concatenate(
        [
            slabs(first_sum[:, :qkv_width]),
            map_grads(time_low, near_all[:, 2 * own_width :]),
            slabs(rest_sum[:, : 4 * own_width]),
            map_grads(ada_low, near_all[:, : 2 * own_width]),
            map_grads(ada_low, far_all),
        ],
        0,
    )
    rows_sum = jnp.concatenate([first_sum[:, qkv_width:], rest_sum[:, 4 * own_width :]], 1)
    grad_rows = rows_sum.reshape(own_depth, 5, own_width).transpose(1, 2, 0)
    bias_cols_sum = jnp.concatenate([near_sum[2:4], bias_up_sum, near_sum[:2], far_sum], 0)

    cols_state = adam_step(weight_cols, grad_cols, first_cols, second_cols, ema_cols, rate_matrix)
    rows_state = adam_step(weight_rows, grad_rows, first_rows, second_rows, ema_rows, rate_matrix)
    bias_cols_state = adam_step(
        bias_cols, bias_cols_sum, first_bias_cols, second_bias_cols, ema_bias_cols, rate_vector
    )
    bias_rows_state = adam_step(
        bias_rows, bias_rows_sum, first_bias_rows, second_bias_rows, ema_bias_rows, rate_vector
    )
    return (out_tokens, input_grads) + cols_state + rows_state + bias_cols_state + bias_rows_state


def solution(mesh):
    cols, rows, bias = P(None, "dp", "mp"), P(None, "mp", "dp"), P(None, "mp")
    state = (cols, rows, bias, P())
    placed = (P("dp", None), P("dp"), P("dp", None), P("dp", None)) + state * 4
    given = (P("dp", None), P("dp", None)) + (cols,) * 4 + (rows,) * 4 + (bias,) * 4 + (P(),) * 4
    return jax.shard_map(
        per_device, mesh=mesh, in_specs=placed, out_specs=given, check_vma=False
    )
```

time: 839 us -> 663 us (0.79)
  Pallas kernels: 41.2 us -> 208 us
  matrix products: 133 us -> 9.41 us
  local copies, waits for them, and re-layouts: 199 us -> 101 us
  other arithmetic: 126 us -> 40.4 us
  blocking collectives: 44.8 us -> 0 us
  starting transfers between devices: 86.8 us -> 103 us
    pallas_call x4 -> x28, Pallas kernels: 41.2 us -> 208 us  [the longest x17 98.8 us: row_call(): pl.pallas_call(body, grid_spec=pltpu.PrefetchScalarGridSpec(num_scalar_pr...]
    dot_general x32 -> x6, matrix products: 125 us -> 8.21 us  [dot_as(): return lax.dot_general(left, right, dims, preferred_element_type=wide)]
    dynamic_update_slice x17 -> x0, local copies, waits for them, and re-layouts: 51.2 us -> none  [put(): return lax.dynamic_update_slice_in_dim(whole, piece, at, 0)]
    psum x1 -> x0, blocking collectives: 44.8 us -> none  [per_device(): lax.psum(jnp.stack([bias_row_one, bias_row_two], 0), ('dp', 'mp'))]
    convert_element_type x22 -> x13, other arithmetic: 47.4 us -> 12.1 us  [the longest x8 10.7 us: group_scatter(): passed = (kept[quarter:] + got[quarter:].astype(wide)).astype(low)]
    reduce_sum x23 -> x6, other arithmetic: 35.3 us -> 0.31 us  [the longest x1 0.1 us: per_device(): near_sum = jnp.sum(near_all.astype(wide), axis=0).reshape(4, own_width)]
    ppermute x9 -> x11, waiting for transfers between devices: 45.6 us -> 29.7 us  [group_gather(): chip = lax.ppermute(own, 'mp', CHIP_SWAP)]
    ppermute x34 -> x52, waiting for transfers between devices: 83.4 us -> 98 us  [the longest x8 55.9 us: group_scatter(): return (kept, got, lax.ppermute(passed, 'mp', CHIP_SWAP))]
  transfers between devices with their start and end apart: 94 -> 117, of which waited for: 32 -> 39; matrix products, arithmetic and copies ran while one was open for 50% -> 11% of each run, Pallas kernels for 5% -> 29%
where the time goes in v2:
time: 663 us; the launch traced here: 654 us
  Pallas kernels  208 us (31%)
  waiting for transfers between devices  148 us (22%)
  starting transfers between devices  103 us (16%)
  local copies, waits for them, and re-layouts  101 us (15%)
  between operations  42.5 us (6%)
  other arithmetic  40.4 us (6%)
  matrix products  9.41 us (1%)
    pallas_call x17, Pallas kernels, row_call(): pl.pallas_call(body, grid_spec=pltpu.PrefetchScalarGridSpec(num_scalar_pr...  98.8 us
    ppermute x8, waiting for transfers between devices, group_scatter(): return (kept, got, lax.ppermute(passed, 'mp', CHIP_SWAP))  55.9 us
    unnamed x318, local copies, waits for them, and re-layouts  55.5 us
    pallas_call x2, Pallas kernels, attend_backward(): pl.pallas_call(body, out_shape=(shape_of((row_len, 3 * width), low), shap...  43.7 us
    pallas_call x2, Pallas kernels, weight_grad(): pl.pallas_call(body, grid=(3,), in_specs=specs, out_specs=pl.BlockSpec((t...  31.5 us
    ppermute x11, waiting for transfers between devices, group_gather(): chip = lax.ppermute(own, 'mp', CHIP_SWAP)  29.7 us
    ppermute x20, starting transfers between devices, travel(): running = lax.ppermute(running, 'dp', perm).astype(wide)  27.9 us
    pallas_call x2, Pallas kernels, attend_forward(): pl.pallas_call(body, out_shape=(shape_of((row_len, width), low), shape_of...  20.4 us
  transfers between devices with their start and end apart: 117, of which 39 were waited for; matrix products, arithmetic and copies ran while one was open for 11% of the time, Pallas kernels for 29%

profile of v2, /device:TPU:0, one launch (start us, length us, event | category | flops | bytes accessed | tf_op | source)
XLA Modules:
  0.0 653.7 jit_solution(6185186938019482476)
XLA Ops:
  89.1 5.8 collective-permute-done.18.refs_6_
  111.4 6.3 open_row.3
  119.1 10.2 %attend_forward.3 = (bf16[1024,288]{1,0:T(8,128)(2,1)S(1)}, f32[512,1152]{1,0:T(8,128)S(1)}, bf16[512,1152]{1,0:T(8,128)(2,1)}) custom-call(s32[1]{0:T(128)} %bitcast.8.place_ref.refs_0_, bf16[1024,864]{1,0:T(8,128)(2,1)S(1)} %get-tuple-element.112.refs_1_, s32[1024,1]{1,0:T(8,128)S(1)} %copy-done.46, s32[1,1024]{1,0:T(1,128)S(1)} %bitcast.196, ...), custom_call_target="tpu_custom_call" | custom-call | flops 1434451968 | bytes 8257536 | tf_op jit(solution)/shard_map/attend_forward/pallas_call | solution.py:289
  140.4 5.7 open_row.2
  147.5 10.2 %attend_forward.2 = (bf16[1024,288]{1,0:T(8,128)(2,1)S(1)}, f32[512,1152]{1,0:T(8,128)S(1)}, bf16[512,1152]{1,0:T(8,128)(2,1)}) custom-call(s32[1]{0:T(128)} %bitcast.8.place_ref.refs_0_, bf16[1024,864]{1,0:T(8,128)(2,1)S(1)} %get-tuple-element.100.refs_1_, s32[1024,1]{1,0:T(8,128)S(1)} %copy-done.48, s32[1,1024]{1,0:T(1,128)S(1)} %bitcast.193, ...), custom_call_target="tpu_custom_call" | custom-call | flops 1434451968 | bytes 8257536 | tf_op jit(solution)/shard_map/attend_forward/pallas_call | solution.py:289
  171.0 9.6 %collective-permute-done.39.refs_4_ = bf16[144,2304]{1,0:T(8,128)(2,1)} collective-permute-done((bf16[144,2304]{1,0:T(8,128)(2,1)}, bf16[144,2304]{1,0:T(8,128)(2,1)}, u32[]{:S(2)}, u32[]{:S(2)}) %collective-permute-start.39) | collective-permute-done | bytes 663584 | tf_op jit(solution)/shard_map/ppermute | solution.py:67
  189.6 6.5 collective-permute-done.22.passed_ref
  204.6 4.2 collective-permute-done.51.a1_ref.refs_6_
  210.8 8.4 %collective-permute-done.42.refs_7_ = bf16[64,2304]{1,0:T(8,128)(2,1)S(1)} collective-permute-done((bf16[64,2304]{1,0:T(8,128)(2,1)S(1)}, bf16[64,2304]{1,0:T(8,128)(2,1)S(1)}, u32[]{:S(2)}, u32[]{:S(2)}) %collective-permute-start.42) | collective-permute-done | bytes 294944 | tf_op jit(solution)/shard_map/ppermute | solution.py:72
  226.7 6.5 down_back.3
  236.0 14.5 %up_and_back.3 = (bf16[1024,1152]{1,0:T(8,128)(2,1)S(1)}, bf16[1024,1152]{1,0:T(8,128)(2,1)S(1)}, f32[512,1152]{1,0:T(8,128)}, bf16[512,1152]{1,0:T(8,128)(2,1)}, f32[4,8,1152]{2,1,0:T(8,128)S(1)}) custom-call(bf16[256,1152]{1,0:T(8,128)(2,1)} %get-tuple-element.115.a0_ref.refs_5_, bf16[256,1152]{1,0:T(8,128)(2,1)} %collective-permute-done.51.a1_ref.refs_6_, ...), custom_call_target="tpu_custom_call" | custom-call | flops 5435817984 | bytes 18436608 | tf_op jit(solution)/shard_map/up_and_back/pallas_call | solution.py:499
  252.4 6.9 %down_back.2 = (bf16[1024,1152]{1,0:T(8,128)(2,1)S(1)}, bf16[1024,1152]{1,0:T(8,128)(2,1)S(1)}) custom-call(s32[1]{0:T(128)} %bitcast.8.place_ref.refs_0_, bf16[2048,1152]{1,0:T(8,128)(2,1)S(1)} %bitcast.188, f32[4,4,4608]{2,1,0:T(4,128)S(1)} %squeeze.248.tab_ref, bf16[1152,2304]{1,0:T(8,128)(2,1)} %copy-done), custom_call_target="tpu_custom_call" | custom-call | flops 2717908992 | bytes 15040512 | tf_op jit(solution)/shard_map/down_back/pallas_call | solution.py:499
  262.1 14.3 %up_and_back.2 = (bf16[1024,1152]{1,0:T(8,128)(2,1)S(1)}, bf16[1024,1152]{1,0:T(8,128)(2,1)S(1)}, f32[512,1152]{1,0:T(8,128)}, bf16[512,1152]{1,0:T(8,128)(2,1)S(1)}, f32[4,8,1152]{2,1,0:T(8,128)S(1)}) custom-call(bf16[256,1152]{1,0:T(8,128)(2,1)} %get-tuple-element.104.a0_ref.refs_0_, bf16[256,1152]{1,0:T(8,128)(2,1)} %collective-permute-done.33.a1_ref.refs_1_, ...), custom_call_target="tpu_custom_call" | custom-call | flops 5435817984 | bytes 18436608 | tf_op jit(solution)/shard_map/up_and_back/pallas_call | solution.py:499
  279.8 7.9 %down.3 = (f32[512,1152]{1,0:T(8,128)S(1)}, bf16[512,1152]{1,0:T(8,128)(2,1)}) custom-call(bf16[1024,1152]{1,0:T(8,128)(2,1)S(1)} %copy-done.101, bf16[1152,2304]{1,0:T(8,128)(2,1)} %copy-done), custom_call_target="tpu_custom_call" | custom-call | flops 2717908992 | bytes 11206656 | tf_op jit(solution)/shard_map/down/pallas_call | solution.py:499
  287.8 8.0 %down.2 = (f32[512,1152]{1,0:T(8,128)S(1)}, bf16[512,1152]{1,0:T(8,128)(2,1)S(1)}) custom-call(bf16[1024,1152]{1,0:T(8,128)(2,1)S(1)} %copy-done.103, bf16[1152,2304]{1,0:T(8,128)(2,1)} %copy-done), custom_call_target="tpu_custom_call" | custom-call | flops 2717908992 | bytes 11206656 | tf_op jit(solution)/shard_map/down/pallas_call | solution.py:499
  305.0 8.2 %collective-permute-done.70.passed_ref = bf16[256,1152]{1,0:T(8,128)(2,1)} collective-permute-done((bf16[256,1152]{1,0:T(8,128)(2,1)}, bf16[256,1152]{1,0:T(8,128)(2,1)}, u32[]{:S(2)}, u32[]{:S(2)}) %collective-permute-start.70) | collective-permute-done | bytes 589856 | tf_op jit(solution)/shard_map/ppermute | solution.py:146
  329.5 9.0 %collective-permute-done.55.passed_ref = bf16[256,1152]{1,0:T(8,128)(2,1)} collective-permute-done((bf16[256,1152]{1,0:T(8,128)(2,1)}, bf16[256,1152]{1,0:T(8,128)(2,1)}, u32[]{:S(2)}, u32[]{:S(2)}) %collective-permute-start.55) | collective-permute-done | bytes 589856 | tf_op jit(solution)/shard_map/ppermute | solution.py:146
  341.2 9.5 %collective-permute-done.45.passed_ref = bf16[256,1152]{1,0:T(8,128)(2,1)} collective-permute-done((bf16[256,1152]{1,0:T(8,128)(2,1)}, bf16[256,1152]{1,0:T(8,128)(2,1)}, u32[]{:S(2)}, u32[]{:S(2)}) %collective-permute-start.45) | collective-permute-done | bytes 589856 | tf_op jit(solution)/shard_map/ppermute | solution.py:146
  372.8 19.0 %grad_rest.1 = bf16[1152,2304]{1,0:T(8,128)(2,1)} custom-call(bf16[256,1152]{1,0:T(8,128)(2,1)} %get-tuple-element.104.a0_ref.refs_0_, bf16[256,1152]{1,0:T(8,128)(2,1)} %collective-permute-done.33.a1_ref.refs_1_, bf16[256,1152]{1,0:T(8,128)(2,1)S(1)} %copy-done.96, bf16[256,1152]{1,0:T(8,128)(2,1)} %copy-done.97, bf16[1024,1152]{1,0:T(8,128)(2,1)} %copy-done.107, ...), custom_call_target="tpu_custom_call" | custom-call | flops 10871635968 | bytes 24182784 | tf_op jit(solution)/shard_map/grad_rest/pallas_call | solution.py:552
  416.7 21.9 %attend_backward.3 = (bf16[1024,864]{1,0:T(8,128)(2,1)S(1)}, f32[512,1152]{1,0:T(8,128)}, bf16[512,1152]{1,0:T(8,128)(2,1)}, f32[16,864]{1,0:T(8,128)S(1)}) custom-call(s32[1]{0:T(128)} %bitcast.8.place_ref.refs_0_, bf16[1024,864]{1,0:T(8,128)(2,1)} %copy-done.90, bf16[256,1152]{1,0:T(8,128)(2,1)S(1)} %copy-done.93, ...), custom_call_target="tpu_custom_call" | custom-call | flops 4605345792 | bytes 13565952 | tf_op jit(solution)/shard_map/attend_backward/pallas_call | solution.py:317
  440.4 21.8 %attend_backward.2 = (bf16[1024,864]{1,0:T(8,128)(2,1)S(1)}, f32[512,1152]{1,0:T(8,128)}, bf16[512,1152]{1,0:T(8,128)(2,1)}, f32[16,864]{1,0:T(8,128)S(1)}) custom-call(s32[1]{0:T(128)} %bitcast.8.place_ref.refs_0_, bf16[1024,864]{1,0:T(8,128)(2,1)} %copy-done.91, bf16[256,1152]{1,0:T(8,128)(2,1)} %get-tuple-element.125.refs_2_.refs_4_, ...), custom_call_target="tpu_custom_call" | custom-call | flops 4605345792 | bytes 13565952 | tf_op jit(solution)/shard_map/attend_backward/pallas_call | solution.py:317
  464.1 12.5 %grad_first.1 = bf16[1152,1152]{1,0:T(8,128)(2,1)} custom-call(bf16[1024,1152]{1,0:T(8,128)(2,1)} %copy-done.85, bf16[1024,864]{1,0:T(8,128)(2,1)} %copy-done.105, bf16[1024,1152]{1,0:T(8,128)(2,1)} %copy-done.84, bf16[1024,864]{1,0:T(8,128)(2,1)} %copy-done.104, bf16[256,1152]{1,0:T(8,128)(2,1)} %get-tuple-element.125.refs_2_.refs_4_, ...), custom_call_target="tpu_custom_call" | custom-call | flops 5435817984 | bytes 16809984 | tf_op jit(solution)/shard_map/grad_first/pallas_call | solution.py:552
  487.9 6.5 collective-permute-start.83
  513.7 5.7 collective-permute-done.46.refs_1_
  519.4 12.6 %collective-permute-done.75.passed_ref = bf16[256,1152]{1,0:T(8,128)(2,1)} collective-permute-done((bf16[256,1152]{1,0:T(8,128)(2,1)}, bf16[256,1152]{1,0:T(8,128)(2,1)}, u32[]{:S(2)}, u32[]{:S(2)}) %collective-permute-start.75) | collective-permute-done | bytes 589856 | tf_op jit(solution)/shard_map/ppermute | solution.py:146
  535.4 6.5 collective-permute-done.65.passed_ref
  550.6 4.6 place_pieces.7
  590.2 7.5 %collective-permute-done.76.refs_5_ = bf16[256,1152]{1,0:T(8,128)(2,1)S(1)} collective-permute-done((bf16[256,1152]{1,0:T(8,128)(2,1)S(1)}, bf16[256,1152]{1,0:T(8,128)(2,1)S(1)}, u32[]{:S(2)}, u32[]{:S(2)}) %collective-permute-start.76) | collective-permute-done | bytes 589856 | tf_op jit(solution)/shard_map/ppermute | solution.py:150
  597.7 8.6 %collective-permute-done.66.refs_1_ = bf16[256,1152]{1,0:T(8,128)(2,1)S(1)} collective-permute-done((bf16[256,1152]{1,0:T(8,128)(2,1)S(1)}, bf16[256,1152]{1,0:T(8,128)(2,1)S(1)}, u32[]{:S(2)}, u32[]{:S(2)}) %collective-permute-start.66) | collective-permute-done | bytes 589856 | tf_op jit(solution)/shard_map/ppermute | solution.py:150
  617.1 6.1 widen_pieces.1
  632.2 5.0 multiply_add_fusion.2
  638.6 7.7 %multiply_add_fusion = (f32[15,144,288]{2,1,0:T(8,128)}, f32[15,144,288]{2,1,0:T(8,128)}, f32[15,144,288]{2,1,0:T(8,128)}, f32[15,144,288]{2,1,0:T(8,128)}) fusion(f32[15,144,288]{2,1,0:T(8,128)S(1)} %copy-done.112, f32[15,144,288]{2,1,0:T(8,128)S(1)} %copy-done.108, f32[15,144,288]{2,1,0:T(8,128)S(1)} %copy-done.109, f32[15,144,288]{2,1,0:T(8,128)S(1)} %copy-done.113, ...), kind=kLoop, calls=%fused_computation.2 | loop fusion | flops 11197440 | bytes 22394880 | tf_op jit(solution)/shard_map/add | solution.py:620
  (743 shorter events, 313.6 us)
Async XLA Ops:
  7.2 616.1 %reduce-scatter.2.cloned.1.call-start = ((), (), s32[]{:S(2)}) async-start(), calls=%async_computation.1 | async-start | bytes 5971968 | tf_op jit(solution)/shard_map/reduce_scatter | solution.py:882
  12.4 50.5 %collective-permute-start.14 = (bf16[144,1152]{1,0:T(8,128)(2,1)S(1)}, bf16[144,1152]{1,0:T(8,128)(2,1)S(1)}, u32[]{:S(2)}, u32[]{:S(2)}) collective-permute-start(bf16[144,1152]{1,0:T(8,128)(2,1)S(1)} %concatenate.79.refs_0_), channel_id=1, source_target_pairs={{8,0},{16,8},{24,16},{28,24},{20,28},{12,20},{4,12},{0,4},{9,1},{1... | collective-permute-start | bytes 995336 | tf_op jit(solution)/shard_map/ppermute | solution.py:67
  15.4 49.4 %collective-permute-start.13 = (bf16[144,1152]{1,0:T(8,128)(2,1)S(1)}, bf16[144,1152]{1,0:T(8,128)(2,1)S(1)}, u32[]{:S(2)}, u32[]{:S(2)}) collective-permute-start(bf16[144,1152]{1,0:T(8,128)(2,1)S(1)} %concatenate.79.refs_0_), channel_id=1, source_target_pairs={{0,8},{8,16},{16,24},{24,28},{28,20},{20,12},{12,4},{4,0},{1,9},{9... | collective-permute-start | bytes 995336 | tf_op jit(solution)/shard_map/ppermute | solution.py:66
  62.9 23.4 %collective-permute-start.16 = (bf16[144,1152]{1,0:T(8,128)(2,1)S(1)}, bf16[144,1152]{1,0:T(8,128)(2,1)S(1)}, u32[]{:S(2)}, u32[]{:S(2)}) collective-permute-start(bf16[144,1152]{1,0:T(8,128)(2,1)S(1)} %collective-permute-done.14.refs_2_), channel_id=1, source_target_pairs={{8,0},{16,8},{24,16},{28,24},{20,28},{12,20},{4,12},{0,4},{9,1},{1... | collective-permute-start | bytes 995336 | tf_op jit(solution)/shard_map/ppermute | solution.py:67
  131.6 33.3 %collective-permute-start.49 = (bf16[512,1152]{1,0:T(8,128)(2,1)}, bf16[512,1152]{1,0:T(8,128)(2,1)}, u32[]{:S(2)}, u32[]{:S(2)}) collective-permute-start(bf16[512,1152]{1,0:T(8,128)(2,1)} %get-tuple-element.114), channel_id=1, source_target_pairs={{0,1},{1,0},{2,3},{3,2},{4,5},{5,4},{6,7},{7,6},{8,9},{9,8},{10,11... | collective-permute-start | bytes 3538952 | tf_op jit(solution)/shard_map/ppermute | solution.py:144
  138.1 24.7 %collective-permute-start.37 = (bf16[144,2304]{1,0:T(8,128)(2,1)}, bf16[144,2304]{1,0:T(8,128)(2,1)}, u32[]{:S(2)}, u32[]{:S(2)}) collective-permute-start(bf16[144,2304]{1,0:T(8,128)(2,1)} %concatenate.82.refs_0_), channel_id=1, source_target_pairs={{8,0},{16,8},{24,16},{28,24},{20,28},{12,20},{4,12},{0,4},{9,1},{1... | collective-permute-start | bytes 1990664 | tf_op jit(solution)/shard_map/ppermute | solution.py:67
  139.2 24.8 %collective-permute-start.36 = (bf16[144,2304]{1,0:T(8,128)(2,1)}, bf16[144,2304]{1,0:T(8,128)(2,1)}, u32[]{:S(2)}, u32[]{:S(2)}) collective-permute-start(bf16[144,2304]{1,0:T(8,128)(2,1)} %concatenate.82.refs_0_), channel_id=1, source_target_pairs={{0,8},{8,16},{16,24},{24,28},{28,20},{20,12},{12,4},{4,0},{1,9},{9... | collective-permute-start | bytes 1990664 | tf_op jit(solution)/shard_map/ppermute | solution.py:66
  170.0 26.1 %collective-permute-start.22 = (bf16[256,1152]{1,0:T(8,128)(2,1)}, bf16[256,1152]{1,0:T(8,128)(2,1)}, u32[]{:S(2)}, u32[]{:S(2)}) collective-permute-start(bf16[256,1152]{1,0:T(8,128)(2,1)} %add_convert_fusion.7), channel_id=1, source_target_pairs={{0,2},{1,3},{2,0},{3,1},{4,6},{5,7},{6,4},{7,5},{8,10},{9,11},{10,... | collective-permute-start | bytes 1769480 | tf_op jit(solution)/shard_map/ppermute | solution.py:146
  181.6 27.1 %collective-permute-start.40 = (bf16[144,2304]{1,0:T(8,128)(2,1)}, bf16[144,2304]{1,0:T(8,128)(2,1)}, u32[]{:S(2)}, u32[]{:S(2)}) collective-permute-start(bf16[144,2304]{1,0:T(8,128)(2,1)} %collective-permute-done.38.refs_3_), channel_id=1, source_target_pairs={{0,8},{8,16},{16,24},{24,28},{28,20},{20,12},{12,4},{4,0},{1,9},{9... | collective-permute-start | bytes 1990664 | tf_op jit(solution)/shard_map/ppermute | solution.py:66
  204.6 31.4 %collective-permute-start.52 = (bf16[256,1152]{1,0:T(8,128)(2,1)}, bf16[256,1152]{1,0:T(8,128)(2,1)}, u32[]{:S(2)}, u32[]{:S(2)}) collective-permute-start(bf16[256,1152]{1,0:T(8,128)(2,1)} %get-tuple-element.115.a0_ref.refs_5_), channel_id=1, source_target_pairs={{0,1},{1,0},{2,3},{3,2},{4,5},{5,4},{6,7},{7,6},{8,9},{9,8},{10,11... | collective-permute-start | bytes 1769480 | tf_op jit(solution)/shard_map/ppermute | solution.py:151
  208.7 27.3 %collective-permute-start.53 = (bf16[256,1152]{1,0:T(8,128)(2,1)}, bf16[256,1152]{1,0:T(8,128)(2,1)}, u32[]{:S(2)}, u32[]{:S(2)}) collective-permute-start(bf16[256,1152]{1,0:T(8,128)(2,1)} %collective-permute-done.51.a1_ref.refs_6_), channel_id=1, source_target_pairs={{0,1},{1,0},{2,3},{3,2},{4,5},{5,4},{6,7},{7,6},{8,9},{9,8},{10,11... | collective-permute-start | bytes 1769480 | tf_op jit(solution)/shard_map/ppermute | solution.py:152
  219.2 42.9 %collective-permute-start.34 = (bf16[256,1152]{1,0:T(8,128)(2,1)}, bf16[256,1152]{1,0:T(8,128)(2,1)S(1)}, u32[]{:S(2)}, u32[]{:S(2)}) collective-permute-start(bf16[256,1152]{1,0:T(8,128)(2,1)} %get-tuple-element.104.a0_ref.refs_0_), channel_id=1, source_target_pairs={{0,1},{1,0},{2,3},{3,2},{4,5},{5,4},{6,7},{7,6},{8,9},{9,8},{10,11... | collective-permute-start | bytes 1769480 | tf_op jit(solution)/shard_map/ppermute | solution.py:151
  220.3 41.8 %collective-permute-start.35 = (bf16[256,1152]{1,0:T(8,128)(2,1)}, bf16[256,1152]{1,0:T(8,128)(2,1)S(1)}, u32[]{:S(2)}, u32[]{:S(2)}) collective-permute-start(bf16[256,1152]{1,0:T(8,128)(2,1)} %collective-permute-done.33.a1_ref.refs_1_), channel_id=1, source_target_pairs={{0,1},{1,0},{2,3},{3,2},{4,5},{5,4},{6,7},{7,6},{8,9},{9,8},{10,11... | collective-permute-start | bytes 1769480 | tf_op jit(solution)/shard_map/ppermute | solution.py:152
  251.9 44.0 %collective-permute-start.69 = (bf16[512,1152]{1,0:T(8,128)(2,1)}, bf16[512,1152]{1,0:T(8,128)(2,1)S(1)}, u32[]{:S(2)}, u32[]{:S(2)}) collective-permute-start(bf16[512,1152]{1,0:T(8,128)(2,1)} %get-tuple-element.131), channel_id=1, source_target_pairs={{0,1},{1,0},{2,3},{3,2},{4,5},{5,4},{6,7},{7,6},{8,9},{9,8},{10,11... | collective-permute-start | bytes 3538952 | tf_op jit(solution)/shard_map/ppermute | solution.py:144
  299.0 26.8 %collective-permute-start.60 = (bf16[256,1152]{1,0:T(8,128)(2,1)}, bf16[256,1152]{1,0:T(8,128)(2,1)}, u32[]{:S(2)}, u32[]{:S(2)}) collective-permute-start(bf16[256,1152]{1,0:T(8,128)(2,1)} %add_convert_fusion.3), channel_id=1, source_target_pairs={{0,2},{1,3},{2,0},{3,1},{4,6},{5,7},{6,4},{7,5},{8,10},{9,11},{10,... | collective-permute-start | bytes 1769480 | tf_op jit(solution)/shard_map/ppermute | solution.py:146
  301.1 37.4 %collective-permute-start.55 = (bf16[256,1152]{1,0:T(8,128)(2,1)}, bf16[256,1152]{1,0:T(8,128)(2,1)}, u32[]{:S(2)}, u32[]{:S(2)}) collective-permute-start(bf16[256,1152]{1,0:T(8,128)(2,1)} %add_convert_fusion.4), channel_id=1, source_target_pairs={{0,2},{1,3},{2,0},{3,1},{4,6},{5,7},{6,4},{7,5},{8,10},{9,11},{10,... | collective-permute-start | bytes 1769480 | tf_op jit(solution)/shard_map/ppermute | solution.py:146
  304.0 46.7 %collective-permute-start.45 = (bf16[256,1152]{1,0:T(8,128)(2,1)}, bf16[256,1152]{1,0:T(8,128)(2,1)}, u32[]{:S(2)}, u32[]{:S(2)}) collective-permute-start(bf16[256,1152]{1,0:T(8,128)(2,1)} %add_convert_fusion.6), channel_id=1, source_target_pairs={{0,2},{1,3},{2,0},{3,1},{4,6},{5,7},{6,4},{7,5},{8,10},{9,11},{10,... | collective-permute-start | bytes 1769480 | tf_op jit(solution)/shard_map/ppermute | solution.py:146
  368.1 37.7 %collective-permute-start.71 = (bf16[256,1152]{1,0:T(8,128)(2,1)S(1)}, bf16[256,1152]{1,0:T(8,128)(2,1)S(1)}, u32[]{:S(2)}, u32[]{:S(2)}) collective-permute-start(bf16[256,1152]{1,0:T(8,128)(2,1)S(1)} %copy-done.93), channel_id=1, source_target_pairs={{0,2},{1,3},{2,0},{3,1},{4,6},{5,7},{6,4},{7,5},{8,10},{9,11},{10,... | collective-permute-start | bytes 1769480 | tf_op jit(solution)/shard_map/ppermute | solution.py:150
  391.8 24.1 %collective-permute-start.61 = (bf16[256,1152]{1,0:T(8,128)(2,1)}, bf16[256,1152]{1,0:T(8,128)(2,1)}, u32[]{:S(2)}, u32[]{:S(2)}) collective-permute-start(bf16[256,1152]{1,0:T(8,128)(2,1)} %get-tuple-element.125.refs_2_.refs_4_), channel_id=1, source_target_pairs={{0,2},{1,3},{2,0},{3,1},{4,6},{5,7},{6,4},{7,5},{8,10},{9,11},{10,... | collective-permute-start | bytes 1769480 | tf_op jit(solution)/shard_map/ppermute | solution.py:150
  414.5 25.9 %collective-permute-start.62 = (bf16[256,1152]{1,0:T(8,128)(2,1)}, bf16[256,1152]{1,0:T(8,128)(2,1)S(1)}, u32[]{:S(2)}, u32[]{:S(2)}) collective-permute-start(bf16[256,1152]{1,0:T(8,128)(2,1)} %get-tuple-element.125.refs_2_.refs_4_), channel_id=1, source_target_pairs={{0,1},{1,0},{2,3},{3,2},{4,5},{5,4},{6,7},{7,6},{8,9},{9,8},{10,11... | collective-permute-start | bytes 1769480 | tf_op jit(solution)/shard_map/ppermute | solution.py:151
  415.0 98.2 %collective-permute-start.56 = (bf16[256,1152]{1,0:T(8,128)(2,1)}, bf16[256,1152]{1,0:T(8,128)(2,1)}, u32[]{:S(2)}, u32[]{:S(2)}) collective-permute-start(bf16[256,1152]{1,0:T(8,128)(2,1)} %get-tuple-element.121.refs_4_), channel_id=1, source_target_pairs={{0,2},{1,3},{2,0},{3,1},{4,6},{5,7},{6,4},{7,5},{8,10},{9,11},{10,... | collective-permute-start | bytes 1769480 | tf_op jit(solution)/shard_map/ppermute | solution.py:150
  416.0 24.4 %collective-permute-start.63 = (bf16[256,1152]{1,0:T(8,128)(2,1)}, bf16[256,1152]{1,0:T(8,128)(2,1)}, u32[]{:S(2)}, u32[]{:S(2)}) collective-permute-start(bf16[256,1152]{1,0:T(8,128)(2,1)} %collective-permute-done.61.refs_3_.refs_5_), channel_id=1, source_target_pairs={{0,1},{1,0},{2,3},{3,2},{4,5},{5,4},{6,7},{7,6},{8,9},{9,8},{10,11... | collective-permute-start | bytes 1769480 | tf_op jit(solution)/shard_map/ppermute | solution.py:152
  439.9 57.8 %collective-permute-start.74 = (bf16[512,1152]{1,0:T(8,128)(2,1)}, bf16[512,1152]{1,0:T(8,128)(2,1)S(1)}, u32[]{:S(2)}, u32[]{:S(2)}) collective-permute-start(bf16[512,1152]{1,0:T(8,128)(2,1)} %get-tuple-element.135), channel_id=1, source_target_pairs={{0,1},{1,0},{2,3},{3,2},{4,5},{5,4},{6,7},{7,6},{8,9},{9,8},{10,11... | collective-permute-start | bytes 3538952 | tf_op jit(solution)/shard_map/ppermute | solution.py:144
  463.5 35.1 %collective-permute-start.64 = (bf16[512,1152]{1,0:T(8,128)(2,1)}, bf16[512,1152]{1,0:T(8,128)(2,1)}, u32[]{:S(2)}, u32[]{:S(2)}) collective-permute-start(bf16[512,1152]{1,0:T(8,128)(2,1)} %get-tuple-element.127), channel_id=1, source_target_pairs={{0,1},{1,0},{2,3},{3,2},{4,5},{5,4},{6,7},{7,6},{8,9},{9,8},{10,11... | collective-permute-start | bytes 3538952 | tf_op jit(solution)/shard_map/ppermute | solution.py:144
  503.4 28.7 %collective-permute-start.75 = (bf16[256,1152]{1,0:T(8,128)(2,1)}, bf16[256,1152]{1,0:T(8,128)(2,1)}, u32[]{:S(2)}, u32[]{:S(2)}) collective-permute-start(bf16[256,1152]{1,0:T(8,128)(2,1)} %add_convert_fusion), channel_id=1, source_target_pairs={{0,2},{1,3},{2,0},{3,1},{4,6},{5,7},{6,4},{7,5},{8,10},{9,11},{10,... | collective-permute-start | bytes 1769480 | tf_op jit(solution)/shard_map/ppermute | solution.py:146
  504.8 37.0 %collective-permute-start.65 = (bf16[256,1152]{1,0:T(8,128)(2,1)}, bf16[256,1152]{1,0:T(8,128)(2,1)}, u32[]{:S(2)}, u32[]{:S(2)}) collective-permute-start(bf16[256,1152]{1,0:T(8,128)(2,1)} %add_convert_fusion.2), channel_id=1, source_target_pairs={{0,2},{1,3},{2,0},{3,1},{4,6},{5,7},{6,4},{7,5},{8,10},{9,11},{10,... | collective-permute-start | bytes 1769480 | tf_op jit(solution)/shard_map/ppermute | solution.py:146
  510.8 35.4 %collective-permute-start.57 = (bf16[256,1152]{1,0:T(8,128)(2,1)}, bf16[256,1152]{1,0:T(8,128)(2,1)}, u32[]{:S(2)}, u32[]{:S(2)}) collective-permute-start(bf16[256,1152]{1,0:T(8,128)(2,1)} %get-tuple-element.121.refs_4_), channel_id=1, source_target_pairs={{0,1},{1,0},{2,3},{3,2},{4,5},{5,4},{6,7},{7,6},{8,9},{9,8},{10,11... | collective-permute-start | bytes 1769480 | tf_op jit(solution)/shard_map/ppermute | solution.py:151
  513.3 33.7 %collective-permute-start.47 = (bf16[256,1152]{1,0:T(8,128)(2,1)}, bf16[256,1152]{1,0:T(8,128)(2,1)}, u32[]{:S(2)}, u32[]{:S(2)}) collective-permute-start(bf16[256,1152]{1,0:T(8,128)(2,1)} %get-tuple-element.111.refs_0_), channel_id=1, source_target_pairs={{0,1},{1,0},{2,3},{3,2},{4,5},{5,4},{6,7},{7,6},{8,9},{9,8},{10,11... | collective-permute-start | bytes 1769480 | tf_op jit(solution)/shard_map/ppermute | solution.py:151
  519.4 28.9 %collective-permute-start.58 = (bf16[256,1152]{1,0:T(8,128)(2,1)}, bf16[256,1152]{1,0:T(8,128)(2,1)}, u32[]{:S(2)}, u32[]{:S(2)}) collective-permute-start(bf16[256,1152]{1,0:T(8,128)(2,1)} %collective-permute-done.56.refs_5_), channel_id=1, source_target_pairs={{0,1},{1,0},{2,3},{3,2},{4,5},{5,4},{6,7},{7,6},{8,9},{9,8},{10,11... | collective-permute-start | bytes 1769480 | tf_op jit(solution)/shard_map/ppermute | solution.py:152
  582.2 34.9 %collective-permute-start.77 = (bf16[256,1152]{1,0:T(8,128)(2,1)S(1)}, bf16[256,1152]{1,0:T(8,128)(2,1)S(1)}, u32[]{:S(2)}, u32[]{:S(2)}) collective-permute-start(bf16[256,1152]{1,0:T(8,128)(2,1)S(1)} %copy-done.45), channel_id=1, source_target_pairs={{0,1},{1,0},{2,3},{3,2},{4,5},{5,4},{6,7},{7,6},{8,9},{9,8},{10,11... | collective-permute-start | bytes 1769480 | tf_op jit(solution)/shard_map/ppermute | solution.py:151
  582.2 24.1 %collective-permute-start.66 = (bf16[256,1152]{1,0:T(8,128)(2,1)S(1)}, bf16[256,1152]{1,0:T(8,128)(2,1)S(1)}, u32[]{:S(2)}, u32[]{:S(2)}) collective-permute-start(bf16[256,1152]{1,0:T(8,128)(2,1)S(1)} %get-tuple-element.129.refs_0_), channel_id=1, source_target_pairs={{0,2},{1,3},{2,0},{3,1},{4,6},{5,7},{6,4},{7,5},{8,10},{9,11},{10,... | collective-permute-start | bytes 1769480 | tf_op jit(solution)/shard_map/ppermute | solution.py:150
  583.5 33.6 %collective-permute-start.67 = (bf16[256,1152]{1,0:T(8,128)(2,1)S(1)}, bf16[256,1152]{1,0:T(8,128)(2,1)S(1)}, u32[]{:S(2)}, u32[]{:S(2)}) collective-permute-start(bf16[256,1152]{1,0:T(8,128)(2,1)S(1)} %get-tuple-element.129.refs_0_), channel_id=1, source_target_pairs={{0,1},{1,0},{2,3},{3,2},{4,5},{5,4},{6,7},{7,6},{8,9},{9,8},{10,11... | collective-permute-start | bytes 1769480 | tf_op jit(solution)/shard_map/ppermute | solution.py:151
  (242 other events, 2169.5 us)
Sparse Core Ops, SparseCore 0:
  392.0 108.8 reduce-scatter.1

commit v3 on v2

v3 whole, which is shorter than its diff:
```python
import math

import jax
import jax.numpy as jnp
from jax import lax
from jax.experimental import pallas as pl
from jax.experimental.pallas import tpu as pltpu
from jax.sharding import PartitionSpec as P

HEAD_DIM = 72
STEP = 10
UNIT = 64
REACH = 192


highest = lax.Precision.HIGHEST
beta_one = 0.9
beta_two = 0.999
adam_eps = 1e-08
decay_rate = 0.1
rate_matrix = 0.05
rate_vector = 0.5
ema_keep = 0.7
norm_eps = 1e-06
neg_large = -1e30
score_scale = HEAD_DIM**-0.5
low = jnp.bfloat16
wide = jnp.float32

DOT_NN = (((1,), (0,)), ((), ()))
DOT_NT = (((1,), (1,)), ((), ()))
DOT_TN = (((0,), (0,)), ((), ()))

COST = 10
VMEM_GRANT = 58 * 2**20
SMEM_SPEC = pl.BlockSpec(memory_space=pltpu.SMEM)

CORE_SWAP = [(i, i ^ 1) for i in range(4)]
CHIP_SWAP = [(i, i ^ 2) for i in range(4)]


def dot_as(left, right, dims):
    return lax.dot_general(left, right, dims, preferred_element_type=wide)


def ring_order(count):
    return list(range(0, count, 2)) + list(range(count - 1, 0, -2))


def ring_perms(count):
    order = ring_order(count)
    onward = [(order[i], order[(i + 1) % count]) for i in range(count)]
    return onward, [(b, a) for a, b in onward]


def ring_place(count):
    order = ring_order(count)
    spots = [order.index(i) for i in range(count)]
    return jnp.array(order), jnp.array(spots)[lax.axis_index("dp")]


def ring_start(shard, count):
    onward, backward = ring_perms(count)
    return lax.ppermute(shard, "dp", onward), lax.ppermute(shard, "dp", backward)


def ring_finish(ahead, behind, count):
    onward, backward = ring_perms(count)
    cut = ahead.shape[0] // 32 * 16
    return lax.ppermute(ahead[:cut], "dp", onward), lax.ppermute(behind[cut:], "dp", backward)


def ring_places(rows, count):
    order, spot = ring_place(count)
    at = [order[spot] * rows]
    for hop in range(1, count // 2):
        at += [order[(spot - hop) % count] * rows, order[(spot + hop) % count] * rows]
    far = order[(spot + count // 2) % count] * rows
    return jnp.stack(at + [far, far + rows // 32 * 16]).astype(jnp.int32)


def place_kernel(at_ref, *refs):
    pieces, (out_ref, held, sem_in, sem_out) = refs[:-4], refs[-4:]
    arrive, leave = [], []
    base = 0
    for i, piece in enumerate(pieces):
        count = piece.shape[0]
        spot = held.at[pl.ds(base, count)]
        arrive.append(pltpu.make_async_copy(piece, spot, sem_in.at[i]))
        to = out_ref.at[pl.ds(pl.multiple_of(at_ref[i], 16), count)]
        leave.append(pltpu.make_async_copy(spot, to, sem_out.at[i]))
        base += count
    for copy in arrive:
        copy.start()
    for first, second in zip(arrive, leave):
        first.wait()
        second.start()
    for copy in leave:
        copy.wait()


def place_pieces(at, pieces):
    whole = (sum(piece.shape[0] for piece in pieces),) + pieces[0].shape[1:]
    return pl.pallas_call(
        place_kernel,
        out_shape=jax.ShapeDtypeStruct(whole, pieces[0].dtype),
        in_specs=[SMEM_SPEC] + [pl.BlockSpec(memory_space=pl.ANY)] * len(pieces),
        out_specs=pl.BlockSpec(memory_space=pl.ANY),
        scratch_shapes=[pltpu.VMEM(whole, pieces[0].dtype)]
        + [pltpu.SemaphoreType.DMA((len(pieces),))] * 2,
        compiler_params=pltpu.CompilerParams(vmem_limit_bytes=VMEM_GRANT),
        cost_estimate=pl.CostEstimate(
            flops=0, bytes_accessed=4 * COST * math.prod(whole), transcendentals=0
        ),
        name="place_pieces",
    )(at, *pieces)


class RingSum:
    def __init__(self, parts, count):
        self.parts, self.rows = parts, parts.shape[0] // count
        self.onward, self.backward = ring_perms(count)
        self.order, self.spot = ring_place(count)
        self.count, self.left = count, count // 2 - 1
        self.send(self.chunk(count // 2), self.chunk(1 - count // 2))

    def chunk(self, ahead):
        at = self.order[(self.spot + ahead) % self.count] * self.rows
        return lax.dynamic_slice_in_dim(self.parts, at, self.rows, 0).astype(wide)

    def send(self, ahead, behind):
        self.ahead = lax.ppermute(ahead.astype(low), "dp", self.onward)
        if behind is not None:
            self.behind = lax.ppermute(behind.astype(low), "dp", self.backward)

    def hop(self, token):
        if not self.left:
            return token
        token, ahead, behind = lax.optimization_barrier((token, self.ahead, self.behind))
        self.behind = behind
        ahead = ahead.astype(wide) + self.chunk(self.left)
        if self.left > 1:
            behind = behind.astype(wide) + self.chunk(1 - self.left)
        else:
            behind = None
        self.send(ahead, behind)
        self.left -= 1
        return token

    def total(self):
        return self.ahead.astype(wide) + self.behind.astype(wide) + self.chunk(0)


def halving_hop(parts, step, count):
    pairs = parts.reshape((parts.shape[0] // 2, 2) + parts.shape[1:])
    bit = lax.axis_index("dp") // step % 2
    sent = lax.dynamic_index_in_dim(pairs, 1 - bit, 1, keepdims=False).astype(low)
    kept = lax.dynamic_index_in_dim(pairs, bit, 1, keepdims=False).astype(wide)
    got = lax.ppermute(sent, "dp", [(i, i ^ step) for i in range(count)])
    return kept + got.astype(wide)


def doubling_gather(shard, count, between):
    if count not in (4, 8):
        return lax.all_gather(shard, "dp", axis=0, tiled=True)
    spot = lax.axis_index("dp")
    known = shard[None]
    step = count // 2
    while step:
        known = lax.optimization_barrier((known, between[0]))[0]
        between = between[1:]
        got = lax.ppermute(known, "dp", [(i, i ^ step) for i in range(count)])
        second = spot // step % 2 == 1
        known = jnp.stack([jnp.where(second, got, known), jnp.where(second, known, got)], 1)
        known = known.reshape((-1,) + shard.shape)
        step //= 2
    return known.reshape((-1,) + shard.shape[1:])


def share_hop(known, reach, count):
    return known + lax.ppermute(known, "dp", [(i, i ^ reach) for i in range(count)])


def group_scatter(kept, sent):
    quarter = kept.shape[0] // 2
    got = lax.ppermute(sent, "mp", CORE_SWAP)
    passed = (kept[quarter:] + got[quarter:].astype(wide)).astype(low)
    return (kept, got, lax.ppermute(passed, "mp", CHIP_SWAP)), passed


def group_gather(own, between=None):
    chip = lax.ppermute(own, "mp", CHIP_SWAP)
    if between is not None:
        chip = lax.optimization_barrier((chip, between))[0]
    core = lax.ppermute(own, "mp", CORE_SWAP)
    both = lax.ppermute(chip, "mp", CORE_SWAP)
    return [own, chip, core, both]


def in_group_order(pieces, place):
    stacked = jnp.stack(pieces, 0)
    return [
        lax.dynamic_index_in_dim(stacked, jnp.bitwise_xor(place, j), 0, keepdims=False)
        for j in range(4)
    ]


def key_windows(row_len, block):
    return [
        (at, max(0, at - REACH), min(row_len, at + block + REACH))
        for at in range(0, row_len, block)
    ]


def relative_at(place, j, block):
    return pl.multiple_of(jnp.bitwise_xor(place, j) * block, block)


def attend_forward_kernel(
    place_ref, qkv_ref, seg_col_ref, seg_row_ref, w_ref, out_ref, kept_ref, sent_ref, q_s, k_s, v_s, *, heads
):
    row_len = qkv_ref.shape[0]
    width = heads * HEAD_DIM
    block = row_len // 4
    place = place_ref[0]
    for j in range(4):
        at = relative_at(place, j, block)
        to = slice(j * block, (j + 1) * block)
        for h in range(heads):
            c = h * HEAD_DIM
            q_s[h, to, :] = qkv_ref[pl.ds(at, block), c : c + HEAD_DIM]
            k_s[h, to, :] = qkv_ref[pl.ds(at, block), width + c : width + c + HEAD_DIM]
            v_s[h, to, :] = qkv_ref[pl.ds(at, block), 2 * width + c : 2 * width + c + HEAD_DIM]
    for j, (at, start, stop) in enumerate(key_windows(row_len, block)):
        same = seg_col_ref[start:stop, :] == seg_row_ref[:, at : at + block]
        mixed = []
        for h in range(heads):
            scores = dot_as(k_s[h, start:stop, :], q_s[h, at : at + block, :], DOT_NT)
            scores = jnp.where(same, scores, neg_large)
            top = jnp.max(scores, axis=0, keepdims=True)
            weights = jnp.exp((scores - top) * score_scale)
            total = jnp.sum(weights, axis=0, keepdims=True)
            gathered = dot_as(v_s[h, start:stop, :], weights.astype(low), DOT_TN)
            mixed.append(gathered * (1.0 / total))
        out_ref[pl.ds(relative_at(place, j, block), block), :] = (
            jnp.concatenate(mixed, axis=0).T.astype(low)
        )
    w_out = w_ref[:, 3 * width :]
    half = row_len // 2
    kept_ref[...] = dot_as(out_ref[:half, :], w_out, DOT_NT)
    sent_ref[...] = dot_as(out_ref[half:, :], w_out, DOT_NT).astype(low)


def attend_backward_kernel(
    place_ref, qkv_ref, g0_ref, g1_ref, g2_ref, g3_ref, seg_col_ref, seg_row_ref, w_ref,
    out_ref, kept_ref, sent_ref, sums_ref, q_s, k_s, v_s, g_s, dk_s, dv_s, *, heads
):
    row_len = qkv_ref.shape[0]
    width = heads * HEAD_DIM
    block = row_len // 4
    place = place_ref[0]
    dk_s[...] = jnp.zeros_like(dk_s)
    dv_s[...] = jnp.zeros_like(dv_s)
    w_out = w_ref[:, 3 * width :]
    for j, g_ref in enumerate((g0_ref, g1_ref, g2_ref, g3_ref)):
        grad = dot_as(g_ref[...], w_out, DOT_NN).astype(low)
        at = relative_at(place, j, block)
        for h in range(heads):
            g_s[h, pl.ds(at, block), :] = grad[:, h * HEAD_DIM : (h + 1) * HEAD_DIM]
    for j in range(4):
        at = relative_at(place, j, block)
        to = slice(j * block, (j + 1) * block)
        for h in range(heads):
            c = h * HEAD_DIM
            q_s[h, to, :] = qkv_ref[pl.ds(at, block), c : c + HEAD_DIM]
            k_s[h, to, :] = qkv_ref[pl.ds(at, block), width + c : width + c + HEAD_DIM]
            v_s[h, to, :] = qkv_ref[pl.ds(at, block), 2 * width + c : 2 * width + c + HEAD_DIM]
    for j, (at, start, stop) in enumerate(key_windows(row_len, block)):
        same = seg_col_ref[start:stop, :] == seg_row_ref[:, at : at + block]
        grads = []
        for h in range(heads):
            query = q_s[h, at : at + block, :]
            grad = g_s[h, at : at + block, :]
            keys = k_s[h, start:stop, :]
            scores = jnp.where(same, dot_as(keys, query, DOT_NT), neg_large)
            top = jnp.max(scores, axis=0, keepdims=True)
            weights = jnp.exp((scores - top) * score_scale)
            probs = weights * (1.0 / jnp.sum(weights, axis=0, keepdims=True))
            grad_probs = dot_as(v_s[h, start:stop, :], grad, DOT_NT)
            inner = jnp.sum(grad_probs * probs, axis=0, keepdims=True)
            grad_scores = (probs * (grad_probs - inner)).astype(low)
            dv_s[h, start:stop, :] += dot_as(probs.astype(low), grad, DOT_NN)
            dk_s[h, start:stop, :] += dot_as(grad_scores, query, DOT_NN)
            grads.append(dot_as(keys, grad_scores, DOT_TN) * score_scale)
        out_ref[pl.ds(relative_at(place, j, block), block), 0:width] = (
            jnp.concatenate(grads, axis=0).T.astype(low)
        )
    for j in range(4):
        at = slice(j * block, (j + 1) * block)
        to = relative_at(place, j, block)
        out_ref[pl.ds(to, block), width : 2 * width] = jnp.concatenate(
            [(dk_s[h, at, :] * score_scale).astype(low) for h in range(heads)], axis=1
        )
        out_ref[pl.ds(to, block), 2 * width : 3 * width] = jnp.concatenate(
            [dv_s[h, at, :].astype(low) for h in range(heads)], axis=1
        )
    half = row_len // 2
    w_qkv = w_ref[:, : 3 * width]
    kept_ref[...] = dot_as(out_ref[:half, :], w_qkv, DOT_NT)
    sent_ref[...] = dot_as(out_ref[half:, :], w_qkv, DOT_NT).astype(low)
    for u in range(row_len // UNIT):
        sums_ref[u : u + 1, :] = jnp.sum(
            out_ref[u * UNIT : (u + 1) * UNIT, :].astype(wide), axis=0, keepdims=True
        )


def shape_of(shape, kind):
    return jax.ShapeDtypeStruct(shape, kind)


def attend_forward(place, qkv, seg_row, weights):
    row_len, width = qkv.shape[0], qkv.shape[1] // 3
    heads = width // HEAD_DIM
    full = weights.shape[0]
    args = (qkv, seg_row.reshape(row_len, 1), seg_row.reshape(1, row_len), weights)
    shapes = (
        shape_of((row_len, width), low),
        shape_of((row_len // 2, full), wide),
        shape_of((row_len // 2, full), low),
    )

    def body(*refs):
        attend_forward_kernel(*refs, heads=heads)

    return row_call(
        body,
        "attend_forward",
        place,
        args,
        [fixed_spec(arg.shape) for arg in args],
        tuple(fixed_spec(shape.shape) for shape in shapes),
        shapes,
        scratch=[pltpu.VMEM((heads, row_len, HEAD_DIM), low)] * 3,
        flops=4 * row_len * 640 * width + 2 * row_len * width * full,
        exps=heads * row_len * 640,
    )


def attend_backward(place, qkv, grads, seg_row, weights):
    row_len, width = qkv.shape[0], qkv.shape[1] // 3
    heads = width // HEAD_DIM
    full = weights.shape[0]
    args = (qkv, *grads, seg_row.reshape(row_len, 1), seg_row.reshape(1, row_len), weights)
    shapes = (
        shape_of((row_len, 3 * width), low),
        shape_of((row_len // 2, full), wide),
        shape_of((row_len // 2, full), low),
        shape_of((row_len // UNIT, 3 * width), wide),
    )

    def body(*refs):
        attend_backward_kernel(*refs, heads=heads)

    return row_call(
        body,
        "attend_backward",
        place,
        args,
        [fixed_spec(arg.shape) for arg in args],
        tuple(fixed_spec(shape.shape) for shape in shapes),
        shapes,
        scratch=[pltpu.VMEM((heads, row_len, HEAD_DIM), low)] * 4
        + [pltpu.VMEM((heads, row_len, HEAD_DIM), wide)] * 2,
        flops=10 * row_len * 640 * width + 8 * row_len * width * full,
        exps=heads * row_len * 640,
    )


def norm_parts(values):
    centre = values - jnp.mean(values, axis=-1, keepdims=True)
    inverse = lax.rsqrt(jnp.mean(centre * centre, axis=-1, keepdims=True) + norm_eps)
    return centre * inverse, inverse


def norm_back(normed, inverse, grad):
    return inverse * (
        grad
        - jnp.mean(grad, axis=-1, keepdims=True)
        - normed * jnp.mean(grad * normed, axis=-1, keepdims=True)
    )


def unit_rows(ref):
    return [(u, slice(u * UNIT, (u + 1) * UNIT)) for u in range(ref.shape[0] // UNIT)]


def column(values, index, width):
    return values[:, index * width : (index + 1) * width]


def open_kernel(
    place_ref, x0_ref, x1_ref, tab0_ref, tab1_ref, add0_ref, add1_ref, w_ref, a_ref, qkv_ref
):
    width = x0_ref.shape[1]
    quarter = x0_ref.shape[0]
    for j, (x_ref, tab_ref) in enumerate(((x0_ref, tab0_ref), (x1_ref, tab1_ref))):
        for u, at in unit_rows(x_ref):
            normed, _ = norm_parts(x_ref[at, :].astype(wide))
            table = tab_ref[0, u : u + 1, :]
            out = normed * (1.0 + column(table, 1, width)) + column(table, 0, width)
            a_ref[j * quarter + u * UNIT : j * quarter + (u + 1) * UNIT, :] = out.astype(low)
    qkv = dot_as(a_ref[...], w_ref[:, : qkv_ref.shape[1]], DOT_NN)
    for j, add_ref in enumerate((add0_ref, add1_ref)):
        for u in range(quarter // UNIT):
            at = slice(j * quarter + u * UNIT, j * quarter + (u + 1) * UNIT)
            qkv_ref[at, :] = (qkv[at, :] + add_ref[0, u : u + 1, :]).astype(low)


def first_kernel(place_ref, x_ref, kept_ref, got_ref, passed_ref, bias_ref, tab_ref, att_ref, hid_ref, a_ref):
    width = x_ref.shape[1]
    for u, at in unit_rows(x_ref):
        table = tab_ref[0, u : u + 1, :]
        attended = kept_ref[at, :] + got_ref[at, :].astype(wide) + passed_ref[at, :].astype(wide)
        attended = attended + bias_ref[0:1, :]
        hidden = x_ref[at, :].astype(wide) + column(table, 0, width) * attended
        normed, _ = norm_parts(hidden)
        att_ref[at, :] = attended
        hid_ref[at, :] = hidden
        a_ref[at, :] = (normed * (1.0 + column(table, 2, width)) + column(table, 1, width)).astype(low)


def down_back_kernel(place_ref, cot0_ref, cot1_ref, tab0_ref, tab1_ref, w_ref, grad_ref, dm_ref):
    width = cot0_ref.shape[1]
    quarter = cot0_ref.shape[0]
    for j, (cot_ref, tab_ref) in enumerate(((cot0_ref, tab0_ref), (cot1_ref, tab1_ref))):
        for u, at in unit_rows(cot_ref):
            gate = column(tab_ref[0, u : u + 1, :], 3, width)
            out = (cot_ref[at, :].astype(wide) * gate).astype(low)
            grad_ref[j * quarter + u * UNIT : j * quarter + (u + 1) * UNIT, :] = out
    dm_ref[...] = dot_as(grad_ref[...], w_ref[...], DOT_NN).astype(low)


def gelu_both(values):
    scale = math.sqrt(2.0 / math.pi)
    square = values * values
    turned = jnp.tanh(scale * values * (1.0 + 0.044715 * square))
    upper = 0.5 * (1.0 + turned)
    slope = upper + 0.5 * values * (1.0 - turned * turned) * scale * (1.0 + 3 * 0.044715 * square)
    return values * upper, slope


def up_kernel(
    place_ref, a0_ref, a1_ref, a2_ref, a3_ref, dm_ref, bias_ref, w_ref, m_ref, dz_ref, kept_ref, sent_ref, sums_ref, a_s
):
    step = pl.program_id(0)
    quarter = a0_ref.shape[0]
    for j, piece in enumerate((a0_ref, a1_ref, a2_ref, a3_ref)):

        @pl.when(step == j // 2)
        def _(piece=piece, j=j):
            a_s[j % 2 * quarter : (j % 2 + 1) * quarter, :] = piece[...]

    sums = jnp.zeros(sums_ref.shape[1:], wide)
    for j in range(2):
        at = slice(j * quarter, (j + 1) * quarter)
        inner = dot_as(a_s[at, :], w_ref[...], DOT_NN) + bias_ref[...]
        active, slope = gelu_both(inner)
        m_ref[at, :] = active.astype(low)
        grad = (dm_ref[at, :].astype(wide) * slope).astype(low)
        dz_ref[at, :] = grad
        sums = sums + jnp.sum(grad.astype(wide).reshape(-1, 8, grad.shape[1]), axis=0)
    sums_ref[0] = sums
    back = dot_as(dz_ref[...], w_ref[...], DOT_NT)

    @pl.when(step == 0)
    def _():
        kept_ref[...] = back

    @pl.when(step == 1)
    def _():
        sent_ref[...] = back.astype(low)


def down_kernel(place_ref, m_ref, w_ref, kept_ref, sent_ref):
    step = pl.program_id(0)
    out = dot_as(m_ref[...], w_ref[...], DOT_NT)

    @pl.when(step == 0)
    def _():
        kept_ref[...] = out

    @pl.when(step == 1)
    def _():
        sent_ref[...] = out.astype(low)


def second_kernel(
    place_ref, cot_ref, kept_ref, got_ref, passed_ref, hid_ref, att_ref, tab_ref, gh_ref, ga_ref, sums_ref
):
    width = cot_ref.shape[1]
    bias = jnp.zeros((1, width), wide)
    sums_ref[...] = jnp.zeros_like(sums_ref)
    for u, at in unit_rows(cot_ref):
        table = tab_ref[0, u : u + 1, :]
        grad_two = kept_ref[at, :] + got_ref[at, :].astype(wide) + passed_ref[at, :].astype(wide)
        normed, inverse = norm_parts(hid_ref[at, :])
        grad = cot_ref[at, :].astype(wide) + norm_back(
            normed, inverse, grad_two * (1.0 + column(table, 2, width))
        )
        grad_att = grad * column(table, 0, width)
        gh_ref[at, :] = grad
        ga_ref[at, :] = grad_att.astype(low)
        bias = bias + jnp.sum(grad_att, axis=0, keepdims=True)
        sums_ref[u : u + 1, :] = jnp.sum(grad * att_ref[at, :], axis=0, keepdims=True)
        sums_ref[4 + u : 5 + u, :] = jnp.sum(grad_two, axis=0, keepdims=True)
        sums_ref[8 + u : 9 + u, :] = jnp.sum(grad_two * normed, axis=0, keepdims=True)
    sums_ref[12:13, :] = bias


def out_kernel(
    place_ref, cot_ref, kept_ref, got_ref, passed_ref, hid_ref, bias_ref, tab_ref, out_ref, sums_ref
):
    width = cot_ref.shape[1]
    bias = jnp.zeros((1, width), wide)
    sums_ref[...] = jnp.zeros_like(sums_ref)
    for u, at in unit_rows(cot_ref):
        gate = column(tab_ref[0, u : u + 1, :], 3, width)
        mlp = kept_ref[at, :] + got_ref[at, :].astype(wide) + passed_ref[at, :].astype(wide)
        mlp = mlp + bias_ref[1:2, :]
        out_ref[at, :] = (hid_ref[at, :] + gate * mlp).astype(low)
        cot = cot_ref[at, :].astype(wide)
        sums_ref[u : u + 1, :] = jnp.sum(cot * mlp, axis=0, keepdims=True)
        bias = bias + jnp.sum(cot, axis=0, keepdims=True) * gate
    sums_ref[4:5, :] = bias


def third_kernel(place_ref, x_ref, kept_ref, got_ref, passed_ref, gh_ref, tab_ref, out_ref, sums_ref):
    width = x_ref.shape[1]
    for u, at in unit_rows(x_ref):
        grad_one = kept_ref[at, :] + got_ref[at, :].astype(wide) + passed_ref[at, :].astype(wide)
        normed, inverse = norm_parts(x_ref[at, :].astype(wide))
        table = tab_ref[0, u : u + 1, :]
        back = norm_back(normed, inverse, grad_one * (1.0 + column(table, 1, width)))
        out_ref[at, :] = (gh_ref[at, :] + back).astype(low)
        sums_ref[u : u + 1, :] = jnp.sum(grad_one, axis=0, keepdims=True)
        sums_ref[4 + u : 5 + u, :] = jnp.sum(grad_one * normed, axis=0, keepdims=True)


def row_call(body, name, place, args, in_specs, out_specs, out_shape, grid=1, scratch=(), flops=0, exps=0, aliases=None):
    moved = sum(math.prod(a.shape) * a.dtype.itemsize for a in args)
    shapes = out_shape if isinstance(out_shape, tuple) else (out_shape,)
    moved += sum(math.prod(o.shape) * o.dtype.itemsize for o in shapes)
    return pl.pallas_call(
        body,
        grid_spec=pltpu.PrefetchScalarGridSpec(
            num_scalar_prefetch=1,
            grid=(grid,),
            in_specs=in_specs,
            out_specs=out_specs,
            scratch_shapes=scratch,
        ),
        out_shape=out_shape,
        input_output_aliases=aliases or {},
        compiler_params=pltpu.CompilerParams(vmem_limit_bytes=VMEM_GRANT),
        cost_estimate=pl.CostEstimate(
            flops=COST * flops, bytes_accessed=COST * moved, transcendentals=COST * exps
        ),
        name=name,
    )(place, *args)


def block_spec(shape, index):
    return pl.BlockSpec(shape, index)


def fixed_spec(shape):
    return pl.BlockSpec(shape, lambda *_: (0,) * len(shape))


def unit_tables(mp_arg, onehot, pieces, fields):
    units, slots = onehot.shape
    own = pieces[0].shape[1]

    def body(mp_ref, hot_ref, *refs):
        out_ref = refs[-1]
        mp_place = mp_ref[0]
        for i, piece in enumerate(refs[:-1]):
            for j in range(4):

                @pl.when(jnp.bitwise_xor(mp_place, i) == j)
                def _(piece=piece, j=j):
                    for f in range(fields):
                        at = f * 4 * own + j * own
                        out_ref[:, at : at + own] = dot_as(
                            hot_ref[...], piece[f * slots : (f + 1) * slots, :], DOT_NN
                        )

    return row_call(
        body,
        "unit_tables",
        mp_arg,
        (onehot, *pieces),
        [fixed_spec(onehot.shape)] + [fixed_spec(pieces[0].shape)] * 4,
        fixed_spec((units, fields * 4 * own)),
        shape_of((units, fields * 4 * own), wide),
        flops=8 * units * slots * own * fields,
    )


def weight_grad(place, pairs, name):
    depth = pairs[0][0][0][0].shape[1]
    tile = depth // 3
    widths = [pair[0][1].shape[1] for pair in pairs]
    args, specs, plan = [], [], []
    flops = 0
    for pair in pairs:
        rows = []
        for left, right in pair:
            rows.append((len(args), len(left)))
            args += list(left) + [right]
            specs += [pl.BlockSpec((piece.shape[0], tile), lambda i, p: (0, i)) for piece in left]
            specs.append(fixed_spec(right.shape))
            flops += 2 * depth * math.prod(right.shape)
        plan.append(rows)

    def body(place_ref, *refs):
        out_ref = refs[-1]
        at = 0
        for rows, cols in zip(plan, widths):
            total = None
            for first, count in rows:
                left = [ref[...] for ref in refs[first : first + count]]
                left = left[0] if count == 1 else jnp.concatenate(left, axis=0)
                part = dot_as(left, refs[first + count][...], DOT_TN)
                total = part if total is None else total + part
            out_ref[:, at : at + cols] = total.astype(low)
            at += cols

    return row_call(
        body,
        name,
        place,
        args,
        specs,
        pl.BlockSpec((tile, sum(widths)), lambda i, p: (i, 0)),
        shape_of((depth, sum(widths)), low),
        grid=3,
        flops=flops,
    )


def widen_row(place, pieces, row, rows, before):
    quarter, width = pieces[0].shape

    def body(place_ref, *refs):
        step = pl.program_id(0)
        for i, piece in enumerate(refs[:4]):

            @pl.when(step == i)
            def _(piece=piece):
                refs[-1][...] = piece[...].astype(wide)

    return row_call(
        body,
        "widen_row",
        place,
        tuple(pieces) + before,
        [fixed_spec((quarter, width))] * 4 + [pl.BlockSpec(memory_space=pl.ANY)] * len(before),
        pl.BlockSpec((quarter, width), lambda i, p: (row * 4 + jnp.bitwise_xor(p[0], i), 0)),
        shape_of((rows * 4 * quarter, width), wide),
        grid=4,
        aliases={5: 0} if before else None,
    )


def adam_step(weight, gradient, first_old, second_old, ema_old, step_rate):
    first_new = beta_one * first_old + (1.0 - beta_one) * gradient
    second_new = beta_two * second_old + (1.0 - beta_two) * gradient * gradient
    first_hat = first_new * (1.0 / (1.0 - beta_one**STEP))
    second_hat = second_new * (1.0 / (1.0 - beta_two**STEP))
    weight_new = weight - step_rate * (
        first_hat / (jnp.sqrt(second_hat) + adam_eps) + decay_rate * weight
    )
    ema_new = ema_keep * ema_old + (1.0 - ema_keep) * weight_new
    return (first_new, second_new, weight_new, ema_new)


def adam_slabs(token, plan, grads, make_grad, groups, before, name):
    slab = groups[0][0].shape[1:]
    count, held = len(plan), 4 * len(groups)
    turns = [[i for i, (which, _) in enumerate(plan) if which == g] for g in range(len(groups))]
    ids = [plan[max([i for i in mine if i <= n], default=mine[0])][1] for mine in turns for n in range(count)]
    ids = lax.optimization_barrier((jnp.array(ids, jnp.int32), token))[0]

    def block(group):
        return pl.BlockSpec((1,) + slab, lambda i, ids: (ids[group * count + i], 0, 0))

    def body(ids_ref, *refs):
        grad_refs, state_refs = refs[: len(grads)], refs[len(grads) : len(grads) + held]
        out_refs, grad_s = refs[-held - 1 : -1], refs[-1]
        step = pl.program_id(0)
        for n in range(count):

            @pl.when(step == n)
            def _(n=n):
                grad_s[...] = make_grad(n, grad_refs)

        for group, mine in enumerate(turns):

            @pl.when((step >= mine[0]) & (step <= mine[-1]))
            def _(group=group):
                weight, *old = [ref[0] for ref in state_refs[4 * group : 4 * group + 4]]
                new = adam_step(weight, grad_s[...], *old, rate_matrix)
                for ref, value in zip(out_refs[4 * group : 4 * group + 4], new):
                    ref[0] = value

    flat = [x for group in groups for x in group]
    specs = [block(g) for g in range(len(groups)) for _ in range(4)]
    kept, aliases = [], {}
    for g, arrays in enumerate(before):
        for i, x in enumerate(arrays or ()):
            aliases[1 + len(grads) + held + len(kept)] = 4 * g + i
            kept.append(x)
    return row_call(
        body,
        name,
        ids,
        (*grads, *flat, *kept),
        [fixed_spec(grad.shape) for grad in grads]
        + specs
        + [pl.BlockSpec(memory_space=pl.ANY)] * len(kept),
        tuple(specs),
        tuple(shape_of(x.shape, wide) for x in flat),
        grid=count,
        scratch=[pltpu.VMEM(slab, wide)],
        aliases=aliases,
    )


def per_device(
    tokens,
    seg_ids,
    time_steps,
    cotangent,
    weight_cols,
    weight_rows,
    bias_cols,
    bias_rows,
    first_cols,
    first_rows,
    first_bias_cols,
    first_bias_rows,
    second_cols,
    second_rows,
    second_bias_cols,
    second_bias_rows,
    ema_cols,
    ema_rows,
    ema_bias_cols,
    ema_bias_rows,
):
    own_width = weight_cols.shape[2]
    own_depth = weight_cols.shape[1]
    width = tokens.shape[1]
    rows = time_steps.shape[0]
    slots = time_steps.shape[1]
    token_count = tokens.shape[0]
    row_len = token_count // rows
    units = row_len // UNIT
    quarter = row_len // 4
    own_units = units // 4
    dp_count = width // own_depth
    dp_place = lax.axis_index("dp")
    slot_count = rows * slots
    mp_place = lax.axis_index("mp")
    core, chip = mp_place % 2, mp_place // 2
    place = (2 * core + chip).astype(jnp.int32)
    place_arg = place.reshape(1)

    def tied(*others):
        return lax.optimization_barrier((place_arg,) + others)[0]

    ring = dp_count in (4, 8)
    cols_low = weight_cols.astype(low)
    own_rows = weight_rows.astype(low).transpose(2, 0, 1).reshape(own_depth, 5 * own_width)
    own_first = jnp.concatenate([cols_low[0], cols_low[1], cols_low[2], own_rows[:, :own_width]], 1)
    own_rest = jnp.concatenate([cols_low[5 + i] for i in range(4)] + [own_rows[:, own_width:]], 1)

    half_width = width // 2
    feature = dp_place * own_depth + jnp.arange(own_depth)
    is_cos = feature < half_width
    index = jnp.where(is_cos, feature, feature - half_width).astype(wide)
    frequency = jnp.exp(-math.log(10000.0) * index / half_width)

    def embed(steps):
        angles = steps.astype(wide)[:, None] * frequency[None, :]
        table = jnp.where(is_cos[None, :], jnp.cos(angles), jnp.sin(angles))
        return table.astype(low), jax.nn.silu(table).astype(low)

    def slot_products(left, maps):
        out = jnp.stack([dot_as(left, maps[j], DOT_NN).astype(low) for j in range(maps.shape[0])], 0)
        return out.reshape(-1, dp_count, rows * slots, own_width).transpose(1, 0, 2, 3)

    def near_products(time_low, ada_low):
        return jnp.concatenate(
            [slot_products(ada_low, cols_low[9:11]), slot_products(time_low, cols_low[3:5])], 1
        )

    if ring:
        known = jnp.zeros((dp_count,) + time_steps.shape, time_steps.dtype)
        known = lax.dynamic_update_slice_in_dim(known, time_steps[None], dp_place, 0)
        onward, backward = ring_perms(dp_count)
        ahead, behind = ring_start(own_first, dp_count)
        pieces = [own_first, ahead, behind]
        known = share_hop(known, 1, dp_count)
        known = share_hop(known, 2, dp_count)
        known, ahead, behind = lax.optimization_barrier((known, ahead, behind))
        if dp_count == 8:
            ahead = lax.ppermute(ahead, "dp", onward)
            behind = lax.ppermute(behind, "dp", backward)
            pieces += [ahead, behind]
            known = share_hop(known, 4, dp_count)
        time_low, ada_low = embed(known.reshape(-1))
        near = near_products(time_low, ada_low)
        near, ahead, behind = lax.optimization_barrier((near, ahead, behind))
        if dp_count == 8:
            ahead = lax.ppermute(ahead, "dp", onward)
            behind = lax.ppermute(behind, "dp", backward)
            pieces += [ahead, behind]
        near = halving_hop(near, 1, dp_count)
        near = halving_hop(near, 2, dp_count)
        near, ahead, behind, own_rest = lax.optimization_barrier((near, ahead, behind, own_rest))
        pieces += ring_finish(ahead, behind, dp_count)
        rest_pieces = [own_rest, *ring_start(own_rest, dp_count)]
        if dp_count == 8:
            near = halving_hop(near, 4, dp_count)
        near = near[0]
        w_first = place_pieces(ring_places(own_depth, dp_count), pieces)
    else:
        w_first = lax.all_gather(own_first, "dp", axis=0, tiled=True)
        rest_pieces = [lax.all_gather(own_rest, "dp", axis=0, tiled=True)]
        time_low, ada_low = embed(lax.all_gather(time_steps, "dp", axis=0, tiled=True).reshape(-1))
        near = near_products(time_low, ada_low)
        near = lax.psum_scatter(near, "dp", scatter_dimension=0, tiled=True)[0].astype(wide)

    seg_grid = seg_ids.reshape(rows, row_len)
    unit_seg = seg_grid.reshape(rows, units, UNIT)[:, :, 0]
    onehot = unit_seg[:, :, None] == jnp.arange(slots, dtype=jnp.int32)
    blocks = onehot[:, :, None, :] & (jnp.arange(rows)[:, None] == jnp.arange(rows))[:, None, :, None]
    blocks = blocks.reshape(rows * units, rows * slots)
    mp_arg = mp_place.astype(jnp.int32).reshape(1)

    def tables(own, biases):
        fields = own.shape[0]
        own = (own + biases[:, None, :]).astype(low).reshape(-1, own_width)
        pieces = group_gather(own)
        pieces = [pieces[0], pieces[2], pieces[1], pieces[3]]
        out = unit_tables(mp_arg, blocks.astype(low), pieces, fields)
        return out.reshape(rows, 4, own_units, fields * width)

    far = [slot_products(lax.optimization_barrier((ada_low, near))[0], cols_low[11:15])]

    def far_hop(token):
        if not ring:
            return token
        token, held = lax.optimization_barrier((token, far[-1]))
        if held.shape[0] > 1:
            far.append(halving_hop(held, dp_count // held.shape[0], dp_count))
        return token

    near_tab = tables(near[:2], bias_cols[6:8])
    time_add = jnp.concatenate(
        [near[2] + bias_cols[0], jnp.zeros((rows * slots, own_width), wide), near[3] + bias_cols[1]], 1
    )
    add_tab = jnp.dot(blocks.astype(wide), time_add, precision=highest)
    add_tab = add_tab.reshape(rows, 4, own_units, 3 * own_width)

    block, half_block = (quarter, width), (row_len // 2, width)
    qkv_width = 3 * own_width
    half = row_len // 2
    lows = lambda *shape: shape_of(shape, low)
    wides = lambda *shape: shape_of(shape, wide)

    def own_block(r):
        return pl.BlockSpec(block, lambda i, p: (r * 4 + p[0], 0))

    def moved_blocks(r):
        return [
            pl.BlockSpec(block, lambda i, p: (r * 4 + jnp.bitwise_xor(p[0], 2 * i), 0)),
            pl.BlockSpec(block, lambda i, p: (r * 4 + jnp.bitwise_xor(p[0], 2 * i + 1), 0)),
        ]

    def moved_tables(tab):
        shape = (1,) + tab.shape[2:]
        return [
            pl.BlockSpec(shape, lambda i, p: (jnp.bitwise_xor(p[0], 2 * i), 0, 0)),
            pl.BlockSpec(shape, lambda i, p: (jnp.bitwise_xor(p[0], 2 * i + 1), 0, 0)),
        ]

    def own_table(tab):
        return pl.BlockSpec((1,) + tab.shape[2:], lambda i, p: (p[0], 0, 0))

    here = fixed_spec(block)
    half_step = pl.BlockSpec(half_block, lambda i, p: (i, 0))
    half_fixed = fixed_spec(half_block)

    def open_row(r, token):
        return row_call(
            open_kernel,
            "open_row",
            token,
            (tokens, tokens, near_tab[r], near_tab[r], add_tab[r], add_tab[r], w_first),
            moved_blocks(r) + moved_tables(near_tab) + moved_tables(add_tab) + [fixed_spec(w_first.shape)],
            (half_step, pl.BlockSpec((half, qkv_width), lambda i, p: (i, 0))),
            (lows(row_len, width), lows(row_len, qkv_width)),
            grid=2,
            flops=2 * row_len * width * qkv_width,
        )

    def rest_hop(token):
        if not ring:
            return token
        token, ahead, behind = lax.optimization_barrier((token, *rest_pieces[-2:]))
        hops = (len(rest_pieces) - 1) // 2
        if hops < dp_count // 2 - 1:
            rest_pieces.append(lax.ppermute(ahead, "dp", onward))
            rest_pieces.append(lax.ppermute(behind, "dp", backward))
        elif hops < dp_count // 2:
            rest_pieces.extend(ring_finish(ahead, behind, dp_count))
        return token

    inputs_one, qkvs, mixed, parts = [], [], [], []
    token = rest_hop(far_hop(place_arg))
    for r in range(rows):
        a_one, qkv = open_row(r, token)
        token = far_hop(tied(qkv, *[part[1] for part in parts]))
        inputs_one.append(a_one)
        qkvs.append(qkv)
        out, kept, sent = attend_forward(token, qkv, seg_grid[r], w_first)
        token = rest_hop(tied(sent))
        if r == 0:
            token = far_hop(token)
        mixed.append(out)
        parts.append(group_scatter(kept, sent))
    far = far[-1] if ring else lax.psum_scatter(
        far[0].reshape(-1, own_width), "dp", scatter_dimension=0, tiled=True
    )
    far = far.astype(wide).reshape(4, rows * slots, own_width)
    far_tab = tables(far, bias_cols[8:12])

    attendeds, hiddens, inputs_two, down_grads = [], [], [], []

    def first_norm(r, token):
        attended, hidden, a_two = row_call(
            first_kernel,
            "first_norm",
            token,
            (tokens, *parts[r][0], bias_rows, far_tab[r]),
            [own_block(r), here, here, here, fixed_spec(bias_rows.shape), own_table(far_tab)],
            (here, here, here),
            (wides(*block), wides(*block), lows(*block)),
        )
        attendeds.append(attended)
        hiddens.append(hidden)
        inputs_two.append(group_gather(a_two))
        return tied(a_two)

    def down_back(r, token):
        grads = row_call(
            down_back_kernel,
            "down_back",
            token,
            (cotangent, cotangent, far_tab[r], far_tab[r], w_rest),
            moved_blocks(r) + moved_tables(far_tab) + [w_down_spec],
            (half_step, half_step),
            (lows(row_len, width), lows(row_len, width)),
            grid=2,
            flops=2 * row_len * width * width,
        )
        down_grads.append(grads)
        return tied(grads[1])

    token = first_norm(0, token)
    token = tied(inputs_two[0][0], *[part[1] for part in parts[1:]])
    w_rest = place_pieces(ring_places(own_depth, dp_count), rest_pieces) if ring else rest_pieces[0]
    w_down_spec = pl.BlockSpec((width, w_rest.shape[1] // 2), lambda i, p: (0, 1))
    w_up_spec = pl.BlockSpec((width, w_rest.shape[1] // 2), lambda i, p: (0, 0))
    for r in range(rows):
        token = down_back(r, token)
    for r in range(1, rows):
        token = first_norm(r, token)

    bias_up = bias_cols[2:6].reshape(1, -1)
    hidden_width = bias_up.shape[1]
    actives, inner_grads, up_parts, up_sums, down_parts = [], [], [], 0.0, []
    for r in range(rows):
        active, inner_grad, kept, sent, sums = row_call(
            up_kernel,
            "up_and_back",
            token,
            (*inputs_two[r], down_grads[r][1], bias_up, w_rest),
            [here] * 4 + [half_step, fixed_spec(bias_up.shape), w_up_spec],
            (
                pl.BlockSpec((half, hidden_width), lambda i, p: (i, 0)),
                pl.BlockSpec((half, hidden_width), lambda i, p: (i, 0)),
                half_fixed,
                half_fixed,
                pl.BlockSpec((1, 8, hidden_width), lambda i, p: (i, 0, 0)),
            ),
            (
                lows(row_len, hidden_width),
                lows(row_len, hidden_width),
                wides(half, width),
                lows(half, width),
                wides(2, 8, hidden_width),
            ),
            grid=2,
            scratch=[pltpu.VMEM(half_block, low)],
            flops=4 * row_len * width * hidden_width,
        )
        token = tied(sent, *[x for part in up_parts for x in part[0][2:]], *[part[1] for part in down_parts])
        actives.append(active)
        inner_grads.append(inner_grad)
        up_parts.append(group_scatter(kept, sent))
        up_sums = up_sums + jnp.sum(sums, axis=(0, 1))
        kept, sent = row_call(
            down_kernel,
            "down",
            token,
            (active, w_rest),
            [pl.BlockSpec((half, hidden_width), lambda i, p: (i, 0)), w_down_spec],
            (half_fixed, half_fixed),
            (wides(half, width), lows(half, width)),
            grid=2,
            flops=2 * row_len * width * hidden_width,
        )
        token = tied(sent, up_parts[-1][1], *[part[0][2] for part in down_parts])
        down_parts.append(group_scatter(kept, sent))

    grad_hiddens, grad_attendeds, second_sums = [], [], []

    def second_norm(r, token):
        grad_hidden, grad_attended, sums = row_call(
            second_kernel,
            "second_norm",
            token,
            (cotangent, *up_parts[r][0], hiddens[r], attendeds[r], far_tab[r]),
            [own_block(r)] + [here] * 5 + [own_table(far_tab)],
            (here, here, fixed_spec((16, width))),
            (wides(*block), lows(*block), wides(16, width)),
        )
        grad_hiddens.append(grad_hidden)
        grad_attendeds.append(grad_attended)
        second_sums.append(sums)
        return tied(grad_attended)

    token = second_norm(0, token)
    rest_grad = weight_grad(
        token,
        [
            [(inputs_two[r], inner_grads[r]) for r in range(rows)],
            [([down_grads[r][0]], actives[r]) for r in range(rows)],
        ],
        "grad_rest",
    )
    rest_ring = RingSum(rest_grad, dp_count) if ring else None
    token = tied(rest_grad, down_parts[-1][1])
    grad_attendeds[0] = group_gather(grad_attendeds[0], token)
    for r in range(1, rows):
        token = second_norm(r, token)
        grad_attendeds[r] = group_gather(grad_attendeds[r])

    out_pieces, out_sums = [], []

    def out_row(r, token):
        out_own, sums = row_call(
            out_kernel,
            "out_tokens",
            token,
            (cotangent, *down_parts[r][0], hiddens[r], bias_rows, far_tab[r]),
            [own_block(r)] + [here] * 4 + [fixed_spec(bias_rows.shape), own_table(far_tab)],
            (here, fixed_spec((8, width))),
            (lows(*block), wides(8, width)),
        )
        out_pieces.extend(group_gather(out_own))
        out_sums.append(sums)
        return tied(out_own)

    qkv_grads, one_parts, time_sums = [], [], []
    for r in range(rows):
        qkv_grad, kept, sent, sums = attend_backward(
            token, qkvs[r], grad_attendeds[r], seg_grid[r], w_first
        )
        token = tied(sent)
        if ring:
            token = rest_ring.hop(token)
        qkv_grads.append(qkv_grad)
        one_parts.append(group_scatter(kept, sent))
        time_sums.append(sums)
        if r == 0:
            for n in range(rows):
                token = out_row(n, token)
            token = tied(token, one_parts[0][1])

    def exchange(values, between):
        values = values.astype(low)

        def part(held, which, columns):
            return lax.dynamic_slice_in_dim(held, which * columns, columns, 1)

        other = lax.ppermute(part(values, 1 - chip, 2 * own_width), "mp", CHIP_SWAP)
        values = jnp.concatenate([part(values, chip, 2 * own_width), other], 0)
        values = lax.optimization_barrier((values, between))[0]
        other = lax.ppermute(part(values, 1 - core, own_width), "mp", CORE_SWAP)
        return jnp.concatenate([part(values, core, own_width), other], 0)

    by_place = jnp.stack(
        [
            lax.dynamic_index_in_dim(
                onehot.reshape(rows, 4, own_units, slots), jnp.bitwise_xor(place, j), 1, keepdims=False
            )
            for j in range(4)
        ],
        0,
    )

    def slot_matrix(fields, spare, kept_rows):
        same_row = jnp.eye(rows, dtype=bool)
        same_field = jnp.eye(fields, dtype=bool)
        full = (
            by_place.transpose(3, 0, 1, 2)[None, None, :, :, :, None, :]
            & same_row[None, :, None, None, :, None, None]
            & same_field[:, None, None, None, None, :, None]
        )
        full = full.reshape(fields * rows * slots, 4, rows * fields * own_units)
        full = jnp.pad(full, ((0, kept_rows), (0, 0), (0, spare)))
        if spare:
            extra = jnp.arange(spare)
            full = full.at[fields * rows * slots + extra, :, rows * fields * own_units + extra].set(True)
        return full.reshape(full.shape[0], -1).astype(low)

    far_rows = []
    for r in range(rows):
        far_rows += [second_sums[r][:12], out_sums[r][:4]]
    bias_part = [
        sum(second_sums[r][12:13] for r in range(rows)),
        sum(out_sums[r][4:5] for r in range(rows)),
    ]
    far_swapped = exchange(jnp.concatenate(far_rows + bias_part, 0), token)

    first_grad = weight_grad(
        token,
        [
            [([inputs_one[r]], qkv_grads[r]) for r in range(rows)],
            [(grad_attendeds[r], mixed[r]) for r in range(rows)],
        ],
        "grad_first",
    )
    ring_sum = RingSum(first_grad, dp_count) if ring else None
    token = tied(first_grad, one_parts[-1][1])
    after_first = token

    input_pieces, third_sums = [], []

    def third_norm(r, token):
        input_own, sums = row_call(
            third_kernel,
            "third_norm",
            token,
            (tokens, *one_parts[r][0], grad_hiddens[r], near_tab[r]),
            [own_block(r)] + [here] * 4 + [own_table(near_tab)],
            (here, fixed_spec((8, width))),
            (lows(*block), wides(8, width)),
        )
        input_pieces.append(group_gather(input_own))
        third_sums.append(sums)
        return tied(input_own)

    def ring_hop(token):
        return ring_sum.hop(token) if ring else token

    for r in range(rows - 1):
        token = third_norm(r, token)
    if ring:
        token = rest_ring.hop(token)
    after_third = token
    at = jnp.stack(
        [(r * 4 + jnp.bitwise_xor(place, j)) * quarter for r in range(rows) for j in range(4)]
    ).astype(jnp.int32)
    at = lax.optimization_barrier((at, token))[0]
    out_tokens = place_pieces(at, out_pieces)
    token = ring_hop(tied(out_tokens))
    after_place = token
    token = third_norm(rows - 1, token)

    far_slots = dot_as(slot_matrix(4, 2, 16), far_swapped, DOT_NN)
    far_slots = lax.dynamic_update_slice(
        far_slots, up_sums.reshape(4, own_width), (4 * slot_count + 2, 0)
    ).astype(low)
    far_all = doubling_gather(far_slots, dp_count, (after_first, after_third, after_place))
    far_all = far_all.reshape(dp_count, -1, own_width)
    far_sum = jnp.sum(far_all.astype(wide), axis=0)
    far_biases = jnp.sum(far_sum[: 4 * slot_count].reshape(4, slot_count, own_width), axis=1)
    bias_up_sum = far_sum[4 * slot_count + 2 : 4 * slot_count + 6]
    bias_rows_own = group_gather(far_sum[4 * slot_count : 4 * slot_count + 2].astype(low))
    bias_rows_own = [bias_rows_own[0], bias_rows_own[2], bias_rows_own[1], bias_rows_own[3]]
    bias_rows_sum = jnp.concatenate(in_group_order(bias_rows_own, mp_place), 1).astype(wide)

    def columns_of(ref, at):
        return column(ref[...], at, own_width).astype(wide)

    def map_grad(left, right, field):
        right = right[:, field * slot_count : (field + 1) * slot_count, :]
        return dot_as(left[...], right.reshape(-1, own_width), DOT_TN)

    cols_state = (weight_cols, first_cols, second_cols, ema_cols)
    rows_state = [x.transpose(0, 2, 1) for x in (weight_rows, first_rows, second_rows, ema_rows)]

    if ring:
        rest_sum = rest_ring.total()
    else:
        rest_sum = lax.psum_scatter(rest_grad, "dp", scatter_dimension=0, tiled=True)

    near_rows = jnp.concatenate(third_sums, 0)
    cols_new = adam_slabs(
        token,
        [(0, i) for i in (5, 6, 7, 8)],
        (rest_sum,),
        lambda n, refs: columns_of(refs[0], n),
        [cols_state],
        [None],
        "adam_up",
    )
    token = ring_hop(tied(cols_new[0]))
    near_swapped = exchange(near_rows, token)
    rows_new = adam_slabs(
        token,
        [(0, i) for i in (1, 2, 3, 4)],
        (rest_sum,),
        lambda n, refs: columns_of(refs[0], 4 + n),
        [rows_state],
        [None],
        "adam_down",
    )
    token = ring_hop(tied(rows_new[0]))
    after_down = token
    cols_new = adam_slabs(
        token,
        [(0, i) for i in (11, 12, 13, 14)],
        (ada_low, far_all),
        lambda n, refs: map_grad(refs[0], refs[1], n),
        [cols_state],
        [cols_new],
        "adam_far",
    )
    token = tied(cols_new[0])
    after_far = token
    input_grads = ()
    for r in range(rows):
        input_grads = (widen_row(token, input_pieces[r], r, rows, input_grads),)
        token = tied(input_grads[0])
        if r == 0:
            after_widen = token

    unit_sums = jnp.concatenate(time_sums, 0)
    moved = by_place.transpose(1, 0, 2, 3).reshape(rows, units, slots)
    moved = moved[:, :, None, :] & jnp.eye(rows, dtype=bool)[:, None, :, None]
    moved = moved.reshape(rows * units, slot_count).astype(wide)
    time_slots = lax.dot_general(moved, unit_sums, DOT_TN, precision=highest)
    near_slots = jnp.concatenate(
        [
            dot_as(slot_matrix(2, 0, 0), near_swapped, DOT_NN),
            time_slots[:, :own_width],
            time_slots[:, 2 * own_width :],
        ],
        0,
    ).astype(low)
    near_all = doubling_gather(near_slots, dp_count, (after_down, after_far, after_widen))
    near_all = near_all.reshape(dp_count, -1, own_width)
    near_sum = jnp.sum(near_all.astype(wide).reshape(dp_count, 4, slot_count, own_width), axis=(0, 2))
    bias_cols_sum = jnp.concatenate([near_sum[2:4], bias_up_sum, near_sum[:2], far_biases], 0)
    if ring:
        first_sum = ring_sum.total()
    else:
        first_sum = lax.psum_scatter(first_grad, "dp", scatter_dimension=0, tiled=True)

    def late_grad(n, refs):
        ada, time, near, first = refs
        if n < 4:
            return map_grad(ada if n < 2 else time, near, n)
        return columns_of(first, n - 4)

    new = adam_slabs(
        token,
        [(0, i) for i in (9, 10, 3, 4, 0, 1, 2)] + [(1, 0)],
        (ada_low, time_low, near_all, first_sum),
        late_grad,
        [cols_state, rows_state],
        [cols_new, rows_new],
        "adam_late",
    )
    cols_new, rows_new = new[:4], [x.transpose(0, 2, 1) for x in new[4:]]
    bias_cols_new = adam_step(
        bias_cols, bias_cols_sum, first_bias_cols, second_bias_cols, ema_bias_cols, rate_vector
    )
    bias_rows_new = adam_step(
        bias_rows, bias_rows_sum, first_bias_rows, second_bias_rows, ema_bias_rows, rate_vector
    )
    return (out_tokens, input_grads[0], *cols_new, *rows_new, *bias_cols_new, *bias_rows_new)


def solution(mesh):
    cols, rows, bias = P(None, "dp", "mp"), P(None, "mp", "dp"), P(None, "mp")
    state = (cols, rows, bias, P())
    placed = (P("dp", None), P("dp"), P("dp", None), P("dp", None)) + state * 4
    given = (P("dp", None), P("dp", None)) + (cols,) * 4 + (rows,) * 4 + (bias,) * 4 + (P(),) * 4
    return jax.shard_map(
        per_device, mesh=mesh, in_specs=placed, out_specs=given, check_vma=False
    )
```

time: 663 us -> 570 us (0.86)
  waiting for transfers between devices: 148 us -> 83.9 us
  Pallas kernels: 208 us -> 269 us
  local copies, waits for them, and re-layouts: 101 us -> 54.5 us
  between operations: 42.5 us -> 16.8 us
  starting transfers between devices: 103 us -> 86 us
    pallas_call x17 -> x30, Pallas kernels: 98.8 us -> 256 us  [row_call(): pl.pallas_call(body, grid_spec=pltpu.PrefetchScalarGridSpec(num_scalar_pr...]
    pallas_call x6 -> x0, Pallas kernels: 95.7 us -> none  [the longest x2 43.7 us: attend_backward(): pl.pallas_call(body, out_shape=(shape_of((row_len, 3 * width), low), shap...]
    unnamed x318 -> x188, local copies, waits for them, and re-layouts: 55.5 us -> 12.7 us
    ppermute x75 -> x57, waiting for transfers between devices: 118 us -> 80.2 us  [the longest x6 28.3 us: doubling_gather(): got = lax.ppermute(known, 'dp', [(i, i ^ step) for i in range(count)])]
    ppermute x11, waiting for transfers between devices: 29.7 us -> 3.69 us  [group_gather(): chip = lax.ppermute(own, 'mp', CHIP_SWAP)]
    ppermute x75 -> x57, starting transfers between devices: 87.7 us -> 69.5 us  [the longest x2 12.8 us: rest_hop(): rest_pieces.append(lax.ppermute(behind, 'dp', backward))]
    add x4 -> x2, other arithmetic: 14.8 us -> 1.31 us  [adam_step(): ema_new = ema_keep * ema_old + (1.0 - ema_keep) * weight_new]
    reshape x18 -> x1, local copies, waits for them, and re-layouts: 11.9 us -> 1.56 us  [slot_matrix(): return full.reshape(full.shape[0], -1).astype(low)]
  transfers between devices with their start and end apart: 117 -> 98, of which waited for: 39 -> 22; matrix products, arithmetic and copies ran while one was open for 11% -> 15% of each run, Pallas kernels for 29% -> 47%
where the time goes in v3:
time: 570 us; the launch traced here: 559 us
  Pallas kernels  269 us (47%)
  starting transfers between devices  86 us (15%)
  waiting for transfers between devices  83.9 us (15%)
  local copies, waits for them, and re-layouts  54.5 us (10%)
  other arithmetic  38.6 us (7%)
  between operations  16.8 us (3%)
  matrix products  10.5 us (2%)
    pallas_call x30, Pallas kernels, row_call(): pl.pallas_call(body, grid_spec=pltpu.PrefetchScalarGridSpec(num_scalar_pr...  256 us
    ppermute x6, waiting for transfers between devices, doubling_gather(): got = lax.ppermute(known, 'dp', [(i, i ^ step) for i in range(count)])  28.3 us
    ppermute x6, waiting for transfers between devices, halving_hop(): got = lax.ppermute(sent, 'dp', [(i, i ^ step) for i in range(count)])  18.4 us
    pallas_call x3, Pallas kernels, place_pieces(): pl.pallas_call(place_kernel, out_shape=jax.ShapeDtypeStruct(whole, pieces...  13.3 us
    ppermute x8, waiting for transfers between devices, group_scatter(): return ((kept, got, lax.ppermute(passed, 'mp', CHIP_SWAP)), passed)  13.1 us
    ppermute x2, starting transfers between devices, rest_hop(): rest_pieces.append(lax.ppermute(behind, 'dp', backward))  12.8 us
    unnamed x188, local copies, waits for them, and re-layouts  12.7 us
    ppermute x11, starting transfers between devices, group_gather(): chip = lax.ppermute(own, 'mp', CHIP_SWAP)  12.4 us
  transfers between devices with their start and end apart: 98, of which 22 were waited for; matrix products, arithmetic and copies ran while one was open for 15% of the time, Pallas kernels for 47%

profile of v3, /device:TPU:0, one launch (start us, length us, event | category | flops | bytes accessed | tf_op | source)
XLA Modules:
  0.0 559.3 jit_solution(11492991198293359558)
XLA Ops:
  57.6 4.4 collective-permute-done.7
  74.8 5.1 collective-permute-done.19
  103.3 7.7 %open_row.2 = (bf16[1024,1152]{1,0:T(8,128)(2,1)}, bf16[1024,864]{1,0:T(8,128)(2,1)}) custom-call(s32[1]{0:T(128)} %bitcast.8.place_ref.refs_0_, bf16[2048,1152]{1,0:T(8,128)(2,1)} %x_ref.7, bf16[2048,1152]{1,0:T(8,128)(2,1)} %x_ref.7, f32[4,4,2304]{2,1,0:T(4,128)} %squeeze.191.tab0_ref.tab1_ref.tab_ref, f32[4,4,2304]{2,1,0:T(4,128)} %squeeze.191.tab0_ref.tab1_ref.tab_ref, ...), custom_call_target="tpu_custom_call" | custom-call | flops 20384317440 | bytes 166256640 | tf_op jit(solution)/shard_map/open_row/pallas_call | solution.py:553
  111.7 12.8 %attend_forward.2 = (bf16[1024,288]{1,0:T(8,128)(2,1)}, f32[512,1152]{1,0:T(8,128)}, bf16[512,1152]{1,0:T(8,128)(2,1)}) custom-call(s32[1]{0:T(128)} %bitcast.8.place_ref.refs_0_, bf16[1024,864]{1,0:T(8,128)(2,1)} %get-tuple-element.188.refs_1_, s32[1024,1]{1,0:T(8,128)} %copy.164.refs_2_.refs_6_, s32[1,1024]{1,0:T(1,128)} %bitcast.265, ...), custom_call_target="tpu_custom_call" | custom-call | flops 14344519680 | bytes 85606400 | tf_op jit(solution)/shard_map/attend_forward/pallas_call | solution.py:553
  126.1 5.1 collective-permute-done.24
  135.6 11.2 %collective-permute-start.26 = (bf16[144,2304]{1,0:T(8,128)(2,1)}, bf16[144,2304]{1,0:T(8,128)(2,1)S(1)}, u32[]{:S(2)}, u32[]{:S(2)}) collective-permute-start(bf16[144,2304]{1,0:T(8,128)(2,1)} %collective-permute-done.21.refs_4_), channel_id=1, source_target_pairs={{8,0},{16,8},{24,16},{28,24},{20,28},{12,20},{4,12},{0,4},{9,1},{1... | collective-permute-start | bytes 1990664 | tf_op jit(solution)/shard_map/ppermute | solution.py:927
  147.3 7.7 %open_row.3 = (bf16[1024,1152]{1,0:T(8,128)(2,1)}, bf16[1024,864]{1,0:T(8,128)(2,1)}) custom-call(s32[1]{0:T(128)} %bitcast.8.place_ref.refs_0_, bf16[2048,1152]{1,0:T(8,128)(2,1)} %x_ref.7, bf16[2048,1152]{1,0:T(8,128)(2,1)} %x_ref.7, f32[4,4,2304]{2,1,0:T(4,128)} %squeeze.198.tab0_ref.tab1_ref.tab_ref, f32[4,4,2304]{2,1,0:T(4,128)} %squeeze.198.tab0_ref.tab1_ref.tab_ref, ...), custom_call_target="tpu_custom_call" | custom-call | flops 20384317440 | bytes 166256640 | tf_op jit(solution)/shard_map/open_row/pallas_call | solution.py:553
  160.8 12.8 %attend_forward.3 = (bf16[1024,288]{1,0:T(8,128)(2,1)}, f32[512,1152]{1,0:T(8,128)}, bf16[512,1152]{1,0:T(8,128)(2,1)}) custom-call(s32[1]{0:T(128)} %bitcast.8.place_ref.refs_0_, bf16[1024,864]{1,0:T(8,128)(2,1)} %get-tuple-element.199.refs_1_, s32[1024,1]{1,0:T(8,128)} %copy.165.refs_2_.refs_6_, s32[1,1024]{1,0:T(1,128)} %bitcast.261, ...), custom_call_target="tpu_custom_call" | custom-call | flops 14344519680 | bytes 85606400 | tf_op jit(solution)/shard_map/attend_forward/pallas_call | solution.py:553
  185.7 6.2 %collective-permute-done.32.refs_7_ = bf16[64,2304]{1,0:T(8,128)(2,1)S(1)} collective-permute-done((bf16[64,2304]{1,0:T(8,128)(2,1)S(1)}, bf16[64,2304]{1,0:T(8,128)(2,1)S(1)}, u32[]{:S(2)}, u32[]{:S(2)}) %collective-permute-start.32) | collective-permute-done | bytes 294944 | tf_op jit(solution)/shard_map/ppermute | solution.py:70
  193.3 5.2 place_pieces.4.w_ref
  199.9 7.5 %down_back.2 = (bf16[1024,1152]{1,0:T(8,128)(2,1)}, bf16[1024,1152]{1,0:T(8,128)(2,1)}) custom-call(s32[1]{0:T(128)} %bitcast.8.place_ref.refs_0_, bf16[2048,1152]{1,0:T(8,128)(2,1)} %cot_ref.7, bf16[2048,1152]{1,0:T(8,128)(2,1)} %cot_ref.7, f32[4,4,4608]{2,1,0:T(4,128)} %squeeze.201.tab_ref.tab0_ref.tab1_ref, ...), custom_call_target="tpu_custom_call" | custom-call | flops 27179089920 | bytes 200540160 | tf_op jit(solution)/shard_map/down_back/pallas_call | solution.py:553
  207.4 7.2 %down_back.3 = (bf16[1024,1152]{1,0:T(8,128)(2,1)}, bf16[1024,1152]{1,0:T(8,128)(2,1)}) custom-call(s32[1]{0:T(128)} %bitcast.8.place_ref.refs_0_, bf16[2048,1152]{1,0:T(8,128)(2,1)} %cot_ref.7, bf16[2048,1152]{1,0:T(8,128)(2,1)} %cot_ref.7, f32[4,4,4608]{2,1,0:T(4,128)} %squeeze.203.tab0_ref.tab1_ref.tab_ref, ...), custom_call_target="tpu_custom_call" | custom-call | flops 27179089920 | bytes 200540160 | tf_op jit(solution)/shard_map/down_back/pallas_call | solution.py:553
  221.5 15.5 %up_and_back.2 = (bf16[1024,1152]{1,0:T(8,128)(2,1)}, bf16[1024,1152]{1,0:T(8,128)(2,1)}, f32[512,1152]{1,0:T(8,128)}, bf16[512,1152]{1,0:T(8,128)(2,1)}, f32[2,8,1152]{2,1,0:T(8,128)}) custom-call(s32[1]{0:T(128)} %bitcast.8.place_ref.refs_0_, bf16[256,1152]{1,0:T(8,128)(2,1)} %get-tuple-element.209.a0_ref.refs_0_, ...), custom_call_target="tpu_custom_call" | custom-call | flops 54358179840 | bytes 183628800 | tf_op jit(solution)/shard_map/up_and_back/pallas_call | solution.py:553
  237.1 7.9 %down.2 = (f32[512,1152]{1,0:T(8,128)}, bf16[512,1152]{1,0:T(8,128)(2,1)}) custom-call(s32[1]{0:T(128)} %bitcast.8.place_ref.refs_0_, bf16[1024,1152]{1,0:T(8,128)(2,1)} %get-tuple-element.222.m_ref.refs_11_, bf16[1152,2304]{1,0:T(8,128)(2,1)} %place_pieces.4.w_ref), custom_call_target="tpu_custom_call" | custom-call | flops 27179089920 | bytes 112066560 | tf_op jit(solution)/shard_map/down/pallas_call | solution.py:553
  260.8 15.5 %up_and_back.3 = (bf16[1024,1152]{1,0:T(8,128)(2,1)}, bf16[1024,1152]{1,0:T(8,128)(2,1)}, f32[512,1152]{1,0:T(8,128)}, bf16[512,1152]{1,0:T(8,128)(2,1)}, f32[2,8,1152]{2,1,0:T(8,128)}) custom-call(s32[1]{0:T(128)} %bitcast.8.place_ref.refs_0_, bf16[256,1152]{1,0:T(8,128)(2,1)} %get-tuple-element.218.a0_ref.refs_5_, ...), custom_call_target="tpu_custom_call" | custom-call | flops 54358179840 | bytes 183628800 | tf_op jit(solution)/shard_map/up_and_back/pallas_call | solution.py:553
  277.9 8.0 %down.3 = (f32[512,1152]{1,0:T(8,128)}, bf16[512,1152]{1,0:T(8,128)(2,1)}) custom-call(s32[1]{0:T(128)} %bitcast.8.place_ref.refs_0_, bf16[1024,1152]{1,0:T(8,128)(2,1)} %get-tuple-element.229.m_ref.refs_13_, bf16[1152,2304]{1,0:T(8,128)(2,1)} %place_pieces.4.w_ref), custom_call_target="tpu_custom_call" | custom-call | flops 27179089920 | bytes 112066560 | tf_op jit(solution)/shard_map/down/pallas_call | solution.py:553
  287.5 5.3 second_norm.2
  295.0 19.3 %grad_rest.1 = bf16[1152,2304]{1,0:T(8,128)(2,1)} custom-call(s32[1]{0:T(128)} %bitcast.8.place_ref.refs_0_, bf16[256,1152]{1,0:T(8,128)(2,1)} %get-tuple-element.209.a0_ref.refs_0_, bf16[256,1152]{1,0:T(8,128)(2,1)} %collective-permute-done.35.a1_ref.refs_1_, bf16[256,1152]{1,0:T(8,128)(2,1)} %copy-done.88, ...), custom_call_target="tpu_custom_call" | custom-call | flops 108716359680 | bytes 241827840 | tf_op jit(solution)/shard_map/grad_rest/pallas_call | solution.py:553
  322.3 5.1 second_norm.3
  330.5 21.2 %attend_backward.2 = (bf16[1024,864]{1,0:T(8,128)(2,1)}, f32[512,1152]{1,0:T(8,128)}, bf16[512,1152]{1,0:T(8,128)(2,1)}, f32[16,864]{1,0:T(8,128)}) custom-call(s32[1]{0:T(128)} %bitcast.8.place_ref.refs_0_, bf16[1024,864]{1,0:T(8,128)(2,1)} %get-tuple-element.188.refs_1_, bf16[256,1152]{1,0:T(8,128)(2,1)} %get-tuple-element.235.refs_2_.refs_4_, ...), custom_call_target="tpu_custom_call" | custom-call | flops 46053457920 | bytes 121548800 | tf_op jit(solution)/shard_map/attend_backward/pallas_call | solution.py:553
  371.3 21.1 %attend_backward.3 = (bf16[1024,864]{1,0:T(8,128)(2,1)}, f32[512,1152]{1,0:T(8,128)}, bf16[512,1152]{1,0:T(8,128)(2,1)}, f32[16,864]{1,0:T(8,128)}) custom-call(s32[1]{0:T(128)} %bitcast.8.place_ref.refs_0_, bf16[1024,864]{1,0:T(8,128)(2,1)} %get-tuple-element.199.refs_1_, bf16[256,1152]{1,0:T(8,128)(2,1)} %get-tuple-element.245.refs_2_.refs_9_, ...), custom_call_target="tpu_custom_call" | custom-call | flops 46053457920 | bytes 121548800 | tf_op jit(solution)/shard_map/attend_backward/pallas_call | solution.py:553
  393.2 13.1 %grad_first.1 = bf16[1152,1152]{1,0:T(8,128)(2,1)} custom-call(s32[1]{0:T(128)} %bitcast.8.place_ref.refs_0_, bf16[1024,1152]{1,0:T(8,128)(2,1)} %get-tuple-element.257.refs_0_, bf16[1024,864]{1,0:T(8,128)(2,1)} %get-tuple-element.258.refs_1_, bf16[1024,1152]{1,0:T(8,128)(2,1)} %get-tuple-element.259.refs_2_, bf16[1024,864]{1,0:T(8,128)(2,1)} %get-tuple-element.260.refs_3_, ...), custom_call_target="tpu_custom_call" | custom-call | flops 54358179840 | bytes 168099840 | tf_op jit(solution)/shard_map/grad_first/pallas_call | solution.py:553
  418.4 9.3 %collective-permute-done.60.passed_ref = bf16[256,1152]{1,0:T(8,128)(2,1)} collective-permute-done((bf16[256,1152]{1,0:T(8,128)(2,1)}, bf16[256,1152]{1,0:T(8,128)(2,1)}, u32[]{:S(2)}, u32[]{:S(2)}) %collective-permute-start.60) | collective-permute-done | bytes 589856 | tf_op jit(solution)/shard_map/ppermute | solution.py:188
  434.0 4.3 collective-permute-done.79
  443.9 4.8 place_pieces.5
  456.7 19.4 %collective-permute-done.81 = bf16[4,144,288]{2,1,0:T(8,128)(2,1)S(1)} collective-permute-done((bf16[4,144,288]{2,1,0:T(8,128)(2,1)S(1)}, bf16[4,144,288]{2,1,0:T(8,128)(2,1)S(1)}, u32[]{:S(2)}, u32[]{:S(2)}) %collective-permute-start.81) | collective-permute-done | bytes 331808 | tf_op jit(solution)/shard_map/ppermute | solution.py:172
  494.1 6.6 %adam_up.1 = (f32[15,144,288]{2,1,0:T(8,128)}, f32[15,144,288]{2,1,0:T(8,128)}, f32[15,144,288]{2,1,0:T(8,128)}, f32[15,144,288]{2,1,0:T(8,128)}) custom-call(s32[4]{0:T(128)} %constant.425.clone.ids_ref, f32[144,2304]{1,0:T(8,128)} %convert_add_fusion.refs_0_, f32[15,144,288]{2,1,0:T(8,128)} %refs_4_.5, f32[15,144,288]{2,1,0:T(8,128)} %refs_5_.3, ...), custom_call_target="tpu_custom_call" | custom-call | bytes 212336640 | tf_op jit(solution)/shard_map/adam_up/pallas_call | solution.py:553
  505.2 6.7 %adam_down.1 = (f32[5,144,288]{2,1,0:T(8,128)}, f32[5,144,288]{2,1,0:T(8,128)}, f32[5,144,288]{2,1,0:T(8,128)}, f32[5,144,288]{2,1,0:T(8,128)}) custom-call(s32[4]{0:T(128)} %constant.426.clone.ids_ref, f32[144,2304]{1,0:T(8,128)} %convert_add_fusion.refs_0_, f32[5,144,288]{2,1,0:T(8,128)} %bitcast.225, f32[5,144,288]{2,1,0:T(8,128)} %bitcast.227, ...), custom_call_target="tpu_custom_call" | custom-call | bytes 79626240 | tf_op jit(solution)/shard_map/adam_down/pallas_call | solution.py:553
  514.4 6.7 %adam_far.1 = (f32[15,144,288]{2,1,0:T(8,128)}, f32[15,144,288]{2,1,0:T(8,128)}, f32[15,144,288]{2,1,0:T(8,128)}, f32[15,144,288]{2,1,0:T(8,128)}) custom-call(s32[4]{0:T(128)} %constant.427.clone.ids_ref, bf16[256,144]{1,0:T(8,128)(2,1)} %copy-done.1, ...), custom_call_target="tpu_custom_call", output_to_operand_aliasing={{0}: (7, {}), {1}: (8, {}), {2}: (9, {}), {3}: (10, {})} | custom-call | bytes 305971200 | tf_op jit(solution)/shard_map/adam_far/pallas_call | solution.py:553
  525.9 4.2 widen_row.2.refs_4_
  542.4 11.5 %adam_late.1 = (f32[15,144,288]{2,1,0:T(8,128)}, f32[15,144,288]{2,1,0:T(8,128)}, f32[15,144,288]{2,1,0:T(8,128)}, f32[15,144,288]{2,1,0:T(8,128)}, f32[5,144,28...) custom-call(s32[16]{0:T(128)} %constant.428.clone.ids_ref, ...), custom_call_target="tpu_custom_call", output_to_operand_aliasing={{0}: (13, {}), {1}: (14, {}), {2}: (15, {}), {3}: (16, {}),... | custom-call | bytes 412139520 | tf_op jit(solution)/shard_map/adam_late/pallas_call | solution.py:553
  554.7 4.2 widen_row.3
  (570 shorter events, 239.9 us)
Async XLA Ops:
  8.1 27.8 %collective-permute-start.3 = (bf16[144,1152]{1,0:T(8,128)(2,1)S(1)}, bf16[144,1152]{1,0:T(8,128)(2,1)}, u32[]{:S(2)}, u32[]{:S(2)}) collective-permute-start(bf16[144,1152]{1,0:T(8,128)(2,1)S(1)} %concatenate.64.refs_0_), channel_id=1, source_target_pairs={{8,0},{16,8},{24,16},{28,24},{20,28},{12,20},{4,12},{0,4},{9,1},{1... | collective-permute-start | bytes 995336 | tf_op jit(solution)/shard_map/ppermute | solution.py:64
  11.1 24.8 %collective-permute-start.2 = (bf16[144,1152]{1,0:T(8,128)(2,1)S(1)}, bf16[144,1152]{1,0:T(8,128)(2,1)}, u32[]{:S(2)}, u32[]{:S(2)}) collective-permute-start(bf16[144,1152]{1,0:T(8,128)(2,1)S(1)} %concatenate.64.refs_0_), channel_id=1, source_target_pairs={{0,8},{8,16},{16,24},{24,28},{28,20},{20,12},{12,4},{4,0},{1,9},{9... | collective-permute-start | bytes 995336 | tf_op jit(solution)/shard_map/ppermute | solution.py:64
  100.9 23.6 %collective-permute-start.20 = (bf16[144,2304]{1,0:T(8,128)(2,1)}, bf16[144,2304]{1,0:T(8,128)(2,1)}, u32[]{:S(2)}, u32[]{:S(2)}) collective-permute-start(bf16[144,2304]{1,0:T(8,128)(2,1)} %collective-permute-done.11.refs_1_), channel_id=1, source_target_pairs={{0,8},{8,16},{16,24},{24,28},{28,20},{20,12},{12,4},{4,0},{1,9},{9... | collective-permute-start | bytes 1990664 | tf_op jit(solution)/shard_map/ppermute | solution.py:926
  101.7 22.8 %collective-permute-start.21 = (bf16[144,2304]{1,0:T(8,128)(2,1)}, bf16[144,2304]{1,0:T(8,128)(2,1)}, u32[]{:S(2)}, u32[]{:S(2)}) collective-permute-start(bf16[144,2304]{1,0:T(8,128)(2,1)} %collective-permute-done.12.refs_2_), channel_id=1, source_target_pairs={{8,0},{16,8},{24,16},{28,24},{20,28},{12,20},{4,12},{0,4},{9,1},{1... | collective-permute-start | bytes 1990664 | tf_op jit(solution)/shard_map/ppermute | solution.py:927
  135.2 24.0 %collective-permute-start.23 = (bf16[512,1152]{1,0:T(8,128)(2,1)}, bf16[512,1152]{1,0:T(8,128)(2,1)S(1)}, u32[]{:S(2)}, u32[]{:S(2)}) collective-permute-start(bf16[512,1152]{1,0:T(8,128)(2,1)} %get-tuple-element.192), channel_id=1, source_target_pairs={{0,1},{1,0},{2,3},{3,2},{4,5},{5,4},{6,7},{7,6},{8,9},{9,8},{10,11... | collective-permute-start | bytes 3538952 | tf_op jit(solution)/shard_map/ppermute | solution.py:186
  135.2 39.3 %collective-permute-start.25 = (bf16[144,2304]{1,0:T(8,128)(2,1)}, bf16[144,2304]{1,0:T(8,128)(2,1)S(1)}, u32[]{:S(2)}, u32[]{:S(2)}) collective-permute-start(bf16[144,2304]{1,0:T(8,128)(2,1)} %collective-permute-done.20.refs_3_), channel_id=1, source_target_pairs={{0,8},{8,16},{16,24},{24,28},{28,20},{20,12},{12,4},{4,0},{1,9},{9... | collective-permute-start | bytes 1990664 | tf_op jit(solution)/shard_map/ppermute | solution.py:926
  135.6 38.9 %collective-permute-start.26 = (bf16[144,2304]{1,0:T(8,128)(2,1)}, bf16[144,2304]{1,0:T(8,128)(2,1)S(1)}, u32[]{:S(2)}, u32[]{:S(2)}) collective-permute-start(bf16[144,2304]{1,0:T(8,128)(2,1)} %collective-permute-done.21.refs_4_), channel_id=1, source_target_pairs={{8,0},{16,8},{24,16},{28,24},{20,28},{12,20},{4,12},{0,4},{9,1},{1... | collective-permute-start | bytes 1990664 | tf_op jit(solution)/shard_map/ppermute | solution.py:927
  173.6 25.6 %collective-permute-start.31 = (bf16[512,1152]{1,0:T(8,128)(2,1)}, bf16[512,1152]{1,0:T(8,128)(2,1)S(1)}, u32[]{:S(2)}, u32[]{:S(2)}) collective-permute-start(bf16[512,1152]{1,0:T(8,128)(2,1)} %get-tuple-element.204), channel_id=1, source_target_pairs={{0,1},{1,0},{2,3},{3,2},{4,5},{5,4},{6,7},{7,6},{8,9},{9,8},{10,11... | collective-permute-start | bytes 3538952 | tf_op jit(solution)/shard_map/ppermute | solution.py:186
  219.2 34.8 %collective-permute-start.39 = (bf16[256,1152]{1,0:T(8,128)(2,1)}, bf16[256,1152]{1,0:T(8,128)(2,1)}, u32[]{:S(2)}, u32[]{:S(2)}) collective-permute-start(bf16[256,1152]{1,0:T(8,128)(2,1)} %get-tuple-element.218.a0_ref.refs_5_), channel_id=1, source_target_pairs={{0,2},{1,3},{2,0},{3,1},{4,6},{5,7},{6,4},{7,5},{8,10},{9,11},{10,... | collective-permute-start | bytes 1769480 | tf_op jit(solution)/shard_map/ppermute | solution.py:192
  258.5 29.0 %collective-permute-start.45 = (bf16[256,1152]{1,0:T(8,128)(2,1)}, bf16[256,1152]{1,0:T(8,128)(2,1)S(1)}, u32[]{:S(2)}, u32[]{:S(2)}) collective-permute-start(bf16[256,1152]{1,0:T(8,128)(2,1)} %add_convert_fusion.9), channel_id=1, source_target_pairs={{0,2},{1,3},{2,0},{3,1},{4,6},{5,7},{6,4},{7,5},{8,10},{9,11},{10,... | collective-permute-start | bytes 1769480 | tf_op jit(solution)/shard_map/ppermute | solution.py:188
  285.9 28.4 %collective-permute-start.46 = (bf16[512,1152]{1,0:T(8,128)(2,1)}, bf16[512,1152]{1,0:T(8,128)(2,1)S(1)}, u32[]{:S(2)}, u32[]{:S(2)}) collective-permute-start(bf16[512,1152]{1,0:T(8,128)(2,1)} %get-tuple-element.230), channel_id=1, source_target_pairs={{0,1},{1,0},{2,3},{3,2},{4,5},{5,4},{6,7},{7,6},{8,9},{9,8},{10,11... | collective-permute-start | bytes 3538952 | tf_op jit(solution)/shard_map/ppermute | solution.py:186
  292.9 36.3 %collective-permute-start.49 = (bf16[256,1152]{1,0:T(8,128)(2,1)}, bf16[256,1152]{1,0:T(8,128)(2,1)}, u32[]{:S(2)}, u32[]{:S(2)}) collective-permute-start(bf16[256,1152]{1,0:T(8,128)(2,1)} %get-tuple-element.235.refs_2_.refs_4_), channel_id=1, source_target_pairs={{0,1},{1,0},{2,3},{3,2},{4,5},{5,4},{6,7},{7,6},{8,9},{9,8},{10,11... | collective-permute-start | bytes 1769480 | tf_op jit(solution)/shard_map/ppermute | solution.py:195
  293.0 22.4 %collective-permute-start.48 = (bf16[256,1152]{1,0:T(8,128)(2,1)}, bf16[256,1152]{1,0:T(8,128)(2,1)}, u32[]{:S(2)}, u32[]{:S(2)}) collective-permute-start(bf16[256,1152]{1,0:T(8,128)(2,1)} %get-tuple-element.235.refs_2_.refs_4_), channel_id=1, source_target_pairs={{0,2},{1,3},{2,0},{3,1},{4,6},{5,7},{6,4},{7,5},{8,10},{9,11},{10,... | collective-permute-start | bytes 1769480 | tf_op jit(solution)/shard_map/ppermute | solution.py:192
  293.5 28.0 %collective-permute-start.47 = (bf16[256,1152]{1,0:T(8,128)(2,1)}, bf16[256,1152]{1,0:T(8,128)(2,1)S(1)}, u32[]{:S(2)}, u32[]{:S(2)}) collective-permute-start(bf16[256,1152]{1,0:T(8,128)(2,1)} %add_convert_fusion.8), channel_id=1, source_target_pairs={{0,2},{1,3},{2,0},{3,1},{4,6},{5,7},{6,4},{7,5},{8,10},{9,11},{10,... | collective-permute-start | bytes 1769480 | tf_op jit(solution)/shard_map/ppermute | solution.py:188
  316.8 34.9 %collective-permute-start.56 = (bf16[144,2304]{1,0:T(8,128)(2,1)S(1)}, bf16[144,2304]{1,0:T(8,128)(2,1)S(1)}, u32[]{:S(2)}, u32[]{:S(2)}) collective-permute-start(bf16[144,2304]{1,0:T(8,128)(2,1)S(1)} %get-tuple-element.348), channel_id=1, source_target_pairs={{8,0},{16,8},{24,16},{28,24},{20,28},{12,20},{4,12},{0,4},{9,1},{1... | collective-permute-start | bytes 1990664 | tf_op jit(solution)/shard_map/ppermute | solution.py:134
  318.6 33.4 %collective-permute-start.55 = (bf16[144,2304]{1,0:T(8,128)(2,1)S(1)}, bf16[144,2304]{1,0:T(8,128)(2,1)S(1)}, u32[]{:S(2)}, u32[]{:S(2)}) collective-permute-start(bf16[144,2304]{1,0:T(8,128)(2,1)S(1)} %get-tuple-element.349), channel_id=1, source_target_pairs={{0,8},{8,16},{16,24},{24,28},{28,20},{20,12},{12,4},{4,0},{1,9},{9... | collective-permute-start | bytes 1990664 | tf_op jit(solution)/shard_map/ppermute | solution.py:132
  321.5 34.0 %collective-permute-start.66 = (bf16[256,1152]{1,0:T(8,128)(2,1)}, bf16[256,1152]{1,0:T(8,128)(2,1)S(1)}, u32[]{:S(2)}, u32[]{:S(2)}) collective-permute-start(bf16[256,1152]{1,0:T(8,128)(2,1)} %add_convert_fusion.7), channel_id=1, source_target_pairs={{0,2},{1,3},{2,0},{3,1},{4,6},{5,7},{6,4},{7,5},{8,10},{9,11},{10,... | collective-permute-start | bytes 1769480 | tf_op jit(solution)/shard_map/ppermute | solution.py:188
  329.2 39.6 %collective-permute-start.53 = (bf16[256,1152]{1,0:T(8,128)(2,1)}, bf16[256,1152]{1,0:T(8,128)(2,1)}, u32[]{:S(2)}, u32[]{:S(2)}) collective-permute-start(bf16[256,1152]{1,0:T(8,128)(2,1)} %get-tuple-element.245.refs_2_.refs_9_), channel_id=1, source_target_pairs={{0,1},{1,0},{2,3},{3,2},{4,5},{5,4},{6,7},{7,6},{8,9},{9,8},{10,11... | collective-permute-start | bytes 1769480 | tf_op jit(solution)/shard_map/ppermute | solution.py:195
  329.3 36.1 %collective-permute-start.52 = (bf16[256,1152]{1,0:T(8,128)(2,1)}, bf16[256,1152]{1,0:T(8,128)(2,1)}, u32[]{:S(2)}, u32[]{:S(2)}) collective-permute-start(bf16[256,1152]{1,0:T(8,128)(2,1)} %get-tuple-element.245.refs_2_.refs_9_), channel_id=1, source_target_pairs={{0,2},{1,3},{2,0},{3,1},{4,6},{5,7},{6,4},{7,5},{8,10},{9,11},{10,... | collective-permute-start | bytes 1769480 | tf_op jit(solution)/shard_map/ppermute | solution.py:192
  363.6 76.7 %collective-permute-start.68 = (bf16[256,1152]{1,0:T(8,128)(2,1)}, bf16[256,1152]{1,0:T(8,128)(2,1)}, u32[]{:S(2)}, u32[]{:S(2)}) collective-permute-start(bf16[256,1152]{1,0:T(8,128)(2,1)} %get-tuple-element.275.refs_4_), channel_id=1, source_target_pairs={{0,1},{1,0},{2,3},{3,2},{4,5},{5,4},{6,7},{7,6},{8,9},{9,8},{10,11... | collective-permute-start | bytes 1769480 | tf_op jit(solution)/shard_map/ppermute | solution.py:195
  365.4 50.0 %collective-permute-start.67 = (bf16[256,1152]{1,0:T(8,128)(2,1)}, bf16[256,1152]{1,0:T(8,128)(2,1)}, u32[]{:S(2)}, u32[]{:S(2)}) collective-permute-start(bf16[256,1152]{1,0:T(8,128)(2,1)} %get-tuple-element.275.refs_4_), channel_id=1, source_target_pairs={{0,2},{1,3},{2,0},{3,1},{4,6},{5,7},{6,4},{7,5},{8,10},{9,11},{10,... | collective-permute-start | bytes 1769480 | tf_op jit(solution)/shard_map/ppermute | solution.py:192
  366.7 48.7 %collective-permute-start.63 = (bf16[256,1152]{1,0:T(8,128)(2,1)}, bf16[256,1152]{1,0:T(8,128)(2,1)}, u32[]{:S(2)}, u32[]{:S(2)}) collective-permute-start(bf16[256,1152]{1,0:T(8,128)(2,1)} %get-tuple-element.273.refs_0_), channel_id=1, source_target_pairs={{0,2},{1,3},{2,0},{3,1},{4,6},{5,7},{6,4},{7,5},{8,10},{9,11},{10,... | collective-permute-start | bytes 1769480 | tf_op jit(solution)/shard_map/ppermute | solution.py:192
  368.8 23.7 %collective-permute-start.58 = (bf16[144,2304]{1,0:T(8,128)(2,1)S(1)}, bf16[144,2304]{1,0:T(8,128)(2,1)S(1)}, u32[]{:S(2)}, u32[]{:S(2)}) collective-permute-start(bf16[144,2304]{1,0:T(8,128)(2,1)S(1)} %get-tuple-element.346), channel_id=1, source_target_pairs={{8,0},{16,8},{24,16},{28,24},{20,28},{12,20},{4,12},{0,4},{9,1},{1... | collective-permute-start | bytes 1990664 | tf_op jit(solution)/shard_map/ppermute | solution.py:134
  392.5 24.4 %collective-permute-start.59 = (bf16[512,1152]{1,0:T(8,128)(2,1)}, bf16[512,1152]{1,0:T(8,128)(2,1)S(1)}, u32[]{:S(2)}, u32[]{:S(2)}) collective-permute-start(bf16[512,1152]{1,0:T(8,128)(2,1)} %get-tuple-element.251), channel_id=1, source_target_pairs={{0,1},{1,0},{2,3},{3,2},{4,5},{5,4},{6,7},{7,6},{8,9},{9,8},{10,11... | collective-permute-start | bytes 3538952 | tf_op jit(solution)/shard_map/ppermute | solution.py:186
  415.3 25.2 %collective-permute-start.64 = (bf16[256,1152]{1,0:T(8,128)(2,1)}, bf16[256,1152]{1,0:T(8,128)(2,1)S(1)}, u32[]{:S(2)}, u32[]{:S(2)}) collective-permute-start(bf16[256,1152]{1,0:T(8,128)(2,1)} %get-tuple-element.273.refs_0_), channel_id=1, source_target_pairs={{0,1},{1,0},{2,3},{3,2},{4,5},{5,4},{6,7},{7,6},{8,9},{9,8},{10,11... | collective-permute-start | bytes 1769480 | tf_op jit(solution)/shard_map/ppermute | solution.py:195
  442.7 81.6 %collective-permute-start.83 = (bf16[256,1152]{1,0:T(8,128)(2,1)S(1)}, bf16[256,1152]{1,0:T(8,128)(2,1)}, u32[]{:S(2)}, u32[]{:S(2)}) collective-permute-start(bf16[256,1152]{1,0:T(8,128)(2,1)S(1)} %copy-done.27), channel_id=1, source_target_pairs={{0,1},{1,0},{2,3},{3,2},{4,5},{5,4},{6,7},{7,6},{8,9},{9,8},{10,11... | collective-permute-start | bytes 1769480 | tf_op jit(solution)/shard_map/ppermute | solution.py:195
  442.8 71.6 %collective-permute-start.82 = (bf16[256,1152]{1,0:T(8,128)(2,1)S(1)}, bf16[256,1152]{1,0:T(8,128)(2,1)}, u32[]{:S(2)}, u32[]{:S(2)}) collective-permute-start(bf16[256,1152]{1,0:T(8,128)(2,1)S(1)} %copy-done.27), channel_id=1, source_target_pairs={{0,2},{1,3},{2,0},{3,1},{4,6},{5,7},{6,4},{7,5},{8,10},{9,11},{10,... | collective-permute-start | bytes 1769480 | tf_op jit(solution)/shard_map/ppermute | solution.py:192
  449.4 30.7 %collective-permute-start.85 = (bf16[256,1152]{1,0:T(8,128)(2,1)}, bf16[256,1152]{1,0:T(8,128)(2,1)}, u32[]{:S(2)}, u32[]{:S(2)}) collective-permute-start(bf16[256,1152]{1,0:T(8,128)(2,1)} %add_convert_fusion.5), channel_id=1, source_target_pairs={{0,2},{1,3},{2,0},{3,1},{4,6},{5,7},{6,4},{7,5},{8,10},{9,11},{10,... | collective-permute-start | bytes 1769480 | tf_op jit(solution)/shard_map/ppermute | solution.py:188
  450.4 41.3 %collective-permute-start.70 = (bf16[144,2304]{1,0:T(8,128)(2,1)S(1)}, bf16[144,2304]{1,0:T(8,128)(2,1)S(1)}, u32[]{:S(2)}, u32[]{:S(2)}) collective-permute-start(bf16[144,2304]{1,0:T(8,128)(2,1)S(1)} %add_convert_fusion), channel_id=1, source_target_pairs={{0,8},{8,16},{16,24},{24,28},{28,20},{20,12},{12,4},{4,0},{1,9},{9... | collective-permute-start | bytes 1990664 | tf_op jit(solution)/shard_map/ppermute | solution.py:132
  452.8 23.3 %collective-permute-start.81 = (bf16[4,144,288]{2,1,0:T(8,128)(2,1)S(1)}, bf16[4,144,288]{2,1,0:T(8,128)(2,1)S(1)}, u32[]{:S(2)}, u32[]{:S(2)}) collective-permute-start(bf16[4,144,288]{2,1,0:T(8,128)(2,1)S(1)} %bitcast.242), channel_id=1, source_target_pairs={{0,4},{4,0},{8,12},{12,8},{16,20},{20,16},{24,28},{28,24},{1,5},{5... | collective-permute-start | bytes 995336 | tf_op jit(solution)/shard_map/ppermute | solution.py:172
  513.2 41.4 %collective-permute-start.87 = (bf16[256,1152]{1,0:T(8,128)(2,1)}, bf16[256,1152]{1,0:T(8,128)(2,1)}, u32[]{:S(2)}, u32[]{:S(2)}) collective-permute-start(bf16[256,1152]{1,0:T(8,128)(2,1)} %get-tuple-element.309.refs_0_), channel_id=1, source_target_pairs={{0,1},{1,0},{2,3},{3,2},{4,5},{5,4},{6,7},{7,6},{8,9},{9,8},{10,11... | collective-permute-start | bytes 1769480 | tf_op jit(solution)/shard_map/ppermute | solution.py:195
  530.1 24.6 %collective-permute-start.88 = (bf16[256,1152]{1,0:T(8,128)(2,1)}, bf16[256,1152]{1,0:T(8,128)(2,1)}, u32[]{:S(2)}, u32[]{:S(2)}) collective-permute-start(bf16[256,1152]{1,0:T(8,128)(2,1)} %collective-permute-done.86.refs_1_), channel_id=1, source_target_pairs={{0,1},{1,0},{2,3},{3,2},{4,5},{5,4},{6,7},{7,6},{8,9},{9,8},{10,11... | collective-permute-start | bytes 1769480 | tf_op jit(solution)/shard_map/ppermute | solution.py:196
  (160 other events, 1473.6 us)

commit v4 on v3

--- a/solution.py
+++ b/solution.py
@@ -31,7 +31,7 @@
 DOT_NT = (((1,), (1,)), ((), ()))
 DOT_TN = (((0,), (0,)), ((), ()))
 
-COST = 10
+COST = 0
 VMEM_GRANT = 58 * 2**20
 SMEM_SPEC = pl.BlockSpec(memory_space=pltpu.SMEM)
 
@@ -53,30 +53,23 @@
     return onward, [(b, a) for a, b in onward]
 
 
-def ring_place(count):
-    order = ring_order(count)
-    spots = [order.index(i) for i in range(count)]
-    return jnp.array(order), jnp.array(spots)[lax.axis_index("dp")]
-
-
-def ring_start(shard, count):
-    onward, backward = ring_perms(count)
-    return lax.ppermute(shard, "dp", onward), lax.ppermute(shard, "dp", backward)
-
-
-def ring_finish(ahead, behind, count):
-    onward, backward = ring_perms(count)
-    cut = ahead.shape[0] // 32 * 16
-    return lax.ppermute(ahead[:cut], "dp", onward), lax.ppermute(behind[cut:], "dp", backward)
+def ring_spot(count):
+    me = lax.axis_index("dp")
+    return jnp.where(me % 2 == 0, me // 2, count - 1 - me // 2)
+
+
+def ring_at(spot, count):
+    spot = spot % count
+    return jnp.where(spot < count // 2, 2 * spot, 2 * (count - 1 - spot) + 1)
 
 
 def ring_places(rows, count):
-    order, spot = ring_place(count)
-    at = [order[spot] * rows]
+    spot = ring_spot(count)
+    back = [0]
     for hop in range(1, count // 2):
-        at += [order[(spot - hop) % count] * rows, order[(spot + hop) % count] * rows]
-    far = order[(spot + count // 2) % count] * rows
-    return jnp.stack(at + [far, far + rows // 32 * 16]).astype(jnp.int32)
+        back += [-hop, hop]
+    at = ring_at(spot + jnp.array(back + [count // 2] * 2), count) * rows
+    return (at + jnp.array([0] * len(back) + [0, rows // 32 * 16])).astype(jnp.int32)
 
 
 def place_kernel(at_ref, *refs):
@@ -99,9 +92,10 @@
         copy.wait()
 
 
-def place_pieces(at, pieces):
+def place_pieces(chain, at, pieces):
     whole = (sum(piece.shape[0] for piece in pieces),) + pieces[0].shape[1:]
-    return pl.pallas_call(
+    at = chain.tie(at)
+    out = pl.pallas_call(
         place_kernel,
         out_shape=jax.ShapeDtypeStruct(whole, pieces[0].dtype),
         in_specs=[SMEM_SPEC] + [pl.BlockSpec(memory_space=pl.ANY)] * len(pieces),
@@ -110,22 +104,47 @@
         + [pltpu.SemaphoreType.DMA((len(pieces),))] * 2,
         compiler_params=pltpu.CompilerParams(vmem_limit_bytes=VMEM_GRANT),
         cost_estimate=pl.CostEstimate(
-            flops=0, bytes_accessed=4 * COST * math.prod(whole), transcendentals=0
+            flops=0, bytes_accessed=int(4 * COST * math.prod(whole)) + 1, transcendentals=0
         ),
         name="place_pieces",
     )(at, *pieces)
+    return chain.close(out)
+
+
+class Chain:
+    def __init__(self, token):
+        self.token = token
+
+        self.landing = []
+
+    def tie(self, *arrays):
+        self.token, *arrays = lax.optimization_barrier((self.token, *arrays))
+        return arrays[0] if len(arrays) == 1 else tuple(arrays)
+
+    def land(self, *transfers):
+        self.landing += transfers
+
+    def close(self, *arrays):
+        landing, self.landing = self.landing, []
+        values = self.tie(*arrays, *[getattr(held, name) for held, name in landing])
+        values = values if isinstance(values, tuple) else (values,)
+        for (held, name), value in zip(landing, values[len(arrays) :]):
+            setattr(held, name, value)
+        return values[0] if len(arrays) == 1 else values[: len(arrays)]
 
 
 class RingSum:
     def __init__(self, parts, count):
-        self.parts, self.rows = parts, parts.shape[0] // count
-        self.onward, self.backward = ring_perms(count)
-        self.order, self.spot = ring_place(count)
-        self.count, self.left = count, count // 2 - 1
-        self.send(self.chunk(count // 2), self.chunk(1 - count // 2))
+        self.parts, self.count = parts, count
+        self.left = count // 2 - 1 if count in (4, 8) else 0
+        if self.left:
+            self.rows = parts.shape[0] // count
+            self.onward, self.backward = ring_perms(count)
+            self.spot = ring_spot(count)
+            self.send(self.chunk(count // 2), self.chunk(1 - count // 2))
 
     def chunk(self, ahead):
-        at = self.order[(self.spot + ahead) % self.count] * self.rows
+        at = ring_at(self.spot + ahead, self.count) * self.rows
         return lax.dynamic_slice_in_dim(self.parts, at, self.rows, 0).astype(wide)
 
     def send(self, ahead, behind):
@@ -133,68 +152,146 @@
         if behind is not None:
             self.behind = lax.ppermute(behind.astype(low), "dp", self.backward)
 
-    def hop(self, token):
+    def flying(self):
+        return [(self, "ahead"), (self, "behind")] if self.count in (4, 8) else []
+
+    def hop(self):
         if not self.left:
-            return token
-        token, ahead, behind = lax.optimization_barrier((token, self.ahead, self.behind))
-        self.behind = behind
-        ahead = ahead.astype(wide) + self.chunk(self.left)
+            return
+        ahead = self.ahead.astype(wide) + self.chunk(self.left)
+        behind = None
         if self.left > 1:
-            behind = behind.astype(wide) + self.chunk(1 - self.left)
-        else:
-            behind = None
+            behind = self.behind.astype(wide) + self.chunk(1 - self.left)
         self.send(ahead, behind)
         self.left -= 1
-        return token
 
     def total(self):
+        if self.count not in (4, 8):
+            return lax.psum_scatter(self.parts, "dp", scatter_dimension=0, tiled=True).astype(wide)
         return self.ahead.astype(wide) + self.behind.astype(wide) + self.chunk(0)
 
 
-def halving_hop(parts, step, count):
-    pairs = parts.reshape((parts.shape[0] // 2, 2) + parts.shape[1:])
-    bit = lax.axis_index("dp") // step % 2
-    sent = lax.dynamic_index_in_dim(pairs, 1 - bit, 1, keepdims=False).astype(low)
-    kept = lax.dynamic_index_in_dim(pairs, bit, 1, keepdims=False).astype(wide)
-    got = lax.ppermute(sent, "dp", [(i, i ^ step) for i in range(count)])
-    return kept + got.astype(wide)
-
-
-def doubling_gather(shard, count, between):
-    if count not in (4, 8):
-        return lax.all_gather(shard, "dp", axis=0, tiled=True)
-    spot = lax.axis_index("dp")
-    known = shard[None]
-    step = count // 2
-    while step:
-        known = lax.optimization_barrier((known, between[0]))[0]
-        between = between[1:]
-        got = lax.ppermute(known, "dp", [(i, i ^ step) for i in range(count)])
-        second = spot // step % 2 == 1
-        known = jnp.stack([jnp.where(second, got, known), jnp.where(second, known, got)], 1)
-        known = known.reshape((-1,) + shard.shape)
-        step //= 2
-    return known.reshape((-1,) + shard.shape[1:])
+class GroupSum:
+    def __init__(self, kept, sent):
+        self.kept, self.got = kept, lax.ppermute(sent, "mp", CORE_SWAP)
+
+    def cross(self):
+        quarter = self.kept.shape[0] // 2
+        passed = (self.kept[quarter:] + self.got[quarter:].astype(wide)).astype(low)
+        self.last = lax.ppermute(passed, "mp", CHIP_SWAP)
+
+    def terms(self):
+        return self.kept, self.got, self.last
+
+
+class GroupGather:
+    def __init__(self, own):
+        self.own = own
+        self.chip = lax.ppermute(own, "mp", CHIP_SWAP)
+        self.core = lax.ppermute(own, "mp", CORE_SWAP)
+
+    def forward(self):
+        self.both = lax.ppermute(self.chip, "mp", CORE_SWAP)
+
+    def flying(self):
+        return [(self, "chip"), (self, "core")]
+
+    def pieces(self):
+        return [self.own, self.chip, self.core, self.both]
+
+    def in_order(self, mp_place):
+        return in_group_order([self.own, self.core, self.chip, self.both], mp_place)
+
+
+class DoublingGather:
+    def __init__(self, shard, count):
+        self.shard, self.count = shard, count
+        self.known, self.step = shard[None], count // 2 if count in (4, 8) else 0
+        self.send()
+
+    def send(self):
+        if self.step:
+            swap = [(i, i ^ self.step) for i in range(self.count)]
+            self.got = lax.ppermute(self.known, "dp", swap)
+
+    def join(self, got):
+        second = lax.axis_index("dp") // self.step % 2 == 1
+        pair = [jnp.where(second, got, self.known), jnp.where(second, self.known, got)]
+        self.known = jnp.stack(pair, 1).reshape((-1,) + self.shard.shape)
+        self.step //= 2
+
+    def flying(self):
+        return [(self, "got")] if self.step else []
+
+    def hop(self):
+        if self.step > 1:
+            self.join(self.got)
+            self.send()
+
+    def whole(self):
+        if self.step:
+            self.join(self.got)
+        if self.count not in (4, 8):
+            return lax.all_gather(self.shard, "dp", axis=0, tiled=False)
+        return self.known
+
+
+class HalvingSum:
+    def __init__(self, parts, count):
+        self.parts, self.count, self.step = parts, count, 1
+        self.send()
+
+    def send(self):
+        pairs = self.parts.reshape((self.parts.shape[0] // 2, 2) + self.parts.shape[1:])
+        bit = lax.axis_index("dp") // self.step % 2
+        sent = lax.dynamic_index_in_dim(pairs, 1 - bit, 1, keepdims=False).astype(low)
+        self.kept = lax.dynamic_index_in_dim(pairs, bit, 1, keepdims=False).astype(wide)
+        swap = [(i, i ^ self.step) for i in range(self.count)]
+        self.got = lax.ppermute(sent, "dp", swap)
+
+    def flying(self):
+        return [(self, "got")] if self.step < self.count else []
+
+    def hop(self):
+        if self.step < self.count:
+            self.parts = self.kept + self.got.astype(wide)
+            self.step *= 2
+            if self.step < self.count:
+                self.send()
+
+
+class RingGather:
+    def __init__(self, shard, count):
+        self.count, self.left = count, count // 2 - 1
+        self.onward, self.backward = ring_perms(count)
+        self.pieces = [shard]
+        self.send(shard, shard)
+
+    def send(self, ahead, behind):
+        self.ahead = lax.ppermute(ahead, "dp", self.onward)
+        self.behind = lax.ppermute(behind, "dp", self.backward)
+
+    def flying(self):
+        return [(self, "ahead"), (self, "behind")]
+
+    def hop(self):
+        ahead, behind = self.ahead, self.behind
+        self.pieces += [ahead, behind]
+        if self.left > 1:
+            self.send(ahead, behind)
+        elif self.left == 1:
+            cut = ahead.shape[0] // 32 * 16
+            self.send(ahead[:cut], behind[cut:])
+        self.left -= 1
+
+    def place(self, chain):
+        while self.left >= 0:
+            self.hop()
+        return place_pieces(chain, ring_places(self.pieces[0].shape[0], self.count), self.pieces)
 
 
 def share_hop(known, reach, count):
     return known + lax.ppermute(known, "dp", [(i, i ^ reach) for i in range(count)])
-
-
-def group_scatter(kept, sent):
-    quarter = kept.shape[0] // 2
-    got = lax.ppermute(sent, "mp", CORE_SWAP)
-    passed = (kept[quarter:] + got[quarter:].astype(wide)).astype(low)
-    return (kept, got, lax.ppermute(passed, "mp", CHIP_SWAP)), passed
-
-
-def group_gather(own, between=None):
-    chip = lax.ppermute(own, "mp", CHIP_SWAP)
-    if between is not None:
-        chip = lax.optimization_barrier((chip, between))[0]
-    core = lax.ppermute(own, "mp", CORE_SWAP)
-    both = lax.ppermute(chip, "mp", CORE_SWAP)
-    return [own, chip, core, both]
 
 
 def in_group_order(pieces, place):
@@ -318,7 +415,7 @@
     return jax.ShapeDtypeStruct(shape, kind)
 
 
-def attend_forward(place, qkv, seg_row, weights):
+def attend_forward(chain, qkv, seg_row, weights):
     row_len, width = qkv.shape[0], qkv.shape[1] // 3
     heads = width // HEAD_DIM
     full = weights.shape[0]
@@ -335,7 +432,7 @@
     return row_call(
         body,
         "attend_forward",
-        place,
+        chain,
         args,
         [fixed_spec(arg.shape) for arg in args],
         tuple(fixed_spec(shape.shape) for shape in shapes),
@@ -346,7 +443,7 @@
     )
 
 
-def attend_backward(place, qkv, grads, seg_row, weights):
+def attend_backward(chain, qkv, grads, seg_row, weights):
     row_len, width = qkv.shape[0], qkv.shape[1] // 3
     heads = width // HEAD_DIM
     full = weights.shape[0]
@@ -364,7 +461,7 @@
     return row_call(
         body,
         "attend_backward",
-        place,
+        chain,
         args,
         [fixed_spec(arg.shape) for arg in args],
         tuple(fixed_spec(shape.shape) for shape in shapes),
@@ -546,11 +643,14 @@
         sums_ref[4 + u : 5 + u, :] = jnp.sum(grad_one * normed, axis=0, keepdims=True)
 
 
-def row_call(body, name, place, args, in_specs, out_specs, out_shape, grid=1, scratch=(), flops=0, exps=0, aliases=None):
+def row_call(
+    body, name, chain, args, in_specs, out_specs, out_shape, grid=1, scratch=(), flops=0, exps=0, aliases=None, prefetch=None
+):
     moved = sum(math.prod(a.shape) * a.dtype.itemsize for a in args)
     shapes = out_shape if isinstance(out_shape, tuple) else (out_shape,)
     moved += sum(math.prod(o.shape) * o.dtype.itemsize for o in shapes)
-    return pl.pallas_call(
+    prefetch = chain.token if prefetch is None else chain.tie(prefetch)
+    out = pl.pallas_call(
         body,
         grid_spec=pltpu.PrefetchScalarGridSpec(
             num_scalar_prefetch=1,
@@ -563,51 +663,48 @@
         input_output_aliases=aliases or {},
         compiler_params=pltpu.CompilerParams(vmem_limit_bytes=VMEM_GRANT),
         cost_estimate=pl.CostEstimate(
-            flops=COST * flops, bytes_accessed=COST * moved, transcendentals=COST * exps
+            flops=int(COST * flops) + 1, bytes_accessed=int(COST * moved) + 1, transcendentals=0
         ),
         name=name,
-    )(place, *args)
-
-
-def block_spec(shape, index):
-    return pl.BlockSpec(shape, index)
+    )(prefetch, *args)
+    return chain.close(*out) if isinstance(out_shape, tuple) else chain.close(out)
 
 
 def fixed_spec(shape):
     return pl.BlockSpec(shape, lambda *_: (0,) * len(shape))
 
 
-def unit_tables(mp_arg, onehot, pieces, fields):
+def unit_tables(chain, mp_arg, onehot, pieces, fields):
     units, slots = onehot.shape
-    own = pieces[0].shape[1]
+    own = pieces[0].shape[1] // fields
 
     def body(mp_ref, hot_ref, *refs):
         out_ref = refs[-1]
         mp_place = mp_ref[0]
         for i, piece in enumerate(refs[:-1]):
+            spread = dot_as(hot_ref[...], piece[...], DOT_NN)
             for j in range(4):
 
                 @pl.when(jnp.bitwise_xor(mp_place, i) == j)
-                def _(piece=piece, j=j):
+                def _(spread=spread, j=j):
                     for f in range(fields):
                         at = f * 4 * own + j * own
-                        out_ref[:, at : at + own] = dot_as(
-                            hot_ref[...], piece[f * slots : (f + 1) * slots, :], DOT_NN
-                        )
+                        out_ref[:, at : at + own] = column(spread, f, own)
 
     return row_call(
         body,
         "unit_tables",
-        mp_arg,
+        chain,
         (onehot, *pieces),
         [fixed_spec(onehot.shape)] + [fixed_spec(pieces[0].shape)] * 4,
         fixed_spec((units, fields * 4 * own)),
         shape_of((units, fields * 4 * own), wide),
         flops=8 * units * slots * own * fields,
-    )
-
-
-def weight_grad(place, pairs, name):
+        prefetch=mp_arg,
+    )
+
+
+def weight_grad(chain, pairs, name):
     depth = pairs[0][0][0][0].shape[1]
     tile = depth // 3
     widths = [pair[0][1].shape[1] for pair in pairs]
@@ -639,7 +736,7 @@
     return row_call(
         body,
         name,
-        place,
+        chain,
         args,
         specs,
         pl.BlockSpec((tile, sum(widths)), lambda i, p: (i, 0)),
@@ -649,7 +746,7 @@
     )
 
 
-def widen_row(place, pieces, row, rows, before):
+def widen_row(chain, pieces, row, rows, before):
     quarter, width = pieces[0].shape
 
     def body(place_ref, *refs):
@@ -663,7 +760,7 @@
     return row_call(
         body,
         "widen_row",
-        place,
+        chain,
         tuple(pieces) + before,
         [fixed_spec((quarter, width))] * 4 + [pl.BlockSpec(memory_space=pl.ANY)] * len(before),
         pl.BlockSpec((quarter, width), lambda i, p: (row * 4 + jnp.bitwise_xor(p[0], i), 0)),
@@ -685,12 +782,12 @@
     return (first_new, second_new, weight_new, ema_new)
 
 
-def adam_slabs(token, plan, grads, make_grad, groups, before, name):
+def adam_slabs(chain, plan, grads, make_grad, groups, before, name):
     slab = groups[0][0].shape[1:]
     count, held = len(plan), 4 * len(groups)
     turns = [[i for i, (which, _) in enumerate(plan) if which == g] for g in range(len(groups))]
     ids = [plan[max([i for i in mine if i <= n], default=mine[0])][1] for mine in turns for n in range(count)]
-    ids = lax.optimization_barrier((jnp.array(ids, jnp.int32), token))[0]
+    ids = jnp.array(ids, jnp.int32)
 
     def block(group):
         return pl.BlockSpec((1,) + slab, lambda i, ids: (ids[group * count + i], 0, 0))
@@ -724,7 +821,7 @@
     return row_call(
         body,
         name,
-        ids,
+        chain,
         (*grads, *flat, *kept),
         [fixed_spec(grad.shape) for grad in grads]
         + specs
@@ -734,6 +831,7 @@
         grid=count,
         scratch=[pltpu.VMEM(slab, wide)],
         aliases=aliases,
+        prefetch=ids,
     )
 
 
@@ -777,10 +875,12 @@
     place = (2 * core + chip).astype(jnp.int32)
     place_arg = place.reshape(1)
 
-    def tied(*others):
-        return lax.optimization_barrier((place_arg,) + others)[0]
+    chain = Chain(place_arg)
 
     ring = dp_count in (4, 8)
+    known = jnp.zeros((dp_count,) + time_steps.shape, time_steps.dtype)
+    known = lax.dynamic_update_slice_in_dim(known, time_steps[None], dp_place, 0)
+    known, weight_cols, weight_rows = lax.optimization_barrier((known, weight_cols, weight_rows))
     cols_low = weight_cols.astype(low)
     own_rows = weight_rows.astype(low).transpose(2, 0, 1).reshape(own_depth, 5 * own_width)
     own_first = jnp.concatenate([cols_low[0], cols_low[1], cols_low[2], own_rows[:, :own_width]], 1)
@@ -797,50 +897,43 @@
         table = jnp.where(is_cos[None, :], jnp.cos(angles), jnp.sin(angles))
         return table.astype(low), jax.nn.silu(table).astype(low)
 
-    def slot_products(left, maps):
-        out = jnp.stack([dot_as(left, maps[j], DOT_NN).astype(low) for j in range(maps.shape[0])], 0)
-        return out.reshape(-1, dp_count, rows * slots, own_width).transpose(1, 0, 2, 3)
-
-    def near_products(time_low, ada_low):
-        return jnp.concatenate(
-            [slot_products(ada_low, cols_low[9:11]), slot_products(time_low, cols_low[3:5])], 1
-        )
+    near_maps = [jnp.concatenate([cols_low[i], cols_low[i + 1]], 1) for i in (9, 3)]
+    far_maps = jnp.concatenate([cols_low[i] for i in (11, 12, 13, 14)], 1)
+
+    def slot_products(pairs):
+        out = jnp.concatenate([dot_as(left, maps, DOT_NN).astype(low) for left, maps in pairs], 1)
+        return out.reshape(dp_count, rows * slots, -1)
 
     if ring:
-        known = jnp.zeros((dp_count,) + time_steps.shape, time_steps.dtype)
-        known = lax.dynamic_update_slice_in_dim(known, time_steps[None], dp_place, 0)
-        onward, backward = ring_perms(dp_count)
-        ahead, behind = ring_start(own_first, dp_count)
-        pieces = [own_first, ahead, behind]
+        first_gather = RingGather(own_first, dp_count)
+
+        def beside(value):
+            value, first_gather.ahead, first_gather.behind = lax.optimization_barrier(
+                (value, first_gather.ahead, first_gather.behind)
+            )
+            if first_gather.left > 0:
+                first_gather.hop()
+            return value
+
         known = share_hop(known, 1, dp_count)
-        known = share_hop(known, 2, dp_count)
-        known, ahead, behind = lax.optimization_barrier((known, ahead, behind))
+        known = beside(share_hop(known, 2, dp_count))
         if dp_count == 8:
-            ahead = lax.ppermute(ahead, "dp", onward)
-            behind = lax.ppermute(behind, "dp", backward)
-            pieces += [ahead, behind]
             known = share_hop(known, 4, dp_count)
         time_low, ada_low = embed(known.reshape(-1))
-        near = near_products(time_low, ada_low)
-        near, ahead, behind = lax.optimization_barrier((near, ahead, behind))
+        near = beside(slot_products([(ada_low, near_maps[0]), (time_low, near_maps[1])]))
+        near = HalvingSum(near, dp_count)
+        near.hop()
         if dp_count == 8:
-            ahead = lax.ppermute(ahead, "dp", onward)
-            behind = lax.ppermute(behind, "dp", backward)
-            pieces += [ahead, behind]
-        near = halving_hop(near, 1, dp_count)
-        near = halving_hop(near, 2, dp_count)
-        near, ahead, behind, own_rest = lax.optimization_barrier((near, ahead, behind, own_rest))
-        pieces += ring_finish(ahead, behind, dp_count)
-        rest_pieces = [own_rest, *ring_start(own_rest, dp_count)]
-        if dp_count == 8:
-            near = halving_hop(near, 4, dp_count)
-        near = near[0]
-        w_first = place_pieces(ring_places(own_depth, dp_count), pieces)
+            near.hop()
+        own_rest = beside(own_rest)
+        rest_gather = RingGather(own_rest, dp_count)
+        near.hop()
+        near = near.parts[0]
     else:
         w_first = lax.all_gather(own_first, "dp", axis=0, tiled=True)
-        rest_pieces = [lax.all_gather(own_rest, "dp", axis=0, tiled=True)]
+        w_rest = lax.all_gather(own_rest, "dp", axis=0, tiled=True)
         time_low, ada_low = embed(lax.all_gather(time_steps, "dp", axis=0, tiled=True).reshape(-1))
-        near = near_products(time_low, ada_low)
+        near = slot_products([(ada_low, near_maps[0]), (time_low, near_maps[1])])
         near = lax.psum_scatter(near, "dp", scatter_dimension=0, tiled=True)[0].astype(wide)
 
     seg_grid = seg_ids.reshape(rows, row_len)
@@ -850,27 +943,28 @@
     blocks = blocks.reshape(rows * units, rows * slots)
     mp_arg = mp_place.astype(jnp.int32).reshape(1)
 
-    def tables(own, biases):
-        fields = own.shape[0]
-        own = (own + biases[:, None, :]).astype(low).reshape(-1, own_width)
-        pieces = group_gather(own)
-        pieces = [pieces[0], pieces[2], pieces[1], pieces[3]]
-        out = unit_tables(mp_arg, blocks.astype(low), pieces, fields)
-        return out.reshape(rows, 4, own_units, fields * width)
-
-    far = [slot_products(lax.optimization_barrier((ada_low, near))[0], cols_low[11:15])]
-
-    def far_hop(token):
-        if not ring:
-            return token
-        token, held = lax.optimization_barrier((token, far[-1]))
-        if held.shape[0] > 1:
-            far.append(halving_hop(held, dp_count // held.shape[0], dp_count))
-        return token
-
-    near_tab = tables(near[:2], bias_cols[6:8])
+    def tables(spread, fields):
+        spread.forward()
+        pieces = [spread.own, spread.core, spread.chip, spread.both]
+        out = unit_tables(chain, mp_arg, blocks.astype(low), pieces, fields)
+        return out.reshape(rows, 4, own_units, -1)
+
+    far = slot_products([(lax.optimization_barrier((ada_low, near))[0], far_maps)])
+    near_mod = (near[:, : 2 * own_width] + bias_cols[6:8].reshape(1, -1)).astype(low)
+    near_tab = tables(GroupGather(near_mod), 2)
+    if ring:
+        far = HalvingSum(far, dp_count)
+        chain.land(*far.flying(), *rest_gather.flying())
+        w_first = first_gather.place(chain)
+        far.hop()
+        rest_gather.hop()
     time_add = jnp.concatenate(
-        [near[2] + bias_cols[0], jnp.zeros((rows * slots, own_width), wide), near[3] + bias_cols[1]], 1
+        [
+            near[:, 2 * own_width : 3 * own_width] + bias_cols[0],
+            jnp.zeros((rows * slots, own_width), wide),
+            near[:, 3 * own_width :] + bias_cols[1],
+        ],
+        1,
     )
     add_tab = jnp.dot(blocks.astype(wide), time_add, precision=highest)
     add_tab = add_tab.reshape(rows, 4, own_units, 3 * own_width)
@@ -904,11 +998,11 @@
     half_step = pl.BlockSpec(half_block, lambda i, p: (i, 0))
     half_fixed = fixed_spec(half_block)
 
-    def open_row(r, token):
+    def open_row(r):
         return row_call(
             open_kernel,
             "open_row",
-            token,
+            chain,
             (tokens, tokens, near_tab[r], near_tab[r], add_tab[r], add_tab[r], w_first),
             moved_blocks(r) + moved_tables(near_tab) + moved_tables(add_tab) + [fixed_spec(w_first.shape)],
             (half_step, pl.BlockSpec((half, qkv_width), lambda i, p: (i, 0))),
@@ -917,59 +1011,64 @@
             flops=2 * row_len * width * qkv_width,
         )
 
-    def rest_hop(token):
-        if not ring:
-            return token
-        token, ahead, behind = lax.optimization_barrier((token, *rest_pieces[-2:]))
-        hops = (len(rest_pieces) - 1) // 2
-        if hops < dp_count // 2 - 1:
-            rest_pieces.append(lax.ppermute(ahead, "dp", onward))
-            rest_pieces.append(lax.ppermute(behind, "dp", backward))
-        elif hops < dp_count // 2:
-            rest_pieces.extend(ring_finish(ahead, behind, dp_count))
-        return token
-
     inputs_one, qkvs, mixed, parts = [], [], [], []
-    token = rest_hop(far_hop(place_arg))
     for r in range(rows):
-        a_one, qkv = open_row(r, token)
-        token = far_hop(tied(qkv, *[part[1] for part in parts]))
+        if r == 0 and ring:
+            chain.land(*far.flying())
+        if r:
+            chain.land((parts[r - 1], "got"))
+        if r == 1:
+            chain.land(*far_gather.flying())
+        a_one, qkv = open_row(r)
         inputs_one.append(a_one)
         qkvs.append(qkv)
-        out, kept, sent = attend_forward(token, qkv, seg_grid[r], w_first)
-        token = rest_hop(tied(sent))
+        if r:
+            parts[r - 1].cross()
+        if r == 1:
+            if ring:
+                chain.land(*rest_gather.flying())
+            far_tab = tables(far_gather, 4)
+            if ring:
+                rest_gather.hop()
+                chain.land(*rest_gather.flying())
+        if r == 0 and ring:
+            far.hop()
+            chain.land(*far.flying(), *rest_gather.flying())
+        if r:
+            chain.land((parts[r - 1], "last"))
+        out, kept, sent = attend_forward(chain, qkv, seg_grid[r], w_first)
+        mixed.append(out)
+        parts.append(GroupSum(kept, sent))
         if r == 0:
-            token = far_hop(token)
-        mixed.append(out)
-        parts.append(group_scatter(kept, sent))
-    far = far[-1] if ring else lax.psum_scatter(
-        far[0].reshape(-1, own_width), "dp", scatter_dimension=0, tiled=True
-    )
-    far = far.astype(wide).reshape(4, rows * slots, own_width)
-    far_tab = tables(far, bias_cols[8:12])
+            if ring:
+                rest_gather.hop()
+                far.hop()
+                far = far.parts[0]
+            else:
+                far = lax.psum_scatter(far, "dp", scatter_dimension=0, tiled=True)[0].astype(wide)
+            far_gather = GroupGather((far + bias_cols[8:12].reshape(1, -1)).astype(low))
 
     attendeds, hiddens, inputs_two, down_grads = [], [], [], []
 
-    def first_norm(r, token):
+    def first_norm(r):
         attended, hidden, a_two = row_call(
             first_kernel,
             "first_norm",
-            token,
-            (tokens, *parts[r][0], bias_rows, far_tab[r]),
+            chain,
+            (tokens, *parts[r].terms(), bias_rows, far_tab[r]),
             [own_block(r), here, here, here, fixed_spec(bias_rows.shape), own_table(far_tab)],
             (here, here, here),
             (wides(*block), wides(*block), lows(*block)),
         )
         attendeds.append(attended)
         hiddens.append(hidden)
-        inputs_two.append(group_gather(a_two))
-        return tied(a_two)
-
-    def down_back(r, token):
+        inputs_two.append(GroupGather(a_two))
+
+    def down_back(r):
         grads = row_call(
             down_back_kernel,
             "down_back",
-            token,
+            chain,
             (cotangent, cotangent, far_tab[r], far_tab[r], w_rest),
             moved_blocks(r) + moved_tables(far_tab) + [w_down_spec],
             (half_step, half_step),
@@ -978,27 +1077,34 @@
             flops=2 * row_len * width * width,
         )
         down_grads.append(grads)
-        return tied(grads[1])
-
-    token = first_norm(0, token)
-    token = tied(inputs_two[0][0], *[part[1] for part in parts[1:]])
-    w_rest = place_pieces(ring_places(own_depth, dp_count), rest_pieces) if ring else rest_pieces[0]
+
+    chain.land((parts[-1], "got"))
+    first_norm(0)
+    parts[-1].cross()
+    if ring:
+        w_rest = rest_gather.place(chain)
     w_down_spec = pl.BlockSpec((width, w_rest.shape[1] // 2), lambda i, p: (0, 1))
     w_up_spec = pl.BlockSpec((width, w_rest.shape[1] // 2), lambda i, p: (0, 0))
-    for r in range(rows):
-        token = down_back(r, token)
-    for r in range(1, rows):
-        token = first_norm(r, token)
+    chain.land(*inputs_two[0].flying())
+    down_back(0)
+    inputs_two[0].forward()
+    chain.land((inputs_two[0], "both"), (parts[-1], "last"))
+    down_back(1)
+    first_norm(1)
 
     bias_up = bias_cols[2:6].reshape(1, -1)
     hidden_width = bias_up.shape[1]
     actives, inner_grads, up_parts, up_sums, down_parts = [], [], [], 0.0, []
     for r in range(rows):
+        if r + 1 < rows:
+            chain.land(*inputs_two[r + 1].flying())
+        if r:
+            chain.land((up_parts[r - 1], "last"), (down_parts[r - 1], "got"))
         active, inner_grad, kept, sent, sums = row_call(
             up_kernel,
             "up_and_back",
-            token,
-            (*inputs_two[r], down_grads[r][1], bias_up, w_rest),
+            chain,
+            (*inputs_two[r].pieces(), down_grads[r][1], bias_up, w_rest),
             [here] * 4 + [half_step, fixed_spec(bias_up.shape), w_up_spec],
             (
                 pl.BlockSpec((half, hidden_width), lambda i, p: (i, 0)),
@@ -1018,15 +1124,21 @@
             scratch=[pltpu.VMEM(half_block, low)],
             flops=4 * row_len * width * hidden_width,
         )
-        token = tied(sent, *[x for part in up_parts for x in part[0][2:]], *[part[1] for part in down_parts])
         actives.append(active)
         inner_grads.append(inner_grad)
-        up_parts.append(group_scatter(kept, sent))
+        up_parts.append(GroupSum(kept, sent))
         up_sums = up_sums + jnp.sum(sums, axis=(0, 1))
+        chain.land((up_parts[r], "got"))
+        if r + 1 < rows:
+            inputs_two[r + 1].forward()
+            chain.land((inputs_two[r + 1], "both"))
+        if r:
+            down_parts[r - 1].cross()
+            chain.land((down_parts[r - 1], "last"))
         kept, sent = row_call(
             down_kernel,
             "down",
-            token,
+            chain,
             (active, w_rest),
             [pl.BlockSpec((half, hidden_width), lambda i, p: (i, 0)), w_down_spec],
             (half_fixed, half_fixed),
@@ -1034,177 +1146,169 @@
             grid=2,
             flops=2 * row_len * width * hidden_width,
         )
-        token = tied(sent, up_parts[-1][1], *[part[0][2] for part in down_parts])
-        down_parts.append(group_scatter(kept, sent))
-
-    grad_hiddens, grad_attendeds, second_sums = [], [], []
-
-    def second_norm(r, token):
+        down_parts.append(GroupSum(kept, sent))
+        up_parts[r].cross()
+
+    grad_hiddens, grad_gathers, second_sums = [], [], []
+
+    def second_norm(r):
         grad_hidden, grad_attended, sums = row_call(
             second_kernel,
             "second_norm",
-            token,
-            (cotangent, *up_parts[r][0], hiddens[r], attendeds[r], far_tab[r]),
+            chain,
+            (cotangent, *up_parts[r].terms(), hiddens[r], attendeds[r], far_tab[r]),
             [own_block(r)] + [here] * 5 + [own_table(far_tab)],
             (here, here, fixed_spec((16, width))),
             (wides(*block), lows(*block), wides(16, width)),
         )
         grad_hiddens.append(grad_hidden)
-        grad_attendeds.append(grad_attended)
+        grad_gathers.append(GroupGather(grad_attended))
         second_sums.append(sums)
-        return tied(grad_attended)
-
-    token = second_norm(0, token)
+
+    chain.land((down_parts[-1], "got"))
+    second_norm(0)
+    down_parts[-1].cross()
+    chain.land((up_parts[-1], "last"), *grad_gathers[0].flying())
     rest_grad = weight_grad(
-        token,
+        chain,
         [
-            [(inputs_two[r], inner_grads[r]) for r in range(rows)],
+            [(inputs_two[r].pieces(), inner_grads[r]) for r in range(rows)],
             [([down_grads[r][0]], actives[r]) for r in range(rows)],
         ],
         "grad_rest",
     )
-    rest_ring = RingSum(rest_grad, dp_count) if ring else None
-    token = tied(rest_grad, down_parts[-1][1])
-    grad_attendeds[0] = group_gather(grad_attendeds[0], token)
-    for r in range(1, rows):
-        token = second_norm(r, token)
-        grad_attendeds[r] = group_gather(grad_attendeds[r])
-
-    out_pieces, out_sums = [], []
-
-    def out_row(r, token):
+    rest_ring = RingSum(rest_grad, dp_count)
+    grad_gathers[0].forward()
+    chain.land((grad_gathers[0], "both"))
+    second_norm(1)
+
+    out_gathers, out_sums = [], []
+
+    def out_row(r):
         out_own, sums = row_call(
             out_kernel,
             "out_tokens",
-            token,
-            (cotangent, *down_parts[r][0], hiddens[r], bias_rows, far_tab[r]),
+            chain,
+            (cotangent, *down_parts[r].terms(), hiddens[r], bias_rows, far_tab[r]),
             [own_block(r)] + [here] * 4 + [fixed_spec(bias_rows.shape), own_table(far_tab)],
             (here, fixed_spec((8, width))),
             (lows(*block), wides(8, width)),
         )
-        out_pieces.extend(group_gather(out_own))
+        out_gathers.append(GroupGather(out_own))
         out_sums.append(sums)
-        return tied(out_own)
-
-    qkv_grads, one_parts, time_sums = [], [], []
-    for r in range(rows):
-        qkv_grad, kept, sent, sums = attend_backward(
-            token, qkvs[r], grad_attendeds[r], seg_grid[r], w_first
-        )
-        token = tied(sent)
-        if ring:
-            token = rest_ring.hop(token)
-        qkv_grads.append(qkv_grad)
-        one_parts.append(group_scatter(kept, sent))
-        time_sums.append(sums)
-        if r == 0:
-            for n in range(rows):
-                token = out_row(n, token)
-            token = tied(token, one_parts[0][1])
-
-    def exchange(values, between):
-        values = values.astype(low)
-
-        def part(held, which, columns):
-            return lax.dynamic_slice_in_dim(held, which * columns, columns, 1)
-
-        other = lax.ppermute(part(values, 1 - chip, 2 * own_width), "mp", CHIP_SWAP)
-        values = jnp.concatenate([part(values, chip, 2 * own_width), other], 0)
-        values = lax.optimization_barrier((values, between))[0]
-        other = lax.ppermute(part(values, 1 - core, own_width), "mp", CORE_SWAP)
-        return jnp.concatenate([part(values, core, own_width), other], 0)
-
-    by_place = jnp.stack(
+
+    def part(held, which, columns):
+        return lax.dynamic_slice_in_dim(held, which * columns, columns, 1)
+
+    class Exchange:
+        def __init__(self, values):
+            values = values.astype(low)
+            self.mine = part(values, chip, 2 * own_width)
+            self.other = lax.ppermute(part(values, 1 - chip, 2 * own_width), "mp", CHIP_SWAP)
+
+        def cross(self):
+            values = self.whole()
+            self.mine = part(values, core, own_width)
+            self.other = lax.ppermute(part(values, 1 - core, own_width), "mp", CORE_SWAP)
+
+        def whole(self):
+            return jnp.concatenate([self.mine, self.other], 0)
+
+    seg_place = unit_seg.reshape(rows, 4, own_units)
+    seg_place = jnp.stack(
         [
-            lax.dynamic_index_in_dim(
-                onehot.reshape(rows, 4, own_units, slots), jnp.bitwise_xor(place, j), 1, keepdims=False
-            )
+            lax.dynamic_index_in_dim(seg_place, jnp.bitwise_xor(place, j), 1, keepdims=False)
             for j in range(4)
         ],
         0,
     )
-
-    def slot_matrix(fields, spare, kept_rows):
-        same_row = jnp.eye(rows, dtype=bool)
-        same_field = jnp.eye(fields, dtype=bool)
-        full = (
-            by_place.transpose(3, 0, 1, 2)[None, None, :, :, :, None, :]
-            & same_row[None, :, None, None, :, None, None]
-            & same_field[:, None, None, None, None, :, None]
+    row_slots = seg_place + slots * jnp.arange(rows)[None, :, None]
+
+    def field_slots(field):
+        return row_slots + slot_count * field
+
+    def slot_matrix(to, height):
+        to = jnp.concatenate(to, 2).reshape(1, -1)
+        return (jnp.arange(height)[:, None] == to).astype(low)
+
+    def spare_slot(slot):
+        return jnp.broadcast_to(jnp.array([slot, -1, -1, -1]), (4, rows, 4))
+
+    chain.land(*rest_ring.flying())
+    out_row(0)
+    rest_ring.hop()
+    qkv_grads, one_parts, time_sums = [], [], []
+
+    def backward(r):
+        qkv_grad, kept, sent, sums = attend_backward(
+            chain, qkvs[r], grad_gathers[r].pieces(), seg_grid[r], w_first
         )
-        full = full.reshape(fields * rows * slots, 4, rows * fields * own_units)
-        full = jnp.pad(full, ((0, kept_rows), (0, 0), (0, spare)))
-        if spare:
-            extra = jnp.arange(spare)
-            full = full.at[fields * rows * slots + extra, :, rows * fields * own_units + extra].set(True)
-        return full.reshape(full.shape[0], -1).astype(low)
-
-    far_rows = []
-    for r in range(rows):
-        far_rows += [second_sums[r][:12], out_sums[r][:4]]
-    bias_part = [
-        sum(second_sums[r][12:13] for r in range(rows)),
-        sum(out_sums[r][4:5] for r in range(rows)),
-    ]
-    far_swapped = exchange(jnp.concatenate(far_rows + bias_part, 0), token)
-
+        qkv_grads.append(qkv_grad)
+        one_parts.append(GroupSum(kept, sent))
+        time_sums.append(sums)
+
+    chain.land(*rest_ring.flying(), *grad_gathers[1].flying(), (down_parts[-1], "last"))
+    backward(0)
+    rest_ring.hop()
+    grad_gathers[1].forward()
+    chain.land((one_parts[0], "got"), (grad_gathers[1], "both"))
+    out_row(1)
+    one_parts[0].cross()
+    far_swap = Exchange(jnp.concatenate([x for pair in zip(second_sums, out_sums) for x in pair], 0))
+    chain.land(*rest_ring.flying(), (out_gathers[0], "chip"), (one_parts[0], "last"), (far_swap, "other"))
+    backward(1)
+    rest_ring.hop()
+    far_swap.cross()
+    out_gathers[0].forward()
+    chain.land(*rest_ring.flying()[: 1 if dp_count == 8 else 2], (far_swap, "other"), (one_parts[1], "got"))
+    chain.land((out_gathers[0], "both"), (out_gathers[1], "chip"))
     first_grad = weight_grad(
-        token,
+        chain,
         [
             [([inputs_one[r]], qkv_grads[r]) for r in range(rows)],
-            [(grad_attendeds[r], mixed[r]) for r in range(rows)],
+            [(grad_gathers[r].pieces(), mixed[r]) for r in range(rows)],
         ],
         "grad_first",
     )
-    ring_sum = RingSum(first_grad, dp_count) if ring else None
-    token = tied(first_grad, one_parts[-1][1])
-    after_first = token
-
-    input_pieces, third_sums = [], []
-
-    def third_norm(r, token):
+    first_ring = RingSum(first_grad, dp_count)
+    one_parts[1].cross()
+    out_gathers[1].forward()
+    spare = 4 * slot_count
+    to = [field_slots(0), field_slots(1), field_slots(2), spare_slot(spare)]
+    to += [field_slots(3), spare_slot(spare + 1)]
+    far_slots = dot_as(slot_matrix(to, spare + 16), far_swap.whole(), DOT_NN)
+    far_slots = lax.dynamic_update_slice(
+        far_slots, up_sums.reshape(4, own_width), (spare + 2, 0)
+    ).astype(low)
+    far_gather = DoublingGather(far_slots, dp_count)
+
+    input_gathers, third_sums = [], []
+
+    def third_norm(r):
         input_own, sums = row_call(
             third_kernel,
             "third_norm",
-            token,
-            (tokens, *one_parts[r][0], grad_hiddens[r], near_tab[r]),
+            chain,
+            (tokens, *one_parts[r].terms(), grad_hiddens[r], near_tab[r]),
             [own_block(r)] + [here] * 4 + [own_table(near_tab)],
             (here, fixed_spec((8, width))),
             (lows(*block), wides(8, width)),
         )
-        input_pieces.append(group_gather(input_own))
+        input_gathers.append(GroupGather(input_own))
         third_sums.append(sums)
-        return tied(input_own)
-
-    def ring_hop(token):
-        return ring_sum.hop(token) if ring else token
-
-    for r in range(rows - 1):
-        token = third_norm(r, token)
-    if ring:
-        token = rest_ring.hop(token)
-    after_third = token
+
+    chain.land(*far_gather.flying(), (out_gathers[0], "core"), (out_gathers[1], "core"), (out_gathers[1], "both"))
+    third_norm(0)
+    far_gather.hop()
     at = jnp.stack(
         [(r * 4 + jnp.bitwise_xor(place, j)) * quarter for r in range(rows) for j in range(4)]
     ).astype(jnp.int32)
-    at = lax.optimization_barrier((at, token))[0]
-    out_tokens = place_pieces(at, out_pieces)
-    token = ring_hop(tied(out_tokens))
-    after_place = token
-    token = third_norm(rows - 1, token)
-
-    far_slots = dot_as(slot_matrix(4, 2, 16), far_swapped, DOT_NN)
-    far_slots = lax.dynamic_update_slice(
-        far_slots, up_sums.reshape(4, own_width), (4 * slot_count + 2, 0)
-    ).astype(low)
-    far_all = doubling_gather(far_slots, dp_count, (after_first, after_third, after_place))
-    far_all = far_all.reshape(dp_count, -1, own_width)
-    far_sum = jnp.sum(far_all.astype(wide), axis=0)
-    far_biases = jnp.sum(far_sum[: 4 * slot_count].reshape(4, slot_count, own_width), axis=1)
-    bias_up_sum = far_sum[4 * slot_count + 2 : 4 * slot_count + 6]
-    bias_rows_own = group_gather(far_sum[4 * slot_count : 4 * slot_count + 2].astype(low))
-    bias_rows_own = [bias_rows_own[0], bias_rows_own[2], bias_rows_own[1], bias_rows_own[3]]
-    bias_rows_sum = jnp.concatenate(in_group_order(bias_rows_own, mp_place), 1).astype(wide)
+    chain.land(*first_ring.flying(), (one_parts[1], "last"), *far_gather.flying())
+    out_tokens = place_pieces(chain, at, [x for gather in out_gathers for x in gather.pieces()])
+    first_ring.hop()
+    far_gather.hop()
+    third_norm(1)
+    near_swap = Exchange(jnp.concatenate(third_sums, 0))
 
     def columns_of(ref, at):
         return column(ref[...], at, own_width).astype(wide)
@@ -1216,14 +1320,10 @@
     cols_state = (weight_cols, first_cols, second_cols, ema_cols)
     rows_state = [x.transpose(0, 2, 1) for x in (weight_rows, first_rows, second_rows, ema_rows)]
 
-    if ring:
-        rest_sum = rest_ring.total()
-    else:
-        rest_sum = lax.psum_scatter(rest_grad, "dp", scatter_dimension=0, tiled=True)
-
-    near_rows = jnp.concatenate(third_sums, 0)
+    rest_sum = rest_ring.total()
+    chain.land(*first_ring.flying(), *far_gather.flying(), (near_swap, "other"), (input_gathers[0], "chip"))
     cols_new = adam_slabs(
-        token,
+        chain,
         [(0, i) for i in (5, 6, 7, 8)],
         (rest_sum,),
         lambda n, refs: columns_of(refs[0], n),
@@ -1231,10 +1331,12 @@
         [None],
         "adam_up",
     )
-    token = ring_hop(tied(cols_new[0]))
-    near_swapped = exchange(near_rows, token)
+    first_ring.hop()
+    near_swap.cross()
+    input_gathers[0].forward()
+    chain.land(*first_ring.flying(), (near_swap, "other"), (input_gathers[1], "chip"), (input_gathers[0], "core"))
     rows_new = adam_slabs(
-        token,
+        chain,
         [(0, i) for i in (1, 2, 3, 4)],
         (rest_sum,),
         lambda n, refs: columns_of(refs[0], 4 + n),
@@ -1242,10 +1344,31 @@
         [None],
         "adam_down",
     )
-    token = ring_hop(tied(rows_new[0]))
-    after_down = token
+    first_ring.hop()
+    input_gathers[1].forward()
+    unit_sums = jnp.concatenate(time_sums, 0)
+    moved = row_slots.transpose(1, 0, 2).reshape(-1, 1) == jnp.arange(slot_count)[None, :]
+    moved = moved.astype(wide)
+    time_slots = lax.dot_general(moved, unit_sums, DOT_TN, precision=highest)
+    near_slots = jnp.concatenate(
+        [
+            dot_as(
+                slot_matrix([field_slots(0), field_slots(1)], 2 * slot_count), near_swap.whole(), DOT_NN
+            ),
+            time_slots[:, :own_width],
+            time_slots[:, 2 * own_width :],
+        ],
+        0,
+    ).astype(low)
+    near_gather = DoublingGather(near_slots, dp_count)
+    far_all = far_gather.whole()
+    far_sum = jnp.sum(far_all.astype(wide), axis=0)
+    far_biases = jnp.sum(far_sum[: 4 * slot_count].reshape(4, slot_count, own_width), axis=1)
+    bias_up_sum = far_sum[4 * slot_count + 2 : 4 * slot_count + 6]
+    bias_gather = GroupGather(far_sum[4 * slot_count : 4 * slot_count + 2].astype(low))
+    chain.land(*near_gather.flying(), (input_gathers[0], "both"), (input_gathers[1], "core"), (bias_gather, "chip"))
     cols_new = adam_slabs(
-        token,
+        chain,
         [(0, i) for i in (11, 12, 13, 14)],
         (ada_low, far_all),
         lambda n, refs: map_grad(refs[0], refs[1], n),
@@ -1253,36 +1376,22 @@
         [cols_new],
         "adam_far",
     )
-    token = tied(cols_new[0])
-    after_far = token
+    near_gather.hop()
+    bias_gather.forward()
     input_grads = ()
     for r in range(rows):
-        input_grads = (widen_row(token, input_pieces[r], r, rows, input_grads),)
-        token = tied(input_grads[0])
         if r == 0:
-            after_widen = token
-
-    unit_sums = jnp.concatenate(time_sums, 0)
-    moved = by_place.transpose(1, 0, 2, 3).reshape(rows, units, slots)
-    moved = moved[:, :, None, :] & jnp.eye(rows, dtype=bool)[:, None, :, None]
-    moved = moved.reshape(rows * units, slot_count).astype(wide)
-    time_slots = lax.dot_general(moved, unit_sums, DOT_TN, precision=highest)
-    near_slots = jnp.concatenate(
-        [
-            dot_as(slot_matrix(2, 0, 0), near_swapped, DOT_NN),
-            time_slots[:, :own_width],
-            time_slots[:, 2 * own_width :],
-        ],
-        0,
-    ).astype(low)
-    near_all = doubling_gather(near_slots, dp_count, (after_down, after_far, after_widen))
-    near_all = near_all.reshape(dp_count, -1, own_width)
+            chain.land(*near_gather.flying(), (input_gathers[1], "both"), *first_ring.flying()[: 1 if dp_count == 8 else 2])
+        else:
+            chain.land(*near_gather.flying(), (bias_gather, "core"), (bias_gather, "both"))
+        input_grads = (widen_row(chain, input_gathers[r].pieces(), r, rows, input_grads),)
+        near_gather.hop()
+
+    near_all = near_gather.whole()
     near_sum = jnp.sum(near_all.astype(wide).reshape(dp_count, 4, slot_count, own_width), axis=(0, 2))
     bias_cols_sum = jnp.concatenate([near_sum[2:4], bias_up_sum, near_sum[:2], far_biases], 0)
-    if ring:
-        first_sum = ring_sum.total()
-    else:
-        first_sum = lax.psum_scatter(first_grad, "dp", scatter_dimension=0, tiled=True)
+    bias_rows_sum = jnp.concatenate(bias_gather.in_order(mp_place), 1).astype(wide)
+    first_sum = first_ring.total()
 
     def late_grad(n, refs):
         ada, time, near, first = refs
@@ -1291,7 +1400,7 @@
         return columns_of(first, n - 4)
 
     new = adam_slabs(
-        token,
+        chain,
         [(0, i) for i in (9, 10, 3, 4, 0, 1, 2)] + [(1, 0)],
         (ada_low, time_low, near_all, first_sum),
         late_grad,

time: 570 us -> 502 us (0.88)
  local copies, waits for them, and re-layouts: 54.5 us -> 35.4 us
  between operations: 16.8 us -> 2.77 us
  waiting for transfers between devices: 83.9 us -> 70.8 us
  starting transfers between devices: 86 us -> 77.9 us
  other arithmetic: 38.6 us -> 31.8 us
    ppermute x81, waiting for transfers between devices: 79.2 us -> 48.3 us  [the longest x8 10.8 us: cross(): self.last = lax.ppermute(passed, 'mp', CHIP_SWAP)]
    ppermute x3, waiting for transfers between devices: 0.01 us -> 12.5 us  [share_hop(): lax.ppermute(known, 'dp', [(i, i ^ reach) for i in range(count)])]
    ppermute x6, waiting for transfers between devices: 0.66 us -> 6.97 us  [send(): self.behind = lax.ppermute(behind.astype(low), 'dp', self.backward)]
    dot_general x10 -> x5, matrix products: 9.43 us -> 3.23 us  [dot_as(): return lax.dot_general(left, right, dims, preferred_element_type=wide)]
    unnamed x188 -> x208, local copies, waits for them, and re-layouts: 12.7 us -> 10.1 us
  transfers between devices with their start and end apart: 98 -> 98, of which waited for: 22 -> 28; matrix products, arithmetic and copies ran while one was open for 15% -> 10% of each run, Pallas kernels for 47% -> 52%
where the time goes in v4:
time: 502 us; the launch traced here: 493 us
  Pallas kernels  269 us (54%)
  starting transfers between devices  77.9 us (16%)
  waiting for transfers between devices  70.8 us (14%)
  local copies, waits for them, and re-layouts  35.4 us (7%)
  other arithmetic  31.8 us (6%)
  matrix products  5.25 us (1%)
    pallas_call x30, Pallas kernels, row_call(): pl.pallas_call(body, grid_spec=pltpu.PrefetchScalarGridSpec(num_scalar_pr...  256 us
    pallas_call x3, Pallas kernels, place_pieces(): pl.pallas_call(place_kernel, out_shape=jax.ShapeDtypeStruct(whole, pieces...  13.4 us
    ppermute x3, waiting for transfers between devices, share_hop(): lax.ppermute(known, 'dp', [(i, i ^ reach) for i in range(count)])  12.5 us
    ppermute x11, starting transfers between devices, __init__(): self.chip = lax.ppermute(own, 'mp', CHIP_SWAP)  11.9 us
    ppermute x8, starting transfers between devices, send(): self.ahead = lax.ppermute(ahead, 'dp', self.onward)  11.1 us
    ppermute x8, waiting for transfers between devices, cross(): self.last = lax.ppermute(passed, 'mp', CHIP_SWAP)  10.8 us
    unnamed x208, local copies, waits for them, and re-layouts  10.1 us
  transfers between devices with their start and end apart: 98, of which 28 were waited for; matrix products, arithmetic and copies ran while one was open for 10% of the time, Pallas kernels for 52%

profile of v4, /device:TPU:0, one launch (start us, length us, event | category | flops | bytes accessed | tf_op | source)
XLA Modules:
  0.0 493.3 jit_solution(3380030721226732857)
XLA Ops:
  13.0 7.1 %collective-permute-done = s32[8,2,16]{2,1,0:T(2,128)S(1)} collective-permute-done((s32[8,2,16]{2,1,0:T(2,128)S(1)}, s32[8,2,16]{2,1,0:T(2,128)S(1)}, u32[]{:S(2)}, u32[]{:S(2)}) %collective-permute-start) | collective-permute-done | bytes 1056 | tf_op jit(solution)/shard_map/ppermute | solution.py:294
  34.8 6.0 %collective-permute-done.7 = bf16[4,32,1152]{2,1,0:T(8,128)(2,1)S(1)} collective-permute-done((bf16[4,32,1152]{2,1,0:T(8,128)(2,1)S(1)}, bf16[4,32,1152]{2,1,0:T(8,128)(2,1)S(1)}, u32[]{:S(2)}, u32[]{:S(2)}) %collective-permute-start.7) | collective-permute-done | bytes 294944 | tf_op jit(solution)/shard_map/ppermute | solution.py:250
  68.0 7.3 %collective-permute-done.15.refs_7_ = bf16[64,1152]{1,0:T(8,128)(2,1)S(1)} collective-permute-done((bf16[64,1152]{1,0:T(8,128)(2,1)}, bf16[64,1152]{1,0:T(8,128)(2,1)S(1)}, u32[]{:S(2)}, u32[]{:S(2)}) %collective-permute-start.15) | collective-permute-done | bytes 147488 | tf_op jit(solution)/shard_map/ppermute | solution.py:271
  84.2 7.7 %open_row.2 = (bf16[1024,1152]{1,0:T(8,128)(2,1)}, bf16[1024,864]{1,0:T(8,128)(2,1)}) custom-call(s32[1]{0:T(128)} %bitcast.place_ref.refs_0_, bf16[2048,1152]{1,0:T(8,128)(2,1)} %x_ref.7, bf16[2048,1152]{1,0:T(8,128)(2,1)} %x_ref.7, f32[4,4,2304]{2,1,0:T(4,128)} %squeeze.148.tab0_ref.tab1_ref.tab_ref, f32[4,4,2304]{2,1,0:T(4,128)} %squeeze.148.tab0_ref.tab1_ref.tab_ref, ...), custom_call_target="tpu_custom_call" | custom-call | flops 1 | bytes 1 | tf_op jit(solution)/shard_map/open_row/pallas_call | solution.py:653
  96.7 12.8 %attend_forward.2 = (bf16[1024,288]{1,0:T(8,128)(2,1)}, f32[512,1152]{1,0:T(8,128)}, bf16[512,1152]{1,0:T(8,128)(2,1)}) custom-call(s32[1]{0:T(128)} %bitcast.place_ref.refs_0_, bf16[1024,864]{1,0:T(8,128)(2,1)} %get-tuple-element.336.refs_1_, s32[1024,1]{1,0:T(8,128)} %copy.120.refs_2_.refs_6_, s32[1,1024]{1,0:T(1,128)} %bitcast.208, ...), custom_call_target="tpu_custom_call" | custom-call | flops 1 | bytes 1 | tf_op jit(solution)/shard_map/attend_forward/pallas_call | solution.py:653
  115.3 7.6 %open_row.3 = (bf16[1024,1152]{1,0:T(8,128)(2,1)}, bf16[1024,864]{1,0:T(8,128)(2,1)}) custom-call(s32[1]{0:T(128)} %bitcast.place_ref.refs_0_, bf16[2048,1152]{1,0:T(8,128)(2,1)} %x_ref.7, bf16[2048,1152]{1,0:T(8,128)(2,1)} %x_ref.7, f32[4,4,2304]{2,1,0:T(4,128)} %squeeze.151.tab0_ref.tab1_ref.tab_ref, f32[4,4,2304]{2,1,0:T(4,128)} %squeeze.151.tab0_ref.tab1_ref.tab_ref, ...), custom_call_target="tpu_custom_call" | custom-call | flops 1 | bytes 1 | tf_op jit(solution)/shard_map/open_row/pallas_call | solution.py:653
  133.8 12.8 %attend_forward.3 = (bf16[1024,288]{1,0:T(8,128)(2,1)}, f32[512,1152]{1,0:T(8,128)}, bf16[512,1152]{1,0:T(8,128)(2,1)}) custom-call(s32[1]{0:T(128)} %bitcast.place_ref.refs_0_, bf16[1024,864]{1,0:T(8,128)(2,1)} %get-tuple-element.356.refs_1_, s32[1024,1]{1,0:T(8,128)} %copy.121.refs_2_.refs_6_, s32[1,1024]{1,0:T(1,128)} %bitcast.205, ...), custom_call_target="tpu_custom_call" | custom-call | flops 1 | bytes 1 | tf_op jit(solution)/shard_map/attend_forward/pallas_call | solution.py:653
  153.1 5.4 %place_pieces.4.w_ref = bf16[1152,2304]{1,0:T(8,128)(2,1)} custom-call(s32[9]{0:T(128)} %fusion.59.at_ref, bf16[144,2304]{1,0:T(8,128)(2,1)} %copy-done.17, bf16[144,2304]{1,0:T(8,128)(2,1)} %collective-permute-done.18.refs_1_, bf16[144,2304]{1,0:T(8,128)(2,1)} %copy-done.42, bf16[144,2304]{1,0:T(8,128)(2,1)} %collective-permute-done.22.refs_3_, ...), custom_call_target="tpu_custom_call" | custom-call | bytes 1 | tf_op jit(solution)/shard_map/place_pieces/pallas_call | solution.py:98
  160.0 7.5 %down_back.2 = (bf16[1024,1152]{1,0:T(8,128)(2,1)}, bf16[1024,1152]{1,0:T(8,128)(2,1)}) custom-call(s32[1]{0:T(128)} %bitcast.place_ref.refs_0_, bf16[2048,1152]{1,0:T(8,128)(2,1)} %cot_ref.7, bf16[2048,1152]{1,0:T(8,128)(2,1)} %cot_ref.7, f32[4,4,4608]{2,1,0:T(4,128)} %squeeze.155.tab_ref.tab0_ref.tab1_ref, ...), custom_call_target="tpu_custom_call" | custom-call | flops 1 | bytes 1 | tf_op jit(solution)/shard_map/down_back/pallas_call | solution.py:653
  169.9 7.2 %down_back.3 = (bf16[1024,1152]{1,0:T(8,128)(2,1)}, bf16[1024,1152]{1,0:T(8,128)(2,1)}) custom-call(s32[1]{0:T(128)} %bitcast.place_ref.refs_0_, bf16[2048,1152]{1,0:T(8,128)(2,1)} %cot_ref.7, bf16[2048,1152]{1,0:T(8,128)(2,1)} %cot_ref.7, f32[4,4,4608]{2,1,0:T(4,128)} %squeeze.156.tab0_ref.tab1_ref.tab_ref, ...), custom_call_target="tpu_custom_call" | custom-call | flops 1 | bytes 1 | tf_op jit(solution)/shard_map/down_back/pallas_call | solution.py:653
  186.6 15.4 %up_and_back.2 = (bf16[1024,1152]{1,0:T(8,128)(2,1)}, bf16[1024,1152]{1,0:T(8,128)(2,1)}, f32[512,1152]{1,0:T(8,128)}, bf16[512,1152]{1,0:T(8,128)(2,1)}, f32[2,8,1152]{2,1,0:T(8,128)}) custom-call(s32[1]{0:T(128)} %bitcast.place_ref.refs_0_, bf16[256,1152]{1,0:T(8,128)(2,1)} %get-tuple-element.380.a0_ref.refs_0_, bf16[256,1152]{1,0:T(8,128)(2,1)} %copy-done.27, ...), custom_call_target="tpu_custom_call" | custom-call | flops 1 | bytes 1 | tf_op jit(solution)/shard_map/up_and_back/pallas_call | solution.py:653
  202.7 8.5 %down.2 = (f32[512,1152]{1,0:T(8,128)}, bf16[512,1152]{1,0:T(8,128)(2,1)}) custom-call(s32[1]{0:T(128)} %bitcast.place_ref.refs_0_, bf16[1024,1152]{1,0:T(8,128)(2,1)} %get-tuple-element.403.m_ref.refs_11_, bf16[1152,2304]{1,0:T(8,128)(2,1)} %place_pieces.4.w_ref), custom_call_target="tpu_custom_call" | custom-call | flops 1 | bytes 1 | tf_op jit(solution)/shard_map/down/pallas_call | solution.py:653
  213.9 15.6 %up_and_back.3 = (bf16[1024,1152]{1,0:T(8,128)(2,1)}, bf16[1024,1152]{1,0:T(8,128)(2,1)}, f32[512,1152]{1,0:T(8,128)}, bf16[512,1152]{1,0:T(8,128)(2,1)}, f32[2,8,1152]{2,1,0:T(8,128)}) custom-call(s32[1]{0:T(128)} %bitcast.place_ref.refs_0_, bf16[256,1152]{1,0:T(8,128)(2,1)} %get-tuple-element.401.a0_ref.refs_5_, bf16[256,1152]{1,0:T(8,128)(2,1)} %copy-done.30, ...), custom_call_target="tpu_custom_call" | custom-call | flops 1 | bytes 1 | tf_op jit(solution)/shard_map/up_and_back/pallas_call | solution.py:653
  231.3 7.9 %down.3 = (f32[512,1152]{1,0:T(8,128)}, bf16[512,1152]{1,0:T(8,128)(2,1)}) custom-call(s32[1]{0:T(128)} %bitcast.place_ref.refs_0_, bf16[1024,1152]{1,0:T(8,128)(2,1)} %get-tuple-element.421.m_ref.refs_13_, bf16[1152,2304]{1,0:T(8,128)(2,1)} %place_pieces.4.w_ref), custom_call_target="tpu_custom_call" | custom-call | flops 1 | bytes 1 | tf_op jit(solution)/shard_map/down/pallas_call | solution.py:653
  239.2 7.1 %collective-permute-done.45.passed_ref = bf16[256,1152]{1,0:T(8,128)(2,1)S(1)} collective-permute-done((bf16[256,1152]{1,0:T(8,128)(2,1)S(1)}, bf16[256,1152]{1,0:T(8,128)(2,1)S(1)}, u32[]{:S(2)}, u32[]{:S(2)}) %collective-permute-start.45) | collective-permute-done | bytes 589856 | tf_op jit(solution)/shard_map/ppermute | solution.py:181
  247.8 5.1 %second_norm.2 = (f32[256,1152]{1,0:T(8,128)}, bf16[256,1152]{1,0:T(8,128)(2,1)}, f32[16,1152]{1,0:T(8,128)}) custom-call(s32[1]{0:T(128)} %bitcast.place_ref.refs_0_, bf16[2048,1152]{1,0:T(8,128)(2,1)} %cot_ref.7, f32[512,1152]{1,0:T(8,128)} %get-tuple-element.417.kept_ref, bf16[512,1152]{1,0:T(8,128)(2,1)} %copy-done.14, bf16[256,1152]{1,0:T(8,128)(2,1)} %copy-done.57, ...), custom_call_target="tpu_custom_call" | custom-call | flops 1 | bytes 1 | tf_op jit(solution)/shard_map/second_norm/pallas_call | solution.py:653
  254.7 19.2 %grad_rest.1 = bf16[1152,2304]{1,0:T(8,128)(2,1)} custom-call(s32[1]{0:T(128)} %bitcast.place_ref.refs_0_, bf16[256,1152]{1,0:T(8,128)(2,1)} %get-tuple-element.380.a0_ref.refs_0_, bf16[256,1152]{1,0:T(8,128)(2,1)} %copy-done.27, bf16[256,1152]{1,0:T(8,128)(2,1)} %copy-done.26, bf16[256,1152]{1,0:T(8,128)(2,1)} %copy-done.28, ...), custom_call_target="tpu_custom_call" | custom-call | flops 1 | bytes 1 | tf_op jit(solution)/shard_map/grad_rest/pallas_call | solution.py:653
  280.3 5.1 %second_norm.3 = (f32[256,1152]{1,0:T(8,128)}, bf16[256,1152]{1,0:T(8,128)(2,1)}, f32[16,1152]{1,0:T(8,128)}) custom-call(s32[1]{0:T(128)} %bitcast.place_ref.refs_0_, bf16[2048,1152]{1,0:T(8,128)(2,1)} %cot_ref.7, f32[512,1152]{1,0:T(8,128)} %get-tuple-element.440.kept_ref, bf16[512,1152]{1,0:T(8,128)(2,1)} %copy-done.12, bf16[256,1152]{1,0:T(8,128)(2,1)} %copy-done.50, ...), custom_call_target="tpu_custom_call" | custom-call | flops 1 | bytes 1 | tf_op jit(solution)/shard_map/second_norm/pallas_call | solution.py:653
  285.5 3.8 out_tokens.2
  289.3 5.8 %collective-permute-done.52 = bf16[144,2304]{1,0:T(8,128)(2,1)S(1)} collective-permute-done((bf16[144,2304]{1,0:T(8,128)(2,1)}, bf16[144,2304]{1,0:T(8,128)(2,1)S(1)}, u32[]{:S(2)}, u32[]{:S(2)}) %collective-permute-start.52) | collective-permute-done | bytes 663584 | tf_op jit(solution)/shard_map/ppermute | solution.py:153
  302.7 21.0 %attend_backward.2 = (bf16[1024,864]{1,0:T(8,128)(2,1)}, f32[512,1152]{1,0:T(8,128)}, bf16[512,1152]{1,0:T(8,128)(2,1)}, f32[16,864]{1,0:T(8,128)}) custom-call(s32[1]{0:T(128)} %bitcast.place_ref.refs_0_, bf16[1024,864]{1,0:T(8,128)(2,1)} %get-tuple-element.336.refs_1_, bf16[256,1152]{1,0:T(8,128)(2,1)} %get-tuple-element.442.refs_2_.refs_4_, ...), custom_call_target="tpu_custom_call" | custom-call | flops 1 | bytes 1 | tf_op jit(solution)/shard_map/attend_backward/pallas_call | solution.py:653
  341.1 21.2 %attend_backward.3 = (bf16[1024,864]{1,0:T(8,128)(2,1)}, f32[512,1152]{1,0:T(8,128)}, bf16[512,1152]{1,0:T(8,128)(2,1)}, f32[16,864]{1,0:T(8,128)}) custom-call(s32[1]{0:T(128)} %bitcast.place_ref.refs_0_, bf16[1024,864]{1,0:T(8,128)(2,1)} %get-tuple-element.356.refs_1_, bf16[256,1152]{1,0:T(8,128)(2,1)} %get-tuple-element.465.refs_2_.refs_9_, ...), custom_call_target="tpu_custom_call" | custom-call | flops 1 | bytes 1 | tf_op jit(solution)/shard_map/attend_backward/pallas_call | solution.py:653
  370.7 13.1 %grad_first.1 = bf16[1152,1152]{1,0:T(8,128)(2,1)} custom-call(s32[1]{0:T(128)} %bitcast.place_ref.refs_0_, bf16[1024,1152]{1,0:T(8,128)(2,1)} %get-tuple-element.491.refs_0_, bf16[1024,864]{1,0:T(8,128)(2,1)} %get-tuple-element.492.refs_1_, bf16[1024,1152]{1,0:T(8,128)(2,1)} %get-tuple-element.493.refs_2_, bf16[1024,864]{1,0:T(8,128)(2,1)} %get-tuple-element.494.refs_3_, ...), custom_call_target="tpu_custom_call" | custom-call | flops 1 | bytes 1 | tf_op jit(solution)/shard_map/grad_first/pallas_call | solution.py:653
  390.9 4.1 third_norm.2
  401.3 4.8 place_pieces.5
  409.9 4.1 third_norm.3
  425.6 6.7 %adam_up.1 = (f32[15,144,288]{2,1,0:T(8,128)}, f32[15,144,288]{2,1,0:T(8,128)}, f32[15,144,288]{2,1,0:T(8,128)}, f32[15,144,288]{2,1,0:T(8,128)}) custom-call(s32[4]{0:T(128)} %constant.352.clone.ids_ref, f32[144,2304]{1,0:T(8,128)} %convert_add_fusion.refs_0_, f32[15,144,288]{2,1,0:T(8,128)} %refs_4_.4, f32[15,144,288]{2,1,0:T(8,128)} %refs_5_.3, ...), custom_call_target="tpu_custom_call" | custom-call | flops 1 | bytes 1 | tf_op jit(solution)/shard_map/adam_up/pallas_call | solution.py:653
  441.2 6.6 %adam_down.1 = (f32[5,144,288]{2,1,0:T(8,128)}, f32[5,144,288]{2,1,0:T(8,128)}, f32[5,144,288]{2,1,0:T(8,128)}, f32[5,144,288]{2,1,0:T(8,128)}) custom-call(s32[4]{0:T(128)} %constant.353.clone.ids_ref, f32[144,2304]{1,0:T(8,128)} %convert_add_fusion.refs_0_, f32[5,144,288]{2,1,0:T(8,128)} %bitcast.178, f32[5,144,288]{2,1,0:T(8,128)} %bitcast.180, ...), custom_call_target="tpu_custom_call" | custom-call | flops 1 | bytes 1 | tf_op jit(solution)/shard_map/adam_down/pallas_call | solution.py:653
  455.2 6.7 %adam_far.1 = (f32[15,144,288]{2,1,0:T(8,128)}, f32[15,144,288]{2,1,0:T(8,128)}, f32[15,144,288]{2,1,0:T(8,128)}, f32[15,144,288]{2,1,0:T(8,128)}) custom-call(s32[4]{0:T(128)} %constant.354.clone.ids_ref, bf16[256,144]{1,0:T(8,128)(2,1)} %copy-done.32, ...), custom_call_target="tpu_custom_call", output_to_operand_aliasing={{0}: (7, {}), {1}: (8, {}), {2}: (9, {}), {3}: (10, {})} | custom-call | flops 1 | bytes 1 | tf_op jit(solution)/shard_map/adam_far/pallas_call | solution.py:653
  463.2 4.2 widen_row.2.refs_4_
  473.3 4.2 widen_row.3
  480.1 11.5 %adam_late.1 = (f32[15,144,288]{2,1,0:T(8,128)}, f32[15,144,288]{2,1,0:T(8,128)}, f32[15,144,288]{2,1,0:T(8,128)}, f32[15,144,288]{2,1,0:T(8,128)}, f32[5,144,28...) custom-call(s32[16]{0:T(128)} %constant.355.clone.ids_ref, ...), custom_call_target="tpu_custom_call", output_to_operand_aliasing={{0}: (13, {}), {1}: (14, {}), {2}: (15, {}), {3}: (16, {}),... | custom-call | flops 1 | bytes 1 | tf_op jit(solution)/shard_map/adam_late/pallas_call | solution.py:653
  (560 shorter events, 207.6 us)
Async XLA Ops:
  53.8 26.2 %collective-permute-start.19 = (bf16[144,2304]{1,0:T(8,128)(2,1)S(1)}, bf16[144,2304]{1,0:T(8,128)(2,1)S(1)}, u32[]{:S(2)}, u32[]{:S(2)}) collective-permute-start(bf16[144,2304]{1,0:T(8,128)(2,1)S(1)} %concatenate.77.refs_0_), channel_id=1, source_target_pairs={{8,0},{16,8},{24,16},{28,24},{20,28},{12,20},{4,12},{0,4},{9,1},{1... | collective-permute-start | bytes 1990664 | tf_op jit(solution)/shard_map/ppermute | solution.py:272
  54.6 25.4 %collective-permute-start.18 = (bf16[144,2304]{1,0:T(8,128)(2,1)S(1)}, bf16[144,2304]{1,0:T(8,128)(2,1)}, u32[]{:S(2)}, u32[]{:S(2)}) collective-permute-start(bf16[144,2304]{1,0:T(8,128)(2,1)S(1)} %concatenate.77.refs_0_), channel_id=1, source_target_pairs={{0,8},{8,16},{16,24},{24,28},{28,20},{20,12},{12,4},{4,0},{1,9},{9... | collective-permute-start | bytes 1990664 | tf_op jit(solution)/shard_map/ppermute | solution.py:271
  60.4 19.5 %collective-permute-start.17 = (bf16[4,32,1152]{2,1,0:T(8,128)(2,1)S(1)}, bf16[4,32,1152]{2,1,0:T(8,128)(2,1)S(1)}, u32[]{:S(2)}, u32[]{:S(2)}) collective-permute-start(bf16[4,32,1152]{2,1,0:T(8,128)(2,1)S(1)} %dynamic-slice_bitcast_fusion), channel_id=1, source_target_pairs={{0,4},{4,0},{8,12},{12,8},{16,20},{20,16},{24,28},{28,24},{1,5},{5... | collective-permute-start | bytes 884744 | tf_op jit(solution)/shard_map/ppermute | solution.py:250
  81.7 27.7 %collective-permute-start.22 = (bf16[144,2304]{1,0:T(8,128)(2,1)}, bf16[144,2304]{1,0:T(8,128)(2,1)}, u32[]{:S(2)}, u32[]{:S(2)}) collective-permute-start(bf16[144,2304]{1,0:T(8,128)(2,1)} %collective-permute-done.18.refs_1_), channel_id=1, source_target_pairs={{0,8},{8,16},{16,24},{24,28},{28,20},{20,12},{12,4},{4,0},{1,9},{9... | collective-permute-start | bytes 1990664 | tf_op jit(solution)/shard_map/ppermute | solution.py:271
  82.9 26.6 %collective-permute-start.23 = (bf16[144,2304]{1,0:T(8,128)(2,1)S(1)}, bf16[144,2304]{1,0:T(8,128)(2,1)S(1)}, u32[]{:S(2)}, u32[]{:S(2)}) collective-permute-start(bf16[144,2304]{1,0:T(8,128)(2,1)S(1)} %collective-permute-done.19.refs_2_), channel_id=1, source_target_pairs={{8,0},{16,8},{24,16},{28,24},{20,28},{12,20},{4,12},{0,4},{9,1},{1... | collective-permute-start | bytes 1990664 | tf_op jit(solution)/shard_map/ppermute | solution.py:272
  92.0 17.5 %collective-permute-start.21 = (bf16[1,32,1152]{2,1,0:T(8,128)(2,1)S(1)}, bf16[1,32,1152]{2,1,0:T(8,128)(2,1)S(1)}, u32[]{:S(2)}, u32[]{:S(2)}) collective-permute-start(bf16[1,32,1152]{2,1,0:T(8,128)(2,1)S(1)} %dynamic-slice_convert_fusion), channel_id=1, source_target_pairs={{0,16},{4,20},{8,24},{12,28},{16,0},{20,4},{24,8},{28,12},{1,17},{... | collective-permute-start | bytes 221192 | tf_op jit(solution)/shard_map/ppermute | solution.py:250
  113.1 16.8 %collective-permute-start.28 = (bf16[144,2304]{1,0:T(8,128)(2,1)}, bf16[144,2304]{1,0:T(8,128)(2,1)S(1)}, u32[]{:S(2)}, u32[]{:S(2)}) collective-permute-start(bf16[144,2304]{1,0:T(8,128)(2,1)} %collective-permute-done.22.refs_3_), channel_id=1, source_target_pairs={{0,8},{8,16},{16,24},{24,28},{28,20},{20,12},{12,4},{4,0},{1,9},{9... | collective-permute-start | bytes 1990664 | tf_op jit(solution)/shard_map/ppermute | solution.py:271
  124.0 22.7 %collective-permute-start.32 = (bf16[256,1152]{1,0:T(8,128)(2,1)}, bf16[256,1152]{1,0:T(8,128)(2,1)}, u32[]{:S(2)}, u32[]{:S(2)}) collective-permute-start(bf16[256,1152]{1,0:T(8,128)(2,1)} %add_convert_fusion.12), channel_id=1, source_target_pairs={{0,2},{1,3},{2,0},{3,1},{4,6},{5,7},{6,4},{7,5},{8,10},{9,11},{10,... | collective-permute-start | bytes 1769480 | tf_op jit(solution)/shard_map/ppermute | solution.py:181
  158.6 22.1 %collective-permute-start.37 = (bf16[256,1152]{1,0:T(8,128)(2,1)S(1)}, bf16[256,1152]{1,0:T(8,128)(2,1)S(1)}, u32[]{:S(2)}, u32[]{:S(2)}) collective-permute-start(bf16[256,1152]{1,0:T(8,128)(2,1)S(1)} %add_convert_fusion.11), channel_id=1, source_target_pairs={{0,2},{1,3},{2,0},{3,1},{4,6},{5,7},{6,4},{7,5},{8,10},{9,11},{10,... | collective-permute-start | bytes 1769480 | tf_op jit(solution)/shard_map/ppermute | solution.py:181
  212.0 17.5 %collective-permute-start.43 = (bf16[512,1152]{1,0:T(8,128)(2,1)}, bf16[512,1152]{1,0:T(8,128)(2,1)S(1)}, u32[]{:S(2)}, u32[]{:S(2)}) collective-permute-start(bf16[512,1152]{1,0:T(8,128)(2,1)} %get-tuple-element.419), channel_id=1, source_target_pairs={{0,1},{1,0},{2,3},{3,2},{4,5},{5,4},{6,7},{7,6},{8,9},{9,8},{10,11... | collective-permute-start | bytes 3538952 | tf_op jit(solution)/shard_map/ppermute | solution.py:176
  212.3 17.2 %collective-permute-start.42 = (bf16[256,1152]{1,0:T(8,128)(2,1)S(1)}, bf16[256,1152]{1,0:T(8,128)(2,1)S(1)}, u32[]{:S(2)}, u32[]{:S(2)}) collective-permute-start(bf16[256,1152]{1,0:T(8,128)(2,1)S(1)} %add_convert_fusion.10), channel_id=1, source_target_pairs={{0,2},{1,3},{2,0},{3,1},{4,6},{5,7},{6,4},{7,5},{8,10},{9,11},{10,... | collective-permute-start | bytes 1769480 | tf_op jit(solution)/shard_map/ppermute | solution.py:181
  247.2 26.7 %collective-permute-start.47 = (bf16[256,1152]{1,0:T(8,128)(2,1)S(1)}, bf16[256,1152]{1,0:T(8,128)(2,1)S(1)}, u32[]{:S(2)}, u32[]{:S(2)}) collective-permute-start(bf16[256,1152]{1,0:T(8,128)(2,1)S(1)} %add_convert_fusion.8), channel_id=1, source_target_pairs={{0,2},{1,3},{2,0},{3,1},{4,6},{5,7},{6,4},{7,5},{8,10},{9,11},{10,... | collective-permute-start | bytes 1769480 | tf_op jit(solution)/shard_map/ppermute | solution.py:181
  252.9 21.0 %collective-permute-start.49 = (bf16[256,1152]{1,0:T(8,128)(2,1)}, bf16[256,1152]{1,0:T(8,128)(2,1)S(1)}, u32[]{:S(2)}, u32[]{:S(2)}) collective-permute-start(bf16[256,1152]{1,0:T(8,128)(2,1)} %get-tuple-element.442.refs_2_.refs_4_), channel_id=1, source_target_pairs={{0,1},{1,0},{2,3},{3,2},{4,5},{5,4},{6,7},{7,6},{8,9},{9,8},{10,11... | collective-permute-start | bytes 1769480 | tf_op jit(solution)/shard_map/ppermute | solution.py:191
  253.2 22.5 %collective-permute-start.48 = (bf16[256,1152]{1,0:T(8,128)(2,1)}, bf16[256,1152]{1,0:T(8,128)(2,1)S(1)}, u32[]{:S(2)}, u32[]{:S(2)}) collective-permute-start(bf16[256,1152]{1,0:T(8,128)(2,1)} %get-tuple-element.442.refs_2_.refs_4_), channel_id=1, source_target_pairs={{0,2},{1,3},{2,0},{3,1},{4,6},{5,7},{6,4},{7,5},{8,10},{9,11},{10,... | collective-permute-start | bytes 1769480 | tf_op jit(solution)/shard_map/ppermute | solution.py:190
  298.0 28.5 %collective-permute-start.54 = (bf16[144,2304]{1,0:T(8,128)(2,1)S(1)}, bf16[144,2304]{1,0:T(8,128)(2,1)S(1)}, u32[]{:S(2)}, u32[]{:S(2)}) collective-permute-start(bf16[144,2304]{1,0:T(8,128)(2,1)S(1)} %get-tuple-element.618), channel_id=1, source_target_pairs={{8,0},{16,8},{24,16},{28,24},{20,28},{12,20},{4,12},{0,4},{9,1},{1... | collective-permute-start | bytes 1990664 | tf_op jit(solution)/shard_map/ppermute | solution.py:153
  299.5 27.0 %collective-permute-start.53 = (bf16[144,2304]{1,0:T(8,128)(2,1)S(1)}, bf16[144,2304]{1,0:T(8,128)(2,1)S(1)}, u32[]{:S(2)}, u32[]{:S(2)}) collective-permute-start(bf16[144,2304]{1,0:T(8,128)(2,1)S(1)} %get-tuple-element.619), channel_id=1, source_target_pairs={{0,8},{8,16},{16,24},{24,28},{28,20},{20,12},{12,4},{4,0},{1,9},{9... | collective-permute-start | bytes 1990664 | tf_op jit(solution)/shard_map/ppermute | solution.py:151
  300.6 23.1 %collective-permute-start.57 = (bf16[256,1152]{1,0:T(8,128)(2,1)S(1)}, bf16[256,1152]{1,0:T(8,128)(2,1)S(1)}, u32[]{:S(2)}, u32[]{:S(2)}) collective-permute-start(bf16[256,1152]{1,0:T(8,128)(2,1)S(1)} %add_convert_fusion.7), channel_id=1, source_target_pairs={{0,2},{1,3},{2,0},{3,1},{4,6},{5,7},{6,4},{7,5},{8,10},{9,11},{10,... | collective-permute-start | bytes 1769480 | tf_op jit(solution)/shard_map/ppermute | solution.py:181
  301.2 22.5 %collective-permute-start.56 = (bf16[256,1152]{1,0:T(8,128)(2,1)S(1)}, bf16[256,1152]{1,0:T(8,128)(2,1)S(1)}, u32[]{:S(2)}, u32[]{:S(2)}) collective-permute-start(bf16[256,1152]{1,0:T(8,128)(2,1)S(1)} %copy-done.21), channel_id=1, source_target_pairs={{0,1},{1,0},{2,3},{3,2},{4,5},{5,4},{6,7},{7,6},{8,9},{9,8},{10,11... | collective-permute-start | bytes 1769480 | tf_op jit(solution)/shard_map/ppermute | solution.py:191
  301.2 25.3 %collective-permute-start.55 = (bf16[256,1152]{1,0:T(8,128)(2,1)S(1)}, bf16[256,1152]{1,0:T(8,128)(2,1)S(1)}, u32[]{:S(2)}, u32[]{:S(2)}) collective-permute-start(bf16[256,1152]{1,0:T(8,128)(2,1)S(1)} %copy-done.21), channel_id=1, source_target_pairs={{0,2},{1,3},{2,0},{3,1},{4,6},{5,7},{6,4},{7,5},{8,10},{9,11},{10,... | collective-permute-start | bytes 1769480 | tf_op jit(solution)/shard_map/ppermute | solution.py:190
  328.3 34.1 %collective-permute-start.62 = (bf16[256,1152]{1,0:T(8,128)(2,1)}, bf16[256,1152]{1,0:T(8,128)(2,1)}, u32[]{:S(2)}, u32[]{:S(2)}) collective-permute-start(bf16[256,1152]{1,0:T(8,128)(2,1)} %get-tuple-element.483.refs_0_), channel_id=1, source_target_pairs={{0,2},{1,3},{2,0},{3,1},{4,6},{5,7},{6,4},{7,5},{8,10},{9,11},{10,... | collective-permute-start | bytes 1769480 | tf_op jit(solution)/shard_map/ppermute | solution.py:190
  332.2 31.4 %collective-permute-start.61 = (bf16[144,2304]{1,0:T(8,128)(2,1)}, bf16[144,2304]{1,0:T(8,128)(2,1)}, u32[]{:S(2)}, u32[]{:S(2)}) collective-permute-start(bf16[144,2304]{1,0:T(8,128)(2,1)} %get-tuple-element.616), channel_id=1, source_target_pairs={{8,0},{16,8},{24,16},{28,24},{20,28},{12,20},{4,12},{0,4},{9,1},{1... | collective-permute-start | bytes 1990664 | tf_op jit(solution)/shard_map/ppermute | solution.py:153
  333.7 29.9 %collective-permute-start.60 = (bf16[144,2304]{1,0:T(8,128)(2,1)}, bf16[144,2304]{1,0:T(8,128)(2,1)}, u32[]{:S(2)}, u32[]{:S(2)}) collective-permute-start(bf16[144,2304]{1,0:T(8,128)(2,1)} %get-tuple-element.617), channel_id=1, source_target_pairs={{0,8},{8,16},{16,24},{24,28},{28,20},{20,12},{12,4},{4,0},{1,9},{9... | collective-permute-start | bytes 1990664 | tf_op jit(solution)/shard_map/ppermute | solution.py:151
  338.1 25.5 %collective-permute-start.63 = (bf16[256,1152]{1,0:T(8,128)(2,1)S(1)}, bf16[256,1152]{1,0:T(8,128)(2,1)S(1)}, u32[]{:S(2)}, u32[]{:S(2)}) collective-permute-start(bf16[256,1152]{1,0:T(8,128)(2,1)S(1)} %add_convert_fusion.6), channel_id=1, source_target_pairs={{0,2},{1,3},{2,0},{3,1},{4,6},{5,7},{6,4},{7,5},{8,10},{9,11},{10,... | collective-permute-start | bytes 1769480 | tf_op jit(solution)/shard_map/ppermute | solution.py:181
  339.9 23.7 %collective-permute-start.64 = (bf16[48,576]{1,0:T(8,128)(2,1)S(1)}, bf16[48,576]{1,0:T(8,128)(2,1)S(1)}, u32[]{:S(2)}, u32[]{:S(2)}) collective-permute-start(bf16[48,576]{1,0:T(8,128)(2,1)S(1)} %get-tuple-element.666), channel_id=1, source_target_pairs={{0,2},{1,3},{2,0},{3,1},{4,6},{5,7},{6,4},{7,5},{8,10},{9,11},{10,... | collective-permute-start | bytes 165896 | tf_op jit(solution)/shard_map/ppermute | solution.py:1207
  362.4 21.4 %collective-permute-start.69 = (bf16[256,1152]{1,0:T(8,128)(2,1)}, bf16[256,1152]{1,0:T(8,128)(2,1)S(1)}, u32[]{:S(2)}, u32[]{:S(2)}) collective-permute-start(bf16[256,1152]{1,0:T(8,128)(2,1)} %get-tuple-element.501.refs_4_), channel_id=1, source_target_pairs={{0,2},{1,3},{2,0},{3,1},{4,6},{5,7},{6,4},{7,5},{8,10},{9,11},{10,... | collective-permute-start | bytes 1769480 | tf_op jit(solution)/shard_map/ppermute | solution.py:190
  363.6 20.7 %collective-permute-start.68 = (bf16[256,1152]{1,0:T(8,128)(2,1)}, bf16[256,1152]{1,0:T(8,128)(2,1)}, u32[]{:S(2)}, u32[]{:S(2)}) collective-permute-start(bf16[256,1152]{1,0:T(8,128)(2,1)} %collective-permute-done.62.refs_1_), channel_id=1, source_target_pairs={{0,1},{1,0},{2,3},{3,2},{4,5},{5,4},{6,7},{7,6},{8,9},{9,8},{10,11... | collective-permute-start | bytes 1769480 | tf_op jit(solution)/shard_map/ppermute | solution.py:194
  364.4 20.0 %collective-permute-start.67 = (bf16[512,1152]{1,0:T(8,128)(2,1)}, bf16[512,1152]{1,0:T(8,128)(2,1)S(1)}, u32[]{:S(2)}, u32[]{:S(2)}) collective-permute-start(bf16[512,1152]{1,0:T(8,128)(2,1)} %get-tuple-element.499), channel_id=1, source_target_pairs={{0,1},{1,0},{2,3},{3,2},{4,5},{5,4},{6,7},{7,6},{8,9},{9,8},{10,11... | collective-permute-start | bytes 3538952 | tf_op jit(solution)/shard_map/ppermute | solution.py:176
  365.9 18.5 %collective-permute-start.65 = (bf16[144,2304]{1,0:T(8,128)(2,1)S(1)}, bf16[144,2304]{1,0:T(8,128)(2,1)S(1)}, u32[]{:S(2)}, u32[]{:S(2)}) collective-permute-start(bf16[144,2304]{1,0:T(8,128)(2,1)S(1)} %add_convert_fusion), channel_id=1, source_target_pairs={{0,8},{8,16},{16,24},{24,28},{28,20},{20,12},{12,4},{4,0},{1,9},{9... | collective-permute-start | bytes 1990664 | tf_op jit(solution)/shard_map/ppermute | solution.py:151
  389.0 18.3 %collective-permute-start.76 = (bf16[256,1152]{1,0:T(8,128)(2,1)}, bf16[256,1152]{1,0:T(8,128)(2,1)S(1)}, u32[]{:S(2)}, u32[]{:S(2)}) collective-permute-start(bf16[256,1152]{1,0:T(8,128)(2,1)} %add_convert_fusion.5), channel_id=1, source_target_pairs={{0,2},{1,3},{2,0},{3,1},{4,6},{5,7},{6,4},{7,5},{8,10},{9,11},{10,... | collective-permute-start | bytes 1769480 | tf_op jit(solution)/shard_map/ppermute | solution.py:181
  400.2 35.1 %collective-permute-start.82 = (bf16[256,1152]{1,0:T(8,128)(2,1)}, bf16[256,1152]{1,0:T(8,128)(2,1)S(1)}, u32[]{:S(2)}, u32[]{:S(2)}) collective-permute-start(bf16[256,1152]{1,0:T(8,128)(2,1)} %get-tuple-element.542.refs_0_), channel_id=1, source_target_pairs={{0,2},{1,3},{2,0},{3,1},{4,6},{5,7},{6,4},{7,5},{8,10},{9,11},{10,... | collective-permute-start | bytes 1769480 | tf_op jit(solution)/shard_map/ppermute | solution.py:190
  414.9 17.4 %collective-permute-start.81 = (bf16[16,576]{1,0:T(8,128)(2,1)S(1)}, bf16[16,576]{1,0:T(8,128)(2,1)S(1)}, u32[]{:S(2)}, u32[]{:S(2)}) collective-permute-start(bf16[16,576]{1,0:T(8,128)(2,1)S(1)} %get-tuple-element.672), channel_id=1, source_target_pairs={{0,2},{1,3},{2,0},{3,1},{4,6},{5,7},{6,4},{7,5},{8,10},{9,11},{10,... | collective-permute-start | bytes 55304 | tf_op jit(solution)/shard_map/ppermute | solution.py:1207
  432.5 17.4 %collective-permute-start.86 = (bf16[256,1152]{1,0:T(8,128)(2,1)S(1)}, bf16[256,1152]{1,0:T(8,128)(2,1)}, u32[]{:S(2)}, u32[]{:S(2)}) collective-permute-start(bf16[256,1152]{1,0:T(8,128)(2,1)S(1)} %copy-done.46), channel_id=1, source_target_pairs={{0,2},{1,3},{2,0},{3,1},{4,6},{5,7},{6,4},{7,5},{8,10},{9,11},{10,... | collective-permute-start | bytes 1769480 | tf_op jit(solution)/shard_map/ppermute | solution.py:190
  (171 other events, 1473.8 us)

commit v5 on v4

--- a/solution.py
+++ b/solution.py
@@ -72,40 +72,39 @@
     return (at + jnp.array([0] * len(back) + [0, rows // 32 * 16])).astype(jnp.int32)
 
 
-def place_kernel(at_ref, *refs):
-    pieces, (out_ref, held, sem_in, sem_out) = refs[:-4], refs[-4:]
-    arrive, leave = [], []
-    base = 0
-    for i, piece in enumerate(pieces):
-        count = piece.shape[0]
-        spot = held.at[pl.ds(base, count)]
-        arrive.append(pltpu.make_async_copy(piece, spot, sem_in.at[i]))
-        to = out_ref.at[pl.ds(pl.multiple_of(at_ref[i], 16), count)]
-        leave.append(pltpu.make_async_copy(spot, to, sem_out.at[i]))
-        base += count
-    for copy in arrive:
-        copy.start()
-    for first, second in zip(arrive, leave):
-        first.wait()
-        second.start()
-    for copy in leave:
-        copy.wait()
-
-
-def place_pieces(chain, at, pieces):
-    whole = (sum(piece.shape[0] for piece in pieces),) + pieces[0].shape[1:]
+def place_pieces(chain, at, pieces, cuts=None):
+    parts = [(n, *cut) for n, piece in enumerate(pieces) for cut in cuts or [(0, piece.shape[0])]]
+    whole = (sum(count for _, _, count in parts),) + pieces[0].shape[1:]
     at = chain.tie(at)
+
+    def body(at_ref, *refs):
+        out_ref, held, sem_in, sem_out = refs[-4:]
+        arrive, leave = [], []
+        base = 0
+        for i, (n, start, count) in enumerate(parts):
+            spot = held.at[pl.ds(base, count)]
+            piece = refs[n].at[pl.ds(start, count)]
+            arrive.append(pltpu.make_async_copy(piece, spot, sem_in.at[i]))
+            to = out_ref.at[pl.ds(pl.multiple_of(at_ref[i], 16), count)]
+            leave.append(pltpu.make_async_copy(spot, to, sem_out.at[i]))
+            base += count
+        for copy in arrive:
+            copy.start()
+        for first, second in zip(arrive, leave):
+            first.wait()
+            second.start()
+        for copy in leave:
+            copy.wait()
+
     out = pl.pallas_call(
-        place_kernel,
+        body,
         out_shape=jax.ShapeDtypeStruct(whole, pieces[0].dtype),
         in_specs=[SMEM_SPEC] + [pl.BlockSpec(memory_space=pl.ANY)] * len(pieces),
         out_specs=pl.BlockSpec(memory_space=pl.ANY),
         scratch_shapes=[pltpu.VMEM(whole, pieces[0].dtype)]
-        + [pltpu.SemaphoreType.DMA((len(pieces),))] * 2,
+        + [pltpu.SemaphoreType.DMA((len(parts),))] * 2,
         compiler_params=pltpu.CompilerParams(vmem_limit_bytes=VMEM_GRANT),
-        cost_estimate=pl.CostEstimate(
-            flops=0, bytes_accessed=int(4 * COST * math.prod(whole)) + 1, transcendentals=0
-        ),
+        cost_estimate=pl.CostEstimate(flops=1, bytes_accessed=1, transcendentals=0),
         name="place_pieces",
     )(at, *pieces)
     return chain.close(out)
@@ -342,7 +341,7 @@
         out_ref[pl.ds(relative_at(place, j, block), block), :] = (
             jnp.concatenate(mixed, axis=0).T.astype(low)
         )
-    w_out = w_ref[:, 3 * width :]
+    w_out = w_ref[:, w_ref.shape[1] - width :]
     half = row_len // 2
     kept_ref[...] = dot_as(out_ref[:half, :], w_out, DOT_NT)
     sent_ref[...] = dot_as(out_ref[half:, :], w_out, DOT_NT).astype(low)
@@ -434,7 +433,8 @@
         "attend_forward",
         chain,
         args,
-        [fixed_spec(arg.shape) for arg in args],
+        [fixed_spec(arg.shape) for arg in args[:3]]
+        + [pl.BlockSpec((full, weights.shape[1] // 3), lambda i, p: (0, 2))],
         tuple(fixed_spec(shape.shape) for shape in shapes),
         shapes,
         scratch=[pltpu.VMEM((heads, row_len, HEAD_DIM), low)] * 3,
@@ -614,33 +614,47 @@
     sums_ref[12:13, :] = bias
 
 
-def out_kernel(
-    place_ref, cot_ref, kept_ref, got_ref, passed_ref, hid_ref, bias_ref, tab_ref, out_ref, sums_ref
-):
-    width = cot_ref.shape[1]
-    bias = jnp.zeros((1, width), wide)
+def out_kernel(place_ref, bias_ref, *refs):
+    rows = (len(refs) - 2) // 7
+    out_ref, sums_ref = refs[-2:]
+    quarter, width = refs[0].shape
+    total = jnp.zeros((1, width), wide)
+    other = jnp.zeros((1, width), wide)
     sums_ref[...] = jnp.zeros_like(sums_ref)
-    for u, at in unit_rows(cot_ref):
-        gate = column(tab_ref[0, u : u + 1, :], 3, width)
-        mlp = kept_ref[at, :] + got_ref[at, :].astype(wide) + passed_ref[at, :].astype(wide)
-        mlp = mlp + bias_ref[1:2, :]
-        out_ref[at, :] = (hid_ref[at, :] + gate * mlp).astype(low)
-        cot = cot_ref[at, :].astype(wide)
-        sums_ref[u : u + 1, :] = jnp.sum(cot * mlp, axis=0, keepdims=True)
-        bias = bias + jnp.sum(cot, axis=0, keepdims=True) * gate
-    sums_ref[4:5, :] = bias
-
-
-def third_kernel(place_ref, x_ref, kept_ref, got_ref, passed_ref, gh_ref, tab_ref, out_ref, sums_ref):
-    width = x_ref.shape[1]
-    for u, at in unit_rows(x_ref):
-        grad_one = kept_ref[at, :] + got_ref[at, :].astype(wide) + passed_ref[at, :].astype(wide)
-        normed, inverse = norm_parts(x_ref[at, :].astype(wide))
-        table = tab_ref[0, u : u + 1, :]
-        back = norm_back(normed, inverse, grad_one * (1.0 + column(table, 1, width)))
-        out_ref[at, :] = (gh_ref[at, :] + back).astype(low)
-        sums_ref[u : u + 1, :] = jnp.sum(grad_one, axis=0, keepdims=True)
-        sums_ref[4 + u : 5 + u, :] = jnp.sum(grad_one * normed, axis=0, keepdims=True)
+    for r in range(rows):
+        cot_ref, kept_ref, got_ref, passed_ref, hid_ref, tab_ref, second_ref = refs[7 * r : 7 * r + 7]
+        for u, at in unit_rows(cot_ref):
+            gate = column(tab_ref[0, u : u + 1, :], 3, width)
+            mlp = kept_ref[at, :] + got_ref[at, :].astype(wide) + passed_ref[at, :].astype(wide)
+            mlp = mlp + bias_ref[1:2, :]
+            out_ref[r * quarter + u * UNIT : r * quarter + (u + 1) * UNIT, :] = (
+                hid_ref[at, :] + gate * mlp
+            ).astype(low)
+            cot = cot_ref[at, :].astype(wide)
+            sums_ref[8 * r + u : 8 * r + u + 1, :] = jnp.sum(cot * mlp, axis=0, keepdims=True)
+            total = total + jnp.sum(cot, axis=0, keepdims=True) * gate
+        other = other + second_ref[12:13, :]
+    tail = jnp.concatenate([other, total, jnp.zeros((14, width), wide)], axis=0)
+    out_ref[rows * quarter :, :] = tail.astype(low)
+
+
+def third_kernel(place_ref, *refs):
+    rows = (len(refs) - 2) // 6
+    out_ref, sums_ref = refs[-2:]
+    quarter, width = refs[0].shape
+    for r in range(rows):
+        x_ref, kept_ref, got_ref, passed_ref, gh_ref, tab_ref = refs[6 * r : 6 * r + 6]
+        for u, at in unit_rows(x_ref):
+            grad_one = kept_ref[at, :] + got_ref[at, :].astype(wide) + passed_ref[at, :].astype(wide)
+            normed, inverse = norm_parts(x_ref[at, :].astype(wide))
+            table = tab_ref[0, u : u + 1, :]
+            back = norm_back(normed, inverse, grad_one * (1.0 + column(table, 1, width)))
+            out_ref[r * quarter + u * UNIT : r * quarter + (u + 1) * UNIT, :] = (
+                gh_ref[at, :] + back
+            ).astype(low)
+            n = 8 * r + u
+            sums_ref[n : n + 1, :] = jnp.sum(grad_one, axis=0, keepdims=True)
+            sums_ref[n + 4 : n + 5, :] = jnp.sum(grad_one * normed, axis=0, keepdims=True)
 
 
 def row_call(
@@ -674,9 +688,10 @@
     return pl.BlockSpec(shape, lambda *_: (0,) * len(shape))
 
 
-def unit_tables(chain, mp_arg, onehot, pieces, fields):
+def unit_tables(chain, mp_arg, onehot, pieces, fields, group):
     units, slots = onehot.shape
     own = pieces[0].shape[1] // fields
+    shape = (units // group, group, fields * 4 * own)
 
     def body(mp_ref, hot_ref, *refs):
         out_ref = refs[-1]
@@ -689,7 +704,9 @@
                 def _(spread=spread, j=j):
                     for f in range(fields):
                         at = f * 4 * own + j * own
-                        out_ref[:, at : at + own] = column(spread, f, own)
+                        values = column(spread, f, own)
+                        for n in range(units // group):
+                            out_ref[n, :, at : at + own] = values[n * group : (n + 1) * group, :]
 
     return row_call(
         body,
@@ -697,8 +714,8 @@
         chain,
         (onehot, *pieces),
         [fixed_spec(onehot.shape)] + [fixed_spec(pieces[0].shape)] * 4,
-        fixed_spec((units, fields * 4 * own)),
-        shape_of((units, fields * 4 * own), wide),
+        fixed_spec(shape),
+        shape_of(shape, wide),
         flops=8 * units * slots * own * fields,
         prefetch=mp_arg,
     )
@@ -746,27 +763,32 @@
     )
 
 
-def widen_row(chain, pieces, row, rows, before):
-    quarter, width = pieces[0].shape
+def widen_rows(chain, pieces, rows):
+    quarter, width = pieces[0].shape[0] // rows, pieces[0].shape[1]
 
     def body(place_ref, *refs):
-        step = pl.program_id(0)
-        for i, piece in enumerate(refs[:4]):
-
-            @pl.when(step == i)
-            def _(piece=piece):
-                refs[-1][...] = piece[...].astype(wide)
+        out_ref, wide_s, sems = refs[-3:]
+        copies = []
+        for r in range(rows):
+            for j, piece in enumerate(refs[:4]):
+                held = wide_s.at[r, j]
+                held[...] = piece[r * quarter : (r + 1) * quarter, :].astype(wide)
+                at = (r * 4 + jnp.bitwise_xor(place_ref[0], j)) * quarter
+                to = out_ref.at[pl.ds(pl.multiple_of(at, quarter), quarter)]
+                copies.append(pltpu.make_async_copy(held, to, sems.at[r, j]))
+                copies[-1].start()
+        for copy in copies:
+            copy.wait()
 
     return row_call(
         body,
-        "widen_row",
+        "widen_rows",
         chain,
-        tuple(pieces) + before,
-        [fixed_spec((quarter, width))] * 4 + [pl.BlockSpec(memory_space=pl.ANY)] * len(before),
-        pl.BlockSpec((quarter, width), lambda i, p: (row * 4 + jnp.bitwise_xor(p[0], i), 0)),
+        tuple(pieces),
+        [fixed_spec(pieces[0].shape)] * 4,
+        pl.BlockSpec(memory_space=pl.ANY),
         shape_of((rows * 4 * quarter, width), wide),
-        grid=4,
-        aliases={5: 0} if before else None,
+        scratch=[pltpu.VMEM((rows, 4, quarter, width), wide), pltpu.SemaphoreType.DMA((rows, 4))],
     )
 
 
@@ -785,53 +807,49 @@
 def adam_slabs(chain, plan, grads, make_grad, groups, before, name):
     slab = groups[0][0].shape[1:]
     count, held = len(plan), 4 * len(groups)
-    turns = [[i for i, (which, _) in enumerate(plan) if which == g] for g in range(len(groups))]
-    ids = [plan[max([i for i in mine if i <= n], default=mine[0])][1] for mine in turns for n in range(count)]
-    ids = jnp.array(ids, jnp.int32)
-
-    def block(group):
-        return pl.BlockSpec((1,) + slab, lambda i, ids: (ids[group * count + i], 0, 0))
-
-    def body(ids_ref, *refs):
+
+    def body(place_ref, *refs):
         grad_refs, state_refs = refs[: len(grads)], refs[len(grads) : len(grads) + held]
-        out_refs, grad_s = refs[-held - 1 : -1], refs[-1]
-        step = pl.program_id(0)
+        out_refs = refs[-held - 4 : -4]
+        old_s, new_s, arrive, leave = refs[-4:]
+        reads, writes = [], []
+        for n, (group, at) in enumerate(plan):
+            for i in range(4):
+                old = state_refs[4 * group + i].at[at]
+                reads.append(pltpu.make_async_copy(old, old_s.at[n, i], arrive.at[n, i]))
+                new = out_refs[4 * group + i].at[at]
+                writes.append(pltpu.make_async_copy(new_s.at[n, i], new, leave.at[n, i]))
+        for copy in reads:
+            copy.start()
         for n in range(count):
-
-            @pl.when(step == n)
-            def _(n=n):
-                grad_s[...] = make_grad(n, grad_refs)
-
-        for group, mine in enumerate(turns):
-
-            @pl.when((step >= mine[0]) & (step <= mine[-1]))
-            def _(group=group):
-                weight, *old = [ref[0] for ref in state_refs[4 * group : 4 * group + 4]]
-                new = adam_step(weight, grad_s[...], *old, rate_matrix)
-                for ref, value in zip(out_refs[4 * group : 4 * group + 4], new):
-                    ref[0] = value
+            grad = make_grad(n, grad_refs)
+            for copy in reads[4 * n : 4 * n + 4]:
+                copy.wait()
+            weight, *old = [old_s[n, i] for i in range(4)]
+            for i, value in enumerate(adam_step(weight, grad, *old, rate_matrix)):
+                new_s[n, i] = value
+            for copy in writes[4 * n : 4 * n + 4]:
+                copy.start()
+        for copy in writes:
+            copy.wait()
 
     flat = [x for group in groups for x in group]
-    specs = [block(g) for g in range(len(groups)) for _ in range(4)]
     kept, aliases = [], {}
     for g, arrays in enumerate(before):
         for i, x in enumerate(arrays or ()):
             aliases[1 + len(grads) + held + len(kept)] = 4 * g + i
             kept.append(x)
+    anywhere = pl.BlockSpec(memory_space=pl.ANY)
     return row_call(
         body,
         name,
         chain,
         (*grads, *flat, *kept),
-        [fixed_spec(grad.shape) for grad in grads]
-        + specs
-        + [pl.BlockSpec(memory_space=pl.ANY)] * len(kept),
-        tuple(specs),
+        [fixed_spec(grad.shape) for grad in grads] + [anywhere] * (held + len(kept)),
+        (anywhere,) * held,
         tuple(shape_of(x.shape, wide) for x in flat),
-        grid=count,
-        scratch=[pltpu.VMEM(slab, wide)],
+        scratch=[pltpu.VMEM((count, 4) + slab, wide)] * 2 + [pltpu.SemaphoreType.DMA((count, 4))] * 2,
         aliases=aliases,
-        prefetch=ids,
     )
 
 
@@ -905,6 +923,8 @@
         return out.reshape(dp_count, rows * slots, -1)
 
     if ring:
+        known = share_hop(known, 1, dp_count)
+        known, own_first = lax.optimization_barrier((known, own_first))
         first_gather = RingGather(own_first, dp_count)
 
         def beside(value):
@@ -915,7 +935,6 @@
                 first_gather.hop()
             return value
 
-        known = share_hop(known, 1, dp_count)
         known = beside(share_hop(known, 2, dp_count))
         if dp_count == 8:
             known = share_hop(known, 4, dp_count)
@@ -924,8 +943,10 @@
         near = HalvingSum(near, dp_count)
         near.hop()
         if dp_count == 8:
-            near.hop()
-        own_rest = beside(own_rest)
+            near.parts = beside(near.kept + near.got.astype(wide))
+            near.step *= 2
+            near.send()
+        near.got, own_rest = beside((near.got, own_rest))
         rest_gather = RingGather(own_rest, dp_count)
         near.hop()
         near = near.parts[0]
@@ -941,23 +962,53 @@
     onehot = unit_seg[:, :, None] == jnp.arange(slots, dtype=jnp.int32)
     blocks = onehot[:, :, None, :] & (jnp.arange(rows)[:, None] == jnp.arange(rows))[:, None, :, None]
     blocks = blocks.reshape(rows * units, rows * slots)
+    seg_place = unit_seg.reshape(rows, 4, own_units)
+    seg_place = jnp.stack(
+        [
+            lax.dynamic_index_in_dim(seg_place, jnp.bitwise_xor(place, j), 1, keepdims=False)
+            for j in range(4)
+        ],
+        0,
+    )
+    row_slots = seg_place + slots * jnp.arange(rows)[None, :, None]
+
+    def field_slots(field):
+        return row_slots + slot_count * field
+
+    def slot_matrix(to, height):
+        to = jnp.concatenate(to, 1).reshape(1, -1)
+        return (jnp.arange(height)[:, None] == to).astype(low)
+
+    spare = 4 * slot_count
+    far_to = []
+    for r in range(rows):
+        far_to += [field_slots(f)[:, r] for f in range(3)] + [jnp.full((4, own_units), -1)]
+    for r in range(rows):
+        far_to += [field_slots(3)[:, r], jnp.full((4, 4), -1)]
+    near_to = [field_slots(f)[:, r] for r in range(rows) for f in range(2)]
+    moved = row_slots.transpose(1, 0, 2).reshape(-1, 1) == jnp.arange(slot_count)[None, :]
+    quarters = [(r * 4 + jnp.bitwise_xor(place, j)) * quarter for j in range(4) for r in range(rows)]
+    hot, far_matrix, near_matrix, moved, at = chain.tie(
+        blocks.astype(low),
+        slot_matrix(far_to, spare + 16),
+        slot_matrix(near_to, 2 * slot_count),
+        moved.astype(wide),
+        jnp.stack(quarters).astype(jnp.int32),
+    )
+
     mp_arg = mp_place.astype(jnp.int32).reshape(1)
 
     def tables(spread, fields):
         spread.forward()
         pieces = [spread.own, spread.core, spread.chip, spread.both]
-        out = unit_tables(chain, mp_arg, blocks.astype(low), pieces, fields)
-        return out.reshape(rows, 4, own_units, -1)
+        return unit_tables(chain, mp_arg, hot, pieces, fields, own_units)
 
     far = slot_products([(lax.optimization_barrier((ada_low, near))[0], far_maps)])
     near_mod = (near[:, : 2 * own_width] + bias_cols[6:8].reshape(1, -1)).astype(low)
     near_tab = tables(GroupGather(near_mod), 2)
     if ring:
         far = HalvingSum(far, dp_count)
-        chain.land(*far.flying(), *rest_gather.flying())
         w_first = first_gather.place(chain)
-        far.hop()
-        rest_gather.hop()
     time_add = jnp.concatenate(
         [
             near[:, 2 * own_width : 3 * own_width] + bias_cols[0],
@@ -967,7 +1018,7 @@
         1,
     )
     add_tab = jnp.dot(blocks.astype(wide), time_add, precision=highest)
-    add_tab = add_tab.reshape(rows, 4, own_units, 3 * own_width)
+    add_tab = add_tab.reshape(rows * 4, own_units, 3 * own_width)
 
     block, half_block = (quarter, width), (row_len // 2, width)
     qkv_width = 3 * own_width
@@ -984,15 +1035,15 @@
             pl.BlockSpec(block, lambda i, p: (r * 4 + jnp.bitwise_xor(p[0], 2 * i + 1), 0)),
         ]
 
-    def moved_tables(tab):
-        shape = (1,) + tab.shape[2:]
+    def moved_tables(tab, r):
+        shape = (1,) + tab.shape[1:]
         return [
-            pl.BlockSpec(shape, lambda i, p: (jnp.bitwise_xor(p[0], 2 * i), 0, 0)),
-            pl.BlockSpec(shape, lambda i, p: (jnp.bitwise_xor(p[0], 2 * i + 1), 0, 0)),
+            pl.BlockSpec(shape, lambda i, p: (r * 4 + jnp.bitwise_xor(p[0], 2 * i), 0, 0)),
+            pl.BlockSpec(shape, lambda i, p: (r * 4 + jnp.bitwise_xor(p[0], 2 * i + 1), 0, 0)),
         ]
 
-    def own_table(tab):
-        return pl.BlockSpec((1,) + tab.shape[2:], lambda i, p: (p[0], 0, 0))
+    def own_table(tab, r):
+        return pl.BlockSpec((1,) + tab.shape[1:], lambda i, p: (r * 4 + p[0], 0, 0))
 
     here = fixed_spec(block)
     half_step = pl.BlockSpec(half_block, lambda i, p: (i, 0))
@@ -1003,8 +1054,8 @@
             open_kernel,
             "open_row",
             chain,
-            (tokens, tokens, near_tab[r], near_tab[r], add_tab[r], add_tab[r], w_first),
-            moved_blocks(r) + moved_tables(near_tab) + moved_tables(add_tab) + [fixed_spec(w_first.shape)],
+            (tokens, tokens, near_tab, near_tab, add_tab, add_tab, w_first),
+            moved_blocks(r) + moved_tables(near_tab, r) + moved_tables(add_tab, r) + [fixed_spec(w_first.shape)],
             (half_step, pl.BlockSpec((half, qkv_width), lambda i, p: (i, 0))),
             (lows(row_len, width), lows(row_len, qkv_width)),
             grid=2,
@@ -1012,41 +1063,48 @@
         )
 
     inputs_one, qkvs, mixed, parts = [], [], [], []
-    for r in range(rows):
-        if r == 0 and ring:
-            chain.land(*far.flying())
-        if r:
-            chain.land((parts[r - 1], "got"))
-        if r == 1:
-            chain.land(*far_gather.flying())
+
+    def open_attend(r, between):
         a_one, qkv = open_row(r)
         inputs_one.append(a_one)
         qkvs.append(qkv)
-        if r:
-            parts[r - 1].cross()
-        if r == 1:
-            if ring:
-                chain.land(*rest_gather.flying())
-            far_tab = tables(far_gather, 4)
-            if ring:
-                rest_gather.hop()
-                chain.land(*rest_gather.flying())
-        if r == 0 and ring:
-            far.hop()
-            chain.land(*far.flying(), *rest_gather.flying())
-        if r:
-            chain.land((parts[r - 1], "last"))
+        between()
         out, kept, sent = attend_forward(chain, qkv, seg_grid[r], w_first)
         mixed.append(out)
         parts.append(GroupSum(kept, sent))
-        if r == 0:
-            if ring:
-                rest_gather.hop()
-                far.hop()
-                far = far.parts[0]
-            else:
-                far = lax.psum_scatter(far, "dp", scatter_dimension=0, tiled=True)[0].astype(wide)
-            far_gather = GroupGather((far + bias_cols[8:12].reshape(1, -1)).astype(low))
+
+    def both_hop():
+        if ring:
+            far.hop()
+            rest_gather.hop()
+            chain.land(*far.flying(), *rest_gather.flying())
+
+    def far_spread():
+        held = far.parts[0] if ring else lax.psum_scatter(far, "dp", scatter_dimension=0, tiled=True)[0]
+        return GroupGather((held.astype(wide) + bias_cols[8:12].reshape(1, -1)).astype(low))
+
+    def second_between():
+        parts[0].cross()
+        chain.land((parts[0], "last"))
+        if ring:
+            far.hop()
+            chain.land(*rest_gather.flying())
+        spreads.append(far_spread())
+        chain.land(*spreads[0].flying())
+
+    spreads = []
+    if ring:
+        chain.land(*far.flying(), *rest_gather.flying())
+    open_attend(0, both_hop)
+    if ring:
+        far.hop()
+        rest_gather.hop()
+        chain.land(*far.flying())
+    chain.land((parts[0], "got"))
+    open_attend(1, second_between)
+    if ring:
+        rest_gather.hop()
+    far_tab = tables(spreads[0], 4)
 
     attendeds, hiddens, inputs_two, down_grads = [], [], [], []
 
@@ -1055,8 +1113,8 @@
             first_kernel,
             "first_norm",
             chain,
-            (tokens, *parts[r].terms(), bias_rows, far_tab[r]),
-            [own_block(r), here, here, here, fixed_spec(bias_rows.shape), own_table(far_tab)],
+            (tokens, *parts[r].terms(), bias_rows, far_tab),
+            [own_block(r), here, here, here, fixed_spec(bias_rows.shape), own_table(far_tab, r)],
             (here, here, here),
             (wides(*block), wides(*block), lows(*block)),
         )
@@ -1069,8 +1127,8 @@
             down_back_kernel,
             "down_back",
             chain,
-            (cotangent, cotangent, far_tab[r], far_tab[r], w_rest),
-            moved_blocks(r) + moved_tables(far_tab) + [w_down_spec],
+            (cotangent, cotangent, far_tab, far_tab, w_rest),
+            moved_blocks(r) + moved_tables(far_tab, r) + [w_down_spec],
             (half_step, half_step),
             (lows(row_len, width), lows(row_len, width)),
             grid=2,
@@ -1156,8 +1214,8 @@
             second_kernel,
             "second_norm",
             chain,
-            (cotangent, *up_parts[r].terms(), hiddens[r], attendeds[r], far_tab[r]),
-            [own_block(r)] + [here] * 5 + [own_table(far_tab)],
+            (cotangent, *up_parts[r].terms(), hiddens[r], attendeds[r], far_tab),
+            [own_block(r)] + [here] * 5 + [own_table(far_tab, r)],
             (here, here, fixed_spec((16, width))),
             (wides(*block), lows(*block), wides(16, width)),
         )
@@ -1182,20 +1240,21 @@
     chain.land((grad_gathers[0], "both"))
     second_norm(1)
 
-    out_gathers, out_sums = [], []
-
-    def out_row(r):
-        out_own, sums = row_call(
+    def out_rows():
+        args, specs = [bias_rows], [fixed_spec(bias_rows.shape)]
+        for r in range(rows):
+            args += [cotangent, *down_parts[r].terms(), hiddens[r], far_tab, second_sums[r]]
+            specs += [own_block(r)] + [here] * 4 + [own_table(far_tab, r), fixed_spec((16, width))]
+        own, sums = row_call(
             out_kernel,
             "out_tokens",
             chain,
-            (cotangent, *down_parts[r].terms(), hiddens[r], bias_rows, far_tab[r]),
-            [own_block(r)] + [here] * 4 + [fixed_spec(bias_rows.shape), own_table(far_tab)],
-            (here, fixed_spec((8, width))),
-            (lows(*block), wides(8, width)),
+            args,
+            specs,
+            (fixed_spec((rows * quarter + 16, width)), fixed_spec((8 * rows, width))),
+            (lows(rows * quarter + 16, width), wides(8 * rows, width)),
         )
-        out_gathers.append(GroupGather(out_own))
-        out_sums.append(sums)
+        return GroupGather(own), sums
 
     def part(held, which, columns):
         return lax.dynamic_slice_in_dim(held, which * columns, columns, 1)
@@ -1214,29 +1273,6 @@
         def whole(self):
             return jnp.concatenate([self.mine, self.other], 0)
 
-    seg_place = unit_seg.reshape(rows, 4, own_units)
-    seg_place = jnp.stack(
-        [
-            lax.dynamic_index_in_dim(seg_place, jnp.bitwise_xor(place, j), 1, keepdims=False)
-            for j in range(4)
-        ],
-        0,
-    )
-    row_slots = seg_place + slots * jnp.arange(rows)[None, :, None]
-
-    def field_slots(field):
-        return row_slots + slot_count * field
-
-    def slot_matrix(to, height):
-        to = jnp.concatenate(to, 2).reshape(1, -1)
-        return (jnp.arange(height)[:, None] == to).astype(low)
-
-    def spare_slot(slot):
-        return jnp.broadcast_to(jnp.array([slot, -1, -1, -1]), (4, rows, 4))
-
-    chain.land(*rest_ring.flying())
-    out_row(0)
-    rest_ring.hop()
     qkv_grads, one_parts, time_sums = [], [], []
 
     def backward(r):
@@ -1252,16 +1288,14 @@
     rest_ring.hop()
     grad_gathers[1].forward()
     chain.land((one_parts[0], "got"), (grad_gathers[1], "both"))
-    out_row(1)
+    out_gather, out_sums = out_rows()
     one_parts[0].cross()
-    far_swap = Exchange(jnp.concatenate([x for pair in zip(second_sums, out_sums) for x in pair], 0))
-    chain.land(*rest_ring.flying(), (out_gathers[0], "chip"), (one_parts[0], "last"), (far_swap, "other"))
+    far_swap = Exchange(jnp.concatenate(second_sums + [out_sums], 0))
+    last_hop = slice(0, 1 if dp_count == 8 else 2)
+    chain.land(*rest_ring.flying(), (one_parts[0], "last"), (out_gather, "core"))
     backward(1)
     rest_ring.hop()
-    far_swap.cross()
-    out_gathers[0].forward()
-    chain.land(*rest_ring.flying()[: 1 if dp_count == 8 else 2], (far_swap, "other"), (one_parts[1], "got"))
-    chain.land((out_gathers[0], "both"), (out_gathers[1], "chip"))
+    chain.land(*rest_ring.flying(), (one_parts[1], "got"), (out_gather, "chip"), (far_swap, "other"))
     first_grad = weight_grad(
         chain,
         [
@@ -1272,43 +1306,44 @@
     )
     first_ring = RingSum(first_grad, dp_count)
     one_parts[1].cross()
-    out_gathers[1].forward()
-    spare = 4 * slot_count
-    to = [field_slots(0), field_slots(1), field_slots(2), spare_slot(spare)]
-    to += [field_slots(3), spare_slot(spare + 1)]
-    far_slots = dot_as(slot_matrix(to, spare + 16), far_swap.whole(), DOT_NN)
+    rest_ring.hop()
+    out_gather.forward()
+    far_swap.cross()
+
+    cols_state = (weight_cols, first_cols, second_cols, ema_cols)
+    rows_state = [x.transpose(0, 2, 1) for x in (weight_rows, first_rows, second_rows, ema_rows)]
+    cuts = [(r * quarter, quarter) for r in range(rows)]
+    chain.land((out_gather, "both"), (far_swap, "other"))
+    third_args, third_specs = [], []
+    for r in range(rows):
+        third_args += [tokens, *one_parts[r].terms(), grad_hiddens[r], near_tab]
+        third_specs += [own_block(r)] + [here] * 4 + [own_table(near_tab, r)]
+    out_tokens = place_pieces(chain, at, out_gather.pieces(), cuts)
+    far_slots = dot_as(far_matrix, far_swap.whole(), DOT_NN)
+    own, across, core_own, core_across = [
+        x[rows * quarter : rows * quarter + 2].astype(wide) for x in out_gather.pieces()
+    ]
+    bias_part = (own + across) + (core_own + core_across)
     far_slots = lax.dynamic_update_slice(
-        far_slots, up_sums.reshape(4, own_width), (spare + 2, 0)
+        far_slots,
+        jnp.concatenate([up_sums.reshape(4, own_width), bias_part.reshape(8, own_width)], 0),
+        (spare, 0),
     ).astype(low)
     far_gather = DoublingGather(far_slots, dp_count)
-
-    input_gathers, third_sums = [], []
-
-    def third_norm(r):
-        input_own, sums = row_call(
-            third_kernel,
-            "third_norm",
-            chain,
-            (tokens, *one_parts[r].terms(), grad_hiddens[r], near_tab[r]),
-            [own_block(r)] + [here] * 4 + [own_table(near_tab)],
-            (here, fixed_spec((8, width))),
-            (lows(*block), wides(8, width)),
-        )
-        input_gathers.append(GroupGather(input_own))
-        third_sums.append(sums)
-
-    chain.land(*far_gather.flying(), (out_gathers[0], "core"), (out_gathers[1], "core"), (out_gathers[1], "both"))
-    third_norm(0)
-    far_gather.hop()
-    at = jnp.stack(
-        [(r * 4 + jnp.bitwise_xor(place, j)) * quarter for r in range(rows) for j in range(4)]
-    ).astype(jnp.int32)
-    chain.land(*first_ring.flying(), (one_parts[1], "last"), *far_gather.flying())
-    out_tokens = place_pieces(chain, at, [x for gather in out_gathers for x in gather.pieces()])
+    chain.land(*first_ring.flying(), *rest_ring.flying()[last_hop], *far_gather.flying())
+    input_own, third_sums = row_call(
+        third_kernel,
+        "third_norm",
+        chain,
+        third_args,
+        third_specs,
+        (fixed_spec((rows * quarter, width)), fixed_spec((8 * rows, width))),
+        (lows(rows * quarter, width), wides(8 * rows, width)),
+    )
     first_ring.hop()
     far_gather.hop()
-    third_norm(1)
-    near_swap = Exchange(jnp.concatenate(third_sums, 0))
+    input_gather = GroupGather(input_own)
+    near_swap = Exchange(third_sums)
 
     def columns_of(ref, at):
         return column(ref[...], at, own_width).astype(wide)
@@ -1317,11 +1352,8 @@
         right = right[:, field * slot_count : (field + 1) * slot_count, :]
         return dot_as(left[...], right.reshape(-1, own_width), DOT_TN)
 
-    cols_state = (weight_cols, first_cols, second_cols, ema_cols)
-    rows_state = [x.transpose(0, 2, 1) for x in (weight_rows, first_rows, second_rows, ema_rows)]
-
     rest_sum = rest_ring.total()
-    chain.land(*first_ring.flying(), *far_gather.flying(), (near_swap, "other"), (input_gathers[0], "chip"))
+    chain.land(*first_ring.flying(), *far_gather.flying(), (near_swap, "other"))
     cols_new = adam_slabs(
         chain,
         [(0, i) for i in (5, 6, 7, 8)],
@@ -1333,8 +1365,8 @@
     )
     first_ring.hop()
     near_swap.cross()
-    input_gathers[0].forward()
-    chain.land(*first_ring.flying(), (near_swap, "other"), (input_gathers[1], "chip"), (input_gathers[0], "core"))
+    far_gather.hop()
+    chain.land(*first_ring.flying(), (near_swap, "other"), *far_gather.flying())
     rows_new = adam_slabs(
         chain,
         [(0, i) for i in (1, 2, 3, 4)],
@@ -1345,28 +1377,19 @@
         "adam_down",
     )
     first_ring.hop()
-    input_gathers[1].forward()
+    far_all = far_gather.whole()
     unit_sums = jnp.concatenate(time_sums, 0)
-    moved = row_slots.transpose(1, 0, 2).reshape(-1, 1) == jnp.arange(slot_count)[None, :]
-    moved = moved.astype(wide)
     time_slots = lax.dot_general(moved, unit_sums, DOT_TN, precision=highest)
     near_slots = jnp.concatenate(
         [
-            dot_as(
-                slot_matrix([field_slots(0), field_slots(1)], 2 * slot_count), near_swap.whole(), DOT_NN
-            ),
+            dot_as(near_matrix, near_swap.whole(), DOT_NN),
             time_slots[:, :own_width],
             time_slots[:, 2 * own_width :],
         ],
         0,
     ).astype(low)
     near_gather = DoublingGather(near_slots, dp_count)
-    far_all = far_gather.whole()
-    far_sum = jnp.sum(far_all.astype(wide), axis=0)
-    far_biases = jnp.sum(far_sum[: 4 * slot_count].reshape(4, slot_count, own_width), axis=1)
-    bias_up_sum = far_sum[4 * slot_count + 2 : 4 * slot_count + 6]
-    bias_gather = GroupGather(far_sum[4 * slot_count : 4 * slot_count + 2].astype(low))
-    chain.land(*near_gather.flying(), (input_gathers[0], "both"), (input_gathers[1], "core"), (bias_gather, "chip"))
+    chain.land(*near_gather.flying(), *first_ring.flying()[last_hop], (input_gather, "chip"))
     cols_new = adam_slabs(
         chain,
         [(0, i) for i in (11, 12, 13, 14)],
@@ -1377,45 +1400,45 @@
         "adam_far",
     )
     near_gather.hop()
-    bias_gather.forward()
-    input_grads = ()
-    for r in range(rows):
-        if r == 0:
-            chain.land(*near_gather.flying(), (input_gathers[1], "both"), *first_ring.flying()[: 1 if dp_count == 8 else 2])
-        else:
-            chain.land(*near_gather.flying(), (bias_gather, "core"), (bias_gather, "both"))
-        input_grads = (widen_row(chain, input_gathers[r].pieces(), r, rows, input_grads),)
-        near_gather.hop()
-
+    input_gather.forward()
+    first_sum = first_ring.total()
+    chain.land(*near_gather.flying(), (input_gather, "core"), (input_gather, "both"))
+    new = adam_slabs(
+        chain,
+        [(0, i) for i in (0, 1, 2)] + [(1, 0)],
+        (first_sum,),
+        lambda n, refs: columns_of(refs[0], n),
+        [cols_state, rows_state],
+        [cols_new, rows_new],
+        "adam_first",
+    )
+    cols_new, rows_new = new[:4], [x.transpose(0, 2, 1) for x in new[4:]]
+    near_gather.hop()
+    chain.land(*near_gather.flying())
+    input_grads = widen_rows(chain, input_gather.pieces(), rows)
     near_all = near_gather.whole()
+    cols_new = adam_slabs(
+        chain,
+        [(0, i) for i in (9, 10, 3, 4)],
+        (ada_low, time_low, near_all),
+        lambda n, refs: map_grad(refs[n // 2], refs[2], n),
+        [cols_state],
+        [cols_new],
+        "adam_near",
+    )
+    far_sum = jnp.sum(far_all.astype(wide), axis=0)
+    far_biases = jnp.sum(far_sum[:spare].reshape(4, slot_count, own_width), axis=1)
+    bias_up_sum = far_sum[spare : spare + 4]
+    bias_rows_sum = far_sum[spare + 4 : spare + 12].reshape(2, width)
     near_sum = jnp.sum(near_all.astype(wide).reshape(dp_count, 4, slot_count, own_width), axis=(0, 2))
     bias_cols_sum = jnp.concatenate([near_sum[2:4], bias_up_sum, near_sum[:2], far_biases], 0)
-    bias_rows_sum = jnp.concatenate(bias_gather.in_order(mp_place), 1).astype(wide)
-    first_sum = first_ring.total()
-
-    def late_grad(n, refs):
-        ada, time, near, first = refs
-        if n < 4:
-            return map_grad(ada if n < 2 else time, near, n)
-        return columns_of(first, n - 4)
-
-    new = adam_slabs(
-        chain,
-        [(0, i) for i in (9, 10, 3, 4, 0, 1, 2)] + [(1, 0)],
-        (ada_low, time_low, near_all, first_sum),
-        late_grad,
-        [cols_state, rows_state],
-        [cols_new, rows_new],
-        "adam_late",
-    )
-    cols_new, rows_new = new[:4], [x.transpose(0, 2, 1) for x in new[4:]]
     bias_cols_new = adam_step(
         bias_cols, bias_cols_sum, first_bias_cols, second_bias_cols, ema_bias_cols, rate_vector
     )
     bias_rows_new = adam_step(
         bias_rows, bias_rows_sum, first_bias_rows, second_bias_rows, ema_bias_rows, rate_vector
     )
-    return (out_tokens, input_grads[0], *cols_new, *rows_new, *bias_cols_new, *bias_rows_new)
+    return (out_tokens, input_grads, *cols_new, *rows_new, *bias_cols_new, *bias_rows_new)
 
 
 def solution(mesh):

time: 502 us -> 484 us (0.964)
  Pallas kernels: 269 us -> 257 us
  local copies, waits for them, and re-layouts: 35.4 us -> 29.2 us
    pallas_call x30 -> x28, Pallas kernels: 256 us -> 244 us  [row_call(): pl.pallas_call(body, grid_spec=pltpu.PrefetchScalarGridSpec(num_scalar_pr...]
    ppermute x3, waiting for transfers between devices: 12.5 us -> 5.22 us  [share_hop(): lax.ppermute(known, 'dp', [(i, i ^ reach) for i in range(count)])]
    ppermute x6, waiting for transfers between devices: 8.65 us -> 14.1 us  [send(): self.got = lax.ppermute(sent, 'dp', swap)]
    ppermute x6, waiting for transfers between devices: 6.97 us -> 1.55 us  [send(): self.behind = lax.ppermute(behind.astype(low), 'dp', self.backward)]
    ppermute x11 -> x8, starting transfers between devices: 11.9 us -> 8.84 us  [__init__(): self.chip = lax.ppermute(own, 'mp', CHIP_SWAP)]
    unnamed x208 -> x172, local copies, waits for them, and re-layouts: 10.1 us -> 9.65 us
  transfers between devices with their start and end apart: 98 -> 89, of which waited for: 28 -> 24; matrix products, arithmetic and copies ran while one was open for 10% -> 11% of each run, Pallas kernels for 52% -> 52%
where the time goes in v5:
time: 484 us; the launch traced here: 474 us
  Pallas kernels  257 us (53%)
  starting transfers between devices  80.6 us (17%)
  waiting for transfers between devices  66.6 us (14%)
  other arithmetic  34 us (7%)
  local copies, waits for them, and re-layouts  29.2 us (6%)
    pallas_call x28, Pallas kernels, row_call(): pl.pallas_call(body, grid_spec=pltpu.PrefetchScalarGridSpec(num_scalar_pr...  244 us
    ppermute x6, waiting for transfers between devices, send(): self.got = lax.ppermute(sent, 'dp', swap)  14.1 us
    pallas_call x3, Pallas kernels, place_pieces(): pl.pallas_call(body, out_shape=jax.ShapeDtypeStruct(whole, pieces[0].dtyp...  13.3 us
    ppermute x6, starting transfers between devices, send(): self.got = lax.ppermute(self.known, 'dp', swap)  11.5 us
    ppermute x8, waiting for transfers between devices, cross(): self.last = lax.ppermute(passed, 'mp', CHIP_SWAP)  11.4 us
    ppermute x8, waiting for transfers between devices, send(): self.ahead = lax.ppermute(ahead, 'dp', self.onward)  10.8 us
    ppermute x8, starting transfers between devices, send(): self.ahead = lax.ppermute(ahead.astype(low), 'dp', self.onward)  9.92 us
  transfers between devices with their start and end apart: 89, of which 24 were waited for; matrix products, arithmetic and copies ran while one was open for 11% of the time, Pallas kernels for 52%

profile of v5, /device:TPU:0, one launch (start us, length us, event | category | flops | bytes accessed | tf_op | source)
XLA Modules:
  0.0 474.5 jit_solution(3188674539857356644)
XLA Ops:
  14.7 5.2 %collective-permute-done.1 = s32[8,2,16]{2,1,0:T(2,128)S(1)} collective-permute-done((s32[8,2,16]{2,1,0:T(2,128)S(1)}, s32[8,2,16]{2,1,0:T(2,128)S(1)}, u32[]{:S(2)}, u32[]{:S(2)}) %collective-permute-start.1) | collective-permute-done | bytes 1056 | tf_op jit(solution)/shard_map/ppermute | solution.py:293
  46.5 6.2 %collective-permute-done.9.refs_5_ = bf16[144,1152]{1,0:T(8,128)(2,1)S(1)} collective-permute-done((bf16[144,1152]{1,0:T(8,128)(2,1)}, bf16[144,1152]{1,0:T(8,128)(2,1)S(1)}, u32[]{:S(2)}, u32[]{:S(2)}) %collective-permute-start.9) | collective-permute-done | bytes 331808 | tf_op jit(solution)/shard_map/ppermute | solution.py:270
  76.5 7.7 %open_row.2 = (bf16[1024,1152]{1,0:T(8,128)(2,1)}, bf16[1024,864]{1,0:T(8,128)(2,1)}) custom-call(s32[1]{0:T(128)} %bitcast.place_ref.refs_0_, bf16[2048,1152]{1,0:T(8,128)(2,1)} %refs_6_.2, bf16[2048,1152]{1,0:T(8,128)(2,1)} %refs_6_.2, f32[8,4,2304]{2,1,0:T(4,128)} %unit_tables.2.tab0_ref.tab1_ref.refs_5_.refs_11_, ...), custom_call_target="tpu_custom_call" | custom-call | flops 1 | bytes 1 | tf_op jit(solution)/shard_map/open_row/pallas_call | solution.py:667
  84.2 5.3 %collective-permute-done.17 = bf16[4,32,1152]{2,1,0:T(8,128)(2,1)S(1)} collective-permute-done((bf16[4,32,1152]{2,1,0:T(8,128)(2,1)S(1)}, bf16[4,32,1152]{2,1,0:T(8,128)(2,1)S(1)}, u32[]{:S(2)}, u32[]{:S(2)}) %collective-permute-start.17) | collective-permute-done | bytes 294944 | tf_op jit(solution)/shard_map/ppermute | solution.py:249
  93.1 12.2 %attend_forward.2 = (bf16[1024,288]{1,0:T(8,128)(2,1)}, f32[512,1152]{1,0:T(8,128)}, bf16[512,1152]{1,0:T(8,128)(2,1)}) custom-call(s32[1]{0:T(128)} %bitcast.place_ref.refs_0_, bf16[1024,864]{1,0:T(8,128)(2,1)} %get-tuple-element.343.refs_1_, s32[1024,1]{1,0:T(8,128)} %copy.138.refs_2_.refs_6_, s32[1,1024]{1,0:T(1,128)} %bitcast.207, ...), custom_call_target="tpu_custom_call" | custom-call | flops 1 | bytes 1 | tf_op jit(solution)/shard_map/attend_forward/pallas_call | solution.py:667
  114.3 7.6 %open_row.3 = (bf16[1024,1152]{1,0:T(8,128)(2,1)}, bf16[1024,864]{1,0:T(8,128)(2,1)}) custom-call(s32[1]{0:T(128)} %bitcast.place_ref.refs_0_, bf16[2048,1152]{1,0:T(8,128)(2,1)} %refs_6_.2, bf16[2048,1152]{1,0:T(8,128)(2,1)} %refs_6_.2, f32[8,4,2304]{2,1,0:T(4,128)} %unit_tables.2.tab0_ref.tab1_ref.refs_5_.refs_11_, ...), custom_call_target="tpu_custom_call" | custom-call | flops 1 | bytes 1 | tf_op jit(solution)/shard_map/open_row/pallas_call | solution.py:667
  125.5 12.2 %attend_forward.3 = (bf16[1024,288]{1,0:T(8,128)(2,1)}, f32[512,1152]{1,0:T(8,128)}, bf16[512,1152]{1,0:T(8,128)(2,1)}) custom-call(s32[1]{0:T(128)} %bitcast.place_ref.refs_0_, bf16[1024,864]{1,0:T(8,128)(2,1)} %get-tuple-element.356.refs_1_, s32[1024,1]{1,0:T(8,128)} %copy.143.refs_2_.refs_6_, s32[1,1024]{1,0:T(1,128)} %bitcast.204, ...), custom_call_target="tpu_custom_call" | custom-call | flops 1 | bytes 1 | tf_op jit(solution)/shard_map/attend_forward/pallas_call | solution.py:667
  154.2 5.2 %place_pieces.4.w_ref = bf16[1152,2304]{1,0:T(8,128)(2,1)} custom-call(s32[9]{0:T(128)} %fusion.53.at_ref, bf16[144,2304]{1,0:T(8,128)(2,1)} %copy-done.16, bf16[144,2304]{1,0:T(8,128)(2,1)} %copy-done.40, bf16[144,2304]{1,0:T(8,128)(2,1)} %copy-done.39, bf16[144,2304]{1,0:T(8,128)(2,1)} %copy-done.41, bf16[144,2304]{1,0:T(8,128)(2,1)} %collective-permute-done.22.refs_4_, ...), custom_call_target="tpu_custom_call" | custom-call | flops 1 | bytes 1 | tf_op jit(solution)/shard_map/place_pieces/pallas_call | solution.py:99
  161.1 7.1 %down_back.2 = (bf16[1024,1152]{1,0:T(8,128)(2,1)}, bf16[1024,1152]{1,0:T(8,128)(2,1)}) custom-call(s32[1]{0:T(128)} %bitcast.place_ref.refs_0_, bf16[2048,1152]{1,0:T(8,128)(2,1)} %refs_7_.1, bf16[2048,1152]{1,0:T(8,128)(2,1)} %refs_7_.1, f32[8,4,4608]{2,1,0:T(4,128)} %unit_tables.3.tab_ref.tab0_ref.tab1_ref.refs_5_.refs_12_, ...), custom_call_target="tpu_custom_call" | custom-call | flops 1 | bytes 1 | tf_op jit(solution)/shard_map/down_back/pallas_call | solution.py:667
  168.6 7.3 %down_back.3 = (bf16[1024,1152]{1,0:T(8,128)(2,1)}, bf16[1024,1152]{1,0:T(8,128)(2,1)}) custom-call(s32[1]{0:T(128)} %bitcast.place_ref.refs_0_, bf16[2048,1152]{1,0:T(8,128)(2,1)} %refs_7_.1, bf16[2048,1152]{1,0:T(8,128)(2,1)} %refs_7_.1, f32[8,4,4608]{2,1,0:T(4,128)} %unit_tables.3.tab_ref.tab0_ref.tab1_ref.refs_5_.refs_12_, ...), custom_call_target="tpu_custom_call" | custom-call | flops 1 | bytes 1 | tf_op jit(solution)/shard_map/down_back/pallas_call | solution.py:667
  175.9 4.7 collective-permute-done.37.passed_ref
  186.6 15.4 %up_and_back.2 = (bf16[1024,1152]{1,0:T(8,128)(2,1)}, bf16[1024,1152]{1,0:T(8,128)(2,1)}, f32[512,1152]{1,0:T(8,128)}, bf16[512,1152]{1,0:T(8,128)(2,1)}, f32[2,8,1152]{2,1,0:T(8,128)}) custom-call(s32[1]{0:T(128)} %bitcast.place_ref.refs_0_, bf16[256,1152]{1,0:T(8,128)(2,1)} %get-tuple-element.386.a0_ref.refs_0_, bf16[256,1152]{1,0:T(8,128)(2,1)} %copy-done.22, ...), custom_call_target="tpu_custom_call" | custom-call | flops 1 | bytes 1 | tf_op jit(solution)/shard_map/up_and_back/pallas_call | solution.py:667
  203.4 8.1 %down.2 = (f32[512,1152]{1,0:T(8,128)}, bf16[512,1152]{1,0:T(8,128)(2,1)}) custom-call(s32[1]{0:T(128)} %bitcast.place_ref.refs_0_, bf16[1024,1152]{1,0:T(8,128)(2,1)} %get-tuple-element.409.m_ref.refs_11_, bf16[1152,2304]{1,0:T(8,128)(2,1)} %place_pieces.4.w_ref), custom_call_target="tpu_custom_call" | custom-call | flops 1 | bytes 1 | tf_op jit(solution)/shard_map/down/pallas_call | solution.py:667
  215.2 15.6 %up_and_back.3 = (bf16[1024,1152]{1,0:T(8,128)(2,1)}, bf16[1024,1152]{1,0:T(8,128)(2,1)}, f32[512,1152]{1,0:T(8,128)}, bf16[512,1152]{1,0:T(8,128)(2,1)}, f32[2,8,1152]{2,1,0:T(8,128)}) custom-call(s32[1]{0:T(128)} %bitcast.place_ref.refs_0_, bf16[256,1152]{1,0:T(8,128)(2,1)} %get-tuple-element.407.a0_ref.refs_5_, bf16[256,1152]{1,0:T(8,128)(2,1)} %copy-done.25, ...), custom_call_target="tpu_custom_call" | custom-call | flops 1 | bytes 1 | tf_op jit(solution)/shard_map/up_and_back/pallas_call | solution.py:667
  233.1 8.1 %down.3 = (f32[512,1152]{1,0:T(8,128)}, bf16[512,1152]{1,0:T(8,128)(2,1)}) custom-call(s32[1]{0:T(128)} %bitcast.place_ref.refs_0_, bf16[1024,1152]{1,0:T(8,128)(2,1)} %get-tuple-element.427.m_ref.refs_13_, bf16[1152,2304]{1,0:T(8,128)(2,1)} %place_pieces.4.w_ref), custom_call_target="tpu_custom_call" | custom-call | flops 1 | bytes 1 | tf_op jit(solution)/shard_map/down/pallas_call | solution.py:667
  241.2 6.7 %collective-permute-done.45.refs_3_ = bf16[256,1152]{1,0:T(8,128)(2,1)S(1)} collective-permute-done((bf16[256,1152]{1,0:T(8,128)(2,1)}, bf16[256,1152]{1,0:T(8,128)(2,1)S(1)}, u32[]{:S(2)}, u32[]{:S(2)}) %collective-permute-start.45) | collective-permute-done | bytes 589856 | tf_op jit(solution)/shard_map/ppermute | solution.py:180
  250.9 5.1 %second_norm.2 = (f32[256,1152]{1,0:T(8,128)}, bf16[256,1152]{1,0:T(8,128)(2,1)}, f32[16,1152]{1,0:T(8,128)}) custom-call(s32[1]{0:T(128)} %bitcast.place_ref.refs_0_, bf16[2048,1152]{1,0:T(8,128)(2,1)} %refs_7_.1, f32[512,1152]{1,0:T(8,128)} %get-tuple-element.423.kept_ref, bf16[512,1152]{1,0:T(8,128)(2,1)} %copy-done.15, bf16[256,1152]{1,0:T(8,128)(2,1)} %copy-done.47, ...), custom_call_target="tpu_custom_call" | custom-call | flops 1 | bytes 1 | tf_op jit(solution)/shard_map/second_norm/pallas_call | solution.py:667
  257.5 19.2 %grad_rest.1 = bf16[1152,2304]{1,0:T(8,128)(2,1)} custom-call(s32[1]{0:T(128)} %bitcast.place_ref.refs_0_, bf16[256,1152]{1,0:T(8,128)(2,1)} %get-tuple-element.386.a0_ref.refs_0_, bf16[256,1152]{1,0:T(8,128)(2,1)} %copy-done.22, bf16[256,1152]{1,0:T(8,128)(2,1)} %copy-done.21, bf16[256,1152]{1,0:T(8,128)(2,1)} %copy-done.23, ...), custom_call_target="tpu_custom_call" | custom-call | flops 1 | bytes 1 | tf_op jit(solution)/shard_map/grad_rest/pallas_call | solution.py:667
  283.2 5.1 %second_norm.3 = (f32[256,1152]{1,0:T(8,128)}, bf16[256,1152]{1,0:T(8,128)(2,1)}, f32[16,1152]{1,0:T(8,128)}) custom-call(s32[1]{0:T(128)} %bitcast.place_ref.refs_0_, bf16[2048,1152]{1,0:T(8,128)(2,1)} %refs_7_.1, f32[512,1152]{1,0:T(8,128)} %get-tuple-element.446.kept_ref, bf16[512,1152]{1,0:T(8,128)(2,1)} %collective-permute-done.44.got_ref, ...), custom_call_target="tpu_custom_call" | custom-call | flops 1 | bytes 1 | tf_op jit(solution)/shard_map/second_norm/pallas_call | solution.py:667
  289.7 21.3 %attend_backward.2 = (bf16[1024,864]{1,0:T(8,128)(2,1)}, f32[512,1152]{1,0:T(8,128)}, bf16[512,1152]{1,0:T(8,128)(2,1)}, f32[16,864]{1,0:T(8,128)}) custom-call(s32[1]{0:T(128)} %bitcast.place_ref.refs_0_, bf16[1024,864]{1,0:T(8,128)(2,1)} %get-tuple-element.343.refs_1_, bf16[256,1152]{1,0:T(8,128)(2,1)} %get-tuple-element.448.refs_2_.refs_4_, ...), custom_call_target="tpu_custom_call" | custom-call | flops 1 | bytes 1 | tf_op jit(solution)/shard_map/attend_backward/pallas_call | solution.py:667
  312.6 5.6 %out_tokens.1 = (bf16[528,1152]{1,0:T(8,128)(2,1)}, f32[16,1152]{1,0:T(8,128)}) custom-call(s32[1]{0:T(128)} %bitcast.place_ref.refs_0_, f32[2,1152]{1,0:T(2,128)} %bias_ref.5, bf16[2048,1152]{1,0:T(8,128)(2,1)} %refs_7_.1, f32[512,1152]{1,0:T(8,128)} %get-tuple-element.431.refs_1_, bf16[512,1152]{1,0:T(8,128)(2,1)} %copy-done.10, ...), custom_call_target="tpu_custom_call" | custom-call | flops 1 | bytes 1 | tf_op jit(solution)/shard_map/out_tokens/pallas_call | solution.py:667
  327.1 21.1 %attend_backward.3 = (bf16[1024,864]{1,0:T(8,128)(2,1)}, f32[512,1152]{1,0:T(8,128)}, bf16[512,1152]{1,0:T(8,128)(2,1)}, f32[16,864]{1,0:T(8,128)}) custom-call(s32[1]{0:T(128)} %bitcast.place_ref.refs_0_, bf16[1024,864]{1,0:T(8,128)(2,1)} %get-tuple-element.356.refs_1_, bf16[256,1152]{1,0:T(8,128)(2,1)} %get-tuple-element.465.refs_2_.refs_9_, ...), custom_call_target="tpu_custom_call" | custom-call | flops 1 | bytes 1 | tf_op jit(solution)/shard_map/attend_backward/pallas_call | solution.py:667
  355.5 13.2 %grad_first.1 = bf16[1152,1152]{1,0:T(8,128)(2,1)} custom-call(s32[1]{0:T(128)} %bitcast.place_ref.refs_0_, bf16[1024,1152]{1,0:T(8,128)(2,1)} %get-tuple-element.490.refs_0_, bf16[1024,864]{1,0:T(8,128)(2,1)} %get-tuple-element.491.refs_1_, bf16[1024,1152]{1,0:T(8,128)(2,1)} %get-tuple-element.492.refs_2_, bf16[1024,864]{1,0:T(8,128)(2,1)} %get-tuple-element.493.refs_3_, ...), custom_call_target="tpu_custom_call" | custom-call | flops 1 | bytes 1 | tf_op jit(solution)/shard_map/grad_first/pallas_call | solution.py:667
  380.2 4.8 %place_pieces.5 = bf16[2048,1152]{1,0:T(8,128)(2,1)} custom-call(s32[8]{0:T(128)} %stack.109.at_ref, bf16[528,1152]{1,0:T(8,128)(2,1)} %get-tuple-element.488.refs_0_, bf16[528,1152]{1,0:T(8,128)(2,1)} %collective-permute-done.65.refs_1_, bf16[528,1152]{1,0:T(8,128)(2,1)} %collective-permute-done.61.refs_2_, bf16[528,1152]{1,0:T(8,128)(2,1)} %copy-done.30), custom_call_target="tpu_custom_call" | custom-call | flops 1 | bytes 1 | tf_op jit(solution)/shard_map/place_pieces/pallas_call | solution.py:99
  388.1 6.8 %third_norm.1 = (bf16[512,1152]{1,0:T(8,128)(2,1)}, f32[16,1152]{1,0:T(8,128)}) custom-call(s32[1]{0:T(128)} %bitcast.place_ref.refs_0_, bf16[2048,1152]{1,0:T(8,128)(2,1)} %refs_6_.2, f32[512,1152]{1,0:T(8,128)} %get-tuple-element.486.refs_1_, bf16[512,1152]{1,0:T(8,128)(2,1)} %copy-done.9, bf16[256,1152]{1,0:T(8,128)(2,1)} %copy-done.42, ...), custom_call_target="tpu_custom_call" | custom-call | flops 1 | bytes 1 | tf_op jit(solution)/shard_map/third_norm/pallas_call | solution.py:667
  413.1 4.9 %adam_up.1 = (f32[15,144,288]{2,1,0:T(8,128)}, f32[15,144,288]{2,1,0:T(8,128)}, f32[15,144,288]{2,1,0:T(8,128)}, f32[15,144,288]{2,1,0:T(8,128)}) custom-call(s32[1]{0:T(128)} %bitcast.place_ref.refs_0_, f32[144,2304]{1,0:T(8,128)} %convert_add_fusion.refs_0_, f32[15,144,288]{2,1,0:T(8,128)} %refs_3_.6, f32[15,144,288]{2,1,0:T(8,128)} %refs_4_.7, ...), custom_call_target="tpu_custom_call" | custom-call | flops 1 | bytes 1 | tf_op jit(solution)/shard_map/adam_up/pallas_call | solution.py:667
  423.7 4.9 %adam_down.1 = (f32[5,144,288]{2,1,0:T(8,128)}, f32[5,144,288]{2,1,0:T(8,128)}, f32[5,144,288]{2,1,0:T(8,128)}, f32[5,144,288]{2,1,0:T(8,128)}) custom-call(s32[1]{0:T(128)} %bitcast.place_ref.refs_0_, f32[144,2304]{1,0:T(8,128)} %convert_add_fusion.refs_0_, f32[5,144,288]{2,1,0:T(8,128)} %bitcast.178, f32[5,144,288]{2,1,0:T(8,128)} %bitcast.180, ...), custom_call_target="tpu_custom_call" | custom-call | flops 1 | bytes 1 | tf_op jit(solution)/shard_map/adam_down/pallas_call | solution.py:667
  432.2 6.2 %collective-permute-done.81 = bf16[4,144,288]{2,1,0:T(8,128)(2,1)S(1)} collective-permute-done((bf16[4,144,288]{2,1,0:T(8,128)(2,1)S(1)}, bf16[4,144,288]{2,1,0:T(8,128)(2,1)S(1)}, u32[]{:S(2)}, u32[]{:S(2)}) %collective-permute-start.81) | collective-permute-done | bytes 331808 | tf_op jit(solution)/shard_map/ppermute | solution.py:214
  441.8 5.4 %adam_far.1 = (f32[15,144,288]{2,1,0:T(8,128)}, f32[15,144,288]{2,1,0:T(8,128)}, f32[15,144,288]{2,1,0:T(8,128)}, f32[15,144,288]{2,1,0:T(8,128)}) custom-call(s32[1]{0:T(128)} %bitcast.place_ref.refs_0_, bf16[256,144]{1,0:T(8,128)(2,1)} %copy-done.27, ...), custom_call_target="tpu_custom_call", output_to_operand_aliasing={{0}: (7, {}), {1}: (8, {}), {2}: (9, {}), {3}: (10, {})} | custom-call | flops 1 | bytes 1 | tf_op jit(solution)/shard_map/adam_far/pallas_call | solution.py:667
  451.5 4.7 adam_first.1
  459.5 6.1 %widen_rows.1 = f32[2048,1152]{1,0:T(8,128)} custom-call(s32[1]{0:T(128)} %bitcast.place_ref.refs_0_, bf16[512,1152]{1,0:T(8,128)(2,1)} %get-tuple-element.559.refs_0_, bf16[512,1152]{1,0:T(8,128)(2,1)} %collective-permute-done.84.refs_1_, bf16[512,1152]{1,0:T(8,128)(2,1)} %collective-permute-done.86.refs_2_, bf16[512,1152]{1,0:T(8,128)(2,1)} %collective-permute-done.87.refs_3_), custom_call_target="tpu_custom_call" | custom-call | flops 1 | bytes 1 | tf_op jit(solution)/shard_map/widen_rows/pallas_call | solution.py:667
  467.9 5.5 %adam_near.1 = (f32[15,144,288]{2,1,0:T(8,128)}, f32[15,144,288]{2,1,0:T(8,128)}, f32[15,144,288]{2,1,0:T(8,128)}, f32[15,144,288]{2,1,0:T(8,128)}) custom-call(s32[1]{0:T(128)} %bitcast.place_ref.refs_0_, bf16[256,144]{1,0:T(8,128)(2,1)} %copy-done.27, ...), custom_call_target="tpu_custom_call", output_to_operand_aliasing={{0}: (8, {}), {1}: (9, {}), {2}: (10, {}), {3}: (11, {})} | custom-call | flops 1 | bytes 1 | tf_op jit(solution)/shard_map/adam_near/pallas_call | solution.py:667
  (500 shorter events, 197.1 us)
Async XLA Ops:
  64.6 24.9 %collective-permute-start.19 = (bf16[144,2304]{1,0:T(8,128)(2,1)S(1)}, bf16[144,2304]{1,0:T(8,128)(2,1)S(1)}, u32[]{:S(2)}, u32[]{:S(2)}) collective-permute-start(bf16[144,2304]{1,0:T(8,128)(2,1)S(1)} %concatenate.75.refs_0_), channel_id=1, source_target_pairs={{8,0},{16,8},{24,16},{28,24},{20,28},{12,20},{4,12},{0,4},{9,1},{1... | collective-permute-start | bytes 1990664 | tf_op jit(solution)/shard_map/ppermute | solution.py:271
  65.9 23.6 %collective-permute-start.18 = (bf16[144,2304]{1,0:T(8,128)(2,1)S(1)}, bf16[144,2304]{1,0:T(8,128)(2,1)S(1)}, u32[]{:S(2)}, u32[]{:S(2)}) collective-permute-start(bf16[144,2304]{1,0:T(8,128)(2,1)S(1)} %concatenate.75.refs_0_), channel_id=1, source_target_pairs={{0,8},{8,16},{16,24},{24,28},{28,20},{20,12},{12,4},{4,0},{1,9},{9... | collective-permute-start | bytes 1990664 | tf_op jit(solution)/shard_map/ppermute | solution.py:270
  67.1 22.5 %collective-permute-start.17 = (bf16[4,32,1152]{2,1,0:T(8,128)(2,1)S(1)}, bf16[4,32,1152]{2,1,0:T(8,128)(2,1)S(1)}, u32[]{:S(2)}, u32[]{:S(2)}) collective-permute-start(bf16[4,32,1152]{2,1,0:T(8,128)(2,1)S(1)} %dynamic-slice_bitcast_fusion), channel_id=1, source_target_pairs={{0,4},{4,0},{8,12},{12,8},{16,20},{20,16},{24,28},{28,24},{1,5},{5... | collective-permute-start | bytes 884744 | tf_op jit(solution)/shard_map/ppermute | solution.py:249
  89.6 20.0 %collective-permute-start.21 = (bf16[144,2304]{1,0:T(8,128)(2,1)S(1)}, bf16[144,2304]{1,0:T(8,128)(2,1)S(1)}, u32[]{:S(2)}, u32[]{:S(2)}) collective-permute-start(bf16[144,2304]{1,0:T(8,128)(2,1)S(1)} %collective-permute-done.18.refs_1_), channel_id=1, source_target_pairs={{0,8},{8,16},{16,24},{24,28},{28,20},{20,12},{12,4},{4,0},{1,9},{9... | collective-permute-start | bytes 1990664 | tf_op jit(solution)/shard_map/ppermute | solution.py:270
  89.6 19.9 %collective-permute-start.22 = (bf16[144,2304]{1,0:T(8,128)(2,1)S(1)}, bf16[144,2304]{1,0:T(8,128)(2,1)}, u32[]{:S(2)}, u32[]{:S(2)}) collective-permute-start(bf16[144,2304]{1,0:T(8,128)(2,1)S(1)} %collective-permute-done.19.refs_2_), channel_id=1, source_target_pairs={{8,0},{16,8},{24,16},{28,24},{20,28},{12,20},{4,12},{0,4},{9,1},{1... | collective-permute-start | bytes 1990664 | tf_op jit(solution)/shard_map/ppermute | solution.py:271
  91.9 17.6 %collective-permute-start.20 = (bf16[2,32,1152]{2,1,0:T(8,128)(2,1)S(1)}, bf16[2,32,1152]{2,1,0:T(8,128)(2,1)S(1)}, u32[]{:S(2)}, u32[]{:S(2)}) collective-permute-start(bf16[2,32,1152]{2,1,0:T(8,128)(2,1)S(1)} %fusion.16), channel_id=1, source_target_pairs={{0,8},{4,12},{8,0},{12,4},{16,24},{20,28},{24,16},{28,20},{1,9},{5... | collective-permute-start | bytes 442376 | tf_op jit(solution)/shard_map/ppermute | solution.py:249
  112.1 25.6 %collective-permute-start.26 = (bf16[144,2304]{1,0:T(8,128)(2,1)}, bf16[144,2304]{1,0:T(8,128)(2,1)}, u32[]{:S(2)}, u32[]{:S(2)}) collective-permute-start(bf16[144,2304]{1,0:T(8,128)(2,1)} %copy-done.41), channel_id=1, source_target_pairs={{0,8},{8,16},{16,24},{24,28},{28,20},{20,12},{12,4},{4,0},{1,9},{9... | collective-permute-start | bytes 1990664 | tf_op jit(solution)/shard_map/ppermute | solution.py:270
  112.3 25.5 %collective-permute-start.27 = (bf16[144,2304]{1,0:T(8,128)(2,1)}, bf16[144,2304]{1,0:T(8,128)(2,1)}, u32[]{:S(2)}, u32[]{:S(2)}) collective-permute-start(bf16[144,2304]{1,0:T(8,128)(2,1)} %collective-permute-done.22.refs_4_), channel_id=1, source_target_pairs={{8,0},{16,8},{24,16},{28,24},{20,28},{12,20},{4,12},{0,4},{9,1},{1... | collective-permute-start | bytes 1990664 | tf_op jit(solution)/shard_map/ppermute | solution.py:271
  159.6 21.1 %collective-permute-start.37 = (bf16[256,1152]{1,0:T(8,128)(2,1)S(1)}, bf16[256,1152]{1,0:T(8,128)(2,1)S(1)}, u32[]{:S(2)}, u32[]{:S(2)}) collective-permute-start(bf16[256,1152]{1,0:T(8,128)(2,1)S(1)} %add_convert_fusion.11), channel_id=1, source_target_pairs={{0,2},{1,3},{2,0},{3,1},{4,6},{5,7},{6,4},{7,5},{8,10},{9,11},{10,... | collective-permute-start | bytes 1769480 | tf_op jit(solution)/shard_map/ppermute | solution.py:180
  211.6 19.2 %collective-permute-start.43 = (bf16[512,1152]{1,0:T(8,128)(2,1)}, bf16[512,1152]{1,0:T(8,128)(2,1)S(1)}, u32[]{:S(2)}, u32[]{:S(2)}) collective-permute-start(bf16[512,1152]{1,0:T(8,128)(2,1)} %get-tuple-element.425), channel_id=1, source_target_pairs={{0,1},{1,0},{2,3},{3,2},{4,5},{5,4},{6,7},{7,6},{8,9},{9,8},{10,11... | collective-permute-start | bytes 3538952 | tf_op jit(solution)/shard_map/ppermute | solution.py:175
  250.1 26.5 %collective-permute-start.47 = (bf16[256,1152]{1,0:T(8,128)(2,1)}, bf16[256,1152]{1,0:T(8,128)(2,1)S(1)}, u32[]{:S(2)}, u32[]{:S(2)}) collective-permute-start(bf16[256,1152]{1,0:T(8,128)(2,1)} %add_convert_fusion.8), channel_id=1, source_target_pairs={{0,2},{1,3},{2,0},{3,1},{4,6},{5,7},{6,4},{7,5},{8,10},{9,11},{10,... | collective-permute-start | bytes 1769480 | tf_op jit(solution)/shard_map/ppermute | solution.py:180
  256.0 20.6 %collective-permute-start.49 = (bf16[256,1152]{1,0:T(8,128)(2,1)}, bf16[256,1152]{1,0:T(8,128)(2,1)}, u32[]{:S(2)}, u32[]{:S(2)}) collective-permute-start(bf16[256,1152]{1,0:T(8,128)(2,1)} %get-tuple-element.448.refs_2_.refs_4_), channel_id=1, source_target_pairs={{0,1},{1,0},{2,3},{3,2},{4,5},{5,4},{6,7},{7,6},{8,9},{9,8},{10,11... | collective-permute-start | bytes 1769480 | tf_op jit(solution)/shard_map/ppermute | solution.py:190
  256.1 22.5 %collective-permute-start.48 = (bf16[256,1152]{1,0:T(8,128)(2,1)}, bf16[256,1152]{1,0:T(8,128)(2,1)}, u32[]{:S(2)}, u32[]{:S(2)}) collective-permute-start(bf16[256,1152]{1,0:T(8,128)(2,1)} %get-tuple-element.448.refs_2_.refs_4_), channel_id=1, source_target_pairs={{0,2},{1,3},{2,0},{3,1},{4,6},{5,7},{6,4},{7,5},{8,10},{9,11},{10,... | collective-permute-start | bytes 1769480 | tf_op jit(solution)/shard_map/ppermute | solution.py:189
  280.0 31.0 %collective-permute-start.52 = (bf16[144,2304]{1,0:T(8,128)(2,1)S(1)}, bf16[144,2304]{1,0:T(8,128)(2,1)S(1)}, u32[]{:S(2)}, u32[]{:S(2)}) collective-permute-start(bf16[144,2304]{1,0:T(8,128)(2,1)S(1)} %get-tuple-element.620), channel_id=1, source_target_pairs={{8,0},{16,8},{24,16},{28,24},{20,28},{12,20},{4,12},{0,4},{9,1},{1... | collective-permute-start | bytes 1990664 | tf_op jit(solution)/shard_map/ppermute | solution.py:152
  280.4 30.7 %collective-permute-start.51 = (bf16[144,2304]{1,0:T(8,128)(2,1)S(1)}, bf16[144,2304]{1,0:T(8,128)(2,1)S(1)}, u32[]{:S(2)}, u32[]{:S(2)}) collective-permute-start(bf16[144,2304]{1,0:T(8,128)(2,1)S(1)} %get-tuple-element.621), channel_id=1, source_target_pairs={{0,8},{8,16},{16,24},{24,28},{28,20},{20,12},{12,4},{4,0},{1,9},{9... | collective-permute-start | bytes 1990664 | tf_op jit(solution)/shard_map/ppermute | solution.py:150
  282.4 28.6 %collective-permute-start.55 = (bf16[256,1152]{1,0:T(8,128)(2,1)S(1)}, bf16[256,1152]{1,0:T(8,128)(2,1)S(1)}, u32[]{:S(2)}, u32[]{:S(2)}) collective-permute-start(bf16[256,1152]{1,0:T(8,128)(2,1)S(1)} %add_convert_fusion.7), channel_id=1, source_target_pairs={{0,2},{1,3},{2,0},{3,1},{4,6},{5,7},{6,4},{7,5},{8,10},{9,11},{10,... | collective-permute-start | bytes 1769480 | tf_op jit(solution)/shard_map/ppermute | solution.py:180
  288.3 22.7 %collective-permute-start.54 = (bf16[256,1152]{1,0:T(8,128)(2,1)}, bf16[256,1152]{1,0:T(8,128)(2,1)S(1)}, u32[]{:S(2)}, u32[]{:S(2)}) collective-permute-start(bf16[256,1152]{1,0:T(8,128)(2,1)} %get-tuple-element.465.refs_2_.refs_9_), channel_id=1, source_target_pairs={{0,1},{1,0},{2,3},{3,2},{4,5},{5,4},{6,7},{7,6},{8,9},{9,8},{10,11... | collective-permute-start | bytes 1769480 | tf_op jit(solution)/shard_map/ppermute | solution.py:190
  288.4 22.7 %collective-permute-start.53 = (bf16[256,1152]{1,0:T(8,128)(2,1)}, bf16[256,1152]{1,0:T(8,128)(2,1)S(1)}, u32[]{:S(2)}, u32[]{:S(2)}) collective-permute-start(bf16[256,1152]{1,0:T(8,128)(2,1)} %get-tuple-element.465.refs_2_.refs_9_), channel_id=1, source_target_pairs={{0,2},{1,3},{2,0},{3,1},{4,6},{5,7},{6,4},{7,5},{8,10},{9,11},{10,... | collective-permute-start | bytes 1769480 | tf_op jit(solution)/shard_map/ppermute | solution.py:189
  318.2 30.0 %collective-permute-start.61 = (bf16[528,1152]{1,0:T(8,128)(2,1)}, bf16[528,1152]{1,0:T(8,128)(2,1)}, u32[]{:S(2)}, u32[]{:S(2)}) collective-permute-start(bf16[528,1152]{1,0:T(8,128)(2,1)} %get-tuple-element.488.refs_0_), channel_id=1, source_target_pairs={{0,1},{1,0},{2,3},{3,2},{4,5},{5,4},{6,7},{7,6},{8,9},{9,8},{10,11... | collective-permute-start | bytes 3649544 | tf_op jit(solution)/shard_map/ppermute | solution.py:190
  322.0 26.2 %collective-permute-start.59 = (bf16[144,2304]{1,0:T(8,128)(2,1)}, bf16[144,2304]{1,0:T(8,128)(2,1)S(1)}, u32[]{:S(2)}, u32[]{:S(2)}) collective-permute-start(bf16[144,2304]{1,0:T(8,128)(2,1)} %get-tuple-element.618), channel_id=1, source_target_pairs={{8,0},{16,8},{24,16},{28,24},{20,28},{12,20},{4,12},{0,4},{9,1},{1... | collective-permute-start | bytes 1990664 | tf_op jit(solution)/shard_map/ppermute | solution.py:152
  322.3 25.9 %collective-permute-start.58 = (bf16[144,2304]{1,0:T(8,128)(2,1)}, bf16[144,2304]{1,0:T(8,128)(2,1)}, u32[]{:S(2)}, u32[]{:S(2)}) collective-permute-start(bf16[144,2304]{1,0:T(8,128)(2,1)} %get-tuple-element.619), channel_id=1, source_target_pairs={{0,8},{8,16},{16,24},{24,28},{28,20},{20,12},{12,4},{4,0},{1,9},{9... | collective-permute-start | bytes 1990664 | tf_op jit(solution)/shard_map/ppermute | solution.py:150
  325.1 23.1 %collective-permute-start.60 = (bf16[256,1152]{1,0:T(8,128)(2,1)}, bf16[256,1152]{1,0:T(8,128)(2,1)S(1)}, u32[]{:S(2)}, u32[]{:S(2)}) collective-permute-start(bf16[256,1152]{1,0:T(8,128)(2,1)} %add_convert_fusion.6), channel_id=1, source_target_pairs={{0,2},{1,3},{2,0},{3,1},{4,6},{5,7},{6,4},{7,5},{8,10},{9,11},{10,... | collective-permute-start | bytes 1769480 | tf_op jit(solution)/shard_map/ppermute | solution.py:180
  325.9 42.8 %collective-permute-start.65 = (bf16[528,1152]{1,0:T(8,128)(2,1)S(1)}, bf16[528,1152]{1,0:T(8,128)(2,1)}, u32[]{:S(2)}, u32[]{:S(2)}) collective-permute-start(bf16[528,1152]{1,0:T(8,128)(2,1)S(1)} %copy-done.29), channel_id=1, source_target_pairs={{0,2},{1,3},{2,0},{3,1},{4,6},{5,7},{6,4},{7,5},{8,10},{9,11},{10,... | collective-permute-start | bytes 3649544 | tf_op jit(solution)/shard_map/ppermute | solution.py:189
  349.2 20.6 %collective-permute-start.64 = (bf16[512,1152]{1,0:T(8,128)(2,1)}, bf16[512,1152]{1,0:T(8,128)(2,1)S(1)}, u32[]{:S(2)}, u32[]{:S(2)}) collective-permute-start(bf16[512,1152]{1,0:T(8,128)(2,1)} %get-tuple-element.498), channel_id=1, source_target_pairs={{0,1},{1,0},{2,3},{3,2},{4,5},{5,4},{6,7},{7,6},{8,9},{9,8},{10,11... | collective-permute-start | bytes 3538952 | tf_op jit(solution)/shard_map/ppermute | solution.py:175
  352.2 17.6 %collective-permute-start.63 = (bf16[144,2304]{1,0:T(8,128)(2,1)}, bf16[144,2304]{1,0:T(8,128)(2,1)}, u32[]{:S(2)}, u32[]{:S(2)}) collective-permute-start(bf16[144,2304]{1,0:T(8,128)(2,1)} %get-tuple-element.616), channel_id=1, source_target_pairs={{8,0},{16,8},{24,16},{28,24},{20,28},{12,20},{4,12},{0,4},{9,1},{1... | collective-permute-start | bytes 1990664 | tf_op jit(solution)/shard_map/ppermute | solution.py:152
  352.6 17.2 %collective-permute-start.62 = (bf16[144,2304]{1,0:T(8,128)(2,1)S(1)}, bf16[144,2304]{1,0:T(8,128)(2,1)}, u32[]{:S(2)}, u32[]{:S(2)}) collective-permute-start(bf16[144,2304]{1,0:T(8,128)(2,1)S(1)} %get-tuple-element.617), channel_id=1, source_target_pairs={{0,8},{8,16},{16,24},{24,28},{28,20},{20,12},{12,4},{4,0},{1,9},{9... | collective-permute-start | bytes 1990664 | tf_op jit(solution)/shard_map/ppermute | solution.py:150
  374.3 20.6 %collective-permute-start.71 = (bf16[144,1152]{1,0:T(8,128)(2,1)}, bf16[144,1152]{1,0:T(8,128)(2,1)}, u32[]{:S(2)}, u32[]{:S(2)}) collective-permute-start(bf16[144,1152]{1,0:T(8,128)(2,1)} %get-tuple-element.626), channel_id=1, source_target_pairs={{8,0},{16,8},{24,16},{28,24},{20,28},{12,20},{4,12},{0,4},{9,1},{1... | collective-permute-start | bytes 995336 | tf_op jit(solution)/shard_map/ppermute | solution.py:152
  375.5 19.3 %collective-permute-start.70 = (bf16[144,1152]{1,0:T(8,128)(2,1)}, bf16[144,1152]{1,0:T(8,128)(2,1)}, u32[]{:S(2)}, u32[]{:S(2)}) collective-permute-start(bf16[144,1152]{1,0:T(8,128)(2,1)} %get-tuple-element.627), channel_id=1, source_target_pairs={{0,8},{8,16},{16,24},{24,28},{28,20},{20,12},{12,4},{4,0},{1,9},{9... | collective-permute-start | bytes 995336 | tf_op jit(solution)/shard_map/ppermute | solution.py:150
  378.6 20.6 %collective-permute-start.72 = (bf16[144,2304]{1,0:T(8,128)(2,1)}, bf16[144,2304]{1,0:T(8,128)(2,1)S(1)}, u32[]{:S(2)}, u32[]{:S(2)}) collective-permute-start(bf16[144,2304]{1,0:T(8,128)(2,1)} %add_convert_fusion), channel_id=1, source_target_pairs={{0,8},{8,16},{16,24},{24,28},{28,20},{20,12},{12,4},{4,0},{1,9},{9... | collective-permute-start | bytes 1990664 | tf_op jit(solution)/shard_map/ppermute | solution.py:150
  400.8 17.2 %collective-permute-start.77 = (bf16[16,576]{1,0:T(8,128)(2,1)S(1)}, bf16[16,576]{1,0:T(8,128)(2,1)S(1)}, u32[]{:S(2)}, u32[]{:S(2)}) collective-permute-start(bf16[16,576]{1,0:T(8,128)(2,1)S(1)} %get-tuple-element.666), channel_id=1, source_target_pairs={{0,2},{1,3},{2,0},{3,1},{4,6},{5,7},{6,4},{7,5},{8,10},{9,11},{10,... | collective-permute-start | bytes 55304 | tf_op jit(solution)/shard_map/ppermute | solution.py:1266
  409.7 37.6 %collective-permute-start.84 = (bf16[512,1152]{1,0:T(8,128)(2,1)}, bf16[512,1152]{1,0:T(8,128)(2,1)}, u32[]{:S(2)}, u32[]{:S(2)}) collective-permute-start(bf16[512,1152]{1,0:T(8,128)(2,1)} %get-tuple-element.559.refs_0_), channel_id=1, source_target_pairs={{0,2},{1,3},{2,0},{3,1},{4,6},{5,7},{6,4},{7,5},{8,10},{9,11},{10,... | collective-permute-start | bytes 3538952 | tf_op jit(solution)/shard_map/ppermute | solution.py:189
  428.7 27.5 %collective-permute-start.86 = (bf16[512,1152]{1,0:T(8,128)(2,1)}, bf16[512,1152]{1,0:T(8,128)(2,1)}, u32[]{:S(2)}, u32[]{:S(2)}) collective-permute-start(bf16[512,1152]{1,0:T(8,128)(2,1)} %get-tuple-element.559.refs_0_), channel_id=1, source_target_pairs={{0,1},{1,0},{2,3},{3,2},{4,5},{5,4},{6,7},{7,6},{8,9},{9,8},{10,11... | collective-permute-start | bytes 3538952 | tf_op jit(solution)/shard_map/ppermute | solution.py:190
  (144 other events, 1213.2 us)

commit v6 on v5

--- a/solution.py
+++ b/solution.py
@@ -24,6 +24,7 @@
 norm_eps = 1e-06
 neg_large = -1e30
 score_scale = HEAD_DIM**-0.5
+two_scale = score_scale * math.log2(math.e)
 low = jnp.bfloat16
 wide = jnp.float32
 
@@ -167,7 +168,8 @@
     def total(self):
         if self.count not in (4, 8):
             return lax.psum_scatter(self.parts, "dp", scatter_dimension=0, tiled=True).astype(wide)
-        return self.ahead.astype(wide) + self.behind.astype(wide) + self.chunk(0)
+        total = self.ahead.astype(wide) + self.behind.astype(wide) + self.chunk(0)
+        return total.astype(low)
 
 
 class GroupSum:
@@ -176,7 +178,8 @@
 
     def cross(self):
         quarter = self.kept.shape[0] // 2
-        passed = (self.kept[quarter:] + self.got[quarter:].astype(wide)).astype(low)
+        passed = self.kept[quarter:].astype(wide) + self.got[quarter:].astype(wide)
+        passed = passed.astype(low)
         self.last = lax.ppermute(passed, "mp", CHIP_SWAP)
 
     def terms(self):
@@ -313,7 +316,7 @@
 
 
 def attend_forward_kernel(
-    place_ref, qkv_ref, seg_col_ref, seg_row_ref, w_ref, out_ref, kept_ref, sent_ref, q_s, k_s, v_s, *, heads
+    place_ref, qkv_ref, seg_row_ref, w_ref, out_ref, kept_ref, sent_ref, q_s, k_s, v_s, *, heads
 ):
     row_len = qkv_ref.shape[0]
     width = heads * HEAD_DIM
@@ -328,13 +331,14 @@
             k_s[h, to, :] = qkv_ref[pl.ds(at, block), width + c : width + c + HEAD_DIM]
             v_s[h, to, :] = qkv_ref[pl.ds(at, block), 2 * width + c : 2 * width + c + HEAD_DIM]
     for j, (at, start, stop) in enumerate(key_windows(row_len, block)):
-        same = seg_col_ref[start:stop, :] == seg_row_ref[:, at : at + block]
+        keys_seg = jnp.broadcast_to(seg_row_ref[:, start:stop], (8, stop - start)).T[:, :1]
+        same = keys_seg == seg_row_ref[:, at : at + block]
         mixed = []
         for h in range(heads):
             scores = dot_as(k_s[h, start:stop, :], q_s[h, at : at + block, :], DOT_NT)
             scores = jnp.where(same, scores, neg_large)
             top = jnp.max(scores, axis=0, keepdims=True)
-            weights = jnp.exp((scores - top) * score_scale)
+            weights = jnp.exp2((scores - top) * two_scale)
             total = jnp.sum(weights, axis=0, keepdims=True)
             gathered = dot_as(v_s[h, start:stop, :], weights.astype(low), DOT_TN)
             mixed.append(gathered * (1.0 / total))
@@ -343,12 +347,12 @@
         )
     w_out = w_ref[:, w_ref.shape[1] - width :]
     half = row_len // 2
-    kept_ref[...] = dot_as(out_ref[:half, :], w_out, DOT_NT)
+    kept_ref[...] = dot_as(out_ref[:half, :], w_out, DOT_NT).astype(low)
     sent_ref[...] = dot_as(out_ref[half:, :], w_out, DOT_NT).astype(low)
 
 
 def attend_backward_kernel(
-    place_ref, qkv_ref, g0_ref, g1_ref, g2_ref, g3_ref, seg_col_ref, seg_row_ref, w_ref,
+    place_ref, qkv_ref, g0_ref, g1_ref, g2_ref, g3_ref, seg_row_ref, w_ref,
     out_ref, kept_ref, sent_ref, sums_ref, q_s, k_s, v_s, g_s, dk_s, dv_s, *, heads
 ):
     row_len = qkv_ref.shape[0]
@@ -372,7 +376,8 @@
             k_s[h, to, :] = qkv_ref[pl.ds(at, block), width + c : width + c + HEAD_DIM]
             v_s[h, to, :] = qkv_ref[pl.ds(at, block), 2 * width + c : 2 * width + c + HEAD_DIM]
     for j, (at, start, stop) in enumerate(key_windows(row_len, block)):
-        same = seg_col_ref[start:stop, :] == seg_row_ref[:, at : at + block]
+        keys_seg = jnp.broadcast_to(seg_row_ref[:, start:stop], (8, stop - start)).T[:, :1]
+        same = keys_seg == seg_row_ref[:, at : at + block]
         grads = []
         for h in range(heads):
             query = q_s[h, at : at + block, :]
@@ -380,7 +385,7 @@
             keys = k_s[h, start:stop, :]
             scores = jnp.where(same, dot_as(keys, query, DOT_NT), neg_large)
             top = jnp.max(scores, axis=0, keepdims=True)
-            weights = jnp.exp((scores - top) * score_scale)
+            weights = jnp.exp2((scores - top) * two_scale)
             probs = weights * (1.0 / jnp.sum(weights, axis=0, keepdims=True))
             grad_probs = dot_as(v_s[h, start:stop, :], grad, DOT_NT)
             inner = jnp.sum(grad_probs * probs, axis=0, keepdims=True)
@@ -402,7 +407,7 @@
         )
     half = row_len // 2
     w_qkv = w_ref[:, : 3 * width]
-    kept_ref[...] = dot_as(out_ref[:half, :], w_qkv, DOT_NT)
+    kept_ref[...] = dot_as(out_ref[:half, :], w_qkv, DOT_NT).astype(low)
     sent_ref[...] = dot_as(out_ref[half:, :], w_qkv, DOT_NT).astype(low)
     for u in range(row_len // UNIT):
         sums_ref[u : u + 1, :] = jnp.sum(
@@ -418,10 +423,10 @@
     row_len, width = qkv.shape[0], qkv.shape[1] // 3
     heads = width // HEAD_DIM
     full = weights.shape[0]
-    args = (qkv, seg_row.reshape(row_len, 1), seg_row.reshape(1, row_len), weights)
+    args = (qkv, seg_row, weights)
     shapes = (
         shape_of((row_len, width), low),
-        shape_of((row_len // 2, full), wide),
+        shape_of((row_len // 2, full), low),
         shape_of((row_len // 2, full), low),
     )
 
@@ -433,7 +438,7 @@
         "attend_forward",
         chain,
         args,
-        [fixed_spec(arg.shape) for arg in args[:3]]
+        [fixed_spec(arg.shape) for arg in args[:2]]
         + [pl.BlockSpec((full, weights.shape[1] // 3), lambda i, p: (0, 2))],
         tuple(fixed_spec(shape.shape) for shape in shapes),
         shapes,
@@ -447,10 +452,10 @@
     row_len, width = qkv.shape[0], qkv.shape[1] // 3
     heads = width // HEAD_DIM
     full = weights.shape[0]
-    args = (qkv, *grads, seg_row.reshape(row_len, 1), seg_row.reshape(1, row_len), weights)
+    args = (qkv, *grads, seg_row, weights)
     shapes = (
         shape_of((row_len, 3 * width), low),
-        shape_of((row_len // 2, full), wide),
+        shape_of((row_len // 2, full), low),
         shape_of((row_len // 2, full), low),
         shape_of((row_len // UNIT, 3 * width), wide),
     )
@@ -517,7 +522,7 @@
     width = x_ref.shape[1]
     for u, at in unit_rows(x_ref):
         table = tab_ref[0, u : u + 1, :]
-        attended = kept_ref[at, :] + got_ref[at, :].astype(wide) + passed_ref[at, :].astype(wide)
+        attended = kept_ref[at, :].astype(wide) + got_ref[at, :].astype(wide) + passed_ref[at, :].astype(wide)
         attended = attended + bias_ref[0:1, :]
         hidden = x_ref[at, :].astype(wide) + column(table, 0, width) * attended
         normed, _ = norm_parts(hidden)
@@ -571,7 +576,7 @@
 
     @pl.when(step == 0)
     def _():
-        kept_ref[...] = back
+        kept_ref[...] = back.astype(low)
 
     @pl.when(step == 1)
     def _():
@@ -584,7 +589,7 @@
 
     @pl.when(step == 0)
     def _():
-        kept_ref[...] = out
+        kept_ref[...] = out.astype(low)
 
     @pl.when(step == 1)
     def _():
@@ -599,7 +604,7 @@
     sums_ref[...] = jnp.zeros_like(sums_ref)
     for u, at in unit_rows(cot_ref):
         table = tab_ref[0, u : u + 1, :]
-        grad_two = kept_ref[at, :] + got_ref[at, :].astype(wide) + passed_ref[at, :].astype(wide)
+        grad_two = kept_ref[at, :].astype(wide) + got_ref[at, :].astype(wide) + passed_ref[at, :].astype(wide)
         normed, inverse = norm_parts(hid_ref[at, :])
         grad = cot_ref[at, :].astype(wide) + norm_back(
             normed, inverse, grad_two * (1.0 + column(table, 2, width))
@@ -625,7 +630,7 @@
         cot_ref, kept_ref, got_ref, passed_ref, hid_ref, tab_ref, second_ref = refs[7 * r : 7 * r + 7]
         for u, at in unit_rows(cot_ref):
             gate = column(tab_ref[0, u : u + 1, :], 3, width)
-            mlp = kept_ref[at, :] + got_ref[at, :].astype(wide) + passed_ref[at, :].astype(wide)
+            mlp = kept_ref[at, :].astype(wide) + got_ref[at, :].astype(wide) + passed_ref[at, :].astype(wide)
             mlp = mlp + bias_ref[1:2, :]
             out_ref[r * quarter + u * UNIT : r * quarter + (u + 1) * UNIT, :] = (
                 hid_ref[at, :] + gate * mlp
@@ -645,7 +650,7 @@
     for r in range(rows):
         x_ref, kept_ref, got_ref, passed_ref, gh_ref, tab_ref = refs[6 * r : 6 * r + 6]
         for u, at in unit_rows(x_ref):
-            grad_one = kept_ref[at, :] + got_ref[at, :].astype(wide) + passed_ref[at, :].astype(wide)
+            grad_one = kept_ref[at, :].astype(wide) + got_ref[at, :].astype(wide) + passed_ref[at, :].astype(wide)
             normed, inverse = norm_parts(x_ref[at, :].astype(wide))
             table = tab_ref[0, u : u + 1, :]
             back = norm_back(normed, inverse, grad_one * (1.0 + column(table, 1, width)))
@@ -946,8 +951,7 @@
             near.parts = beside(near.kept + near.got.astype(wide))
             near.step *= 2
             near.send()
-        near.got, own_rest = beside((near.got, own_rest))
-        rest_gather = RingGather(own_rest, dp_count)
+        near.got = beside(near.got)
         near.hop()
         near = near.parts[0]
     else:
@@ -988,13 +992,16 @@
     near_to = [field_slots(f)[:, r] for r in range(rows) for f in range(2)]
     moved = row_slots.transpose(1, 0, 2).reshape(-1, 1) == jnp.arange(slot_count)[None, :]
     quarters = [(r * 4 + jnp.bitwise_xor(place, j)) * quarter for j in range(4) for r in range(rows)]
-    hot, far_matrix, near_matrix, moved, at = chain.tie(
+    seg_rows = [seg_grid[r].reshape(1, row_len) for r in range(rows)]
+    hot, far_matrix, near_matrix, moved, at, *segs = chain.tie(
         blocks.astype(low),
         slot_matrix(far_to, spare + 16),
         slot_matrix(near_to, 2 * slot_count),
         moved.astype(wide),
         jnp.stack(quarters).astype(jnp.int32),
-    )
+        *seg_rows,
+    )
+    seg_rows = segs
 
     mp_arg = mp_place.astype(jnp.int32).reshape(1)
 
@@ -1005,9 +1012,13 @@
 
     far = slot_products([(lax.optimization_barrier((ada_low, near))[0], far_maps)])
     near_mod = (near[:, : 2 * own_width] + bias_cols[6:8].reshape(1, -1)).astype(low)
-    near_tab = tables(GroupGather(near_mod), 2)
+    near_spread = GroupGather(near_mod)
     if ring:
         far = HalvingSum(far, dp_count)
+        near_spread.chip, own_rest = lax.optimization_barrier((near_spread.chip, own_rest))
+        rest_gather = RingGather(own_rest, dp_count)
+    near_tab = tables(near_spread, 2)
+    if ring:
         w_first = first_gather.place(chain)
     time_add = jnp.concatenate(
         [
@@ -1069,7 +1080,7 @@
         inputs_one.append(a_one)
         qkvs.append(qkv)
         between()
-        out, kept, sent = attend_forward(chain, qkv, seg_grid[r], w_first)
+        out, kept, sent = attend_forward(chain, qkv, seg_rows[r], w_first)
         mixed.append(out)
         parts.append(GroupSum(kept, sent))
 
@@ -1174,7 +1185,7 @@
             (
                 lows(row_len, hidden_width),
                 lows(row_len, hidden_width),
-                wides(half, width),
+                lows(half, width),
                 lows(half, width),
                 wides(2, 8, hidden_width),
             ),
@@ -1200,7 +1211,7 @@
             (active, w_rest),
             [pl.BlockSpec((half, hidden_width), lambda i, p: (i, 0)), w_down_spec],
             (half_fixed, half_fixed),
-            (wides(half, width), lows(half, width)),
+            (lows(half, width), lows(half, width)),
             grid=2,
             flops=2 * row_len * width * hidden_width,
         )
@@ -1277,7 +1288,7 @@
 
     def backward(r):
         qkv_grad, kept, sent, sums = attend_backward(
-            chain, qkvs[r], grad_gathers[r].pieces(), seg_grid[r], w_first
+            chain, qkvs[r], grad_gathers[r].pieces(), seg_rows[r], w_first
         )
         qkv_grads.append(qkv_grad)
         one_parts.append(GroupSum(kept, sent))

time: 484 us -> 475 us (0.981)
  Pallas kernels: 257 us -> 252 us
    pallas_call x28, Pallas kernels: 244 us -> 239 us  [row_call(): pl.pallas_call(body, grid_spec=pltpu.PrefetchScalarGridSpec(num_scalar_pr...]
  transfers between devices with their start and end apart: 89 -> 89, of which waited for: 24 -> 26; matrix products, arithmetic and copies ran while one was open for 11% -> 11% of each run, Pallas kernels for 52% -> 52%
where the time goes in v6:
time: 475 us; the launch traced here: 466 us
  Pallas kernels  252 us (53%)
  starting transfers between devices  81.3 us (17%)
  waiting for transfers between devices  65 us (14%)
  other arithmetic  31.3 us (7%)
  local copies, waits for them, and re-layouts  27.8 us (6%)
  matrix products  5.37 us (1%)
    pallas_call x28, Pallas kernels, row_call(): pl.pallas_call(body, grid_spec=pltpu.PrefetchScalarGridSpec(num_scalar_pr...  239 us
    ppermute x6, waiting for transfers between devices, send(): self.got = lax.ppermute(sent, 'dp', swap)  13.5 us
    ppermute x8, starting transfers between devices, send(): self.ahead = lax.ppermute(ahead.astype(low), 'dp', self.onward)  13.3 us
    pallas_call x3, Pallas kernels, place_pieces(): pl.pallas_call(body, out_shape=jax.ShapeDtypeStruct(whole, pieces[0].dtyp...  13.3 us
    ppermute x8, waiting for transfers between devices, cross(): self.last = lax.ppermute(passed, 'mp', CHIP_SWAP)  11.3 us
    ppermute x6, starting transfers between devices, send(): self.got = lax.ppermute(self.known, 'dp', swap)  9.9 us
  transfers between devices with their start and end apart: 89, of which 26 were waited for; matrix products, arithmetic and copies ran while one was open for 11% of the time, Pallas kernels for 52%

profile of v6, /device:TPU:0, one launch (start us, length us, event | category | flops | bytes accessed | tf_op | source)
XLA Modules:
  0.0 465.6 jit_solution(1348062868226332225)
XLA Ops:
  16.8 5.1 %collective-permute-done.1 = s32[8,2,16]{2,1,0:T(2,128)S(1)} collective-permute-done((s32[8,2,16]{2,1,0:T(2,128)S(1)}, s32[8,2,16]{2,1,0:T(2,128)S(1)}, u32[]{:S(2)}, u32[]{:S(2)}) %collective-permute-start.1) | collective-permute-done | bytes 1056 | tf_op jit(solution)/shard_map/ppermute | solution.py:296
  36.3 4.6 collective-permute-done.7
  47.6 5.3 %collective-permute-done.9.refs_5_ = bf16[144,1152]{1,0:T(8,128)(2,1)S(1)} collective-permute-done((bf16[144,1152]{1,0:T(8,128)(2,1)}, bf16[144,1152]{1,0:T(8,128)(2,1)S(1)}, u32[]{:S(2)}, u32[]{:S(2)}) %collective-permute-start.9) | collective-permute-done | bytes 331808 | tf_op jit(solution)/shard_map/ppermute | solution.py:273
  78.8 7.6 %open_row.2 = (bf16[1024,1152]{1,0:T(8,128)(2,1)}, bf16[1024,864]{1,0:T(8,128)(2,1)}) custom-call(s32[1]{0:T(128)} %bitcast.place_ref.refs_0_, bf16[2048,1152]{1,0:T(8,128)(2,1)} %refs_6_.2, bf16[2048,1152]{1,0:T(8,128)(2,1)} %refs_6_.2, f32[8,4,2304]{2,1,0:T(4,128)} %unit_tables.2.tab0_ref.tab1_ref.refs_5_.refs_11_, ...), custom_call_target="tpu_custom_call" | custom-call | flops 1 | bytes 1 | tf_op jit(solution)/shard_map/open_row/pallas_call | solution.py:672
  92.6 11.7 %attend_forward.2 = (bf16[1024,288]{1,0:T(8,128)(2,1)}, bf16[512,1152]{1,0:T(8,128)(2,1)}, bf16[512,1152]{1,0:T(8,128)(2,1)}) custom-call(s32[1]{0:T(128)} %bitcast.place_ref.refs_0_, bf16[1024,864]{1,0:T(8,128)(2,1)} %get-tuple-element.347.refs_1_, s32[1,1024]{1,0:T(1,128)} %bitcast.204, bf16[1152,1152]{1,0:T(8,128)(2,1)} %place_pieces.3.w_ref.refs_3_.refs_7_), custom_call_target="tpu_custom_call" | custom-call | flops 1 | bytes 1 | tf_op jit(solution)/shard_map/attend_forward/pallas_call | solution.py:672
  112.7 7.6 %open_row.3 = (bf16[1024,1152]{1,0:T(8,128)(2,1)}, bf16[1024,864]{1,0:T(8,128)(2,1)}) custom-call(s32[1]{0:T(128)} %bitcast.place_ref.refs_0_, bf16[2048,1152]{1,0:T(8,128)(2,1)} %refs_6_.2, bf16[2048,1152]{1,0:T(8,128)(2,1)} %refs_6_.2, f32[8,4,2304]{2,1,0:T(4,128)} %unit_tables.2.tab0_ref.tab1_ref.refs_5_.refs_11_, ...), custom_call_target="tpu_custom_call" | custom-call | flops 1 | bytes 1 | tf_op jit(solution)/shard_map/open_row/pallas_call | solution.py:672
  124.3 11.7 %attend_forward.3 = (bf16[1024,288]{1,0:T(8,128)(2,1)}, bf16[512,1152]{1,0:T(8,128)(2,1)}, bf16[512,1152]{1,0:T(8,128)(2,1)}) custom-call(s32[1]{0:T(128)} %bitcast.place_ref.refs_0_, bf16[1024,864]{1,0:T(8,128)(2,1)} %get-tuple-element.361.refs_1_, s32[1,1024]{1,0:T(1,128)} %bitcast.202, bf16[1152,1152]{1,0:T(8,128)(2,1)} %place_pieces.3.w_ref.refs_3_.refs_7_), custom_call_target="tpu_custom_call" | custom-call | flops 1 | bytes 1 | tf_op jit(solution)/shard_map/attend_forward/pallas_call | solution.py:672
  153.0 5.2 %place_pieces.4.w_ref = bf16[1152,2304]{1,0:T(8,128)(2,1)} custom-call(s32[9]{0:T(128)} %fusion.53.at_ref, bf16[144,2304]{1,0:T(8,128)(2,1)} %copy-done.13, bf16[144,2304]{1,0:T(8,128)(2,1)} %copy-done.44, bf16[144,2304]{1,0:T(8,128)(2,1)} %copy-done.43, bf16[144,2304]{1,0:T(8,128)(2,1)} %collective-permute-done.21.refs_3_, ...), custom_call_target="tpu_custom_call" | custom-call | flops 1 | bytes 1 | tf_op jit(solution)/shard_map/place_pieces/pallas_call | solution.py:100
  159.4 7.1 %down_back.2 = (bf16[1024,1152]{1,0:T(8,128)(2,1)}, bf16[1024,1152]{1,0:T(8,128)(2,1)}) custom-call(s32[1]{0:T(128)} %bitcast.place_ref.refs_0_, bf16[2048,1152]{1,0:T(8,128)(2,1)} %refs_7_.1, bf16[2048,1152]{1,0:T(8,128)(2,1)} %refs_7_.1, f32[8,4,4608]{2,1,0:T(4,128)} %unit_tables.3.tab_ref.tab0_ref.tab1_ref.refs_5_.refs_12_, ...), custom_call_target="tpu_custom_call" | custom-call | flops 1 | bytes 1 | tf_op jit(solution)/shard_map/down_back/pallas_call | solution.py:672
  166.8 7.3 %down_back.3 = (bf16[1024,1152]{1,0:T(8,128)(2,1)}, bf16[1024,1152]{1,0:T(8,128)(2,1)}) custom-call(s32[1]{0:T(128)} %bitcast.place_ref.refs_0_, bf16[2048,1152]{1,0:T(8,128)(2,1)} %refs_7_.1, bf16[2048,1152]{1,0:T(8,128)(2,1)} %refs_7_.1, f32[8,4,4608]{2,1,0:T(4,128)} %unit_tables.3.tab_ref.tab0_ref.tab1_ref.refs_5_.refs_12_, ...), custom_call_target="tpu_custom_call" | custom-call | flops 1 | bytes 1 | tf_op jit(solution)/shard_map/down_back/pallas_call | solution.py:672
  174.1 4.7 %collective-permute-done.37.passed_ref = bf16[256,1152]{1,0:T(8,128)(2,1)S(1)} collective-permute-done((bf16[256,1152]{1,0:T(8,128)(2,1)S(1)}, bf16[256,1152]{1,0:T(8,128)(2,1)S(1)}, u32[]{:S(2)}, u32[]{:S(2)}) %collective-permute-start.37) | collective-permute-done | bytes 589856 | tf_op jit(solution)/shard_map/ppermute | solution.py:183
  185.1 15.0 %up_and_back.2 = (bf16[1024,1152]{1,0:T(8,128)(2,1)}, bf16[1024,1152]{1,0:T(8,128)(2,1)}, bf16[512,1152]{1,0:T(8,128)(2,1)}, bf16[512,1152]{1,0:T(8,128)(2,1)}, f32[2,8,1152]{2,1,0:T(8,128)}) custom-call(s32[1]{0:T(128)} %bitcast.place_ref.refs_0_, bf16[256,1152]{1,0:T(8,128)(2,1)} %get-tuple-element.392.a0_ref.refs_0_, bf16[256,1152]{1,0:T(8,128)(2,1)} %copy-done.25, ...), custom_call_target="tpu_custom_call" | custom-call | flops 1 | bytes 1 | tf_op jit(solution)/shard_map/up_and_back/pallas_call | solution.py:672
  200.8 7.7 %down.2 = (bf16[512,1152]{1,0:T(8,128)(2,1)}, bf16[512,1152]{1,0:T(8,128)(2,1)}) custom-call(s32[1]{0:T(128)} %bitcast.place_ref.refs_0_, bf16[1024,1152]{1,0:T(8,128)(2,1)} %get-tuple-element.415.m_ref.refs_11_, bf16[1152,2304]{1,0:T(8,128)(2,1)} %place_pieces.4.w_ref), custom_call_target="tpu_custom_call" | custom-call | flops 1 | bytes 1 | tf_op jit(solution)/shard_map/down/pallas_call | solution.py:672
  210.4 15.2 %up_and_back.3 = (bf16[1024,1152]{1,0:T(8,128)(2,1)}, bf16[1024,1152]{1,0:T(8,128)(2,1)}, bf16[512,1152]{1,0:T(8,128)(2,1)}, bf16[512,1152]{1,0:T(8,128)(2,1)}, f32[2,8,1152]{2,1,0:T(8,128)}) custom-call(s32[1]{0:T(128)} %bitcast.place_ref.refs_0_, bf16[256,1152]{1,0:T(8,128)(2,1)} %get-tuple-element.413.a0_ref.refs_5_, bf16[256,1152]{1,0:T(8,128)(2,1)} %copy-done.28, ...), custom_call_target="tpu_custom_call" | custom-call | flops 1 | bytes 1 | tf_op jit(solution)/shard_map/up_and_back/pallas_call | solution.py:672
  227.9 7.5 %down.3 = (bf16[512,1152]{1,0:T(8,128)(2,1)}, bf16[512,1152]{1,0:T(8,128)(2,1)}) custom-call(s32[1]{0:T(128)} %bitcast.place_ref.refs_0_, bf16[1024,1152]{1,0:T(8,128)(2,1)} %get-tuple-element.433.m_ref.refs_13_, bf16[1152,2304]{1,0:T(8,128)(2,1)} %place_pieces.4.w_ref), custom_call_target="tpu_custom_call" | custom-call | flops 1 | bytes 1 | tf_op jit(solution)/shard_map/down/pallas_call | solution.py:672
  235.3 6.5 %collective-permute-done.45.refs_3_ = bf16[256,1152]{1,0:T(8,128)(2,1)S(1)} collective-permute-done((bf16[256,1152]{1,0:T(8,128)(2,1)S(1)}, bf16[256,1152]{1,0:T(8,128)(2,1)S(1)}, u32[]{:S(2)}, u32[]{:S(2)}) %collective-permute-start.45) | collective-permute-done | bytes 589856 | tf_op jit(solution)/shard_map/ppermute | solution.py:183
  244.2 4.9 %second_norm.2 = (f32[256,1152]{1,0:T(8,128)}, bf16[256,1152]{1,0:T(8,128)(2,1)}, f32[16,1152]{1,0:T(8,128)}) custom-call(s32[1]{0:T(128)} %bitcast.place_ref.refs_0_, bf16[2048,1152]{1,0:T(8,128)(2,1)} %refs_7_.1, bf16[512,1152]{1,0:T(8,128)(2,1)} %get-tuple-element.429.kept_ref, bf16[512,1152]{1,0:T(8,128)(2,1)} %copy-done.12, ...), custom_call_target="tpu_custom_call" | custom-call | flops 1 | bytes 1 | tf_op jit(solution)/shard_map/second_norm/pallas_call | solution.py:672
  250.2 19.2 %grad_rest.1 = bf16[1152,2304]{1,0:T(8,128)(2,1)} custom-call(s32[1]{0:T(128)} %bitcast.place_ref.refs_0_, bf16[256,1152]{1,0:T(8,128)(2,1)} %get-tuple-element.392.a0_ref.refs_0_, bf16[256,1152]{1,0:T(8,128)(2,1)} %copy-done.25, bf16[256,1152]{1,0:T(8,128)(2,1)} %copy-done.24, bf16[256,1152]{1,0:T(8,128)(2,1)} %copy-done.26, ...), custom_call_target="tpu_custom_call" | custom-call | flops 1 | bytes 1 | tf_op jit(solution)/shard_map/grad_rest/pallas_call | solution.py:672
  278.3 5.0 %second_norm.3 = (f32[256,1152]{1,0:T(8,128)}, bf16[256,1152]{1,0:T(8,128)(2,1)}, f32[16,1152]{1,0:T(8,128)}) custom-call(s32[1]{0:T(128)} %bitcast.place_ref.refs_0_, bf16[2048,1152]{1,0:T(8,128)(2,1)} %refs_7_.1, bf16[512,1152]{1,0:T(8,128)(2,1)} %get-tuple-element.452.kept_ref, bf16[512,1152]{1,0:T(8,128)(2,1)} %copy-done.6, ...), custom_call_target="tpu_custom_call" | custom-call | flops 1 | bytes 1 | tf_op jit(solution)/shard_map/second_norm/pallas_call | solution.py:672
  284.3 20.9 %attend_backward.2 = (bf16[1024,864]{1,0:T(8,128)(2,1)}, bf16[512,1152]{1,0:T(8,128)(2,1)}, bf16[512,1152]{1,0:T(8,128)(2,1)}, f32[16,864]{1,0:T(8,128)}) custom-call(s32[1]{0:T(128)} %bitcast.place_ref.refs_0_, bf16[1024,864]{1,0:T(8,128)(2,1)} %get-tuple-element.347.refs_1_, bf16[256,1152]{1,0:T(8,128)(2,1)} %get-tuple-element.454.refs_2_.refs_4_, ...), custom_call_target="tpu_custom_call" | custom-call | flops 1 | bytes 1 | tf_op jit(solution)/shard_map/attend_backward/pallas_call | solution.py:672
  306.8 5.4 %out_tokens.1 = (bf16[528,1152]{1,0:T(8,128)(2,1)}, f32[16,1152]{1,0:T(8,128)}) custom-call(s32[1]{0:T(128)} %bitcast.place_ref.refs_0_, f32[2,1152]{1,0:T(2,128)} %bias_ref.5, bf16[2048,1152]{1,0:T(8,128)(2,1)} %refs_7_.1, bf16[512,1152]{1,0:T(8,128)(2,1)} %get-tuple-element.437.refs_1_, bf16[512,1152]{1,0:T(8,128)(2,1)} %copy-done.2, ...), custom_call_target="tpu_custom_call" | custom-call | flops 1 | bytes 1 | tf_op jit(solution)/shard_map/out_tokens/pallas_call | solution.py:672
  321.1 20.7 %attend_backward.3 = (bf16[1024,864]{1,0:T(8,128)(2,1)}, bf16[512,1152]{1,0:T(8,128)(2,1)}, bf16[512,1152]{1,0:T(8,128)(2,1)}, f32[16,864]{1,0:T(8,128)}) custom-call(s32[1]{0:T(128)} %bitcast.place_ref.refs_0_, bf16[1024,864]{1,0:T(8,128)(2,1)} %get-tuple-element.361.refs_1_, bf16[256,1152]{1,0:T(8,128)(2,1)} %get-tuple-element.471.refs_2_.refs_9_, ...), custom_call_target="tpu_custom_call" | custom-call | flops 1 | bytes 1 | tf_op jit(solution)/shard_map/attend_backward/pallas_call | solution.py:672
  349.5 13.2 %grad_first.1 = bf16[1152,1152]{1,0:T(8,128)(2,1)} custom-call(s32[1]{0:T(128)} %bitcast.place_ref.refs_0_, bf16[1024,1152]{1,0:T(8,128)(2,1)} %get-tuple-element.496.refs_0_, bf16[1024,864]{1,0:T(8,128)(2,1)} %get-tuple-element.497.refs_1_, bf16[1024,1152]{1,0:T(8,128)(2,1)} %get-tuple-element.498.refs_2_, bf16[1024,864]{1,0:T(8,128)(2,1)} %get-tuple-element.499.refs_3_, ...), custom_call_target="tpu_custom_call" | custom-call | flops 1 | bytes 1 | tf_op jit(solution)/shard_map/grad_first/pallas_call | solution.py:672
  373.4 4.8 %place_pieces.5 = bf16[2048,1152]{1,0:T(8,128)(2,1)} custom-call(s32[8]{0:T(128)} %stack.109.at_ref, bf16[528,1152]{1,0:T(8,128)(2,1)} %get-tuple-element.494.refs_0_, bf16[528,1152]{1,0:T(8,128)(2,1)} %collective-permute-done.65.refs_1_, bf16[528,1152]{1,0:T(8,128)(2,1)} %collective-permute-done.61.refs_2_, bf16[528,1152]{1,0:T(8,128)(2,1)} %copy-done.34), custom_call_target="tpu_custom_call" | custom-call | flops 1 | bytes 1 | tf_op jit(solution)/shard_map/place_pieces/pallas_call | solution.py:100
  381.8 6.5 %third_norm.1 = (bf16[512,1152]{1,0:T(8,128)(2,1)}, f32[16,1152]{1,0:T(8,128)}) custom-call(s32[1]{0:T(128)} %bitcast.place_ref.refs_0_, bf16[2048,1152]{1,0:T(8,128)(2,1)} %refs_6_.2, bf16[512,1152]{1,0:T(8,128)(2,1)} %get-tuple-element.492.refs_1_, bf16[512,1152]{1,0:T(8,128)(2,1)} %copy-done.15, bf16[256,1152]{1,0:T(8,128)(2,1)} %copy-done.50, ...), custom_call_target="tpu_custom_call" | custom-call | flops 1 | bytes 1 | tf_op jit(solution)/shard_map/third_norm/pallas_call | solution.py:672
  406.1 4.7 %adam_up.1 = (f32[15,144,288]{2,1,0:T(8,128)}, f32[15,144,288]{2,1,0:T(8,128)}, f32[15,144,288]{2,1,0:T(8,128)}, f32[15,144,288]{2,1,0:T(8,128)}) custom-call(s32[1]{0:T(128)} %bitcast.place_ref.refs_0_, bf16[144,2304]{1,0:T(8,128)(2,1)} %add_convert_fusion.refs_0_, f32[15,144,288]{2,1,0:T(8,128)} %refs_3_.6, f32[15,144,288]{2,1,0:T(8,128)} %refs_4_.7, ...), custom_call_target="tpu_custom_call" | custom-call | flops 1 | bytes 1 | tf_op jit(solution)/shard_map/adam_up/pallas_call | solution.py:672
  415.8 4.9 %adam_down.1 = (f32[5,144,288]{2,1,0:T(8,128)}, f32[5,144,288]{2,1,0:T(8,128)}, f32[5,144,288]{2,1,0:T(8,128)}, f32[5,144,288]{2,1,0:T(8,128)}) custom-call(s32[1]{0:T(128)} %bitcast.place_ref.refs_0_, bf16[144,2304]{1,0:T(8,128)(2,1)} %add_convert_fusion.refs_0_, f32[5,144,288]{2,1,0:T(8,128)} %bitcast.176, f32[5,144,288]{2,1,0:T(8,128)} %bitcast.178, ...), custom_call_target="tpu_custom_call" | custom-call | flops 1 | bytes 1 | tf_op jit(solution)/shard_map/adam_down/pallas_call | solution.py:672
  423.5 6.1 %collective-permute-done.81 = bf16[4,144,288]{2,1,0:T(8,128)(2,1)S(1)} collective-permute-done((bf16[4,144,288]{2,1,0:T(8,128)(2,1)S(1)}, bf16[4,144,288]{2,1,0:T(8,128)(2,1)S(1)}, u32[]{:S(2)}, u32[]{:S(2)}) %collective-permute-start.81) | collective-permute-done | bytes 331808 | tf_op jit(solution)/shard_map/ppermute | solution.py:217
  434.7 5.4 %adam_far.1 = (f32[15,144,288]{2,1,0:T(8,128)}, f32[15,144,288]{2,1,0:T(8,128)}, f32[15,144,288]{2,1,0:T(8,128)}, f32[15,144,288]{2,1,0:T(8,128)}) custom-call(s32[1]{0:T(128)} %bitcast.place_ref.refs_0_, bf16[256,144]{1,0:T(8,128)(2,1)} %copy-done.30, ...), custom_call_target="tpu_custom_call", output_to_operand_aliasing={{0}: (7, {}), {1}: (8, {}), {2}: (9, {}), {3}: (10, {})} | custom-call | flops 1 | bytes 1 | tf_op jit(solution)/shard_map/adam_far/pallas_call | solution.py:672
  442.9 4.6 adam_first.1
  451.2 6.1 %widen_rows.1 = f32[2048,1152]{1,0:T(8,128)} custom-call(s32[1]{0:T(128)} %bitcast.place_ref.refs_0_, bf16[512,1152]{1,0:T(8,128)(2,1)} %get-tuple-element.565.refs_0_, bf16[512,1152]{1,0:T(8,128)(2,1)} %collective-permute-done.84.refs_1_, bf16[512,1152]{1,0:T(8,128)(2,1)} %collective-permute-done.86.refs_2_, bf16[512,1152]{1,0:T(8,128)(2,1)} %collective-permute-done.87.refs_3_), custom_call_target="tpu_custom_call" | custom-call | flops 1 | bytes 1 | tf_op jit(solution)/shard_map/widen_rows/pallas_call | solution.py:672
  459.0 5.5 %adam_near.1 = (f32[15,144,288]{2,1,0:T(8,128)}, f32[15,144,288]{2,1,0:T(8,128)}, f32[15,144,288]{2,1,0:T(8,128)}, f32[15,144,288]{2,1,0:T(8,128)}) custom-call(s32[1]{0:T(128)} %bitcast.place_ref.refs_0_, bf16[256,144]{1,0:T(8,128)(2,1)} %copy-done.30, ...), custom_call_target="tpu_custom_call", output_to_operand_aliasing={{0}: (8, {}), {1}: (9, {}), {2}: (10, {}), {3}: (11, {})} | custom-call | flops 1 | bytes 1 | tf_op jit(solution)/shard_map/adam_near/pallas_call | solution.py:672
  (534 shorter events, 194.6 us)
Async XLA Ops:
  67.2 22.9 %collective-permute-start.19 = (bf16[144,2304]{1,0:T(8,128)(2,1)S(1)}, bf16[144,2304]{1,0:T(8,128)(2,1)S(1)}, u32[]{:S(2)}, u32[]{:S(2)}) collective-permute-start(bf16[144,2304]{1,0:T(8,128)(2,1)S(1)} %concatenate.75.refs_0_), channel_id=1, source_target_pairs={{8,0},{16,8},{24,16},{28,24},{20,28},{12,20},{4,12},{0,4},{9,1},{1... | collective-permute-start | bytes 1990664 | tf_op jit(solution)/shard_map/ppermute | solution.py:274
  68.6 21.5 %collective-permute-start.18 = (bf16[144,2304]{1,0:T(8,128)(2,1)S(1)}, bf16[144,2304]{1,0:T(8,128)(2,1)S(1)}, u32[]{:S(2)}, u32[]{:S(2)}) collective-permute-start(bf16[144,2304]{1,0:T(8,128)(2,1)S(1)} %concatenate.75.refs_0_), channel_id=1, source_target_pairs={{0,8},{8,16},{16,24},{24,28},{28,20},{20,12},{12,4},{4,0},{1,9},{9... | collective-permute-start | bytes 1990664 | tf_op jit(solution)/shard_map/ppermute | solution.py:273
  69.2 20.9 %collective-permute-start.17 = (bf16[4,32,1152]{2,1,0:T(8,128)(2,1)S(1)}, bf16[4,32,1152]{2,1,0:T(8,128)(2,1)S(1)}, u32[]{:S(2)}, u32[]{:S(2)}) collective-permute-start(bf16[4,32,1152]{2,1,0:T(8,128)(2,1)S(1)} %dynamic-slice_bitcast_fusion), channel_id=1, source_target_pairs={{0,4},{4,0},{8,12},{12,8},{16,20},{20,16},{24,28},{28,24},{1,5},{5... | collective-permute-start | bytes 884744 | tf_op jit(solution)/shard_map/ppermute | solution.py:252
  90.1 18.7 %collective-permute-start.21 = (bf16[144,2304]{1,0:T(8,128)(2,1)S(1)}, bf16[144,2304]{1,0:T(8,128)(2,1)}, u32[]{:S(2)}, u32[]{:S(2)}) collective-permute-start(bf16[144,2304]{1,0:T(8,128)(2,1)S(1)} %collective-permute-done.18.refs_1_), channel_id=1, source_target_pairs={{0,8},{8,16},{16,24},{24,28},{28,20},{20,12},{12,4},{4,0},{1,9},{9... | collective-permute-start | bytes 1990664 | tf_op jit(solution)/shard_map/ppermute | solution.py:273
  90.2 18.7 %collective-permute-start.22 = (bf16[144,2304]{1,0:T(8,128)(2,1)S(1)}, bf16[144,2304]{1,0:T(8,128)(2,1)}, u32[]{:S(2)}, u32[]{:S(2)}) collective-permute-start(bf16[144,2304]{1,0:T(8,128)(2,1)S(1)} %collective-permute-done.19.refs_2_), channel_id=1, source_target_pairs={{8,0},{16,8},{24,16},{28,24},{20,28},{12,20},{4,12},{0,4},{9,1},{1... | collective-permute-start | bytes 1990664 | tf_op jit(solution)/shard_map/ppermute | solution.py:274
  110.5 25.6 %collective-permute-start.26 = (bf16[144,2304]{1,0:T(8,128)(2,1)}, bf16[144,2304]{1,0:T(8,128)(2,1)}, u32[]{:S(2)}, u32[]{:S(2)}) collective-permute-start(bf16[144,2304]{1,0:T(8,128)(2,1)} %collective-permute-done.21.refs_3_), channel_id=1, source_target_pairs={{0,8},{8,16},{16,24},{24,28},{28,20},{20,12},{12,4},{4,0},{1,9},{9... | collective-permute-start | bytes 1990664 | tf_op jit(solution)/shard_map/ppermute | solution.py:273
  110.6 25.5 %collective-permute-start.27 = (bf16[144,2304]{1,0:T(8,128)(2,1)}, bf16[144,2304]{1,0:T(8,128)(2,1)S(1)}, u32[]{:S(2)}, u32[]{:S(2)}) collective-permute-start(bf16[144,2304]{1,0:T(8,128)(2,1)} %collective-permute-done.22.refs_4_), channel_id=1, source_target_pairs={{8,0},{16,8},{24,16},{28,24},{20,28},{12,20},{4,12},{0,4},{9,1},{1... | collective-permute-start | bytes 1990664 | tf_op jit(solution)/shard_map/ppermute | solution.py:274
  158.4 20.4 %collective-permute-start.37 = (bf16[256,1152]{1,0:T(8,128)(2,1)S(1)}, bf16[256,1152]{1,0:T(8,128)(2,1)S(1)}, u32[]{:S(2)}, u32[]{:S(2)}) collective-permute-start(bf16[256,1152]{1,0:T(8,128)(2,1)S(1)} %add_convert_fusion.12), channel_id=1, source_target_pairs={{0,2},{1,3},{2,0},{3,1},{4,6},{5,7},{6,4},{7,5},{8,10},{9,11},{10,... | collective-permute-start | bytes 1769480 | tf_op jit(solution)/shard_map/ppermute | solution.py:183
  183.2 16.9 %collective-permute-start.38 = (bf16[256,1152]{1,0:T(8,128)(2,1)}, bf16[256,1152]{1,0:T(8,128)(2,1)S(1)}, u32[]{:S(2)}, u32[]{:S(2)}) collective-permute-start(bf16[256,1152]{1,0:T(8,128)(2,1)} %get-tuple-element.413.a0_ref.refs_5_), channel_id=1, source_target_pairs={{0,2},{1,3},{2,0},{3,1},{4,6},{5,7},{6,4},{7,5},{8,10},{9,11},{10,... | collective-permute-start | bytes 1769480 | tf_op jit(solution)/shard_map/ppermute | solution.py:192
  208.5 17.2 %collective-permute-start.43 = (bf16[512,1152]{1,0:T(8,128)(2,1)}, bf16[512,1152]{1,0:T(8,128)(2,1)S(1)}, u32[]{:S(2)}, u32[]{:S(2)}) collective-permute-start(bf16[512,1152]{1,0:T(8,128)(2,1)} %get-tuple-element.431), channel_id=1, source_target_pairs={{0,1},{1,0},{2,3},{3,2},{4,5},{5,4},{6,7},{7,6},{8,9},{9,8},{10,11... | collective-permute-start | bytes 3538952 | tf_op jit(solution)/shard_map/ppermute | solution.py:177
  243.1 26.3 %collective-permute-start.47 = (bf16[256,1152]{1,0:T(8,128)(2,1)}, bf16[256,1152]{1,0:T(8,128)(2,1)}, u32[]{:S(2)}, u32[]{:S(2)}) collective-permute-start(bf16[256,1152]{1,0:T(8,128)(2,1)} %add_convert_fusion.9), channel_id=1, source_target_pairs={{0,2},{1,3},{2,0},{3,1},{4,6},{5,7},{6,4},{7,5},{8,10},{9,11},{10,... | collective-permute-start | bytes 1769480 | tf_op jit(solution)/shard_map/ppermute | solution.py:183
  249.2 20.2 %collective-permute-start.49 = (bf16[256,1152]{1,0:T(8,128)(2,1)}, bf16[256,1152]{1,0:T(8,128)(2,1)S(1)}, u32[]{:S(2)}, u32[]{:S(2)}) collective-permute-start(bf16[256,1152]{1,0:T(8,128)(2,1)} %get-tuple-element.454.refs_2_.refs_4_), channel_id=1, source_target_pairs={{0,1},{1,0},{2,3},{3,2},{4,5},{5,4},{6,7},{7,6},{8,9},{9,8},{10,11... | collective-permute-start | bytes 1769480 | tf_op jit(solution)/shard_map/ppermute | solution.py:193
  249.3 22.2 %collective-permute-start.48 = (bf16[256,1152]{1,0:T(8,128)(2,1)}, bf16[256,1152]{1,0:T(8,128)(2,1)S(1)}, u32[]{:S(2)}, u32[]{:S(2)}) collective-permute-start(bf16[256,1152]{1,0:T(8,128)(2,1)} %get-tuple-element.454.refs_2_.refs_4_), channel_id=1, source_target_pairs={{0,2},{1,3},{2,0},{3,1},{4,6},{5,7},{6,4},{7,5},{8,10},{9,11},{10,... | collective-permute-start | bytes 1769480 | tf_op jit(solution)/shard_map/ppermute | solution.py:192
  274.0 31.3 %collective-permute-start.52 = (bf16[144,2304]{1,0:T(8,128)(2,1)}, bf16[144,2304]{1,0:T(8,128)(2,1)S(1)}, u32[]{:S(2)}, u32[]{:S(2)}) collective-permute-start(bf16[144,2304]{1,0:T(8,128)(2,1)} %get-tuple-element.626), channel_id=1, source_target_pairs={{8,0},{16,8},{24,16},{28,24},{20,28},{12,20},{4,12},{0,4},{9,1},{1... | collective-permute-start | bytes 1990664 | tf_op jit(solution)/shard_map/ppermute | solution.py:153
  274.3 31.0 %collective-permute-start.51 = (bf16[144,2304]{1,0:T(8,128)(2,1)S(1)}, bf16[144,2304]{1,0:T(8,128)(2,1)S(1)}, u32[]{:S(2)}, u32[]{:S(2)}) collective-permute-start(bf16[144,2304]{1,0:T(8,128)(2,1)S(1)} %get-tuple-element.627), channel_id=1, source_target_pairs={{0,8},{8,16},{16,24},{24,28},{28,20},{20,12},{12,4},{4,0},{1,9},{9... | collective-permute-start | bytes 1990664 | tf_op jit(solution)/shard_map/ppermute | solution.py:151
  277.1 28.1 %collective-permute-start.55 = (bf16[256,1152]{1,0:T(8,128)(2,1)}, bf16[256,1152]{1,0:T(8,128)(2,1)S(1)}, u32[]{:S(2)}, u32[]{:S(2)}) collective-permute-start(bf16[256,1152]{1,0:T(8,128)(2,1)} %add_convert_fusion.8), channel_id=1, source_target_pairs={{0,2},{1,3},{2,0},{3,1},{4,6},{5,7},{6,4},{7,5},{8,10},{9,11},{10,... | collective-permute-start | bytes 1769480 | tf_op jit(solution)/shard_map/ppermute | solution.py:183
  283.2 22.1 %collective-permute-start.54 = (bf16[256,1152]{1,0:T(8,128)(2,1)}, bf16[256,1152]{1,0:T(8,128)(2,1)S(1)}, u32[]{:S(2)}, u32[]{:S(2)}) collective-permute-start(bf16[256,1152]{1,0:T(8,128)(2,1)} %get-tuple-element.471.refs_2_.refs_9_), channel_id=1, source_target_pairs={{0,1},{1,0},{2,3},{3,2},{4,5},{5,4},{6,7},{7,6},{8,9},{9,8},{10,11... | collective-permute-start | bytes 1769480 | tf_op jit(solution)/shard_map/ppermute | solution.py:193
  283.3 22.0 %collective-permute-start.53 = (bf16[256,1152]{1,0:T(8,128)(2,1)}, bf16[256,1152]{1,0:T(8,128)(2,1)S(1)}, u32[]{:S(2)}, u32[]{:S(2)}) collective-permute-start(bf16[256,1152]{1,0:T(8,128)(2,1)} %get-tuple-element.471.refs_2_.refs_9_), channel_id=1, source_target_pairs={{0,2},{1,3},{2,0},{3,1},{4,6},{5,7},{6,4},{7,5},{8,10},{9,11},{10,... | collective-permute-start | bytes 1769480 | tf_op jit(solution)/shard_map/ppermute | solution.py:192
  312.2 29.7 %collective-permute-start.61 = (bf16[528,1152]{1,0:T(8,128)(2,1)}, bf16[528,1152]{1,0:T(8,128)(2,1)}, u32[]{:S(2)}, u32[]{:S(2)}) collective-permute-start(bf16[528,1152]{1,0:T(8,128)(2,1)} %get-tuple-element.494.refs_0_), channel_id=1, source_target_pairs={{0,1},{1,0},{2,3},{3,2},{4,5},{5,4},{6,7},{7,6},{8,9},{9,8},{10,11... | collective-permute-start | bytes 3649544 | tf_op jit(solution)/shard_map/ppermute | solution.py:193
  315.9 26.0 %collective-permute-start.59 = (bf16[144,2304]{1,0:T(8,128)(2,1)}, bf16[144,2304]{1,0:T(8,128)(2,1)S(1)}, u32[]{:S(2)}, u32[]{:S(2)}) collective-permute-start(bf16[144,2304]{1,0:T(8,128)(2,1)} %get-tuple-element.624), channel_id=1, source_target_pairs={{8,0},{16,8},{24,16},{28,24},{20,28},{12,20},{4,12},{0,4},{9,1},{1... | collective-permute-start | bytes 1990664 | tf_op jit(solution)/shard_map/ppermute | solution.py:153
  316.2 25.6 %collective-permute-start.58 = (bf16[144,2304]{1,0:T(8,128)(2,1)}, bf16[144,2304]{1,0:T(8,128)(2,1)}, u32[]{:S(2)}, u32[]{:S(2)}) collective-permute-start(bf16[144,2304]{1,0:T(8,128)(2,1)} %get-tuple-element.625), channel_id=1, source_target_pairs={{0,8},{8,16},{16,24},{24,28},{28,20},{20,12},{12,4},{4,0},{1,9},{9... | collective-permute-start | bytes 1990664 | tf_op jit(solution)/shard_map/ppermute | solution.py:151
  319.1 22.8 %collective-permute-start.60 = (bf16[256,1152]{1,0:T(8,128)(2,1)}, bf16[256,1152]{1,0:T(8,128)(2,1)S(1)}, u32[]{:S(2)}, u32[]{:S(2)}) collective-permute-start(bf16[256,1152]{1,0:T(8,128)(2,1)} %add_convert_fusion.7), channel_id=1, source_target_pairs={{0,2},{1,3},{2,0},{3,1},{4,6},{5,7},{6,4},{7,5},{8,10},{9,11},{10,... | collective-permute-start | bytes 1769480 | tf_op jit(solution)/shard_map/ppermute | solution.py:183
  320.2 42.5 %collective-permute-start.65 = (bf16[528,1152]{1,0:T(8,128)(2,1)S(1)}, bf16[528,1152]{1,0:T(8,128)(2,1)}, u32[]{:S(2)}, u32[]{:S(2)}) collective-permute-start(bf16[528,1152]{1,0:T(8,128)(2,1)S(1)} %copy-done.33), channel_id=1, source_target_pairs={{0,2},{1,3},{2,0},{3,1},{4,6},{5,7},{6,4},{7,5},{8,10},{9,11},{10,... | collective-permute-start | bytes 3649544 | tf_op jit(solution)/shard_map/ppermute | solution.py:192
  342.9 20.6 %collective-permute-start.64 = (bf16[512,1152]{1,0:T(8,128)(2,1)}, bf16[512,1152]{1,0:T(8,128)(2,1)S(1)}, u32[]{:S(2)}, u32[]{:S(2)}) collective-permute-start(bf16[512,1152]{1,0:T(8,128)(2,1)} %get-tuple-element.504), channel_id=1, source_target_pairs={{0,1},{1,0},{2,3},{3,2},{4,5},{5,4},{6,7},{7,6},{8,9},{9,8},{10,11... | collective-permute-start | bytes 3538952 | tf_op jit(solution)/shard_map/ppermute | solution.py:177
  345.9 17.6 %collective-permute-start.63 = (bf16[144,2304]{1,0:T(8,128)(2,1)}, bf16[144,2304]{1,0:T(8,128)(2,1)}, u32[]{:S(2)}, u32[]{:S(2)}) collective-permute-start(bf16[144,2304]{1,0:T(8,128)(2,1)} %get-tuple-element.622), channel_id=1, source_target_pairs={{8,0},{16,8},{24,16},{28,24},{20,28},{12,20},{4,12},{0,4},{9,1},{1... | collective-permute-start | bytes 1990664 | tf_op jit(solution)/shard_map/ppermute | solution.py:153
  346.2 17.2 %collective-permute-start.62 = (bf16[144,2304]{1,0:T(8,128)(2,1)S(1)}, bf16[144,2304]{1,0:T(8,128)(2,1)}, u32[]{:S(2)}, u32[]{:S(2)}) collective-permute-start(bf16[144,2304]{1,0:T(8,128)(2,1)S(1)} %get-tuple-element.623), channel_id=1, source_target_pairs={{0,8},{8,16},{16,24},{24,28},{28,20},{20,12},{12,4},{4,0},{1,9},{9... | collective-permute-start | bytes 1990664 | tf_op jit(solution)/shard_map/ppermute | solution.py:151
  364.4 17.5 %collective-permute-start.69 = (bf16[256,1152]{1,0:T(8,128)(2,1)S(1)}, bf16[256,1152]{1,0:T(8,128)(2,1)}, u32[]{:S(2)}, u32[]{:S(2)}) collective-permute-start(bf16[256,1152]{1,0:T(8,128)(2,1)S(1)} %add_convert_fusion.6), channel_id=1, source_target_pairs={{0,2},{1,3},{2,0},{3,1},{4,6},{5,7},{6,4},{7,5},{8,10},{9,11},{10,... | collective-permute-start | bytes 1769480 | tf_op jit(solution)/shard_map/ppermute | solution.py:183
  367.5 20.8 %collective-permute-start.71 = (bf16[144,1152]{1,0:T(8,128)(2,1)}, bf16[144,1152]{1,0:T(8,128)(2,1)}, u32[]{:S(2)}, u32[]{:S(2)}) collective-permute-start(bf16[144,1152]{1,0:T(8,128)(2,1)} %get-tuple-element.632), channel_id=1, source_target_pairs={{8,0},{16,8},{24,16},{28,24},{20,28},{12,20},{4,12},{0,4},{9,1},{1... | collective-permute-start | bytes 995336 | tf_op jit(solution)/shard_map/ppermute | solution.py:153
  369.1 19.2 %collective-permute-start.70 = (bf16[144,1152]{1,0:T(8,128)(2,1)}, bf16[144,1152]{1,0:T(8,128)(2,1)}, u32[]{:S(2)}, u32[]{:S(2)}) collective-permute-start(bf16[144,1152]{1,0:T(8,128)(2,1)} %get-tuple-element.633), channel_id=1, source_target_pairs={{0,8},{8,16},{16,24},{24,28},{28,20},{20,12},{12,4},{4,0},{1,9},{9... | collective-permute-start | bytes 995336 | tf_op jit(solution)/shard_map/ppermute | solution.py:151
  371.8 20.9 %collective-permute-start.72 = (bf16[144,2304]{1,0:T(8,128)(2,1)}, bf16[144,2304]{1,0:T(8,128)(2,1)S(1)}, u32[]{:S(2)}, u32[]{:S(2)}) collective-permute-start(bf16[144,2304]{1,0:T(8,128)(2,1)} %add_convert_fusion.1), channel_id=1, source_target_pairs={{0,8},{8,16},{16,24},{24,28},{28,20},{20,12},{12,4},{4,0},{1,9},{9... | collective-permute-start | bytes 1990664 | tf_op jit(solution)/shard_map/ppermute | solution.py:151
  402.6 37.6 %collective-permute-start.84 = (bf16[512,1152]{1,0:T(8,128)(2,1)}, bf16[512,1152]{1,0:T(8,128)(2,1)}, u32[]{:S(2)}, u32[]{:S(2)}) collective-permute-start(bf16[512,1152]{1,0:T(8,128)(2,1)} %get-tuple-element.565.refs_0_), channel_id=1, source_target_pairs={{0,2},{1,3},{2,0},{3,1},{4,6},{5,7},{6,4},{7,5},{8,10},{9,11},{10,... | collective-permute-start | bytes 3538952 | tf_op jit(solution)/shard_map/ppermute | solution.py:192
  420.8 26.8 %collective-permute-start.86 = (bf16[512,1152]{1,0:T(8,128)(2,1)}, bf16[512,1152]{1,0:T(8,128)(2,1)}, u32[]{:S(2)}, u32[]{:S(2)}) collective-permute-start(bf16[512,1152]{1,0:T(8,128)(2,1)} %get-tuple-element.565.refs_0_), channel_id=1, source_target_pairs={{0,1},{1,0},{2,3},{3,2},{4,5},{5,4},{6,7},{7,6},{8,9},{9,8},{10,11... | collective-permute-start | bytes 3538952 | tf_op jit(solution)/shard_map/ppermute | solution.py:193
  (162 other events, 1358.9 us)
